TPU v7x, 32 devices: a whole 2x2x4 slice. The times are simulated.
32 devices in a mesh: grp: 8 (over z, x), seq: 4 (over y, core).
Axes of the slice: x: 2, y: 2, z: 4, core: 2. Of those that a mesh axis runs over, the one named last changes fastest.
Arguments:
- tokens: bfloat16 [4096, 1024], P(('grp', 'seq')), may hold values from -6 to 6
- lengths: int32 [8, 3], P('grp'), may hold values from 1 to 128, 256 in all within a row
- cotangent: float32 [4096, 1024], P(('grp', 'seq')), may hold values from -6 to 6
- norm_gain: bfloat16 [2, 2, 1024], P(None, None, 'grp'), may hold values from 0.5 to 1.5
- norm_bias: bfloat16 [2, 2, 1024], P(None, None, 'grp'), may hold values from -2 to 2
- in_weight: bfloat16 [2, 1024, 3072], P(None, None, 'grp'), may hold values from -0.1875 to 0.1875
- in_bias: bfloat16 [2, 3072], P(None, 'grp'), may hold values from -2 to 2
- conv_weight: bfloat16 [2, 3, 3072], P(None, None, 'grp'), may hold values from -3 to 3
- conv_bias: bfloat16 [2, 3072], P(None, 'grp'), may hold values from -2 to 2
- skip_bias: bfloat16 [2, 1024], P(None, 'grp'), may hold values from -4 to 4
- filt_out: bfloat16 [2, 64, 1024], P(None, None, 'grp'), may hold values from -0.25 to 0.25
- out_weight: bfloat16 [2, 1024, 1024], P(None, None, 'grp'), may hold values from -0.1875 to 0.1875
- up_weight: bfloat16 [2, 1024, 4096], P(None, None, 'grp'), may hold values from -0.1875 to 0.1875
- up_bias: bfloat16 [2, 4096], P(None, 'grp'), may hold values from -2 to 2
- down_weight: bfloat16 [2, 4096, 1024], P(None, None, 'grp'), may hold values from -0.09375 to 0.09375
- branch_bias: bfloat16 [2, 2, 1024], P(None, None, 'grp'), may hold values from -2 to 2
- filt_in: float32 [2, 33, 64], replicated, may hold values from -1 to 1
- filt_mid: float32 [2, 64, 64], replicated, may hold values from -0.75 to 0.75
- filt_bias: float32 [2, 2, 64], replicated, may hold values from -3.140625 to 3.140625
- sine_freq: float32 [2, 2, 64], replicated, may hold values from 0.5 to 3
Outputs:
- activations: float32 [4096, 1024], P(('grp', 'seq'))
- input_grad: float32 [4096, 1024], P(('grp', 'seq'))
- norm_gain_grad: float32 [2, 2, 1024], P(None, None, 'grp')
- norm_bias_grad: float32 [2, 2, 1024], P(None, None, 'grp')
- in_weight_grad: float32 [2, 1024, 3072], P(None, None, 'grp')
- in_bias_grad: float32 [2, 3072], P(None, 'grp')
- conv_weight_grad: float32 [2, 3, 3072], P(None, None, 'grp')
- conv_bias_grad: float32 [2, 3072], P(None, 'grp')
- skip_bias_grad: float32 [2, 1024], P(None, 'grp')
- filt_out_grad: float32 [2, 64, 1024], P(None, None, 'grp')
- out_weight_grad: float32 [2, 1024, 1024], P(None, None, 'grp')
- up_weight_grad: float32 [2, 1024, 4096], P(None, None, 'grp')
- up_bias_grad: float32 [2, 4096], P(None, 'grp')
- down_weight_grad: float32 [2, 4096, 1024], P(None, None, 'grp')
- branch_bias_grad: float32 [2, 2, 1024], P(None, None, 'grp')
- filt_in_grad: float32 [2, 33, 64], replicated
- filt_mid_grad: float32 [2, 64, 64], replicated
- filt_bias_grad: float32 [2, 2, 64], replicated
- sine_freq_grad: float32 [2, 2, 64], replicated
Inputs may be any that keep to these rules, and one draw needn't show every extreme that they name: Row g lists the lengths of group g's 3 short sequences in order; they sum to 256, and the longest of each row is 128.
All inputs are finite; a program needn't handle non-finite values.
Results may differ from a plain program's by a relative error of at most 0.022.
Values may be sent and summed in bfloat16 or wider, within the bound.
No kernel may reach another device: no remote copies, remote signals or barrier semaphores. Data moves between devices by JAX's collectives and lax.ppermute only.
A program may use at most 384 MiB of HBM per device.

v0:
```python
from functools import partial
import math

import jax
import jax.numpy as jnp
from jax import lax
from jax.sharding import PartitionSpec as P

SHORT = 1024


EPS = 1e-05
HIGH = lax.Precision.HIGHEST
FAST = math.log(0.01) / 0.3
SLOW = math.log(0.01) / 1.5


def norm_rows(value, gain, shift):
    center = value - jnp.mean(value, axis=-1, keepdims=True)
    spread = jnp.mean(center * center, axis=-1, keepdims=True)
    return center * lax.rsqrt(spread + EPS) * gain + shift


def exact_gelu(value):
    return jax.nn.gelu(value, approximate=False)


def positions(length):
    index = jnp.arange(length, dtype=jnp.int32).astype(jnp.float32)
    tpos = index / (length - 1)
    bands = 0.0001 + (15.0 - 0.0001) * jnp.arange(16, dtype=jnp.int32).astype(jnp.float32) / 15.0
    angle = 2.0 * math.pi / length * index[:, None] * bands[None, :]
    return (jnp.concatenate([tpos[:, None], jnp.cos(angle), -jnp.sin(angle)], axis=1), tpos)


def rates(first, count, width):
    channel = (first + jnp.arange(count, dtype=jnp.int32)).astype(jnp.float32)
    return jnp.abs(FAST + (SLOW - FAST) * channel / (width - 1))


def doc_begin(lens, total):
    starts = total // 2 + jnp.cumsum(lens) - lens
    every = jnp.concatenate([jnp.zeros((1,), jnp.int32), starts])
    where_at = jnp.arange(total, dtype=jnp.int32)
    begin = jnp.max(jnp.where(every[:, None] <= where_at[None, :], every[:, None], 0), axis=0)
    return (starts, begin)


def split_size(size):
    first = 1
    for candidate in range(1, math.isqrt(size) + 1):
        if size % candidate == 0:
            first = candidate
    return (first, size // first)


def tables(size):
    index = jnp.arange(size, dtype=jnp.int32)
    angle = (index[:, None] * index[None, :] % size).astype(jnp.float32) * (2.0 * math.pi / size)
    return (jnp.cos(angle), jnp.sin(angle))


def twiddles(first, second, size):
    product = (
        jnp.arange(first, dtype=jnp.int32)[:, None]
        * jnp.arange(second, dtype=jnp.int32)[None, :]
        % size
    )
    angle = product.astype(jnp.float32) * (2.0 * math.pi / size)
    return (jnp.cos(angle), jnp.sin(angle))


def on_left(table, value):
    return jnp.einsum("ka,...ab->...kb", table, value, precision=HIGH)


def on_right(value, table):
    return jnp.einsum("...ab,bc->...ac", value, table, precision=HIGH)


def spectrum(signal, size):
    first, second = split_size(size)
    grid = signal.reshape(signal.shape[:-1] + (first, second))
    cos_a, sin_a = tables(first)
    cos_b, sin_b = tables(second)
    cos_t, sin_t = twiddles(first, second, size)
    real_one = on_left(cos_a, grid)
    imag_one = -on_left(sin_a, grid)
    real_two = real_one * cos_t + imag_one * sin_t
    imag_two = imag_one * cos_t - real_one * sin_t
    real_out = on_right(real_two, cos_b) + on_right(imag_two, sin_b)
    imag_out = on_right(imag_two, cos_b) - on_right(real_two, sin_b)
    return (real_out, imag_out)


def signal_of(real, imag, size):
    first, second = split_size(size)
    cos_a, sin_a = tables(first)
    cos_b, sin_b = tables(second)
    cos_t, sin_t = twiddles(first, second, size)
    real_one = on_right(real, cos_b) - on_right(imag, sin_b)
    imag_one = on_right(imag, cos_b) + on_right(real, sin_b)
    real_two = real_one * cos_t - imag_one * sin_t
    imag_two = imag_one * cos_t + real_one * sin_t
    grid = on_left(cos_a, real_two) - on_left(sin_a, imag_two)
    return grid.reshape(grid.shape[:-2] + (size,)) / size


def causal(signal, filt):
    length = signal.shape[-1]
    size = 2 * length
    sig_real, sig_imag = spectrum(
        jnp.pad(signal, [(0, 0)] * (signal.ndim - 1) + [(0, length)]), size
    )
    fil_real, fil_imag = spectrum(jnp.pad(filt, [(0, 0)] * (filt.ndim - 1) + [(0, length)]), size)
    joined = signal_of(
        sig_real * fil_real - sig_imag * fil_imag, sig_real * fil_imag + sig_imag * fil_real, size
    )
    return joined[..., :length]


def mix_channels(
    chan,
    taps,
    tap_bias,
    skip,
    filt_in,
    filt_mid,
    filt_bias,
    freq,
    filt_out,
    lens,
    first,
    feats,
    decay,
    most,
):
    count = chan.shape[1]
    total = chan.shape[2]
    width = skip.shape[0]
    long_len = total // 2
    taps_here = lax.dynamic_slice_in_dim(taps.reshape(3, 3, width), first, count, 2)
    bias_here = lax.dynamic_slice_in_dim(tap_bias.reshape(3, width), first, count, 1)
    skip_here = lax.dynamic_slice_in_dim(skip, first, count, 0)
    out_here = lax.dynamic_slice_in_dim(filt_out, first, count, 1)
    inner = jnp.sin(freq[0] * (jnp.dot(feats, filt_in, precision=HIGH) + filt_bias[0]))
    inner = jnp.sin(freq[1] * (jnp.dot(inner, filt_mid, precision=HIGH) + filt_bias[1]))
    filt = jnp.einsum("tk,kc->ct", inner, out_here, precision=HIGH) * decay
    starts, begin = doc_begin(lens, total)
    where_at = jnp.arange(total, dtype=jnp.int32)
    mixed = bias_here[:, :, None] + taps_here[0][:, :, None] * chan
    for lag in (1, 2):
        moved = jnp.pad(chan, ((0, 0), (0, 0), (lag, 0)))[:, :, :total]
        mixed = mixed + taps_here[lag][:, :, None] * jnp.where(where_at - lag >= begin, moved, 0.0)
    prod = mixed[1] * mixed[2]
    head = causal(prod[:, :long_len], filt)
    index = starts[:, None] + jnp.arange(most, dtype=jnp.int32)[None, :]
    padded = jnp.pad(prod, ((0, 0), (0, most)))
    windows = jnp.take(padded, index, axis=1)
    local = causal(windows, filt[:, None, :most])
    keep = jnp.arange(most, dtype=jnp.int32)[None, :] < lens[:, None]
    local = jnp.where(keep, local, 0.0)
    tail = jnp.zeros_like(padded).at[:, index].add(local)
    conv = jnp.concatenate([head, tail[:, long_len:total]], axis=1)
    return mixed[0] * (conv + skip_here[:, None] * prod)


def body(
    tokens,
    lengths,
    cotangent,
    norm_gain,
    norm_bias,
    in_weight,
    in_bias,
    conv_weight,
    conv_bias,
    skip_bias,
    filt_out,
    out_weight,
    up_weight,
    up_bias,
    down_weight,
    branch_bias,
    filt_in,
    filt_mid,
    filt_bias,
    sine_freq,
):
    gathered = (
        lax.all_gather(norm_gain, "grp", axis=2, tiled=True),
        lax.all_gather(norm_bias, "grp", axis=2, tiled=True),
        lax.all_gather(in_weight, "grp", axis=2, tiled=True),
        lax.all_gather(in_bias, "grp", axis=1, tiled=True),
        lax.all_gather(conv_weight, "grp", axis=2, tiled=True),
        lax.all_gather(conv_bias, "grp", axis=1, tiled=True),
        lax.all_gather(skip_bias, "grp", axis=1, tiled=True),
        lax.all_gather(filt_out, "grp", axis=2, tiled=True),
        lax.all_gather(out_weight, "grp", axis=2, tiled=True),
        lax.all_gather(up_weight, "grp", axis=2, tiled=True),
        lax.all_gather(up_bias, "grp", axis=1, tiled=True),
        lax.all_gather(down_weight, "grp", axis=2, tiled=True),
        lax.all_gather(branch_bias, "grp", axis=2, tiled=True),
    )
    (
        gains,
        shifts,
        w_in,
        b_in,
        taps_all,
        tap_bias_all,
        skip_all,
        fout_all,
        w_out,
        w_up,
        b_up,
        w_down,
        b_branch,
    ) = gathered
    depth = norm_gain.shape[0]
    tok_rows = tokens.shape[0]
    width = tokens.shape[1]
    seq_count = lax.axis_size("seq")
    count = width // seq_count
    first = lax.axis_index("seq") * count
    total = tok_rows * seq_count
    slot_width = min(SHORT, total // 4)
    feats, tpos = positions(total // 2)
    decay = jnp.exp(-rates(first, count, width)[:, None] * tpos[None, :])
    lens = lengths[0]
    local_mix = partial(
        mix_channels, lens=lens, first=first, feats=feats, decay=decay, most=slot_width
    )
    state = tokens.astype(jnp.float32)
    saved = []
    for layer in range(depth):
        normed, norm_pull = jax.vjp(
            norm_rows,
            state,
            gains[layer, 0].astype(jnp.float32),
            shifts[layer, 0].astype(jnp.float32),
        )
        normed = normed.astype(jnp.bfloat16)
        proj_cols = lax.dot_general(
            w_in[layer], normed, (((0,), (1,)), ((), ())), preferred_element_type=jnp.float32
        )
        proj_cols = proj_cols + b_in[layer].astype(jnp.float32)[:, None]
        streams = proj_cols.astype(jnp.bfloat16).reshape(3, width, tok_rows)
        chan = lax.all_to_all(streams, "seq", split_axis=1, concat_axis=2, tiled=True)
        mixed, mix_pull = jax.vjp(
            local_mix,
            chan.astype(jnp.float32),
            taps_all[layer].astype(jnp.float32),
            tap_bias_all[layer].astype(jnp.float32),
            skip_all[layer].astype(jnp.float32),
            filt_in[layer],
            filt_mid[layer],
            filt_bias[layer],
            sine_freq[layer],
            fout_all[layer].astype(jnp.float32),
        )
        back = lax.all_to_all(
            mixed.astype(jnp.bfloat16), "seq", split_axis=1, concat_axis=0, tiled=True
        )
        branch = lax.dot_general(
            back, w_out[layer], (((0,), (0,)), ((), ())), preferred_element_type=jnp.float32
        )
        mid = state + branch + b_branch[layer, 0].astype(jnp.float32)
        normed2, norm_pull2 = jax.vjp(
            norm_rows,
            mid,
            gains[layer, 1].astype(jnp.float32),
            shifts[layer, 1].astype(jnp.float32),
        )
        normed2 = normed2.astype(jnp.bfloat16)
        pre = jnp.dot(normed2, w_up[layer], preferred_element_type=jnp.float32) + b_up[
            layer
        ].astype(jnp.float32)
        active, gelu_pull = jax.vjp(exact_gelu, pre)
        hidden = active.astype(jnp.bfloat16)
        state = (
            mid
            + jnp.dot(hidden, w_down[layer], preferred_element_type=jnp.float32)
            + b_branch[layer, 1].astype(jnp.float32)
        )
        saved.append((norm_pull, normed, mix_pull, back, norm_pull2, normed2, gelu_pull, hidden))
    grad = cotangent
    collected = []
    for layer in reversed(range(depth)):
        norm_pull, normed, mix_pull, back, norm_pull2, normed2, gelu_pull, hidden = saved[layer]
        grad_low = grad.astype(jnp.bfloat16)
        g_down = lax.dot_general(
            hidden, grad_low, (((0,), (0,)), ((), ())), preferred_element_type=jnp.float32
        )
        g_bias_two = jnp.sum(grad_low.astype(jnp.float32), axis=0)
        g_hidden = lax.dot_general(
            grad_low, w_down[layer], (((1,), (1,)), ((), ())), preferred_element_type=jnp.float32
        )
        g_pre = gelu_pull(g_hidden)[0].astype(jnp.bfloat16)
        g_up = lax.dot_general(
            normed2, g_pre, (((0,), (0,)), ((), ())), preferred_element_type=jnp.float32
        )
        g_up_bias = jnp.sum(g_pre.astype(jnp.float32), axis=0)
        g_normed2 = lax.dot_general(
            g_pre, w_up[layer], (((1,), (1,)), ((), ())), preferred_element_type=jnp.float32
        )
        g_mid, g_gain_two, g_shift_two = norm_pull2(g_normed2)
        g_mid = g_mid + grad
        mid_low = g_mid.astype(jnp.bfloat16)
        g_out = jnp.dot(back, mid_low, preferred_element_type=jnp.float32)
        g_bias_one = jnp.sum(mid_low.astype(jnp.float32), axis=0)
        g_back = lax.dot_general(
            w_out[layer], mid_low, (((1,), (1,)), ((), ())), preferred_element_type=jnp.float32
        )
        g_chan = lax.all_to_all(
            g_back.astype(jnp.bfloat16), "seq", split_axis=0, concat_axis=1, tiled=True
        )
        pulled = mix_pull(g_chan.astype(jnp.float32))
        g_streams = lax.all_to_all(
            pulled[0].astype(jnp.bfloat16), "seq", split_axis=2, concat_axis=1, tiled=True
        )
        g_proj = g_streams.reshape(3 * width, tok_rows)
        g_in = lax.dot_general(
            normed, g_proj, (((0,), (1,)), ((), ())), preferred_element_type=jnp.float32
        )
        g_in_bias = jnp.sum(g_proj.astype(jnp.float32), axis=1)
        g_normed = lax.dot_general(
            g_proj, w_in[layer], (((0,), (1,)), ((), ())), preferred_element_type=jnp.float32
        )
        g_state, g_gain_one, g_shift_one = norm_pull(g_normed)
        grad = g_mid + g_state
        collected.insert(
            0,
            (
                jnp.stack([g_gain_one, g_gain_two]),
                jnp.stack([g_shift_one, g_shift_two]),
                g_in,
                g_in_bias,
                pulled[1],
                pulled[2],
                pulled[3],
                pulled[8],
                g_out,
                g_up,
                g_up_bias,
                g_down,
                jnp.stack([g_bias_one, g_bias_two]),
                pulled[4],
                pulled[5],
                pulled[6],
                pulled[7],
            ),
        )
    stacked = [jnp.stack([entry[place] for entry in collected]) for place in range(17)]
    pieces = (
        lax.psum_scatter(
            stacked[0].astype(jnp.bfloat16), "grp", scatter_dimension=2, tiled=True
        ).astype(jnp.float32),
        lax.psum_scatter(
            stacked[1].astype(jnp.bfloat16), "grp", scatter_dimension=2, tiled=True
        ).astype(jnp.float32),
        lax.psum_scatter(
            stacked[2].astype(jnp.bfloat16), "grp", scatter_dimension=2, tiled=True
        ).astype(jnp.float32),
        lax.psum_scatter(
            stacked[3].astype(jnp.bfloat16), "grp", scatter_dimension=1, tiled=True
        ).astype(jnp.float32),
        lax.psum_scatter(
            stacked[4].astype(jnp.bfloat16), "grp", scatter_dimension=2, tiled=True
        ).astype(jnp.float32),
        lax.psum_scatter(
            stacked[5].astype(jnp.bfloat16), "grp", scatter_dimension=1, tiled=True
        ).astype(jnp.float32),
        lax.psum_scatter(
            stacked[6].astype(jnp.bfloat16), "grp", scatter_dimension=1, tiled=True
        ).astype(jnp.float32),
        lax.psum_scatter(
            stacked[7].astype(jnp.bfloat16), "grp", scatter_dimension=2, tiled=True
        ).astype(jnp.float32),
        lax.psum_scatter(
            stacked[8].astype(jnp.bfloat16), "grp", scatter_dimension=2, tiled=True
        ).astype(jnp.float32),
        lax.psum_scatter(
            stacked[9].astype(jnp.bfloat16), "grp", scatter_dimension=2, tiled=True
        ).astype(jnp.float32),
        lax.psum_scatter(
            stacked[10].astype(jnp.bfloat16), "grp", scatter_dimension=1, tiled=True
        ).astype(jnp.float32),
        lax.psum_scatter(
            stacked[11].astype(jnp.bfloat16), "grp", scatter_dimension=2, tiled=True
        ).astype(jnp.float32),
        lax.psum_scatter(
            stacked[12].astype(jnp.bfloat16), "grp", scatter_dimension=2, tiled=True
        ).astype(jnp.float32),
    )
    shards = (
        lax.psum(pieces[0].astype(jnp.bfloat16), "seq").astype(jnp.float32),
        lax.psum(pieces[1].astype(jnp.bfloat16), "seq").astype(jnp.float32),
        lax.psum(pieces[2].astype(jnp.bfloat16), "seq").astype(jnp.float32),
        lax.psum(pieces[3].astype(jnp.bfloat16), "seq").astype(jnp.float32),
        lax.psum(pieces[4].astype(jnp.bfloat16), "seq").astype(jnp.float32),
        lax.psum(pieces[5].astype(jnp.bfloat16), "seq").astype(jnp.float32),
        lax.psum(pieces[6].astype(jnp.bfloat16), "seq").astype(jnp.float32),
        lax.psum(pieces[7].astype(jnp.bfloat16), "seq").astype(jnp.float32),
        lax.psum(pieces[8].astype(jnp.bfloat16), "seq").astype(jnp.float32),
        lax.psum(pieces[9].astype(jnp.bfloat16), "seq").astype(jnp.float32),
        lax.psum(pieces[10].astype(jnp.bfloat16), "seq").astype(jnp.float32),
        lax.psum(pieces[11].astype(jnp.bfloat16), "seq").astype(jnp.float32),
        lax.psum(pieces[12].astype(jnp.bfloat16), "seq").astype(jnp.float32),
    )
    shared = lax.psum((stacked[13], stacked[14], stacked[15], stacked[16]), ("grp", "seq"))
    return (
        state,
        grad,
        shards[0],
        shards[1],
        shards[2],
        shards[3],
        shards[4],
        shards[5],
        shards[6],
        shards[7],
        shards[8],
        shards[9],
        shards[10],
        shards[11],
        shards[12],
        shared[0],
        shared[1],
        shared[2],
        shared[3],
    )


def solution(mesh):
    in_specs = (
        P(("grp", "seq"), None),
        P("grp", None),
        P(("grp", "seq"), None),
        P(None, None, "grp"),
        P(None, None, "grp"),
        P(None, None, "grp"),
        P(None, "grp"),
        P(None, None, "grp"),
        P(None, "grp"),
        P(None, "grp"),
        P(None, None, "grp"),
        P(None, None, "grp"),
        P(None, None, "grp"),
        P(None, "grp"),
        P(None, None, "grp"),
        P(None, None, "grp"),
        P(),
        P(),
        P(),
        P(),
    )
    out_specs = (
        P(("grp", "seq"), None),
        P(("grp", "seq"), None),
        P(None, None, "grp"),
        P(None, None, "grp"),
        P(None, None, "grp"),
        P(None, "grp"),
        P(None, None, "grp"),
        P(None, "grp"),
        P(None, "grp"),
        P(None, None, "grp"),
        P(None, None, "grp"),
        P(None, None, "grp"),
        P(None, "grp"),
        P(None, None, "grp"),
        P(None, None, "grp"),
        P(),
        P(),
        P(),
        P(),
    )
    return jax.shard_map(body, mesh=mesh, in_specs=in_specs, out_specs=out_specs, check_vma=False)
```

profile of v0, /device:TPU:0, one launch (start us, length us, event | category | flops | bytes accessed | tf_op | source)
XLA Modules:
  0.0 2616.3 jit_solution(12949277741905164664)
XLA Ops:
  10.3 28.0 %all_gather.39 = bf16[2,3072]{1,0:T(2,128)(2,1)S(1)} all-gather(bf16[2,384]{1,0:T(2,128)(2,1)S(1)} %copy-done.290), channel_id=1, replica_groups=mesh['grp'=8,'seq'=4] {'grp'}, dimensions={1}, use_global_device_ids=true | all-gather | bytes 13824 | tf_op jit(solution)/shard_map/all_gather | solution.py:196
  38.4 34.3 %all_gather.40 = bf16[2,3,3072]{2,0,1:T(2,128)(2,1)S(1)} all-gather(bf16[2,3,384]{2,0,1:T(2,128)(2,1)S(1)} %copy-done.268), channel_id=1, replica_groups=mesh['grp'=8,'seq'=4] {'grp'}, dimensions={2}, use_global_device_ids=true | all-gather | bytes 41472 | tf_op jit(solution)/shard_map/all_gather | solution.py:195
  73.1 27.6 %all_gather.45 = bf16[2,64,1024]{2,1,0:T(8,128)(2,1)S(1)} all-gather(bf16[2,64,128]{2,1,0:T(8,128)(2,1)S(1)} %copy-done.194), channel_id=1, replica_groups=mesh['grp'=8,'seq'=4] {'grp'}, dimensions={2}, use_global_device_ids=true | all-gather | bytes 294912 | tf_op jit(solution)/shard_map/all_gather | solution.py:198
  104.9 28.2 %all_gather.46 = bf16[2,1024]{1,0:T(2,128)(2,1)S(1)} all-gather(bf16[2,128]{1,0:T(2,128)(2,1)S(1)} %copy-done.297), channel_id=1, replica_groups=mesh['grp'=8,'seq'=4] {'grp'}, dimensions={1}, use_global_device_ids=true | all-gather | bytes 4608 | tf_op jit(solution)/shard_map/all_gather | solution.py:197
  133.1 19.7 all_gather.41
  152.8 19.4 all_gather.42
  172.2 26.8 %all_gather.48 = bf16[2,2,1024]{2,1,0:T(2,128)(2,1)S(1)} all-gather(bf16[2,2,128]{2,1,0:T(2,128)(2,1)S(1)} %copy-done.294), channel_id=1, replica_groups=mesh['grp'=8,'seq'=4] {'grp'}, dimensions={2}, use_global_device_ids=true | all-gather | bytes 9216 | tf_op jit(solution)/shard_map/all_gather | solution.py:203
  199.0 26.3 %all_gather.44 = bf16[2,3072]{1,0:T(2,128)(2,1)S(1)} all-gather(bf16[2,384]{1,0:T(2,128)(2,1)S(1)} %copy-done.291), channel_id=1, replica_groups=mesh['grp'=8,'seq'=4] {'grp'}, dimensions={1}, use_global_device_ids=true | all-gather | bytes 13824 | tf_op jit(solution)/shard_map/all_gather | solution.py:194
  225.3 26.7 %all_gather.50 = bf16[2,4096]{1,0:T(2,128)(2,1)S(1)} all-gather(bf16[2,512]{1,0:T(2,128)(2,1)S(1)} %copy-done.279), channel_id=1, replica_groups=mesh['grp'=8,'seq'=4] {'grp'}, dimensions={1}, use_global_device_ids=true | all-gather | bytes 18432 | tf_op jit(solution)/shard_map/all_gather | solution.py:201
  271.8 3.9 fusion.19
  277.7 3.6 all-to-all-start
  281.9 13.8 all-to-all-done
  358.2 4.2 all-to-all-done.1
  365.1 132.8 %all-gather.9.cloned.1.call-done = bf16[2,1024,4096]{2,1,0:T(8,128)(2,1)} async-done(((bf16[2,1024,512]{2,1,0:T(8,128)(2,1)}), bf16[2,1024,4096]{2,1,0:T(8,128)(2,1)}) %all-gather.9.cloned.1.call-update) | async-done | bytes 16777232 | tf_op jit(solution)/shard_map/all_gather | solution.py:200
  497.9 9.1 multiply_convert_fusion.1
  507.0 218.7 %all-gather.11.cloned.1.call-done = bf16[2,4096,1024]{2,1,0:T(8,128)(2,1)} async-done(((bf16[2,4096,128]{2,1,0:T(8,128)(2,1)}), bf16[2,4096,1024]{2,1,0:T(8,128)(2,1)}) %all-gather.11.cloned.1.call-update) | async-done | bytes 16777232 | tf_op jit(solution)/shard_map/all_gather | solution.py:202
  725.8 4.7 fusion.1257
  731.3 4.7 fusion.18
  739.3 3.5 all-to-all-start.2
  747.3 9.9 all-to-all-done.2
  798.4 3.9 scatter_custom_fusion.1
  819.5 4.4 all-to-all-start.3
  824.7 5.4 all-to-all-done.3
  832.8 9.1 multiply_convert_fusion
  841.9 8.1 fusion.1259
  850.0 7.4 multiply_reduce_fusion.16
  860.2 4.3 all-to-all-start.4
  922.3 3.8 all-to-all-start.5
  929.7 10.8 all-to-all-done.5
  941.8 6.0 multiply_reduce_fusion.17
  949.4 10.2 fusion.1260
  959.8 3.5 multiply_reduce_fusion.18
  971.7 4.0 pad_maximum_fusion.3
  975.6 11.3 copy.1238
  986.9 5.6 copy.1253
  1037.1 4.1 scatter_custom_fusion.3
  1048.4 3.5 all-to-all-start.7
  1052.0 4.6 convert_bitcast_fusion.4
  1056.7 9.7 all-to-all-done.7
  1070.7 5.5 pad_maximum_fusion.2
  1076.2 31.6 %copy.1226 = bf16[2,1024,3072]{1,0,2:T(2,128)(2,1)} copy(bf16[2,1024,3072]{2,1,0:T(8,128)(2,1)} %pad_maximum_fusion.2) | data formatting | bytes 25165824
  1107.7 13.0 copy.1250
  1126.9 6.8 pad_maximum_fusion.1
  1133.7 42.0 %copy.1242 = bf16[2,4096,1024]{1,0,2:T(2,128)(2,1)} copy(bf16[2,4096,1024]{2,1,0:T(8,128)(2,1)} %pad_maximum_fusion.1) | data formatting | bytes 33554432
  1175.8 18.7 copy.1254
  1200.9 6.7 pad_maximum_fusion
  1246.2 5.1 fusion.1239
  1259.4 65.9 %reduce-scatter.44.cloned.1.call-done = bf16[384,2048]{1,0:T(8,128)(2,1)} async-done(((bf16[3072,2048]{1,0:T(8,128)(2,1)}), bf16[384,2048]{1,0:T(8,128)(2,1)}) %reduce-scatter.44.cloned.1.call-update) | async-done | bytes 1572880
  1331.3 280.3 %reduce-scatter.60.cloned.1.call-done = bf16[128,8192]{1,0:T(8,128)(2,1)} async-done(((bf16[1024,8192]{1,0:T(8,128)(2,1)}), bf16[128,8192]{1,0:T(8,128)(2,1)}) %reduce-scatter.60.cloned.1.call-update) | async-done | bytes 2097168
  1614.8 4.0 copy.1243
  1618.9 278.2 %reduce-scatter.38.cloned.1.call-done = bf16[2,1024,512]{2,1,0:T(8,128)(2,1)} async-done(((bf16[2,1024,4096]{2,1,0:T(8,128)(2,1)}), bf16[2,1024,512]{2,1,0:T(8,128)(2,1)}) %reduce-scatter.38.cloned.1.call-update) | async-done | bytes 2097168 | tf_op jit(solution)/shard_map/reduce_scatter | solution.py:383
  1898.4 5.5 fusion.83
  1903.9 57.2 %reduce-scatter.62.cloned.1.call-done = bf16[128,4]{1,0:T(8,128)(2,1)} async-done(((bf16[1024,4]{1,0:T(8,128)(2,1)}), bf16[128,4]{1,0:T(8,128)(2,1)}) %reduce-scatter.62.cloned.1.call-update) | async-done | bytes 1040
  1962.6 65.3 %reduce-scatter.58.cloned.1.call-done = bf16[512,2]{1,0:T(8,128)(2,1)} async-done(((bf16[4096,2]{1,0:T(8,128)(2,1)}), bf16[512,2]{1,0:T(8,128)(2,1)}) %reduce-scatter.58.cloned.1.call-update) | async-done | bytes 2064
  2039.1 41.8 %all-reduce.42 = (f32[2,33,64]{2,1,0:T(8,128)S(1)}, f32[2,64,64]{2,1,0:T(8,128)}, f32[2,2,64]{2,1,0:T(2,128)}, f32[2,2,64]{2,1,0:T(2,128)}) all-reduce(f32[2,33,64]{2,1,0:T(8,128)S(1)} %pad_maximum_fusion.8, f32[2,64,64]{2,1,0:T(8,128)S(1)} %pad_maximum_fusion.5, ...), channel_id=1, replica_groups=mesh['grp'=8,'seq'=4] {'grp','seq'}, use_global_device_ids=true, to_apply=%region_82.84 | all-reduce | flops 12928 | bytes 103424 | tf_op jit(solution)/shard_map/psum | solution.py:411
  2081.6 9.9 reduce-scatter.52.cloned.1.call-done
  2092.3 63.9 %reduce-scatter.50.cloned.1.call-done = bf16[384,2]{1,0:T(8,128)(2,1)} async-done(((bf16[3072,2]{1,0:T(8,128)(2,1)}), bf16[384,2]{1,0:T(8,128)(2,1)}) %reduce-scatter.50.cloned.1.call-update) | async-done | bytes 1552
  2157.1 64.3 %reduce-scatter.48.cloned.1.call-done = bf16[384,6]{1,0:T(8,128)(2,1)} async-done(((bf16[3072,6]{1,0:T(8,128)(2,1)}), bf16[384,6]{1,0:T(8,128)(2,1)}) %reduce-scatter.48.cloned.1.call-update) | async-done | bytes 4624
  2222.5 62.2 %reduce-scatter.54.cloned.1.call-done = bf16[128,128]{1,0:T(8,128)(2,1)} async-done(((bf16[1024,128]{1,0:T(8,128)(2,1)}), bf16[128,128]{1,0:T(8,128)(2,1)}) %reduce-scatter.54.cloned.1.call-update) | async-done | bytes 32784
  2288.1 60.1 %reduce-scatter.40.cloned.1.call-done = bf16[128,4]{1,0:T(8,128)(2,1)} async-done(((bf16[1024,4]{1,0:T(8,128)(2,1)}), bf16[128,4]{1,0:T(8,128)(2,1)}) %reduce-scatter.40.cloned.1.call-update) | async-done | bytes 1040
  2349.1 62.5 %reduce-scatter.42.cloned.1.call-done = bf16[128,4]{1,0:T(8,128)(2,1)} async-done(((bf16[1024,4]{1,0:T(8,128)(2,1)}), bf16[128,4]{1,0:T(8,128)(2,1)}) %reduce-scatter.42.cloned.1.call-update) | async-done | bytes 1040
  2412.6 63.8 %reduce-scatter.46.cloned.1.call-done = bf16[384,2]{1,0:T(8,128)(2,1)} async-done(((bf16[3072,2]{1,0:T(8,128)(2,1)}), bf16[384,2]{1,0:T(8,128)(2,1)}) %reduce-scatter.46.cloned.1.call-update) | async-done | bytes 1552
  2477.4 11.2 all-reduce.43
  2493.9 105.6 %all-reduce.47.cloned.1.call-done = (bf16[2,1024,384]{2,1,0:T(8,128)(2,1)}, bf16[2,1024,128]{2,1,0:T(8,128)(2,1)}, bf16[2,1024,512]{2,1,0:T(8,128)(2,1)}, bf16[2,4096,128]{2,1,0:T(8,128)(2,1)}) async-done(((bf16[2,1024,384]{2,1,0:T(8,128)(2,1)}, bf16[2,1024,128]{2,1,0:T(8,128)(2,1)}, bf16[2,1024,512]{2,1,0:T(8,128)(2,1)}, bf16[2,4096,128]{2,1,0:T(8,128)(2,1)}), (bf16[2,1024,384]{2,1,0:T(8,128)(2,1)}, ...) | async-done | bytes 6291472 | tf_op jit(solution)/shard_map/psum | solution.py:399
  (1112 shorter events, 399.0 us)
Async XLA Ops:
  7.2 264.6 %all-gather.5.cloned.1.call-start = ((), (), s32[]{:S(2)}) async-start(), calls=%async_computation.21 | async-start | bytes 14155776 | tf_op jit(solution)/shard_map/all_gather | solution.py:193
  7.9 350.3 %all-gather.7.cloned.1.call-start = ((), (), s32[]{:S(2)}) async-start(), calls=%async_computation.22 | async-start | bytes 4718592 | tf_op jit(solution)/shard_map/all_gather | solution.py:199
  8.7 64.4 %copy-start.194 = (bf16[2,64,128]{2,1,0:T(8,128)(2,1)S(1)}, bf16[2,64,128]{2,1,0:T(8,128)(2,1)}, u32[]{:S(2)}) copy-start(bf16[2,64,128]{2,1,0:T(8,128)(2,1)} %param.32) | copy-start | bytes 98308
  8.7 92.0 %copy-start.286 = (f32[2,2,64]{2,1,0:T(2,128)S(1)}, f32[2,2,64]{2,1,0:T(2,128)}, u32[]{:S(2)}) copy-start(f32[2,2,64]{2,1,0:T(2,128)} %param.40) | copy-start | bytes 3076
  8.7 92.0 %copy-start.287 = (f32[2,2,64]{2,1,0:T(2,128)S(1)}, f32[2,2,64]{2,1,0:T(2,128)}, u32[]{:S(2)}) copy-start(f32[2,2,64]{2,1,0:T(2,128)} %param.41) | copy-start | bytes 3076
  8.7 92.2 %copy-start.188 = (f32[2,33,64]{2,0,1:T(2,128)S(1)}, f32[2,33,64]{2,0,1:T(2,128)}, u32[]{:S(2)}) copy-start(f32[2,33,64]{2,0,1:T(2,128)} %param.38) | copy-start | bytes 50692
  8.7 489.2 %all-gather.9.cloned.1.call-start = ((), (), s32[]{:S(2)}) async-start(), calls=%async_computation.23 | async-start | bytes 18874368 | tf_op jit(solution)/shard_map/all_gather | solution.py:200
  9.5 92.4 %copy-start.172 = (f32[2,64,64]{2,1,0:T(8,128)S(1)}, f32[2,64,64]{2,1,0:T(8,128)}, u32[]{:S(2)}) copy-start(f32[2,64,64]{2,1,0:T(8,128)} %param.39) | copy-start | bytes 98308
  9.5 716.3 %all-gather.11.cloned.1.call-start = ((), (), s32[]{:S(2)}) async-start(), calls=%async_computation.24 | async-start | bytes 18874368 | tf_op jit(solution)/shard_map/all_gather | solution.py:202
  73.1 31.7 %copy-start.173 = (f32[256]{0:T(256)}, f32[256]{0:T(256)S(1)}, u32[]{:S(2)}) copy-start(f32[256]{0:T(256)S(1)} %get-tuple-element.374) | copy-start | bytes 3076
  102.4 153.5 %copy-start.141 = (bf16[1,64,1024]{2,1,0:T(8,128)(2,1)}, bf16[1,64,1024]{2,1,0:T(8,128)(2,1)S(1)}, u32[]{:S(2)}) copy-start(bf16[1,64,1024]{2,1,0:T(8,128)(2,1)S(1)} %get-tuple-element.286) | copy-start | bytes 393220
  102.5 50.3 %copy-start.293 = (bf16[2,2,128]{2,1,0:T(2,128)(2,1)S(1)}, bf16[2,2,128]{2,1,0:T(2,128)(2,1)}, u32[]{:S(2)}) copy-start(bf16[2,2,128]{2,1,0:T(2,128)(2,1)} %param.26) | copy-start | bytes 3076
  102.5 69.7 %copy-start.294 = (bf16[2,2,128]{2,1,0:T(2,128)(2,1)S(1)}, bf16[2,2,128]{2,1,0:T(2,128)(2,1)}, u32[]{:S(2)}) copy-start(bf16[2,2,128]{2,1,0:T(2,128)(2,1)} %param.37) | copy-start | bytes 3076
  102.5 96.5 %copy-start.291 = (bf16[2,384]{1,0:T(2,128)(2,1)S(1)}, bf16[2,384]{1,0:T(2,128)(2,1)}, u32[]{:S(2)}) copy-start(bf16[2,384]{1,0:T(2,128)(2,1)} %param.28) | copy-start | bytes 4612
  102.5 122.8 %copy-start.279 = (bf16[2,512]{1,0:T(2,128)(2,1)S(1)}, bf16[2,512]{1,0:T(2,128)(2,1)}, u32[]{:S(2)}) copy-start(bf16[2,512]{1,0:T(2,128)(2,1)} %param.35) | copy-start | bytes 6148
  103.2 166.3 %copy-start.35 = (f32[256,512]{0,1:T(8,128)}, f32[256,512]{0,1:T(8,128)S(1)}, u32[]{:S(2)}) copy-start(f32[256,512]{0,1:T(8,128)S(1)} %pad.218) | copy-start | bytes 1572868
  103.2 153.8 %copy-start.18 = (bf16[128,1024]{1,0:T(8,128)(2,1)S(1)}, bf16[128,1024]{1,0:T(8,128)(2,1)}, u32[]{:S(2)}) copy-start(bf16[128,1024]{1,0:T(8,128)(2,1)} %param.22) | copy-start | bytes 786436
  104.0 156.5 %copy-start.138 = (f32[256,64]{0,1:T(8,128)}, f32[256,64]{0,1:T(8,128)S(1)}, u32[]{:S(2)}) copy-start(f32[256,64]{0,1:T(8,128)S(1)} %convolution_add_fusion.42) | copy-start | bytes 196612
  265.5 50.4 %copy-start.11 = (f32[256,16,16]{0,2,1:T(8,128)}, f32[256,16,16]{0,2,1:T(8,128)S(1)}, u32[]{:S(2)}) copy-start(f32[256,16,16]{0,2,1:T(8,128)S(1)} %convolution_subtract_fusion.11) | copy-start | bytes 786436
  266.0 49.8 %copy-start.13 = (f32[256,16,16]{0,2,1:T(8,128)}, f32[256,16,16]{0,2,1:T(8,128)S(1)}, u32[]{:S(2)}) copy-start(f32[256,16,16]{0,2,1:T(8,128)S(1)} %convolution_add_fusion.39) | copy-start | bytes 786436
  277.7 18.0 all-to-all-start
  353.1 9.4 all-to-all-start.1
  358.2 139.7 %copy-start.149 = (f32[1,1,1024]{2,1,0:T(1,128)S(1)}, f32[1,1,1024]{2,1,0:T(1,128)}, u32[]{:S(2)}) copy-start(f32[1,1,1024]{2,1,0:T(1,128)} %get-tuple-element.317) | copy-start | bytes 12292
  358.2 139.7 %copy-start.159 = (f32[1,1,1024]{2,1,0:T(1,128)S(1)}, f32[1,1,1024]{2,1,0:T(1,128)}, u32[]{:S(2)}) copy-start(f32[1,1,1024]{2,1,0:T(1,128)} %get-tuple-element.321) | copy-start | bytes 12292
  358.2 139.7 %copy-start.220 = (f32[1,4096]{1,0:T(1,128)S(1)}, f32[1,4096]{1,0:T(1,128)}, u32[]{:S(2)}) copy-start(f32[1,4096]{1,0:T(1,128)} %get-tuple-element.306) | copy-start | bytes 49156
  362.5 135.4 %copy-start.91 = (bf16[256,4,128]{2,0,1:T(8,128)(2,1)}, bf16[256,4,128]{2,0,1:T(8,128)(2,1)S(1)}, u32[]{:S(2)}) copy-start(bf16[256,4,128]{2,0,1:T(8,128)(2,1)S(1)} %all-to-all-done.1) | copy-start | bytes 786436
  364.8 361.0 %copy-start.22 = (f32[128,1024]{1,0:T(8,128)}, f32[128,1024]{1,0:T(8,128)S(1)}, u32[]{:S(2)}) copy-start(f32[128,1024]{1,0:T(8,128)S(1)} %get-tuple-element.339) | copy-start | bytes 1572868
  364.8 142.2 %copy-start.250 = (f32[128]{0:T(128)}, f32[128]{0:T(128)S(1)}, u32[]{:S(2)}) copy-start(f32[128]{0:T(128)S(1)} %broadcast_multiply_fusion.2) | copy-start | bytes 1540
  365.0 132.9 %copy-start.299 = (f32[128]{0:T(128)}, f32[128]{0:T(128)S(1)}, u32[]{:S(2)}) copy-start(f32[128]{0:T(128)S(1)} %multiply_reduce_fusion.24) | copy-start | bytes 1540
  365.1 142.0 %copy-start.260 = (f32[128]{0:T(128)}, f32[128]{0:T(128)S(1)}, u32[]{:S(2)}) copy-start(f32[128]{0:T(128)S(1)} %fusion.787) | copy-start | bytes 1540
  497.9 227.9 %copy-start.274 = (f32[1,1,1024]{2,1,0:T(1,128)S(1)}, f32[1,1,1024]{2,1,0:T(1,128)}, u32[]{:S(2)}) copy-start(f32[1,1,1024]{2,1,0:T(1,128)} %get-tuple-element.313) | copy-start | bytes 12292
  507.0 223.5 %copy-start.82 = (bf16[128,4096]{1,0:T(8,128)(2,1)}, bf16[128,4096]{1,0:T(8,128)(2,1)S(1)}, u32[]{:S(2)}) copy-start(bf16[128,4096]{1,0:T(8,128)(2,1)S(1)} %get-tuple-element.340) | copy-start | bytes 3145732
  739.3 18.0 all-to-all-start.2
  819.5 10.5 all-to-all-start.3
  860.2 10.4 all-to-all-start.4
  922.3 18.2 all-to-all-start.5
  968.0 24.6 all-to-all-start.6
  971.4 285.4 %reduce-scatter.56.cloned.1.call-start = ((), (), s32[]{:S(2)}) async-start(), calls=%async_computation.34 | async-start | bytes 4718592
  1048.4 18.0 all-to-all-start.7
  1051.9 273.4 %reduce-scatter.44.cloned.1.call-start = ((), (), s32[]{:S(2)}) async-start(), calls=%async_computation.28 | async-start | bytes 14155776
  1120.8 490.7 %reduce-scatter.60.cloned.1.call-start = ((), (), s32[]{:S(2)}) async-start(), calls=%async_computation.36 | async-start | bytes 18874368
  1194.6 702.5 %reduce-scatter.38.cloned.1.call-start = ((), (), s32[]{:S(2)}) async-start(), calls=%async_computation.25 | async-start | bytes 18874368 | tf_op jit(solution)/shard_map/reduce_scatter | solution.py:383
  1207.8 753.3 %reduce-scatter.62.cloned.1.call-start = ((), (), s32[]{:S(2)}) async-start(), calls=%async_computation.37 | async-start | bytes 294912
  1215.9 811.9 %reduce-scatter.58.cloned.1.call-start = ((), (), s32[]{:S(2)}) async-start(), calls=%async_computation.35 | async-start | bytes 1179648
  1219.8 871.6 %reduce-scatter.52.cloned.1.call-start = ((), (), s32[]{:S(2)}) async-start(), calls=%async_computation.32 | async-start | bytes 294912
  1228.0 928.1 %reduce-scatter.50.cloned.1.call-start = ((), (), s32[]{:S(2)}) async-start(), calls=%async_computation.31 | async-start | bytes 884736
  1234.4 987.0 %reduce-scatter.48.cloned.1.call-start = ((), (), s32[]{:S(2)}) async-start(), calls=%async_computation.30 | async-start | bytes 884736
  1241.3 1043.4 %reduce-scatter.54.cloned.1.call-start = ((), (), s32[]{:S(2)}) async-start(), calls=%async_computation.33 | async-start | bytes 294912
  1246.1 1102.1 %reduce-scatter.40.cloned.1.call-start = ((), (), s32[]{:S(2)}) async-start(), calls=%async_computation.26 | async-start | bytes 294912
  1253.8 1157.8 %reduce-scatter.42.cloned.1.call-start = ((), (), s32[]{:S(2)}) async-start(), calls=%async_computation.27 | async-start | bytes 294912
  1255.4 1221.0 %reduce-scatter.46.cloned.1.call-start = ((), (), s32[]{:S(2)}) async-start(), calls=%async_computation.29 | async-start | bytes 884736
  1256.8 1342.7 %all-reduce.47.cloned.1.call-start = ((), (), s32[]{:S(2)}) async-start(), calls=%async_computation.38 | async-start | bytes 12582912 | tf_op jit(solution)/shard_map/psum | solution.py:399
  1898.3 131.1 %copy-start.107 = (f32[256,16,32]{0,2,1:T(8,128)S(1)}, f32[256,16,32]{0,2,1:T(8,128)}, u32[]{:S(2)}) copy-start(f32[256,16,32]{0,2,1:T(8,128)} %copy.1063) | copy-start | bytes 1572868
  1898.3 131.1 %copy-start.139 = (f32[256,64]{0,1:T(8,128)S(1)}, f32[256,64]{0,1:T(8,128)}, u32[]{:S(2)}) copy-start(f32[256,64]{0,1:T(8,128)} %copy-done.138) | copy-start | bytes 196612
  1898.3 131.1 %copy-start.200 = (f32[64]{0:T(128)S(1)}, f32[64]{0:T(128)}, u32[]{:S(2)}) copy-start(f32[64]{0:T(128)} %copy-done.199) | copy-start | bytes 772
  1898.3 132.5 %copy-start.145 = (f32[256,64]{0,1:T(8,128)S(1)}, f32[256,64]{0,1:T(8,128)}, u32[]{:S(2)}) copy-start(f32[256,64]{0,1:T(8,128)} %copy-done.144) | copy-start | bytes 196612
  1898.3 133.8 %copy-start.124 = (f32[256,128]{0,1:T(8,128)S(1)}, f32[256,128]{0,1:T(8,128)}, u32[]{:S(2)}) copy-start(f32[256,128]{0,1:T(8,128)} %slice_bitcast_fusion.64) | copy-start | bytes 393220
  1898.4 133.8 %copy-start.137 = (f32[256,64]{0,1:T(8,128)S(1)}, f32[256,64]{0,1:T(8,128)}, u32[]{:S(2)}) copy-start(f32[256,64]{0,1:T(8,128)} %copy-done.136) | copy-start | bytes 196612
  1898.4 135.1 %copy-start.143 = (f32[256,64]{0,1:T(8,128)S(1)}, f32[256,64]{0,1:T(8,128)}, u32[]{:S(2)}) copy-start(f32[256,64]{0,1:T(8,128)} %copy-done.142) | copy-start | bytes 196612
  1903.9 382.5 %copy-start.27 = (f32[128,1024]{1,0:T(8,128)S(1)}, f32[128,1024]{1,0:T(8,128)}, u32[]{:S(2)}) copy-start(f32[128,1024]{1,0:T(8,128)} %copy-done.25) | copy-start | bytes 1572868
  1903.9 382.5 %copy-start.49 = (f32[128,1024]{1,0:T(8,128)S(1)}, f32[128,1024]{1,0:T(8,128)}, u32[]{:S(2)}) copy-start(f32[128,1024]{1,0:T(8,128)} %copy-done.48) | copy-start | bytes 1572868
  1903.9 382.5 %copy-start.109 = (f32[128,1024]{1,0:T(8,128)S(1)}, f32[128,1024]{1,0:T(8,128)}, u32[]{:S(2)}) copy-start(f32[128,1024]{1,0:T(8,128)} %copy-done.108) | copy-start | bytes 1572868
  2037.9 439.4 %copy-start.243 = (bf16[2,512]{1,0:T(2,128)(2,1)S(1)}, bf16[2,512]{1,0:T(2,128)(2,1)}, u32[]{:S(2)}) copy-start(bf16[2,512]{1,0:T(2,128)(2,1)} %copy.1241) | copy-start | bytes 6148
  2037.9 439.4 %copy-start.270 = (bf16[2,2,128]{2,1,0:T(2,128)(2,1)S(1)}, bf16[2,2,128]{2,1,0:T(2,128)(2,1)}, u32[]{:S(2)}) copy-start(bf16[2,2,128]{2,1,0:T(2,128)(2,1)} %copy.1245) | copy-start | bytes 3076
  (274 other events, 1356.6 us)
Sparse Core Ops, SparseCore 0:
  10.1 183.7 all-gather.4
  196.0 73.8 all-gather.6
  271.9 225.9 all-gather.8
  499.8 225.9 all-gather.10
  992.7 86.5 reduce-scatter.55
  1120.9 204.4 reduce-scatter.43
  1329.6 281.8 reduce-scatter.59
  1615.3 281.7 reduce-scatter.37
  1900.8 60.2 reduce-scatter.61
  1965.3 62.5 reduce-scatter.57
  2031.2 60.2 reduce-scatter.51
  2094.6 61.4 reduce-scatter.49
  2159.8 61.5 reduce-scatter.47
  2224.6 60.1 reduce-scatter.53
  2287.9 60.2 reduce-scatter.39
  2351.4 60.2 reduce-scatter.41
  2414.8 61.5 reduce-scatter.45
  2480.1 119.2 all-reduce.46
where the time goes:
time: 2630 us; the launch traced here: 2620 us
  waiting for transfers between devices  1650 us (63%)
  matrix products  291 us (11%)
  blocking collectives  290 us (11%)
  local copies, waits for them, and re-layouts  233 us (9%)
  other arithmetic  100 us (4%)
  starting transfers between devices  31.8 us (1%)
    unnamed x30, waiting for transfers between devices  858 us
    reduce_scatter x1, waiting for transfers between devices, body(): lax.psum_scatter(stacked[9].astype(jnp.bfloat16), 'grp', scatter_dimensio...  278 us
    all_gather x1, waiting for transfers between devices, body(): lax.all_gather(down_weight, 'grp', axis=2, tiled=True)  219 us
    unnamed x668, local copies, waits for them, and re-layouts  179 us
    all_gather x1, waiting for transfers between devices, body(): lax.all_gather(up_weight, 'grp', axis=2, tiled=True)  133 us
    dot_general x96, matrix products, on_right(): return jnp.einsum('...ab,bc->...ac', value, table, precision=HIGH)  108 us
    psum x1, waiting for transfers between devices, body(): lax.psum(pieces[2].astype(jnp.bfloat16), 'seq').astype(jnp.float32)  106 us
    dot_general x48, matrix products, on_left(): return jnp.einsum('ka,...ab->...kb', table, value, precision=HIGH)  63.3 us
  transfers between devices with their start and end apart: 26, of which 22 were waited for; matrix products, arithmetic and copies ran while one was open for 16% of the time, Pallas kernels for 0%

commit v1 on v0

v1 whole, which is shorter than its diff:
```python
import math

import jax
import jax.numpy as jnp
from jax import lax
from jax.sharding import PartitionSpec as P

EPS = 1e-05
HIGH = lax.Precision.HIGHEST
FAST = math.log(0.01) / 0.3
SLOW = math.log(0.01) / 1.5
F32 = jnp.float32
BF = jnp.bfloat16
INV_SQRT2 = 1.0 / math.sqrt(2.0)
INV_SQRT2PI = 1.0 / math.sqrt(2.0 * math.pi)


def dot(a, b, da, db):
    return lax.dot_general(a, b, (((da,), (db,)), ((), ())), preferred_element_type=F32)


def pick(v, index, axis):
    return lax.dynamic_index_in_dim(v, index, axis, keepdims=False)


class Comm:
    def __init__(self):
        self.n_grp = lax.axis_size("grp")
        self.n_seq = lax.axis_size("seq")
        self.nz = self.n_grp // 2
        self.ny = self.n_seq // 2
        g = lax.axis_index("grp")
        s = lax.axis_index("seq")
        self.g, self.s = g, s
        self.z, self.x = g // 2, g % 2
        self.y, self.c = s // 2, s % 2

    @staticmethod
    def flip(v, axis, size):
        return lax.ppermute(v, axis, [(i, i ^ 1) for i in range(size)])

    @staticmethod
    def turn(v, axis, size, k):
        half = size // 2
        perm = [(2 * i + j, 2 * ((i + k) % half) + j) for i in range(half) for j in range(2)]
        return lax.ppermute(v, axis, perm)

    def _gather(self, v, axis, size, major, minor):
        half = size // 2
        if half > 4:
            return lax.all_gather(v, axis, axis=0, tiled=False)
        parts = [v] + [self.turn(v, axis, size, k) for k in range(1, half)]
        others = [self.flip(p, axis, size) for p in parts]
        if half == 2:
            zero = major == 0
            mine = jnp.stack([jnp.where(zero, parts[0], parts[1]), jnp.where(zero, parts[1], parts[0])])
            them = jnp.stack([jnp.where(zero, others[0], others[1]), jnp.where(zero, others[1], others[0])])
        else:
            order = jnp.mod(major - jnp.arange(half), half)
            mine = jnp.stack([pick(jnp.stack(parts), order[i], 0) for i in range(half)])
            them = jnp.stack([pick(jnp.stack(others), order[i], 0) for i in range(half)])
        first = jnp.where(minor == 0, mine, them)
        second = jnp.where(minor == 0, them, mine)
        return jnp.stack([first, second], axis=1).reshape((size,) + v.shape)

    def gather_seq(self, v):
        return self._gather(v, "seq", self.n_seq, self.y, self.c)

    def gather_grp(self, v):
        half = self.nz
        slab = jnp.zeros((half,) + v.shape, v.dtype)
        zeros = (0,) * v.ndim
        for k in range(half):
            part = v if k == 0 else self.turn(v, "grp", self.n_grp, k)
            slab = lax.dynamic_update_slice(slab, part[None], (jnp.mod(self.z - k, half),) + zeros)
        other = self.flip(slab, "grp", self.n_grp)
        first = jnp.where(self.x == 0, slab, other)
        second = jnp.where(self.x == 0, other, slab)
        return jnp.stack([first, second], axis=1).reshape((self.n_grp,) + v.shape)

    def _scatter(self, v, axis, size, major, minor, kind):
        half = size // 2
        if half > 4:
            return lax.psum_scatter(v.astype(kind), axis, scatter_dimension=0, tiled=False).astype(F32)
        v = v.reshape((half, 2) + v.shape[1:])
        got = self.flip(pick(v, 1 - minor, 1).astype(kind), axis, size)
        mine = pick(v, minor, 1).astype(F32) + got.astype(F32)
        total = pick(mine, major, 0)
        for k in range(1, half):
            sent = pick(mine, jnp.mod(major + k, half), 0).astype(kind)
            total = total + self.turn(sent, axis, size, k).astype(F32)
        return total

    def scatter_seq(self, v, kind=BF):
        return self._scatter(v, "seq", self.n_seq, self.y, self.c, kind)

    def scatter_grp(self, v, kind=BF):
        return self._scatter(v, "grp", self.n_grp, self.z, self.x, kind)

    def sum_all(self, v, axis, size):
        half = size // 2
        if half > 4:
            return lax.psum(v, axis)
        v = v + self.flip(v, axis, size)
        total = v
        for k in range(1, half):
            total = total + self.turn(v, axis, size, k)
        return total


def norm_stats(value):
    center = value - jnp.mean(value, axis=-1, keepdims=True)
    scale = lax.rsqrt(jnp.mean(center * center, axis=-1, keepdims=True) + EPS)
    return center * scale, scale


def norm_back(grad, hat, scale, gain):
    inner = grad * gain
    mean_one = jnp.mean(inner, axis=-1, keepdims=True)
    mean_two = jnp.mean(inner * hat, axis=-1, keepdims=True)
    return scale * (inner - mean_one - hat * mean_two), jnp.sum(grad * hat, axis=0), jnp.sum(grad, axis=0)


def positions(length):
    index = jnp.arange(length, dtype=jnp.int32).astype(F32)
    tpos = index / (length - 1)
    bands = 0.0001 + (15.0 - 0.0001) * jnp.arange(16, dtype=jnp.int32).astype(F32) / 15.0
    angle = 2.0 * math.pi / length * index[:, None] * bands[None, :]
    return (jnp.concatenate([tpos[:, None], jnp.cos(angle), -jnp.sin(angle)], axis=1), tpos)


def odd_table(size, place):
    freq = 2 * jnp.arange(size // 2, dtype=jnp.int32) + 1
    turn = jnp.bitwise_and(freq[:, None] * place[None, :], 2 * size - 1)
    angle = turn.astype(F32) * (math.pi / size)
    return jnp.stack([jnp.cos(angle), -jnp.sin(angle)])


def filter_of(fin, fmid, fbias, freq, fout, feats, decay):
    inner = jnp.sin(freq[0] * (jnp.dot(feats, fin, precision=HIGH) + fbias[0]))
    inner = jnp.sin(freq[1] * (jnp.dot(inner, fmid, precision=HIGH) + fbias[1]))
    return jnp.dot(inner, fout, precision=HIGH) * decay


def lagged(v, lag, mask):
    return jnp.where(mask[None, :, None], jnp.pad(v, ((0, 0), (lag, 0), (0, 0)))[:, : v.shape[1]], 0.0)


def ahead(v, lag):
    return jnp.pad(v, ((0, 0), (0, lag), (0, 0)))[:, lag:]


def times(ar, ai, br, bi):
    return ar * br - ai * bi, ar * bi + ai * br


def times_conj(ar, ai, br, bi):
    return ar * br + ai * bi, ai * br - ar * bi


class Mixer:
    def __init__(self, lens, total, most):
        half = total // 2
        self.half, self.most, self.total, self.count = half, most, total, lens.shape[0]
        starts = half + jnp.cumsum(lens) - lens
        place = jnp.arange(total, dtype=jnp.int32)
        begin = jnp.zeros((total,), jnp.int32)
        for k in range(lens.shape[0]):
            begin = jnp.where(starts[k] <= place, starts[k], begin)
        self.masks = [None] + [place - lag >= begin for lag in (1, 2)]
        self.long = odd_table(2 * half, place[:half]).reshape(2 * half, half).astype(BF)
        self.short0 = odd_table(2 * most, place[:most]).reshape(2 * most, most).astype(BF)
        tail = place[half:]
        tables = []
        for k in range(lens.shape[0]):
            rel = tail - starts[k]
            inside = (rel >= 0) & (rel < lens[k])
            table = odd_table(2 * most, jnp.where(inside, rel, 0))
            tables.append(jnp.where(inside[None, None, :], table, 0.0))
        self.short = jnp.stack(tables).reshape(lens.shape[0] * 2 * most, total - half).astype(BF)

    def split(self, long, short):
        chans = long.shape[-1]
        long = long.reshape(2, self.half, chans)
        short = short.reshape(self.count, 2, self.most, chans)
        return long[0], long[1], short[:, 0], short[:, 1]

    def forth(self, v):
        v = v.astype(BF)
        return self.split(dot(self.long, v[: self.half], 1, 0), dot(self.short, v[self.half :], 1, 0))

    def back(self, spec):
        lr, li, sr, si = spec
        long = jnp.stack([lr, li]).reshape(2 * self.half, -1) * (1.0 / self.half)
        short = jnp.stack([sr, si], axis=1).reshape(self.count * 2 * self.most, -1) * (1.0 / self.most)
        return jnp.concatenate([dot(self.long, long.astype(BF), 0, 0), dot(self.short, short.astype(BF), 0, 0)])

    def filt_spec(self, filt):
        filt = filt.astype(BF)
        long = dot(self.long, filt, 1, 0)
        short = dot(self.short0, filt[: self.most], 1, 0)
        return long[: self.half], long[self.half :], short[: self.most], short[self.most :]

    def filt_back(self, grads):
        lr, li, sr, si = grads
        long = jnp.concatenate([lr, li]) * (1.0 / self.half)
        short = jnp.concatenate([sr, si]) * (1.0 / self.most)
        head = dot(self.short0, short.astype(BF), 0, 0)
        return dot(self.long, long.astype(BF), 0, 0) + jnp.pad(head, ((0, self.half - self.most), (0, 0)))


def body(
    tokens,
    lengths,
    cotangent,
    norm_gain,
    norm_bias,
    in_weight,
    in_bias,
    conv_weight,
    conv_bias,
    skip_bias,
    filt_out,
    out_weight,
    up_weight,
    up_bias,
    down_weight,
    branch_bias,
    filt_in,
    filt_mid,
    filt_bias,
    sine_freq,
):
    comm = Comm()
    n_grp, n_seq, s = comm.n_grp, comm.n_seq, comm.s
    depth = norm_gain.shape[0]
    tok_rows, width = tokens.shape
    total = tok_rows * n_seq
    cols = width // n_grp
    q = cols // n_seq
    ff_shard = up_weight.shape[2]
    f = ff_shard // n_seq
    hid = filt_out.shape[1]
    chans = n_grp * q

    def unit_in(l):
        return pick(in_weight[l].T.reshape(3, n_seq, q, width), s, 1).reshape(3 * q, width)

    def unit_out(l):
        return pick(out_weight[l].reshape(n_grp, n_seq, q, cols), s, 1).reshape(chans, cols).T

    def unit_up(l):
        return lax.dynamic_slice_in_dim(up_weight[l], s * f, f, 1).T

    def unit_down(l):
        return pick(down_weight[l].reshape(n_grp, n_seq, f, cols), s, 1).reshape(n_grp * f, cols).T

    tok_small = [norm_gain, norm_bias, branch_bias]
    seq_small = [
        pick(in_bias.reshape(depth, 3, n_seq, q), s, 2),
        pick(conv_weight.reshape(depth, 3, 3, n_seq, q), s, 3),
        pick(conv_bias.reshape(depth, 3, n_seq, q), s, 2),
        pick(skip_bias.reshape(depth, n_seq, q), s, 1),
        pick(filt_out.reshape(depth, hid, n_seq, q), s, 2),
        pick(up_bias.reshape(depth, n_seq, f), s, 1),
    ]
    shapes = [v.shape for v in tok_small + seq_small]
    sizes = [math.prod(shape) for shape in shapes]
    packed = jnp.concatenate([v.reshape(-1) for v in tok_small + seq_small])
    fill = -packed.shape[0] % 2048
    packed = comm.gather_grp(jnp.pad(packed, (0, fill)).reshape(-1, 128)).reshape(n_grp, -1).astype(F32)
    spread, at = [], 0
    for shape, size in zip(shapes, sizes):
        spread.append(packed[:, at : at + size].reshape((n_grp,) + shape))
        at += size

    def last(v):
        return jnp.moveaxis(v, 0, -2).reshape(v.shape[1:-1] + (n_grp * v.shape[-1],))

    def streams(v):
        v = jnp.moveaxis(v, 0, -3)
        return v.reshape(v.shape[:-3] + (3, n_grp * q))

    gains, shifts, b_branch = (last(v) for v in spread[:3])
    b_in, taps, tap_bias = (streams(v) for v in spread[3:6])
    skip, fout, b_up = (last(v) for v in spread[6:9])

    weights = []
    for l in range(depth):
        w_in = comm.gather_grp(unit_in(l)).reshape(3 * chans, width)
        w_out = comm.gather_grp(unit_out(l)).reshape(width, chans)
        w_up = comm.gather_grp(unit_up(l)).reshape(n_grp * f, width)
        w_down = comm.gather_grp(unit_down(l)).reshape(width, n_grp * f)
        weights.append((w_in, w_out, w_up, w_down))

    lens = lengths[0]
    mixer = Mixer(lens, total, total // 4)
    feats, tpos = positions(total // 2)
    channel = (
        jnp.arange(n_grp, dtype=jnp.int32)[:, None] * cols + s * q + jnp.arange(q, dtype=jnp.int32)[None, :]
    ).reshape(-1).astype(F32)
    rate = jnp.abs(FAST + (SLOW - FAST) * channel / (width - 1))
    decay = jnp.exp(-tpos[:, None] * rate[None, :])

    state = tokens.astype(F32)
    saved = []
    for l in range(depth):
        w_in, w_out, w_up, w_down = weights[l]
        filt, filt_pull = jax.vjp(
            lambda *a: filter_of(*a, feats, decay),
            filt_in[l], filt_mid[l], filt_bias[l], sine_freq[l], fout[l],
        )
        hat1, scale1 = norm_stats(state)
        normed = (hat1 * gains[l, 0] + shifts[l, 0]).astype(BF)
        normed = comm.gather_seq(normed).reshape(total, width)
        proj = dot(normed, w_in, 1, 1) + b_in[l].reshape(-1)
        proj = jnp.transpose(proj.astype(BF).reshape(total, 3, chans), (1, 0, 2))
        chan = proj.astype(F32)
        z = tap_bias[l][:, None, :] + taps[l, 0][:, None, :] * chan
        for lag in (1, 2):
            z = z + taps[l, lag][:, None, :] * lagged(chan, lag, mixer.masks[lag])
        prod = z[1] * z[2]
        h_lr, h_li, h_sr, h_si = mixer.filt_spec(filt)
        x_lr, x_li, x_sr, x_si = mixer.forth(prod)
        conv = mixer.back(times(x_lr, x_li, h_lr, h_li) + times(x_sr, x_si, h_sr, h_si))
        inner = conv + skip[l] * prod
        mixed = (z[0] * inner).astype(BF)
        part = dot(mixed, w_out, 1, 1)
        mid = state + comm.scatter_seq(part.reshape(n_seq, tok_rows, width)) + b_branch[l, 0]
        hat2, scale2 = norm_stats(mid)
        normed2 = (hat2 * gains[l, 1] + shifts[l, 1]).astype(BF)
        normed2 = comm.gather_seq(normed2).reshape(total, width)
        pre = dot(normed2, w_up, 1, 1) + b_up[l]
        cdf = 0.5 * (1.0 + lax.erf(pre * INV_SQRT2))
        hidden = (pre * cdf).astype(BF)
        slope = cdf + pre * (jnp.exp(-0.5 * pre * pre) * INV_SQRT2PI)
        part = dot(hidden, w_down, 1, 1)
        state = mid + comm.scatter_seq(part.reshape(n_seq, tok_rows, width)) + b_branch[l, 1]
        saved.append((filt_pull, hat1, scale1, normed, chan, z, prod, inner, (h_lr, h_li, h_sr, h_si),
                      (x_lr, x_li, x_sr, x_si), mixed, hat2, scale2, normed2, slope, hidden))

    grad = cotangent
    units = [None] * depth
    tok_grads, seq_grads, net_grads = [None] * depth, [None] * depth, [None] * depth

    def chunk(v):
        return comm.scatter_grp(v.astype(BF).reshape((n_grp, v.shape[0] // n_grp) + v.shape[1:])).astype(BF)

    for l in reversed(range(depth)):
        w_in, w_out, w_up, w_down = weights[l]
        (filt_pull, hat1, scale1, normed, chan, z, prod, inner, (h_lr, h_li, h_sr, h_si),
         (x_lr, x_li, x_sr, x_si), mixed, hat2, scale2, normed2, slope, hidden) = saved[l]
        low = grad.astype(BF)
        g_two = jnp.sum(low.astype(F32), axis=0)
        low = comm.gather_seq(low).reshape(total, width)
        u_down = chunk(dot(low, hidden, 0, 0))
        g_pre = (dot(low, w_down, 1, 0) * slope).astype(BF)
        g_up_bias = jnp.sum(g_pre.astype(F32), axis=0)
        part = dot(g_pre, w_up, 1, 0)
        u_up = chunk(dot(g_pre, normed2, 0, 0))
        g_normed2 = comm.scatter_seq(part.reshape(n_seq, tok_rows, width))
        g_mid, gain2, shift2 = norm_back(g_normed2, hat2, scale2, gains[l, 1])
        g_mid = g_mid + grad
        low = g_mid.astype(BF)
        g_one = jnp.sum(low.astype(F32), axis=0)
        low = comm.gather_seq(low).reshape(total, width)
        u_out = chunk(dot(low, mixed, 0, 0))
        g_y = dot(low, w_out, 1, 0).astype(BF).astype(F32)
        g_conv = g_y * z[0]
        g_skip = jnp.sum(g_conv * prod, axis=0)
        y_lr, y_li, y_sr, y_si = mixer.forth(g_conv)
        corr = mixer.back(times_conj(y_lr, y_li, h_lr, h_li) + times_conj(y_sr, y_si, h_sr, h_si))
        f_lr, f_li = times_conj(y_lr, y_li, x_lr, x_li)
        f_sr, f_si = times_conj(y_sr, y_si, x_sr, x_si)
        g_filt = mixer.filt_back((f_lr, f_li, jnp.sum(f_sr, axis=0), jnp.sum(f_si, axis=0)))
        g_prod = corr + skip[l] * g_conv
        g_z = jnp.stack([g_y * inner, g_prod * z[2], g_prod * z[1]])
        g_taps = [jnp.sum(g_z * chan, axis=1)]
        g_proj = taps[l, 0][:, None, :] * g_z
        for lag in (1, 2):
            kept = jnp.where(mixer.masks[lag][None, :, None], g_z, 0.0)
            g_taps.append(jnp.sum(g_z * lagged(chan, lag, mixer.masks[lag]), axis=1))
            g_proj = g_proj + taps[l, lag][:, None, :] * ahead(kept, lag)
        g_proj = jnp.transpose(g_proj.astype(BF), (1, 0, 2)).reshape(total, 3 * chans)
        g_in_bias = jnp.sum(g_proj.astype(F32), axis=0).reshape(3, chans)
        part = dot(g_proj, w_in, 1, 0)
        u_in = chunk(dot(g_proj, normed, 0, 0))
        g_normed = comm.scatter_seq(part.reshape(n_seq, tok_rows, width))
        g_state, gain1, shift1 = norm_back(g_normed, hat1, scale1, gains[l, 0])
        grad = g_mid + g_state
        units[l] = (u_in, u_out, u_up, u_down)
        pulled = filt_pull(g_filt)
        net_grads[l] = pulled[:4]
        tok_grads[l] = (jnp.stack([gain1, gain2]), jnp.stack([shift1, shift2]), jnp.stack([g_one, g_two]))
        seq_grads[l] = (g_in_bias, jnp.stack(g_taps), jnp.sum(g_z, axis=1), g_skip, pulled[4], g_up_bias)

    def whole(place):
        return [comm.gather_seq(units[l][place]).astype(F32) for l in range(depth)]

    in_grad = jnp.stack([
        jnp.transpose(v.reshape(n_seq, 3, q, width), (3, 1, 0, 2)).reshape(width, 3 * cols) for v in whole(0)])
    out_grad = jnp.stack([
        jnp.transpose(v.reshape(n_seq, cols, n_grp, q), (2, 0, 3, 1)).reshape(width, cols) for v in whole(1)])
    up_grad = jnp.stack([jnp.transpose(v, (2, 0, 1)).reshape(width, ff_shard) for v in whole(2)])
    down_grad = jnp.stack([
        jnp.transpose(v.reshape(n_seq, cols, n_grp, f), (2, 0, 3, 1)).reshape(n_grp * ff_shard, cols)
        for v in whole(3)])

    def by_owner(v):
        v = v.reshape(v.shape[:-1] + (n_grp, v.shape[-1] // n_grp))
        return jnp.moveaxis(v, -2, 0).reshape(n_grp, -1)

    def by_owner3(v):
        v = v.reshape(v.shape[:-2] + (n_grp, 3, q))
        return jnp.moveaxis(v, -3, 0).reshape(n_grp, -1)

    tok_all = [jnp.stack(v) for v in zip(*tok_grads)]
    seq_all = [jnp.stack(v) for v in zip(*seq_grads)]
    tok_flat = jnp.concatenate([by_owner(v) for v in tok_all], axis=1)
    seq_flat = jnp.concatenate(
        [by_owner3(v) for v in seq_all[:3]] + [by_owner(v) for v in seq_all[3:]], axis=1)
    tok_len, seq_len = tok_flat.shape[1], seq_flat.shape[1]
    flat = jnp.concatenate([tok_flat, seq_flat], axis=1)
    flat = jnp.pad(flat, ((0, 0), (0, -flat.shape[1] % 1024)))
    small = comm.scatter_grp(flat.reshape(n_grp, -1, 128), F32).reshape(-1)
    tok_sum = comm.sum_all(small[:tok_len].reshape(-1, 128), "seq", n_seq).reshape(-1)
    seq_part = jnp.pad(small[tok_len : tok_len + seq_len], (0, -seq_len % 1024)).reshape(-1, 128)
    seq_sum = comm.gather_seq(seq_part).reshape(n_seq, -1)[:, :seq_len]
    norm_gain_grad, norm_bias_grad, branch_grad = tok_sum.reshape(3, depth, 2, cols)
    pieces, at = [], 0
    for shape in shapes[3:]:
        size = math.prod(shape)
        part = seq_sum[:, at : at + size].reshape((n_seq,) + shape)
        at += size
        part = jnp.moveaxis(part, 0, -2)
        pieces.append(part)
    in_bias_grad = pieces[0].reshape(depth, 3 * cols)
    taps_grad = pieces[1].reshape(depth, 3, 3 * cols)
    tap_bias_grad = pieces[2].reshape(depth, 3 * cols)
    skip_grad = pieces[3].reshape(depth, cols)
    fout_grad = pieces[4].reshape(depth, hid, cols)
    up_bias_grad = pieces[5].reshape(depth, ff_shard)

    nets = [jnp.stack(v) for v in zip(*net_grads)]
    flat = jnp.concatenate([v.reshape(-1) for v in nets])
    flat = jnp.pad(flat, (0, -flat.shape[0] % 1024)).reshape(-1, 128)
    flat = comm.sum_all(comm.sum_all(flat, "seq", n_seq), "grp", n_grp).reshape(-1)
    shared, at = [], 0
    for v in nets:
        shared.append(flat[at : at + v.size].reshape(v.shape))
        at += v.size
    return (
        state, grad, norm_gain_grad, norm_bias_grad, in_grad, in_bias_grad, taps_grad, tap_bias_grad,
        skip_grad, fout_grad, out_grad, up_grad, up_bias_grad, down_grad, branch_grad,
        shared[0], shared[1], shared[2], shared[3],
    )


def solution(mesh):
    tok = P(("grp", "seq"), None)
    last3, last2 = P(None, None, "grp"), P(None, "grp")
    in_specs = (
        tok, P("grp", None), tok, last3, last3, last3, last2, last3, last2, last2,
        last3, last3, last3, last2, last3, last3, P(), P(), P(), P(),
    )
    out_specs = (
        tok, tok, last3, last3, last3, last2, last3, last2, last2, last3,
        last3, last3, last2, last3, last3, P(), P(), P(), P(),
    )
    return jax.shard_map(body, mesh=mesh, in_specs=in_specs, out_specs=out_specs, check_vma=False)
```

time: 2630 us -> 764 us (0.29)
  waiting for transfers between devices: 1650 us -> 236 us
  blocking collectives: 290 us -> 0 us
  matrix products: 291 us -> 65.6 us
  starting transfers between devices: 31.8 us -> 165 us
  local copies, waits for them, and re-layouts: 233 us -> 188 us
    unnamed x30 -> x0, waiting for transfers between devices: 858 us -> none
    all_gather x4 -> x0, waiting for transfers between devices: 352 us -> none  [the longest x1 219 us: body(): lax.all_gather(down_weight, 'grp', axis=2, tiled=True)]
    reduce_scatter x1 -> x0, waiting for transfers between devices: 278 us -> none  [body(): lax.psum_scatter(stacked[9].astype(jnp.bfloat16), 'grp', scatter_dimensio...]
    all_gather x9 -> x0, blocking collectives: 237 us -> none  [the longest x1 34.3 us: body(): lax.all_gather(conv_weight, 'grp', axis=2, tiled=True)]
    ppermute x0 -> x147, waiting for transfers between devices: none -> 236 us  [the longest x84 120 us: turn(): return lax.ppermute(v, axis, perm)]
    dot_general x184 -> x64, matrix products: 291 us -> 65.6 us  [the longest x48 48.4 us: dot(): lax.dot_general(a, b, (((da,), (db,)), ((), ())), preferred_element_type=...]
    ppermute x0 -> x147, starting transfers between devices: none -> 165 us  [the longest x84 140 us: turn(): return lax.ppermute(v, axis, perm)]
    unnamed x668 -> x494, local copies, waits for them, and re-layouts: 179 us -> 27.2 us
  transfers between devices with their start and end apart: 26 -> 147, of which waited for: 22 -> 55; matrix products, arithmetic and copies ran while one was open for 16% -> 41% of each run, Pallas kernels for 0% -> 0%
where the time goes in v1:
time: 764 us; the launch traced here: 752 us
  waiting for transfers between devices  236 us (31%)
  local copies, waits for them, and re-layouts  188 us (25%)
  starting transfers between devices  165 us (22%)
  other arithmetic  90.6 us (12%)
  matrix products  65.6 us (9%)
    ppermute x84, starting transfers between devices, turn(): return lax.ppermute(v, axis, perm)  140 us
    ppermute x84, waiting for transfers between devices, turn(): return lax.ppermute(v, axis, perm)  120 us
    ppermute x63, waiting for transfers between devices, flip(): return lax.ppermute(v, axis, [(i, i ^ 1) for i in range(size)])  116 us
    dot_general x48, matrix products, dot(): lax.dot_general(a, b, (((da,), (db,)), ((), ())), preferred_element_type=...  48.4 us
    unnamed x494, local copies, waits for them, and re-layouts  27.2 us
    dynamic_update_slice x36, local copies, waits for them, and re-layouts, gather_grp(): lax.dynamic_update_slice(slab, part[None], (jnp.mod(self.z - k, half),) +...  25.8 us
    ppermute x63, starting transfers between devices, flip(): return lax.ppermute(v, axis, [(i, i ^ 1) for i in range(size)])  25.3 us
  transfers between devices with their start and end apart: 147, of which 55 were waited for; matrix products, arithmetic and copies ran while one was open for 41% of the time, Pallas kernels for 0%

profile of v1, /device:TPU:0, one launch (start us, length us, event | category | flops | bytes accessed | tf_op | source)
XLA Modules:
  0.0 752.2 jit_solution(15672559754679834557)
XLA Ops:
  8.1 5.0 collective-permute-start.2
  55.1 3.9 subtract_select_fusion.2
  62.1 2.5 add_compare_fusion
  65.5 2.3 collective-permute-start.13
  136.8 2.6 collective-permute-done.7
  140.3 2.5 collective-permute-start.24
  146.1 13.2 %collective-permute-done.24 = bf16[128,1024]{1,0:T(8,128)(2,1)S(1)} collective-permute-done((bf16[128,1024]{1,0:T(8,128)(2,1)S(1)}, bf16[128,1024]{1,0:T(8,128)(2,1)S(1)}, u32[]{:S(2)}, u32[]{:S(2)}) %collective-permute-start.24) | collective-permute-done | bytes 262176 | tf_op jit(solution)/shard_map/ppermute | solution.py:46
  159.3 19.2 %collective-permute-start.21 = (bf16[128,1024]{0,1:T(8,128)(2,1)}, bf16[128,1024]{0,1:T(8,128)(2,1)}, u32[]{:S(2)}, u32[]{:S(2)}) collective-permute-start(bf16[128,1024]{0,1:T(8,128)(2,1)} %get-tuple-element.237), channel_id=1, source_target_pairs={{0,16},{4,20},{8,24},{12,28},{16,0},{20,4},{24,8},{28,12},{1,17},{... | collective-permute-start | bytes 786440 | tf_op jit(solution)/shard_map/ppermute | solution.py:46
  180.0 3.8 collective-permute-start.22
  186.4 4.2 collective-permute-done.20
  194.6 11.5 %collective-permute-start.51 = (bf16[128,1024]{1,0:T(8,128)(2,1)}, bf16[128,1024]{1,0:T(8,128)(2,1)}, u32[]{:S(2)}, u32[]{:S(2)}) collective-permute-start(bf16[128,1024]{1,0:T(8,128)(2,1)} %bitcast.223), channel_id=1, source_target_pairs={{0,16},{4,20},{8,24},{12,28},{16,0},{20,4},{24,8},{28,12},{1,17},{... | collective-permute-start | bytes 786440 | tf_op jit(solution)/shard_map/ppermute | solution.py:46
  218.0 15.3 %collective-permute-done.10 = bf16[4,96,1024]{2,1,0:T(8,128)(2,1)S(1)} collective-permute-done((bf16[4,96,1024]{2,1,0:T(8,128)(2,1)S(1)}, bf16[4,96,1024]{2,1,0:T(8,128)(2,1)S(1)}, u32[]{:S(2)}, u32[]{:S(2)}) %collective-permute-start.10) | collective-permute-done | bytes 786464 | tf_op jit(solution)/shard_map/ppermute | solution.py:40
  259.1 4.4 collective-permute-done.16
  265.3 13.0 %collective-permute-done.27 = bf16[4,128,1024]{2,1,0:T(8,128)(2,1)S(1)} collective-permute-done((bf16[4,128,1024]{2,1,0:T(8,128)(2,1)}, bf16[4,128,1024]{2,1,0:T(8,128)(2,1)S(1)}, u32[]{:S(2)}, u32[]{:S(2)}) %collective-permute-start.27) | collective-permute-done | bytes 1048608 | tf_op jit(solution)/shard_map/ppermute | solution.py:40
  282.8 2.7 multiply_convert_fusion.1
  296.6 5.4 collective-permute-done.29
  304.2 3.9 collective-permute-done.36
  314.6 3.1 copy.293
  317.7 3.0 copy.294
  320.8 3.2 multiply_add_fusion
  333.6 4.7 collective-permute-done.42
  340.5 12.2 %collective-permute-done.53 = bf16[4,128,1024]{2,1,0:T(8,128)(2,1)} collective-permute-done((bf16[4,128,1024]{2,1,0:T(8,128)(2,1)}, bf16[4,128,1024]{2,1,0:T(8,128)(2,1)}, u32[]{:S(2)}, u32[]{:S(2)}) %collective-permute-start.53) | collective-permute-done | bytes 1048608 | tf_op jit(solution)/shard_map/ppermute | solution.py:40
  360.0 2.7 convert_reduce_fusion
  372.2 6.9 collective-permute-done.60
  380.0 3.3 collective-permute-done.55
  386.7 6.7 collective-permute-done.134
  397.8 17.3 %collective-permute-done.120 = bf16[4,128,1024]{2,1,0:T(8,128)(2,1)S(1)} collective-permute-done((bf16[4,128,1024]{2,1,0:T(8,128)(2,1)S(1)}, bf16[4,128,1024]{2,1,0:T(8,128)(2,1)S(1)}, u32[]{:S(2)}, u32[]{:S(2)}) %collective-permute-start.120) | collective-permute-done | bytes 1048608 | tf_op jit(solution)/shard_map/ppermute | solution.py:40
  418.1 2.7 collective-permute-start.123
  436.0 2.4 copy.314
  438.3 2.8 copy.381
  441.2 2.4 convolution_convert_fusion.6
  446.7 3.4 reshape.3694
  450.0 4.0 fusion.314
  477.3 3.4 collective-permute-start.109
  483.8 2.9 collective-permute-done.108
  499.9 5.5 collective-permute-done.65
  506.2 4.9 collective-permute-done.89
  512.4 3.8 collective-permute-start.92
  519.8 2.5 copy.353
  522.2 2.3 copy.384
  524.6 8.1 %collective-permute-done.91 = bf16[96,1024]{1,0:T(8,128)(2,1)} collective-permute-done((bf16[96,1024]{1,0:T(8,128)(2,1)S(1)}, bf16[96,1024]{1,0:T(8,128)(2,1)}, u32[]{:S(2)}, u32[]{:S(2)}) %collective-permute-start.91) | collective-permute-done | bytes 196640 | tf_op jit(solution)/shard_map/ppermute | solution.py:46
  536.0 5.5 collective-permute-done.93
  556.6 5.0 collective-permute-done.70
  565.6 11.2 %collective-permute-done.113 = bf16[4,128,1024]{2,1,0:T(8,128)(2,1)S(1)} collective-permute-done((bf16[4,128,1024]{2,1,0:T(8,128)(2,1)S(1)}, bf16[4,128,1024]{2,1,0:T(8,128)(2,1)S(1)}, u32[]{:S(2)}, u32[]{:S(2)}) %collective-permute-start.113) | collective-permute-done | bytes 1048608 | tf_op jit(solution)/shard_map/ppermute | solution.py:40
  577.4 3.8 collective-permute-start.116
  581.2 17.1 %collective-permute-done.127 = bf16[4,128,1024]{2,1,0:T(8,128)(2,1)S(1)} collective-permute-done((bf16[4,128,1024]{2,1,0:T(8,128)(2,1)S(1)}, bf16[4,128,1024]{2,1,0:T(8,128)(2,1)S(1)}, u32[]{:S(2)}, u32[]{:S(2)}) %collective-permute-start.127) | collective-permute-done | bytes 1048608 | tf_op jit(solution)/shard_map/ppermute | solution.py:40
  599.0 4.0 collective-permute-start.130
  604.5 5.5 collective-permute-done.128
  610.0 3.7 collective-permute-done.130
  615.2 7.9 %collective-permute-done.129 = bf16[128,1024]{1,0:T(8,128)(2,1)S(1)} collective-permute-done((bf16[128,1024]{1,0:T(8,128)(2,1)S(1)}, bf16[128,1024]{1,0:T(8,128)(2,1)S(1)}, u32[]{:S(2)}, u32[]{:S(2)}) %collective-permute-start.129) | collective-permute-done | bytes 262176 | tf_op jit(solution)/shard_map/ppermute | solution.py:46
  646.1 3.8 convolution_convert_fusion.5
  657.7 2.6 collective-permute-done.142
  661.1 3.5 collective-permute-done.143
  674.5 2.8 collective-permute-done.99
  684.2 2.5 collective-permute-done.101
  687.4 3.6 collective-permute-done.103
  705.4 4.5 collective-permute-done.75
  714.4 3.8 collective-permute-start.85
  718.3 3.8 collective-permute-start.79
  723.2 4.7 collective-permute-done.77
  729.7 3.1 collective-permute-done.81
  733.9 2.7 collective-permute-done.96
  743.4 3.1 collective-permute-done.86
  749.4 2.4 copy.354
  (1263 shorter events, 406.3 us)
Async XLA Ops:
  8.1 61.1 %collective-permute-start.2 = (bf16[64,128]{1,0:T(8,128)(2,1)}, bf16[64,128]{1,0:T(8,128)(2,1)}, u32[]{:S(2)}, u32[]{:S(2)}) collective-permute-start(bf16[64,128]{1,0:T(8,128)(2,1)} %pad_bitcast_fusion.2), channel_id=1, source_target_pairs={{0,24},{4,28},{8,0},{12,4},{16,8},{20,12},{24,16},{28,20},{1,25},{... | collective-permute-start | bytes 49160 | tf_op jit(solution)/shard_map/ppermute | solution.py:46
  13.2 55.4 %collective-permute-start.1 = (bf16[64,128]{1,0:T(8,128)(2,1)}, bf16[64,128]{1,0:T(8,128)(2,1)}, u32[]{:S(2)}, u32[]{:S(2)}) collective-permute-start(bf16[64,128]{1,0:T(8,128)(2,1)} %pad_bitcast_fusion.2), channel_id=1, source_target_pairs={{0,16},{4,20},{8,24},{12,28},{16,0},{20,4},{24,8},{28,12},{1,17},{... | collective-permute-start | bytes 49160 | tf_op jit(solution)/shard_map/ppermute | solution.py:46
  13.2 52.3 %collective-permute-start = (bf16[64,128]{1,0:T(8,128)(2,1)}, bf16[64,128]{1,0:T(8,128)(2,1)}, u32[]{:S(2)}, u32[]{:S(2)}) collective-permute-start(bf16[64,128]{1,0:T(8,128)(2,1)} %pad_bitcast_fusion.2), channel_id=1, source_target_pairs={{0,8},{4,12},{8,16},{12,20},{16,24},{20,28},{24,0},{28,4},{1,9},{5... | collective-permute-start | bytes 49160 | tf_op jit(solution)/shard_map/ppermute | solution.py:46
  15.3 55.7 %collective-permute-start.12 = (bf16[128,256]{0,1:T(8,128)(2,1)S(1)}, bf16[128,256]{0,1:T(8,128)(2,1)}, u32[]{:S(2)}, u32[]{:S(2)}) collective-permute-start(bf16[128,256]{0,1:T(8,128)(2,1)S(1)} %bitcast.1283), channel_id=1, source_target_pairs={{0,16},{4,20},{8,24},{12,28},{16,0},{20,4},{24,8},{28,12},{1,17},{... | collective-permute-start | bytes 196616 | tf_op jit(solution)/shard_map/ppermute | solution.py:46
  17.3 57.5 %collective-permute-start.11 = (bf16[128,256]{0,1:T(8,128)(2,1)S(1)}, bf16[128,256]{0,1:T(8,128)(2,1)}, u32[]{:S(2)}, u32[]{:S(2)}) collective-permute-start(bf16[128,256]{0,1:T(8,128)(2,1)S(1)} %bitcast.1284), channel_id=1, source_target_pairs={{0,8},{4,12},{8,16},{12,20},{16,24},{20,28},{24,0},{28,4},{1,9},{5... | collective-permute-start | bytes 196616 | tf_op jit(solution)/shard_map/ppermute | solution.py:46
  74.8 59.1 %collective-permute-start.35 = (bf16[96,1024]{1,0:T(8,128)(2,1)}, bf16[96,1024]{1,0:T(8,128)(2,1)}, u32[]{:S(2)}, u32[]{:S(2)}) collective-permute-start(bf16[96,1024]{1,0:T(8,128)(2,1)} %bitcast.153), channel_id=1, source_target_pairs={{0,24},{4,28},{8,0},{12,4},{16,8},{20,12},{24,16},{28,20},{1,25},{... | collective-permute-start | bytes 589832 | tf_op jit(solution)/shard_map/ppermute | solution.py:46
  76.4 55.3 %collective-permute-start.34 = (bf16[96,1024]{1,0:T(8,128)(2,1)}, bf16[96,1024]{1,0:T(8,128)(2,1)}, u32[]{:S(2)}, u32[]{:S(2)}) collective-permute-start(bf16[96,1024]{1,0:T(8,128)(2,1)} %bitcast.153), channel_id=1, source_target_pairs={{0,16},{4,20},{8,24},{12,28},{16,0},{20,4},{24,8},{28,12},{1,17},{... | collective-permute-start | bytes 589832 | tf_op jit(solution)/shard_map/ppermute | solution.py:46
  77.4 51.6 %collective-permute-start.33 = (bf16[96,1024]{1,0:T(8,128)(2,1)}, bf16[96,1024]{1,0:T(8,128)(2,1)}, u32[]{:S(2)}, u32[]{:S(2)}) collective-permute-start(bf16[96,1024]{1,0:T(8,128)(2,1)} %bitcast.153), channel_id=1, source_target_pairs={{0,8},{4,12},{8,16},{12,20},{16,24},{20,28},{24,0},{28,4},{1,9},{5... | collective-permute-start | bytes 589832 | tf_op jit(solution)/shard_map/ppermute | solution.py:46
  79.3 64.4 %collective-permute-start.9 = (bf16[96,1024]{1,0:T(8,128)(2,1)}, bf16[96,1024]{1,0:T(8,128)(2,1)}, u32[]{:S(2)}, u32[]{:S(2)}) collective-permute-start(bf16[96,1024]{1,0:T(8,128)(2,1)} %bitcast.32), channel_id=1, source_target_pairs={{0,24},{4,28},{8,0},{12,4},{16,8},{20,12},{24,16},{28,20},{1,25},{... | collective-permute-start | bytes 589832 | tf_op jit(solution)/shard_map/ppermute | solution.py:46
  85.9 54.4 %collective-permute-start.8 = (bf16[96,1024]{1,0:T(8,128)(2,1)}, bf16[96,1024]{1,0:T(8,128)(2,1)}, u32[]{:S(2)}, u32[]{:S(2)}) collective-permute-start(bf16[96,1024]{1,0:T(8,128)(2,1)} %bitcast.32), channel_id=1, source_target_pairs={{0,16},{4,20},{8,24},{12,28},{16,0},{20,4},{24,8},{28,12},{1,17},{... | collective-permute-start | bytes 589832 | tf_op jit(solution)/shard_map/ppermute | solution.py:46
  131.8 79.5 %collective-permute-start.47 = (bf16[128,1024]{0,1:T(8,128)(2,1)}, bf16[128,1024]{0,1:T(8,128)(2,1)}, u32[]{:S(2)}, u32[]{:S(2)}) collective-permute-start(bf16[128,1024]{0,1:T(8,128)(2,1)} %get-tuple-element.227), channel_id=1, source_target_pairs={{0,16},{4,20},{8,24},{12,28},{16,0},{20,4},{24,8},{28,12},{1,17},{... | collective-permute-start | bytes 786440 | tf_op jit(solution)/shard_map/ppermute | solution.py:46
  133.9 50.6 %collective-permute-start.46 = (bf16[128,1024]{0,1:T(8,128)(2,1)}, bf16[128,1024]{0,1:T(8,128)(2,1)S(1)}, u32[]{:S(2)}, u32[]{:S(2)}) collective-permute-start(bf16[128,1024]{0,1:T(8,128)(2,1)} %get-tuple-element.227), channel_id=1, source_target_pairs={{0,8},{4,12},{8,16},{12,20},{16,24},{20,28},{24,0},{28,4},{1,9},{5... | collective-permute-start | bytes 786440 | tf_op jit(solution)/shard_map/ppermute | solution.py:46
  139.4 39.9 %collective-permute-start.25 = (bf16[128,1024]{1,0:T(8,128)(2,1)S(1)}, bf16[128,1024]{1,0:T(8,128)(2,1)S(1)}, u32[]{:S(2)}, u32[]{:S(2)}) collective-permute-start(bf16[128,1024]{1,0:T(8,128)(2,1)S(1)} %bitcast.1234), channel_id=1, source_target_pairs={{0,16},{4,20},{8,24},{12,28},{16,0},{20,4},{24,8},{28,12},{1,17},{... | collective-permute-start | bytes 786440 | tf_op jit(solution)/shard_map/ppermute | solution.py:46
  140.3 19.1 %collective-permute-start.24 = (bf16[128,1024]{1,0:T(8,128)(2,1)S(1)}, bf16[128,1024]{1,0:T(8,128)(2,1)S(1)}, u32[]{:S(2)}, u32[]{:S(2)}) collective-permute-start(bf16[128,1024]{1,0:T(8,128)(2,1)S(1)} %bitcast.1235), channel_id=1, source_target_pairs={{0,8},{4,12},{8,16},{12,20},{16,24},{20,28},{24,0},{28,4},{1,9},{5... | collective-permute-start | bytes 786440 | tf_op jit(solution)/shard_map/ppermute | solution.py:46
  143.7 36.3 %collective-permute-start.26 = (bf16[128,1024]{1,0:T(8,128)(2,1)S(1)}, bf16[128,1024]{1,0:T(8,128)(2,1)S(1)}, u32[]{:S(2)}, u32[]{:S(2)}) collective-permute-start(bf16[128,1024]{1,0:T(8,128)(2,1)S(1)} %bitcast.1236), channel_id=1, source_target_pairs={{0,24},{4,28},{8,0},{12,4},{16,8},{20,12},{24,16},{28,20},{1,25},{... | collective-permute-start | bytes 786440 | tf_op jit(solution)/shard_map/ppermute | solution.py:46
  159.3 35.2 %collective-permute-start.21 = (bf16[128,1024]{0,1:T(8,128)(2,1)}, bf16[128,1024]{0,1:T(8,128)(2,1)}, u32[]{:S(2)}, u32[]{:S(2)}) collective-permute-start(bf16[128,1024]{0,1:T(8,128)(2,1)} %get-tuple-element.237), channel_id=1, source_target_pairs={{0,16},{4,20},{8,24},{12,28},{16,0},{20,4},{24,8},{28,12},{1,17},{... | collective-permute-start | bytes 786440 | tf_op jit(solution)/shard_map/ppermute | solution.py:46
  180.0 27.1 %collective-permute-start.22 = (bf16[128,1024]{0,1:T(8,128)(2,1)}, bf16[128,1024]{0,1:T(8,128)(2,1)}, u32[]{:S(2)}, u32[]{:S(2)}) collective-permute-start(bf16[128,1024]{0,1:T(8,128)(2,1)} %get-tuple-element.237), channel_id=1, source_target_pairs={{0,24},{4,28},{8,0},{12,4},{16,8},{20,12},{24,16},{28,20},{1,25},{... | collective-permute-start | bytes 786440 | tf_op jit(solution)/shard_map/ppermute | solution.py:46
  184.5 62.8 %collective-permute-start.48 = (bf16[128,1024]{0,1:T(8,128)(2,1)}, bf16[128,1024]{0,1:T(8,128)(2,1)}, u32[]{:S(2)}, u32[]{:S(2)}) collective-permute-start(bf16[128,1024]{0,1:T(8,128)(2,1)} %get-tuple-element.227), channel_id=1, source_target_pairs={{0,24},{4,28},{8,0},{12,4},{16,8},{20,12},{24,16},{28,20},{1,25},{... | collective-permute-start | bytes 786440 | tf_op jit(solution)/shard_map/ppermute | solution.py:46
  190.5 22.5 %collective-permute-start.14 = (bf16[4,128,256]{2,1,0:T(8,128)(2,1)}, bf16[4,128,256]{2,1,0:T(8,128)(2,1)}, u32[]{:S(2)}, u32[]{:S(2)}) collective-permute-start(bf16[4,128,256]{2,1,0:T(8,128)(2,1)} %constant_dynamic-update-slice_fusion.13), channel_id=1, source_target_pairs={{0,4},{4,0},{8,12},{12,8},{16,20},{20,16},{24,28},{28,24},{1,5},{5... | collective-permute-start | bytes 786440 | tf_op jit(solution)/shard_map/ppermute | solution.py:40
  194.6 56.6 %collective-permute-start.51 = (bf16[128,1024]{1,0:T(8,128)(2,1)}, bf16[128,1024]{1,0:T(8,128)(2,1)}, u32[]{:S(2)}, u32[]{:S(2)}) collective-permute-start(bf16[128,1024]{1,0:T(8,128)(2,1)} %bitcast.223), channel_id=1, source_target_pairs={{0,16},{4,20},{8,24},{12,28},{16,0},{20,4},{24,8},{28,12},{1,17},{... | collective-permute-start | bytes 786440 | tf_op jit(solution)/shard_map/ppermute | solution.py:46
  213.0 20.3 %collective-permute-start.10 = (bf16[4,96,1024]{2,1,0:T(8,128)(2,1)S(1)}, bf16[4,96,1024]{2,1,0:T(8,128)(2,1)S(1)}, u32[]{:S(2)}, u32[]{:S(2)}) collective-permute-start(bf16[4,96,1024]{2,1,0:T(8,128)(2,1)S(1)} %bitcast_dynamic-update-slice_fusion.11), channel_id=1, source_target_pairs={{0,4},{4,0},{8,12},{12,8},{16,20},{20,16},{24,28},{28,24},{1,5},{5... | collective-permute-start | bytes 2359304 | tf_op jit(solution)/shard_map/ppermute | solution.py:40
  216.1 32.9 %collective-permute-start.50 = (bf16[128,1024]{1,0:T(8,128)(2,1)}, bf16[128,1024]{1,0:T(8,128)(2,1)}, u32[]{:S(2)}, u32[]{:S(2)}) collective-permute-start(bf16[128,1024]{1,0:T(8,128)(2,1)} %bitcast.223), channel_id=1, source_target_pairs={{0,8},{4,12},{8,16},{12,20},{16,24},{20,28},{24,0},{28,4},{1,9},{5... | collective-permute-start | bytes 786440 | tf_op jit(solution)/shard_map/ppermute | solution.py:46
  216.3 39.3 %collective-permute-start.23 = (bf16[4,128,1024]{2,1,0:T(8,128)(2,1)}, bf16[4,128,1024]{2,1,0:T(8,128)(2,1)}, u32[]{:S(2)}, u32[]{:S(2)}) collective-permute-start(bf16[4,128,1024]{2,1,0:T(8,128)(2,1)} %constant_dynamic-update-slice_fusion.9), channel_id=1, source_target_pairs={{0,4},{4,0},{8,12},{12,8},{16,20},{20,16},{24,28},{28,24},{1,5},{5... | collective-permute-start | bytes 3145736 | tf_op jit(solution)/shard_map/ppermute | solution.py:40
  247.4 80.5 %collective-permute-start.57 = (bf16[128,1024]{1,0:T(8,128)(2,1)}, bf16[128,1024]{1,0:T(8,128)(2,1)}, u32[]{:S(2)}, u32[]{:S(2)}) collective-permute-start(bf16[128,1024]{1,0:T(8,128)(2,1)} %get-tuple-element.136), channel_id=1, source_target_pairs={{0,1},{1,0},{2,3},{3,2},{4,5},{5,4},{6,7},{7,6},{8,9},{9,8},{10,11... | collective-permute-start | bytes 786440 | tf_op jit(solution)/shard_map/ppermute | solution.py:40
  248.9 41.0 %collective-permute-start.56 = (bf16[128,1024]{1,0:T(8,128)(2,1)}, bf16[128,1024]{1,0:T(8,128)(2,1)}, u32[]{:S(2)}, u32[]{:S(2)}) collective-permute-start(bf16[128,1024]{1,0:T(8,128)(2,1)} %get-tuple-element.136), channel_id=1, source_target_pairs={{0,2},{1,3},{2,0},{3,1},{4,6},{5,7},{6,4},{7,5},{8,10},{9,11},{10,... | collective-permute-start | bytes 786440 | tf_op jit(solution)/shard_map/ppermute | solution.py:46
  251.2 36.6 %collective-permute-start.52 = (bf16[128,1024]{1,0:T(8,128)(2,1)}, bf16[128,1024]{1,0:T(8,128)(2,1)S(1)}, u32[]{:S(2)}, u32[]{:S(2)}) collective-permute-start(bf16[128,1024]{1,0:T(8,128)(2,1)} %bitcast.223), channel_id=1, source_target_pairs={{0,24},{4,28},{8,0},{12,4},{16,8},{20,12},{24,16},{28,20},{1,25},{... | collective-permute-start | bytes 786440 | tf_op jit(solution)/shard_map/ppermute | solution.py:46
  253.5 24.7 %collective-permute-start.27 = (bf16[4,128,1024]{2,1,0:T(8,128)(2,1)}, bf16[4,128,1024]{2,1,0:T(8,128)(2,1)S(1)}, u32[]{:S(2)}, u32[]{:S(2)}) collective-permute-start(bf16[4,128,1024]{2,1,0:T(8,128)(2,1)} %bitcast_dynamic-update-slice_fusion.5), channel_id=1, source_target_pairs={{0,4},{4,0},{8,12},{12,8},{16,20},{20,16},{24,28},{28,24},{1,5},{5... | collective-permute-start | bytes 3145736 | tf_op jit(solution)/shard_map/ppermute | solution.py:40
  287.7 20.3 %collective-permute-start.36 = (bf16[4,96,1024]{2,1,0:T(8,128)(2,1)S(1)}, bf16[4,96,1024]{2,1,0:T(8,128)(2,1)S(1)}, u32[]{:S(2)}, u32[]{:S(2)}) collective-permute-start(bf16[4,96,1024]{2,1,0:T(8,128)(2,1)S(1)} %copy-done.30), channel_id=1, source_target_pairs={{0,4},{4,0},{8,12},{12,8},{16,20},{20,16},{24,28},{28,24},{1,5},{5... | collective-permute-start | bytes 2359304 | tf_op jit(solution)/shard_map/ppermute | solution.py:40
  290.0 41.5 %collective-permute-start.49 = (bf16[4,128,1024]{2,1,0:T(8,128)(2,1)}, bf16[4,128,1024]{2,1,0:T(8,128)(2,1)}, u32[]{:S(2)}, u32[]{:S(2)}) collective-permute-start(bf16[4,128,1024]{2,1,0:T(8,128)(2,1)} %constant_dynamic-update-slice_fusion), channel_id=1, source_target_pairs={{0,4},{4,0},{8,12},{12,8},{16,20},{20,16},{24,28},{28,24},{1,5},{5... | collective-permute-start | bytes 3145736 | tf_op jit(solution)/shard_map/ppermute | solution.py:40
  292.4 60.4 %collective-permute-start.53 = (bf16[4,128,1024]{2,1,0:T(8,128)(2,1)}, bf16[4,128,1024]{2,1,0:T(8,128)(2,1)}, u32[]{:S(2)}, u32[]{:S(2)}) collective-permute-start(bf16[4,128,1024]{2,1,0:T(8,128)(2,1)} %bitcast_dynamic-update-slice_fusion.2), channel_id=1, source_target_pairs={{0,4},{4,0},{8,12},{12,8},{16,20},{20,16},{24,28},{28,24},{1,5},{5... | collective-permute-start | bytes 3145736 | tf_op jit(solution)/shard_map/ppermute | solution.py:40
  310.1 17.8 %collective-permute-start.58 = (bf16[128,1024]{1,0:T(8,128)(2,1)}, bf16[128,1024]{1,0:T(8,128)(2,1)}, u32[]{:S(2)}, u32[]{:S(2)}) collective-permute-start(bf16[128,1024]{1,0:T(8,128)(2,1)} %collective-permute-done.56), channel_id=1, source_target_pairs={{0,1},{1,0},{2,3},{3,2},{4,5},{5,4},{6,7},{7,6},{8,9},{9,8},{10,11... | collective-permute-start | bytes 786440 | tf_op jit(solution)/shard_map/ppermute | solution.py:40
  367.3 26.1 %collective-permute-start.134 = (bf16[4,128,1024]{2,1,0:T(8,128)(2,1)S(1)}, bf16[4,128,1024]{2,1,0:T(8,128)(2,1)S(1)}, u32[]{:S(2)}, u32[]{:S(2)}) collective-permute-start(bf16[4,128,1024]{2,1,0:T(8,128)(2,1)S(1)} %dynamic-slice_bitcast_fusion), channel_id=1, source_target_pairs={{0,4},{4,0},{8,12},{12,8},{16,20},{20,16},{24,28},{28,24},{1,5},{5... | collective-permute-start | bytes 3145736 | tf_op jit(solution)/shard_map/ppermute | solution.py:40
  368.9 46.1 %collective-permute-start.120 = (bf16[4,128,1024]{2,1,0:T(8,128)(2,1)S(1)}, bf16[4,128,1024]{2,1,0:T(8,128)(2,1)S(1)}, u32[]{:S(2)}, u32[]{:S(2)}) collective-permute-start(bf16[4,128,1024]{2,1,0:T(8,128)(2,1)S(1)} %dynamic-slice_bitcast_fusion.2), channel_id=1, source_target_pairs={{0,4},{4,0},{8,12},{12,8},{16,20},{20,16},{24,28},{28,24},{1,5},{5... | collective-permute-start | bytes 3145736 | tf_op jit(solution)/shard_map/ppermute | solution.py:40
  385.1 31.4 %collective-permute-start.62 = (bf16[128,1024]{1,0:T(8,128)(2,1)S(1)}, bf16[128,1024]{1,0:T(8,128)(2,1)S(1)}, u32[]{:S(2)}, u32[]{:S(2)}) collective-permute-start(bf16[128,1024]{1,0:T(8,128)(2,1)S(1)} %get-tuple-element.133), channel_id=1, source_target_pairs={{0,1},{1,0},{2,3},{3,2},{4,5},{5,4},{6,7},{7,6},{8,9},{9,8},{10,11... | collective-permute-start | bytes 786440 | tf_op jit(solution)/shard_map/ppermute | solution.py:40
  393.9 33.8 %collective-permute-start.135 = (bf16[128,1024]{1,0:T(8,128)(2,1)S(1)}, bf16[128,1024]{1,0:T(8,128)(2,1)S(1)}, u32[]{:S(2)}, u32[]{:S(2)}) collective-permute-start(bf16[128,1024]{1,0:T(8,128)(2,1)S(1)} %get-tuple-element.160), channel_id=1, source_target_pairs={{0,8},{4,12},{8,16},{12,20},{16,24},{20,28},{24,0},{28,4},{1,9},{5... | collective-permute-start | bytes 786440 | tf_op jit(solution)/shard_map/ppermute | solution.py:46
  395.5 32.2 %collective-permute-start.137 = (bf16[128,1024]{1,0:T(8,128)(2,1)S(1)}, bf16[128,1024]{1,0:T(8,128)(2,1)S(1)}, u32[]{:S(2)}, u32[]{:S(2)}) collective-permute-start(bf16[128,1024]{1,0:T(8,128)(2,1)S(1)} %get-tuple-element.161), channel_id=1, source_target_pairs={{0,24},{4,28},{8,0},{12,4},{16,8},{20,12},{24,16},{28,20},{1,25},{... | collective-permute-start | bytes 786440 | tf_op jit(solution)/shard_map/ppermute | solution.py:46
  397.8 29.9 %collective-permute-start.136 = (bf16[128,1024]{1,0:T(8,128)(2,1)S(1)}, bf16[128,1024]{1,0:T(8,128)(2,1)S(1)}, u32[]{:S(2)}, u32[]{:S(2)}) collective-permute-start(bf16[128,1024]{1,0:T(8,128)(2,1)S(1)} %get-tuple-element.162), channel_id=1, source_target_pairs={{0,16},{4,20},{8,24},{12,28},{16,0},{20,4},{24,8},{28,12},{1,17},{... | collective-permute-start | bytes 786440 | tf_op jit(solution)/shard_map/ppermute | solution.py:46
  416.5 43.1 %collective-permute-start.121 = (bf16[128,1024]{1,0:T(8,128)(2,1)}, bf16[128,1024]{1,0:T(8,128)(2,1)}, u32[]{:S(2)}, u32[]{:S(2)}) collective-permute-start(bf16[128,1024]{1,0:T(8,128)(2,1)} %get-tuple-element.166), channel_id=1, source_target_pairs={{0,8},{4,12},{8,16},{12,20},{16,24},{20,28},{24,0},{28,4},{1,9},{5... | collective-permute-start | bytes 786440 | tf_op jit(solution)/shard_map/ppermute | solution.py:46
  418.1 43.0 %collective-permute-start.123 = (bf16[128,1024]{1,0:T(8,128)(2,1)}, bf16[128,1024]{1,0:T(8,128)(2,1)}, u32[]{:S(2)}, u32[]{:S(2)}) collective-permute-start(bf16[128,1024]{1,0:T(8,128)(2,1)} %get-tuple-element.167), channel_id=1, source_target_pairs={{0,24},{4,28},{8,0},{12,4},{16,8},{20,12},{24,16},{28,20},{1,25},{... | collective-permute-start | bytes 786440 | tf_op jit(solution)/shard_map/ppermute | solution.py:46
  427.7 33.5 %collective-permute-start.122 = (bf16[128,1024]{1,0:T(8,128)(2,1)}, bf16[128,1024]{1,0:T(8,128)(2,1)}, u32[]{:S(2)}, u32[]{:S(2)}) collective-permute-start(bf16[128,1024]{1,0:T(8,128)(2,1)} %get-tuple-element.168), channel_id=1, source_target_pairs={{0,16},{4,20},{8,24},{12,28},{16,0},{20,4},{24,8},{28,12},{1,17},{... | collective-permute-start | bytes 786440 | tf_op jit(solution)/shard_map/ppermute | solution.py:46
  428.6 64.7 %collective-permute-start.139 = (bf16[128,1024]{1,0:T(8,128)(2,1)}, bf16[128,1024]{1,0:T(8,128)(2,1)}, u32[]{:S(2)}, u32[]{:S(2)}) collective-permute-start(bf16[128,1024]{1,0:T(8,128)(2,1)} %fusion.75), channel_id=1, source_target_pairs={{0,1},{1,0},{2,3},{3,2},{4,5},{5,4},{6,7},{7,6},{8,9},{9,8},{10,11... | collective-permute-start | bytes 786440 | tf_op jit(solution)/shard_map/ppermute | solution.py:40
  428.6 52.1 %collective-permute-start.138 = (bf16[128,1024]{1,0:T(8,128)(2,1)}, bf16[128,1024]{1,0:T(8,128)(2,1)}, u32[]{:S(2)}, u32[]{:S(2)}) collective-permute-start(bf16[128,1024]{1,0:T(8,128)(2,1)} %fusion.75), channel_id=1, source_target_pairs={{0,2},{1,3},{2,0},{3,1},{4,6},{5,7},{6,4},{7,5},{8,10},{9,11},{10,... | collective-permute-start | bytes 786440 | tf_op jit(solution)/shard_map/ppermute | solution.py:46
  466.1 22.2 %collective-permute-start.124 = (bf16[128,1024]{1,0:T(8,128)(2,1)}, bf16[128,1024]{1,0:T(8,128)(2,1)}, u32[]{:S(2)}, u32[]{:S(2)}) collective-permute-start(bf16[128,1024]{1,0:T(8,128)(2,1)} %fusion.81), channel_id=1, source_target_pairs={{0,2},{1,3},{2,0},{3,1},{4,6},{5,7},{6,4},{7,5},{8,10},{9,11},{10,... | collective-permute-start | bytes 786440 | tf_op jit(solution)/shard_map/ppermute | solution.py:46
  483.3 16.4 %collective-permute-start.125 = (bf16[128,1024]{1,0:T(8,128)(2,1)}, bf16[128,1024]{1,0:T(8,128)(2,1)S(1)}, u32[]{:S(2)}, u32[]{:S(2)}) collective-permute-start(bf16[128,1024]{1,0:T(8,128)(2,1)} %fusion.81), channel_id=1, source_target_pairs={{0,1},{1,0},{2,3},{3,2},{4,5},{5,4},{6,7},{7,6},{8,9},{9,8},{10,11... | collective-permute-start | bytes 786440 | tf_op jit(solution)/shard_map/ppermute | solution.py:40
  491.1 20.0 %collective-permute-start.89 = (bf16[4,96,1024]{2,1,0:T(8,128)(2,1)S(1)}, bf16[4,96,1024]{2,1,0:T(8,128)(2,1)S(1)}, u32[]{:S(2)}, u32[]{:S(2)}) collective-permute-start(bf16[4,96,1024]{2,1,0:T(8,128)(2,1)S(1)} %copy-done.76), channel_id=1, source_target_pairs={{0,4},{4,0},{8,12},{12,8},{16,20},{20,16},{24,28},{28,24},{1,5},{5... | collective-permute-start | bytes 2359304 | tf_op jit(solution)/shard_map/ppermute | solution.py:40
  516.2 16.5 %collective-permute-start.91 = (bf16[96,1024]{1,0:T(8,128)(2,1)S(1)}, bf16[96,1024]{1,0:T(8,128)(2,1)}, u32[]{:S(2)}, u32[]{:S(2)}) collective-permute-start(bf16[96,1024]{1,0:T(8,128)(2,1)S(1)} %get-tuple-element.192), channel_id=1, source_target_pairs={{0,16},{4,20},{8,24},{12,28},{16,0},{20,4},{24,8},{28,12},{1,17},{... | collective-permute-start | bytes 589832 | tf_op jit(solution)/shard_map/ppermute | solution.py:46
  517.2 18.6 %collective-permute-start.66 = (bf16[128,1024]{1,0:T(8,128)(2,1)S(1)}, bf16[128,1024]{1,0:T(8,128)(2,1)S(1)}, u32[]{:S(2)}, u32[]{:S(2)}) collective-permute-start(bf16[128,1024]{1,0:T(8,128)(2,1)S(1)} %get-tuple-element.130), channel_id=1, source_target_pairs={{0,2},{1,3},{2,0},{3,1},{4,6},{5,7},{6,4},{7,5},{8,10},{9,11},{10,... | collective-permute-start | bytes 786440 | tf_op jit(solution)/shard_map/ppermute | solution.py:46
  524.6 17.0 %collective-permute-start.67 = (bf16[128,1024]{1,0:T(8,128)(2,1)S(1)}, bf16[128,1024]{1,0:T(8,128)(2,1)S(1)}, u32[]{:S(2)}, u32[]{:S(2)}) collective-permute-start(bf16[128,1024]{1,0:T(8,128)(2,1)S(1)} %get-tuple-element.130), channel_id=1, source_target_pairs={{0,1},{1,0},{2,3},{3,2},{4,5},{5,4},{6,7},{7,6},{8,9},{9,8},{10,11... | collective-permute-start | bytes 786440 | tf_op jit(solution)/shard_map/ppermute | solution.py:40
  534.1 19.5 %collective-permute-start.94 = (bf16[96,1024]{1,0:T(8,128)(2,1)S(1)}, bf16[96,1024]{1,0:T(8,128)(2,1)S(1)}, u32[]{:S(2)}, u32[]{:S(2)}) collective-permute-start(bf16[96,1024]{1,0:T(8,128)(2,1)S(1)} %fusion.107), channel_id=1, source_target_pairs={{0,1},{1,0},{2,3},{3,2},{4,5},{5,4},{6,7},{7,6},{8,9},{9,8},{10,11... | collective-permute-start | bytes 589832 | tf_op jit(solution)/shard_map/ppermute | solution.py:40
  550.7 26.1 %collective-permute-start.113 = (bf16[4,128,1024]{2,1,0:T(8,128)(2,1)S(1)}, bf16[4,128,1024]{2,1,0:T(8,128)(2,1)S(1)}, u32[]{:S(2)}, u32[]{:S(2)}) collective-permute-start(bf16[4,128,1024]{2,1,0:T(8,128)(2,1)S(1)} %dynamic-slice_bitcast_fusion.3), channel_id=1, source_target_pairs={{0,4},{4,0},{8,12},{12,8},{16,20},{20,16},{24,28},{28,24},{1,5},{5... | collective-permute-start | bytes 3145736 | tf_op jit(solution)/shard_map/ppermute | solution.py:40
  551.4 47.0 %collective-permute-start.127 = (bf16[4,128,1024]{2,1,0:T(8,128)(2,1)S(1)}, bf16[4,128,1024]{2,1,0:T(8,128)(2,1)S(1)}, u32[]{:S(2)}, u32[]{:S(2)}) collective-permute-start(bf16[4,128,1024]{2,1,0:T(8,128)(2,1)S(1)} %dynamic-slice_bitcast_fusion.1), channel_id=1, source_target_pairs={{0,4},{4,0},{8,12},{12,8},{16,20},{20,16},{24,28},{28,24},{1,5},{5... | collective-permute-start | bytes 3145736 | tf_op jit(solution)/shard_map/ppermute | solution.py:40
  563.5 35.5 %collective-permute-start.71 = (bf16[128,1024]{1,0:T(8,128)(2,1)S(1)}, bf16[128,1024]{1,0:T(8,128)(2,1)S(1)}, u32[]{:S(2)}, u32[]{:S(2)}) collective-permute-start(bf16[128,1024]{1,0:T(8,128)(2,1)S(1)} %get-tuple-element.127), channel_id=1, source_target_pairs={{0,2},{1,3},{2,0},{3,1},{4,6},{5,7},{6,4},{7,5},{8,10},{9,11},{10,... | collective-permute-start | bytes 786440 | tf_op jit(solution)/shard_map/ppermute | solution.py:46
  577.3 25.6 %collective-permute-start.114 = (bf16[128,1024]{1,0:T(8,128)(2,1)S(1)}, bf16[128,1024]{1,0:T(8,128)(2,1)S(1)}, u32[]{:S(2)}, u32[]{:S(2)}) collective-permute-start(bf16[128,1024]{1,0:T(8,128)(2,1)S(1)} %get-tuple-element.163), channel_id=1, source_target_pairs={{0,8},{4,12},{8,16},{12,20},{16,24},{20,28},{24,0},{28,4},{1,9},{5... | collective-permute-start | bytes 786440 | tf_op jit(solution)/shard_map/ppermute | solution.py:46
  577.4 25.6 %collective-permute-start.116 = (bf16[128,1024]{1,0:T(8,128)(2,1)S(1)}, bf16[128,1024]{1,0:T(8,128)(2,1)S(1)}, u32[]{:S(2)}, u32[]{:S(2)}) collective-permute-start(bf16[128,1024]{1,0:T(8,128)(2,1)S(1)} %get-tuple-element.164), channel_id=1, source_target_pairs={{0,24},{4,28},{8,0},{12,4},{16,8},{20,12},{24,16},{28,20},{1,25},{... | collective-permute-start | bytes 786440 | tf_op jit(solution)/shard_map/ppermute | solution.py:46
  581.2 21.9 %collective-permute-start.115 = (bf16[128,1024]{1,0:T(8,128)(2,1)S(1)}, bf16[128,1024]{1,0:T(8,128)(2,1)S(1)}, u32[]{:S(2)}, u32[]{:S(2)}) collective-permute-start(bf16[128,1024]{1,0:T(8,128)(2,1)S(1)} %get-tuple-element.165), channel_id=1, source_target_pairs={{0,16},{4,20},{8,24},{12,28},{16,0},{20,4},{24,8},{28,12},{1,17},{... | collective-permute-start | bytes 786440 | tf_op jit(solution)/shard_map/ppermute | solution.py:46
  603.0 20.1 %collective-permute-start.129 = (bf16[128,1024]{1,0:T(8,128)(2,1)S(1)}, bf16[128,1024]{1,0:T(8,128)(2,1)S(1)}, u32[]{:S(2)}, u32[]{:S(2)}) collective-permute-start(bf16[128,1024]{1,0:T(8,128)(2,1)S(1)} %get-tuple-element.159), channel_id=1, source_target_pairs={{0,16},{4,20},{8,24},{12,28},{16,0},{20,4},{24,8},{28,12},{1,17},{... | collective-permute-start | bytes 786440 | tf_op jit(solution)/shard_map/ppermute | solution.py:46
  603.0 20.9 %collective-permute-start.72 = (bf16[128,1024]{1,0:T(8,128)(2,1)S(1)}, bf16[128,1024]{1,0:T(8,128)(2,1)S(1)}, u32[]{:S(2)}, u32[]{:S(2)}) collective-permute-start(bf16[128,1024]{1,0:T(8,128)(2,1)S(1)} %get-tuple-element.127), channel_id=1, source_target_pairs={{0,1},{1,0},{2,3},{3,2},{4,5},{5,4},{6,7},{7,6},{8,9},{9,8},{10,11... | collective-permute-start | bytes 786440 | tf_op jit(solution)/shard_map/ppermute | solution.py:40
  603.1 20.8 %collective-permute-start.73 = (bf16[128,1024]{1,0:T(8,128)(2,1)S(1)}, bf16[128,1024]{1,0:T(8,128)(2,1)S(1)}, u32[]{:S(2)}, u32[]{:S(2)}) collective-permute-start(bf16[128,1024]{1,0:T(8,128)(2,1)S(1)} %collective-permute-done.71), channel_id=1, source_target_pairs={{0,1},{1,0},{2,3},{3,2},{4,5},{5,4},{6,7},{7,6},{8,9},{9,8},{10,11... | collective-permute-start | bytes 786440 | tf_op jit(solution)/shard_map/ppermute | solution.py:40
  610.0 85.4 %collective-permute-start.118 = (bf16[128,1024]{1,0:T(8,128)(2,1)}, bf16[128,1024]{1,0:T(8,128)(2,1)}, u32[]{:S(2)}, u32[]{:S(2)}) collective-permute-start(bf16[128,1024]{1,0:T(8,128)(2,1)} %fusion.84), channel_id=1, source_target_pairs={{0,1},{1,0},{2,3},{3,2},{4,5},{5,4},{6,7},{7,6},{8,9},{9,8},{10,11... | collective-permute-start | bytes 786440 | tf_op jit(solution)/shard_map/ppermute | solution.py:40
  613.6 67.6 %collective-permute-start.117 = (bf16[128,1024]{1,0:T(8,128)(2,1)}, bf16[128,1024]{1,0:T(8,128)(2,1)}, u32[]{:S(2)}, u32[]{:S(2)}) collective-permute-start(bf16[128,1024]{1,0:T(8,128)(2,1)} %fusion.84), channel_id=1, source_target_pairs={{0,2},{1,3},{2,0},{3,1},{4,6},{5,7},{6,4},{7,5},{8,10},{9,11},{10,... | collective-permute-start | bytes 786440 | tf_op jit(solution)/shard_map/ppermute | solution.py:46
  669.3 17.9 %collective-permute-start.131 = (bf16[128,1024]{1,0:T(8,128)(2,1)S(1)}, bf16[128,1024]{1,0:T(8,128)(2,1)S(1)}, u32[]{:S(2)}, u32[]{:S(2)}) collective-permute-start(bf16[128,1024]{1,0:T(8,128)(2,1)S(1)} %copy-done.75), channel_id=1, source_target_pairs={{0,2},{1,3},{2,0},{3,1},{4,6},{5,7},{6,4},{7,5},{8,10},{9,11},{10,... | collective-permute-start | bytes 786440 | tf_op jit(solution)/shard_map/ppermute | solution.py:46
  691.0 21.5 %collective-permute-start.82 = (bf16[4,96,1024]{2,1,0:T(8,128)(2,1)}, bf16[4,96,1024]{2,1,0:T(8,128)(2,1)}, u32[]{:S(2)}, u32[]{:S(2)}) collective-permute-start(bf16[4,96,1024]{2,1,0:T(8,128)(2,1)} %dynamic-slice_bitcast_fusion.5), channel_id=1, source_target_pairs={{0,4},{4,0},{8,12},{12,8},{16,20},{20,16},{24,28},{28,24},{1,5},{5... | collective-permute-start | bytes 2359304 | tf_op jit(solution)/shard_map/ppermute | solution.py:40
  714.3 25.1 %collective-permute-start.83 = (bf16[96,1024]{1,0:T(8,128)(2,1)S(1)}, bf16[96,1024]{1,0:T(8,128)(2,1)S(1)}, u32[]{:S(2)}, u32[]{:S(2)}) collective-permute-start(bf16[96,1024]{1,0:T(8,128)(2,1)S(1)} %get-tuple-element.187), channel_id=1, source_target_pairs={{0,8},{4,12},{8,16},{12,20},{16,24},{20,28},{24,0},{28,4},{1,9},{5... | collective-permute-start | bytes 589832 | tf_op jit(solution)/shard_map/ppermute | solution.py:46
  714.4 25.0 %collective-permute-start.85 = (bf16[96,1024]{1,0:T(8,128)(2,1)S(1)}, bf16[96,1024]{1,0:T(8,128)(2,1)S(1)}, u32[]{:S(2)}, u32[]{:S(2)}) collective-permute-start(bf16[96,1024]{1,0:T(8,128)(2,1)S(1)} %get-tuple-element.188), channel_id=1, source_target_pairs={{0,24},{4,28},{8,0},{12,4},{16,8},{20,12},{24,16},{28,20},{1,25},{... | collective-permute-start | bytes 589832 | tf_op jit(solution)/shard_map/ppermute | solution.py:46
  (324 other events, 2317.8 us)

commit v2 on v1

--- a/solution.py
+++ b/solution.py
@@ -3,6 +3,8 @@
 import jax
 import jax.numpy as jnp
 from jax import lax
+from jax.experimental import pallas as pl
+from jax.experimental.pallas import tpu as pltpu
 from jax.sharding import PartitionSpec as P
 
 EPS = 1e-05
@@ -209,7 +211,7 @@
         return dot(self.long, long.astype(BF), 0, 0) + jnp.pad(head, ((0, self.half - self.most), (0, 0)))
 
 
-def body(
+def body_any(
     tokens,
     lengths,
     cotangent,
@@ -456,6 +458,813 @@
     )
 
 
+ORDER = (0, 2, 1, 3)
+VMEM_BYTES = 56 * 2**20
+SMALL = 64
+SLOT = 24
+COST = 1000
+UP_AT = 48
+TOK = 52
+
+
+def run(kernel, outs, meta, args, scratch=(), flops=0, alias=None):
+    specs, arrays = [], []
+    for a in args:
+        if isinstance(a, tuple):
+            array, block, place = a
+            if block is None:
+                specs.append(pl.BlockSpec(memory_space=pl.ANY))
+            else:
+                specs.append(pl.BlockSpec(block, place, pipeline_mode=pl.Buffered(1)))
+            arrays.append(array)
+        else:
+            specs.append(pl.BlockSpec(memory_space=pltpu.VMEM))
+            arrays.append(a)
+    out_specs, shapes = [], []
+    for o in outs:
+        shapes.append(jax.ShapeDtypeStruct(o[0], o[1]))
+        if len(o) > 2:
+            out_specs.append(pl.BlockSpec(o[2], o[3], pipeline_mode=pl.Buffered(1)))
+        else:
+            out_specs.append(pl.BlockSpec(memory_space=pltpu.VMEM))
+    moved = sum(o.size * o.dtype.itemsize for o in shapes) + sum(a.size * a.dtype.itemsize for a in arrays)
+    return pl.pallas_call(
+        kernel,
+        out_shape=shapes,
+        grid_spec=pltpu.PrefetchScalarGridSpec(
+            num_scalar_prefetch=1,
+            grid=(1,),
+            in_specs=specs,
+            out_specs=out_specs,
+            scratch_shapes=[pltpu.VMEM(shape, kind) for shape, kind in scratch],
+        ),
+        input_output_aliases=alias or {},
+        compiler_params=pltpu.CompilerParams(vmem_limit_bytes=VMEM_BYTES),
+        cost_estimate=pl.CostEstimate(flops=flops // COST, bytes_accessed=moved // COST, transcendentals=0),
+    )(meta, *arrays)
+
+
+def join(meta, parts, all_ref):
+    rows = parts[0].shape[0]
+    for k, part in enumerate(parts):
+        at = pl.multiple_of((meta[0] ^ ORDER[k]) * rows, rows)
+        all_ref[pl.ds(at, rows), :] = part[...]
+
+
+def owners(meta, refs):
+    if len(refs) == 1:
+        return [(g, refs[0].at[g]) for g in range(refs[0].shape[0])]
+    half = refs[0].shape[0]
+    found = []
+    for k in range(half):
+        at = 2 * lax.rem(meta[1] - k + half, half)
+        found.append((at + meta[2], refs[0].at[k]))
+        found.append((at + 1 - meta[2], refs[1].at[k]))
+    return found
+
+
+def span(g, size):
+    if isinstance(g, int):
+        return pl.ds(g * size, size)
+    return pl.ds(pl.multiple_of(g * size, size), size)
+
+
+def place_wide(meta, refs, wide):
+    rows = wide.shape[0]
+    for g, block in owners(meta, refs):
+        wide[:, span(g, block.shape[-1])] = block[:rows, :]
+
+
+def place_io(meta, refs, wi, wo):
+    n_grp = wi.shape[1] // 128
+    part = wi.shape[0] // n_grp
+    q = part // 3
+    for g, block in owners(meta, refs):
+        for lb in range(n_grp):
+            at = lb * 4 * q
+            wi[span(g, part), lb * 128 : (lb + 1) * 128] = block[at : at + part, :]
+            wo[lb * q : (lb + 1) * q, span(g, 128)] = block[at + part : at + part + q, :]
+
+
+def part_out(meta, value, at, send, keep):
+    rows = value.shape[0] // 4
+    w = value.shape[1]
+    even = jnp.stack([value[:rows], value[2 * rows : 3 * rows]])
+    odd = jnp.stack([value[rows : 2 * rows], value[3 * rows :]])
+    low = meta[4] == 0
+    keep[:, :, at : at + w] = jnp.where(low, even, odd)
+    send[:, :, at : at + w] = jnp.where(low, odd, even).astype(BF)
+
+
+def masks_of(meta, total, wide, count):
+    place = lax.broadcasted_iota(jnp.int32, (total, wide), 0)
+    begin = jnp.zeros((total, wide), jnp.int32)
+    for k in range(count):
+        begin = jnp.where(place >= meta[5 + k], meta[5 + k], begin)
+    return place, [None] + [place - lag >= begin for lag in (1, 2)]
+
+
+def roll_down(v, lag):
+    return pltpu.roll(v, lag, 0)
+
+
+def stream_z(chan, j, wide, rows5, masks):
+    at = j * wide
+    v = chan[:, at : at + wide].astype(F32)
+    z = rows5[4:5, at : at + wide] + rows5[1:2, at : at + wide] * v
+    for lag in (1, 2):
+        z = z + rows5[1 + lag : 2 + lag, at : at + wide] * jnp.where(masks[lag], roll_down(v, lag), 0.0)
+    return z
+
+
+def spectra(v, long, short):
+    half = v.shape[0] // 2
+    low = v.astype(BF)
+    return dot(long[...], low[:half], 1, 0), dot(short[...], low[half:], 1, 0)
+
+
+def filt_spectra(filt, long, short0):
+    low = filt.astype(BF)
+    return dot(long[...], low, 1, 0), dot(short0[...], low[: short0.shape[1]], 1, 0)
+
+
+def each(long, short, count):
+    half = long.shape[0] // 2
+    most = short.shape[0] // count // 2
+    pairs = [(long[:half], long[half:])]
+    for k in range(count):
+        pairs.append((short[2 * k * most : (2 * k + 1) * most], short[(2 * k + 1) * most : (2 * k + 2) * most]))
+    return pairs
+
+
+def unspectra(pairs, long_t, short_t):
+    half, most = pairs[0][0].shape[0], pairs[1][0].shape[0]
+    long = (jnp.concatenate(pairs[0]) * (1.0 / half)).astype(BF)
+    short = (jnp.concatenate([v for pair in pairs[1:] for v in pair]) * (1.0 / most)).astype(BF)
+    return jnp.concatenate([dot(long_t[...], long, 1, 0), dot(short_t[...], short, 1, 0)])
+
+
+def exact(a, b, da, db):
+    return lax.dot_general(a, b, (((da,), (db,)), ((), ())), precision=HIGH, preferred_element_type=F32)
+
+
+def mix_forth_kernel(count, nio, raw, meta, *refs):
+    parts, refs = refs[:4], refs[4:]
+    io, refs = refs[:nio], refs[nio:]
+    (long, long_t, short, short_t, short0, second, decay, fout, rows5, skip, gain, shift,
+     every, chan, inner_ref, mixed_ref, send, keep, wi, wo) = refs
+    join(meta, parts, every)
+    if raw:
+        every[...] = (every[...].astype(F32) * gain[...] + shift[...]).astype(BF)
+    place_io(meta, io, wi, wo)
+    total, wide = mixed_ref.shape
+    _, masks = masks_of(meta, total, wide, count)
+    z = []
+    for j in range(3):
+        at = j * wide
+        proj = dot(every[...], wi[at : at + wide, :], 1, 1) + rows5[0:1, at : at + wide]
+        chan[:, at : at + wide] = proj.astype(BF)
+        z.append(stream_z(chan, j, wide, rows5, masks))
+    prod = z[1] * z[2]
+    filt = exact(second[...], fout[...], 1, 0) * decay[...]
+    hs = each(*filt_spectra(filt, long, short0), 1)
+    xs = each(*spectra(prod, long, short), count)
+    ys = [times(*x, *hs[min(k, 1)]) for k, x in enumerate(xs)]
+    inner = unspectra(ys, long_t, short_t) + skip[...] * prod
+    inner_ref[...] = inner
+    mixed_ref[...] = (z[0] * inner).astype(BF)
+    for n in range(4):
+        w = wo.shape[1] // 4
+        part_out(meta, dot(mixed_ref[...], wo[:, n * w : (n + 1) * w], 1, 0), n * w, send, keep)
+
+
+def mix_back_kernel(count, nio, meta, *refs):
+    parts, refs = refs[:4], refs[4:]
+    io, refs = refs[:nio], refs[nio:]
+    (long, long_t, short, short_t, short0, short0_t, second, decay, fout, rows5, skip, chan, inner,
+     every, g_proj_ref, g_fout, g_second, small, send, keep, wi, wo) = refs
+    join(meta, parts, every)
+    place_io(meta, io, wi, wo)
+    total, wide = inner.shape
+    place, masks = masks_of(meta, total, wide, count)
+    z = [stream_z(chan, j, wide, rows5, masks) for j in range(3)]
+    prod = z[1] * z[2]
+    filt = exact(second[...], fout[...], 1, 0) * decay[...]
+    hs = each(*filt_spectra(filt, long, short0), 1)
+    xs = each(*spectra(prod, long, short), count)
+    g_y = dot(every[...], wo[...], 1, 1).astype(BF).astype(F32)
+    g_conv = g_y * z[0]
+    ys = each(*spectra(g_conv, long, short), count)
+    corr = unspectra([times_conj(*y, *hs[min(k, 1)]) for k, y in enumerate(ys)], long_t, short_t)
+    g_prod = corr + skip[...] * g_conv
+    small[...] = jnp.zeros_like(small)
+    small[5:6, :wide] = jnp.sum(g_conv * prod, axis=0, keepdims=True)
+    for j, g_z in enumerate((g_y * inner[...], g_prod * z[2], g_prod * z[1])):
+        at = j * wide
+        v = chan[:, at : at + wide].astype(F32)
+        small[4:5, at : at + wide] = jnp.sum(g_z, axis=0, keepdims=True)
+        small[1:2, at : at + wide] = jnp.sum(g_z * v, axis=0, keepdims=True)
+        g_proj = rows5[1:2, at : at + wide] * g_z
+        for lag in (1, 2):
+            kept = jnp.where(masks[lag], g_z, 0.0)
+            small[1 + lag : 2 + lag, at : at + wide] = jnp.sum(kept * roll_down(v, lag), axis=0, keepdims=True)
+            moved = jnp.where(place < total - lag, roll_down(kept, total - lag), 0.0)
+            g_proj = g_proj + rows5[1 + lag : 2 + lag, at : at + wide] * moved
+        low = g_proj.astype(BF)
+        g_proj_ref[:, at : at + wide] = low
+        small[0:1, at : at + wide] = jnp.sum(low.astype(F32), axis=0, keepdims=True)
+    for n in range(4):
+        w = wi.shape[1] // 4
+        part_out(meta, dot(g_proj_ref[...], wi[:, n * w : (n + 1) * w], 1, 0), n * w, send, keep)
+    fs = [times_conj(*y, *x) for y, x in zip(ys, xs)]
+    f_short = fs[1]
+    for pair in fs[2:]:
+        f_short = (f_short[0] + pair[0], f_short[1] + pair[1])
+    half, most = fs[0][0].shape[0], f_short[0].shape[0]
+    g_filt = dot(long_t[...], (jnp.concatenate(fs[0]) * (1.0 / half)).astype(BF), 1, 0)
+    head = dot(short0_t[...], (jnp.concatenate(f_short) * (1.0 / most)).astype(BF), 1, 0)
+    g_filt = jnp.concatenate([g_filt[:most] + head, g_filt[most:]]) * decay[...]
+    g_fout[...] = exact(second[...].T, g_filt, 1, 0)
+    g_second[...] = exact(g_filt, fout[...], 1, 1)
+
+
+def mlp_forth_kernel(nup, ndown, meta, *refs):
+    parts, refs = refs[:4], refs[4:]
+    up, refs = refs[:nup], refs[nup:]
+    down, refs = refs[:ndown], refs[ndown:]
+    b_up, every, hidden, slope, send, keep, wide_up, wide_down = refs
+    join(meta, parts, every)
+    place_wide(meta, up, wide_up)
+    tile = wide_up.shape[1] // 4
+    for n in range(4):
+        at = n * tile
+        pre = dot(every[...], wide_up[:, at : at + tile], 1, 0) + b_up[:, at : at + tile]
+        cdf = 0.5 * (1.0 + lax.erf(pre * INV_SQRT2))
+        hidden[:, at : at + tile] = (pre * cdf).astype(BF)
+        slope[:, at : at + tile] = (cdf + pre * (jnp.exp(-0.5 * pre * pre) * INV_SQRT2PI)).astype(BF)
+    place_wide(meta, down, wide_down)
+    tile = wide_down.shape[1] // 4
+    for n in range(4):
+        part_out(meta, dot(hidden[...], wide_down[:, n * tile : (n + 1) * tile], 1, 0), n * tile, send, keep)
+
+
+def mlp_back_kernel(nup, ndown, meta, *refs):
+    parts, refs = refs[:4], refs[4:]
+    up, refs = refs[:nup], refs[nup:]
+    down, refs = refs[:ndown], refs[ndown:]
+    slope, every, g_pre_ref, g_bias, send, keep, wide_up, wide_down = refs
+    join(meta, parts, every)
+    place_wide(meta, down, wide_down)
+    tile = slope.shape[1] // 4
+    for n in range(4):
+        at = n * tile
+        g_hidden = dot(every[...], wide_down[at : at + tile, :], 1, 1)
+        g_pre = (g_hidden * slope[:, at : at + tile].astype(F32)).astype(BF)
+        g_pre_ref[:, at : at + tile] = g_pre
+        g_bias[:, at : at + tile] = jnp.sum(g_pre.astype(F32), axis=0, keepdims=True)
+    place_wide(meta, up, wide_up)
+    tile = wide_up.shape[0] // 4
+    for n in range(4):
+        at = n * tile
+        part_out(meta, dot(g_pre_ref[...], wide_up[at : at + tile, :], 1, 1), at, send, keep)
+
+
+def hat_of(value):
+    center = value - jnp.mean(value, axis=-1, keepdims=True)
+    scale = lax.rsqrt(jnp.mean(center * center, axis=-1, keepdims=True) + EPS)
+    return center * scale, scale
+
+
+def first_norm_kernel(meta, tokens, cotangent, normed, low, sums):
+    hat, _ = hat_of(tokens[...].astype(F32))
+    normed[...] = hat.astype(BF)
+    rounded = cotangent[...].astype(BF)
+    low[...] = rounded
+    sums[...] = jnp.zeros_like(sums)
+    sums[2:3, :] = jnp.sum(rounded.astype(F32), axis=0, keepdims=True)
+
+
+def add_norm_kernel(meta, state, keep, got, crossed, bias, gain, shift, new, normed):
+    value = state[...].astype(F32) + (keep[0] + got[0].astype(F32) + crossed[...].astype(F32)) + bias[...]
+    new[...] = value
+    hat, _ = hat_of(value)
+    normed[...] = (hat * gain[...] + shift[...]).astype(BF)
+
+
+def add_kernel(meta, state, keep, got, crossed, bias, new):
+    new[...] = state[...] + (keep[0] + got[0].astype(F32) + crossed[...].astype(F32)) + bias[...]
+
+
+def norm_back_kernel(meta, grad, keep, got, crossed, value, gain, new, low, sums):
+    g = keep[0] + got[0].astype(F32) + crossed[...].astype(F32)
+    hat, scale = hat_of(value[...].astype(F32))
+    inner = g * gain[...]
+    mean_one = jnp.mean(inner, axis=-1, keepdims=True)
+    mean_two = jnp.mean(inner * hat, axis=-1, keepdims=True)
+    total = grad[...] + scale * (inner - mean_one - hat * mean_two)
+    new[...] = total
+    rounded = total.astype(BF)
+    low[...] = rounded
+    sums[...] = jnp.zeros_like(sums)
+    sums[0:1, :] = jnp.sum(g * hat, axis=0, keepdims=True)
+    sums[1:2, :] = jnp.sum(g, axis=0, keepdims=True)
+    sums[2:3, :] = jnp.sum(rounded.astype(F32), axis=0, keepdims=True)
+
+
+def split_io_kernel(meta, g_in, g_out, send, mine):
+    n_grp = g_in.shape[1] // 128
+    part = g_in.shape[0] // n_grp
+    q = part // 3
+    for k in range(send.shape[0]):
+        for x, target in ((meta[2], mine), (1 - meta[2], send)):
+            g = 2 * k + x
+            for lb in range(n_grp):
+                at = lb * 4 * q
+                target[k, at : at + part, :] = g_in[span(g, part), lb * 128 : (lb + 1) * 128]
+                target[k, at + part : at + part + q, :] = g_out[lb * q : (lb + 1) * q, span(g, 128)]
+
+
+def mlp_grads_kernel(meta, every, g_pre, hidden, low, out):
+    tile = 256
+    rows = every.shape[1]
+    for n in range(low.shape[1] // tile):
+        w = slice(n * tile, (n + 1) * tile)
+        for at, left, right in ((0, every, g_pre), (rows, hidden, low)):
+            value = dot(left[...], right[:, w], 0, 0).astype(BF)
+            out[2 * n, at : at + rows, :] = value[:, :128]
+            out[2 * n + 1, at : at + rows, :] = value[:, 128:]
+
+
+def io_grads_kernel(meta, g_proj, every, mixed, low, send, mine, g_in, g_out):
+    wide = mixed.shape[1]
+    for j in range(g_proj.shape[1] // wide):
+        w = slice(j * wide, (j + 1) * wide)
+        g_in[w, :] = dot(g_proj[:, w], every[...], 0, 0).astype(BF)
+    g_out[...] = dot(mixed[...], low[...], 0, 0).astype(BF)
+    split_io_kernel(meta, g_in, g_out, send, mine)
+
+
+def owner_sum_kernel(meta, mine, got, own, *sends):
+    half = got.shape[0]
+    z = meta[1]
+    own[...] = mine[z].astype(F32) + got[z].astype(F32)
+    for k, send in enumerate(sends, 1):
+        to = lax.rem(z + k, half)
+        send[...] = (mine[to].astype(F32) + got[to].astype(F32)).astype(BF)
+
+
+def last_sum_kernel(meta, own, *refs):
+    got, out = refs[:-1], refs[-1]
+    total = own[...]
+    for v in got:
+        total = total + v[...].astype(F32)
+    out[...] = total.astype(BF)
+
+
+def prep_kernel(small, meta, up, down, w_in, w_out, *refs):
+    if small:
+        in_bias, conv_weight, conv_bias, skip, fout, up_bias, gain, shift, branch = refs[:9]
+        refs = refs[9:]
+    io_out, up_out, down_out, turned = refs[:4]
+    s = meta[0]
+    up_out[...] = up[0]
+    n_grp, f, lanes = down.shape[1], down.shape[3], down.shape[4]
+    q = w_out.shape[3]
+    for g in range(n_grp):
+        down_out[g * f : (g + 1) * f, :] = down[0, g, 0]
+        io_out[g * 4 * q + 3 * q : (g + 1) * 4 * q, :] = w_out[0, g, 0]
+    for k in range(3):
+        turned[...] = w_in[0, :, k * lanes : (k + 1) * lanes].astype(F32).T
+        piece = turned[span(s, q), :].astype(BF)
+        for lb in range(n_grp):
+            io_out[lb * 4 * q + k * q : lb * 4 * q + (k + 1) * q, :] = piece[:, lb * 128 : (lb + 1) * 128]
+    if not small:
+        return
+    (rows,) = refs[4:]
+    depth = up_bias.shape[0]
+    rows[...] = jnp.zeros_like(rows)
+    b_in, w_tap, b_tap = in_bias[...].astype(F32), conv_weight[...].astype(F32), conv_bias[...].astype(F32)
+    skips = skip[...].astype(F32)
+    for l in range(depth):
+        at = l * SLOT
+        outs = fout[l].astype(F32)
+        for b in range(3):
+            w = slice(b * lanes, (b + 1) * lanes)
+            rows[b, at : at + 1, :] = b_in[l : l + 1, w]
+            rows[b, at + 1 : at + 4, :] = w_tap[l][:, w]
+            rows[b, at + 4 : at + 5, :] = b_tap[l : l + 1, w]
+        rows[3, at : at + 4, :] = outs[60:64]
+        rows[3, at + 4 : at + 5, :] = skips[l : l + 1]
+        for b in range(4):
+            rows[b, at + 5 : at + 20, :] = outs[15 * b : 15 * b + 15]
+    lane = lax.broadcasted_iota(jnp.int32, (lanes, lanes), 0)
+    to = lax.broadcasted_iota(jnp.int32, (lanes, lanes), 1)
+    packed = jnp.zeros((2 * SLOT, lanes), F32)
+    for b in range(4):
+        hit = (lane == s * q + to - b * q) & (to >= b * q) & (to < (b + 1) * q)
+        packed = packed + dot(rows[b].astype(BF), jnp.where(hit, 1.0, 0.0).astype(BF), 1, 0)
+    ups = up_bias[:, span(s, lanes)].astype(F32)
+    tail = [ups, jnp.zeros((TOK - UP_AT - depth, lanes), F32)]
+    for v in (gain, shift, branch):
+        v = v[...].astype(F32)
+        tail += [v[l] for l in range(depth)]
+    base = n_grp * 4 * q
+    io_out[base : base + SMALL, :] = jnp.concatenate([packed] + tail).astype(BF)
+
+
+def unpack_kernel(meta, slab, other, e_wide, e_all, tok, rows5, skip, fout, b_up, wide):
+    place_wide(meta, (slab, other), wide)
+    depth = fout.shape[0]
+    tok[...] = wide[TOK:SMALL, :].astype(F32)
+    low = wide[: 2 * SLOT, :]
+    five = dot(low, e_wide[...], 1, 0)
+    for l in range(depth):
+        rows5[l] = five[l * SLOT : l * SLOT + 5]
+        b_up[l] = wide[UP_AT + l : UP_AT + l + 1, :].astype(F32)
+    for b in range(4):
+        found = dot(low, e_all[b], 1, 0)
+        for l in range(depth):
+            at = l * SLOT
+            fout[l, 15 * b : 15 * b + 15, :] = found[at + 5 : at + 20]
+            if b == 3:
+                fout[l, 60:64, :] = found[at : at + 4]
+                skip[l] = found[at + 4 : at + 5]
+
+
+def pack_kernel(depth, meta, *refs):
+    ups, refs = refs[:depth], refs[depth:]
+    smalls, refs = refs[:depth], refs[depth:]
+    fouts, refs = refs[:depth], refs[depth:]
+    toks, refs = refs[: 2 * depth + 1], refs[2 * depth + 1 :]
+    e_wide, e_all, send, mine, rows, wide = refs
+    chans = fouts[0].shape[1]
+    rows[...] = jnp.zeros_like(rows)
+    for l in range(depth):
+        at = l * SLOT
+        rows[4, at : at + 5, :] = smalls[l][:5, :]
+        for b in range(4):
+            rows[b, at + 5 : at + 20, :chans] = fouts[l][15 * b : 15 * b + 15, :]
+        rows[3, at : at + 4, :chans] = fouts[l][60:64, :]
+        rows[3, at + 4 : at + 5, :chans] = smalls[l][5:6, :chans]
+    packed = dot(rows[4].astype(BF), e_wide[...], 1, 1)
+    for b in range(4):
+        packed = packed + dot(rows[b, :, :chans].astype(BF), e_all[b], 1, 1)
+    wide[: 2 * SLOT, :] = packed
+    wide[2 * SLOT :, :] = jnp.zeros((SMALL - 2 * SLOT, wide.shape[1]), F32)
+    for l in range(depth):
+        wide[UP_AT + l : UP_AT + l + 1, :] = ups[l][...]
+        for i in range(2):
+            v = toks[2 * l + i]
+            at = TOK + 2 * l + i
+            wide[at : at + 1, :] = v[0:1, :]
+            wide[at + 2 * depth : at + 2 * depth + 1, :] = v[1:2, :]
+            wide[at + 4 * depth : at + 4 * depth + 1, :] = toks[2 * l + i + 1][2:3, :]
+    for k in range(send.shape[0]):
+        mine[k] = wide[:, span(2 * k + meta[2], 128)].astype(BF)
+        send[k] = wide[:, span(2 * k + 1 - meta[2], 128)].astype(BF)
+
+
+def finish_small_kernel(q, meta, *refs):
+    parts, refs = refs[:4], refs[4:]
+    gain, shift, branch, in_bias, conv_weight, conv_bias, skip, fout, up_bias = refs
+    depth = fout.shape[0]
+    lanes = parts[0].shape[1]
+    lane = lax.broadcasted_iota(jnp.int32, (lanes, lanes), 0)
+    to = lax.broadcasted_iota(jnp.int32, (lanes, lanes), 1)
+    tok = parts[0][...].astype(F32)
+    for part in parts[1:]:
+        tok = tok + part[...].astype(F32)
+    for l in range(depth):
+        for t, v in enumerate((gain, shift, branch)):
+            at = TOK + 2 * depth * t + 2 * l
+            v[l] = tok[at : at + 2]
+    for k, part in enumerate(parts):
+        up_bias[:, span(meta[0] ^ ORDER[k], lanes)] = part[UP_AT : UP_AT + depth, :].astype(F32)
+    for b in range(4):
+        found = jnp.zeros((2 * SLOT, lanes), F32)
+        for k, part in enumerate(parts):
+            s = meta[0] ^ ORDER[k]
+            hit = (to - s * q == lane - b * q) & (lane >= b * q) & (lane < (b + 1) * q)
+            found = found + dot(part[: 2 * SLOT, :], jnp.where(hit, 1.0, 0.0).astype(BF), 1, 0)
+        for l in range(depth):
+            at = l * SLOT
+            fout[l, 15 * b : 15 * b + 15, :] = found[at + 5 : at + 20]
+            if b == 3:
+                fout[l, 60:64, :] = found[at : at + 4]
+                skip[l : l + 1, :] = found[at + 4 : at + 5]
+            else:
+                w = slice(b * lanes, (b + 1) * lanes)
+                in_bias[l : l + 1, w] = found[at : at + 1]
+                conv_weight[l, :, w] = found[at + 1 : at + 4]
+                conv_bias[l : l + 1, w] = found[at + 4 : at + 5]
+
+
+def finish_mlp_kernel(extra, meta, *refs):
+    parts, refs = refs[:4], refs[4:]
+    up, down = refs[extra:]
+    rows = up.shape[1]
+    n_grp, f = down.shape[1], down.shape[3]
+    for k, part in enumerate(parts):
+        s = meta[0] ^ ORDER[k]
+        up[0, :, span(s, part.shape[1])] = part[:rows, :].astype(F32)
+        for g in range(n_grp):
+            down[0, g, s] = part[rows + g * f : rows + (g + 1) * f, :].astype(F32)
+
+
+def finish_io_kernel(extra, meta, *refs):
+    parts, refs = refs[:4], refs[4:]
+    g_in, g_out, turned = refs[extra:]
+    n_grp, q = g_out.shape[1], g_out.shape[3]
+    for k, part in enumerate(parts):
+        s = meta[0] ^ ORDER[k]
+        for lb in range(n_grp):
+            at = lb * 4 * q
+            for j in range(3):
+                row = pl.ds(pl.multiple_of(j * 4 * q + s * q, q), q)
+                turned[row, lb * 128 : (lb + 1) * 128] = part[at + j * q : at + (j + 1) * q, :].astype(F32)
+            g_out[0, lb, s] = part[at + 3 * q : at + 4 * q, :].astype(F32)
+    for j in range(3):
+        g_in[0, :, j * 4 * q : (j + 1) * 4 * q] = turned[j * 4 * q : (j + 1) * 4 * q, :].T
+
+
+def second_layer(fin, fmid, fbias, freq, feats):
+    inner = jnp.sin(freq[0] * (jnp.dot(feats, fin, precision=HIGH) + fbias[0]))
+    return jnp.sin(freq[1] * (jnp.dot(inner, fmid, precision=HIGH) + fbias[1]))
+
+
+def after(value, *others):
+    return lax.optimization_barrier((value,) + others)[0]
+
+
+def body(
+    tokens,
+    lengths,
+    cotangent,
+    norm_gain,
+    norm_bias,
+    in_weight,
+    in_bias,
+    conv_weight,
+    conv_bias,
+    skip_bias,
+    filt_out,
+    out_weight,
+    up_weight,
+    up_bias,
+    down_weight,
+    branch_bias,
+    filt_in,
+    filt_mid,
+    filt_bias,
+    sine_freq,
+):
+    comm = Comm()
+    n_grp, n_seq, s, nz = comm.n_grp, comm.n_seq, comm.s, comm.nz
+    depth = norm_gain.shape[0]
+    tok_rows, width = tokens.shape
+    total = tok_rows * n_seq
+    half, most = total // 2, total // 4
+    cols = width // n_grp
+    q = cols // n_seq
+    ff_shard = up_weight.shape[2]
+    f = ff_shard // n_seq
+    hid = filt_out.shape[1]
+    chans = n_grp * q
+    count = lengths.shape[1]
+    lens = lengths[0]
+    starts = half + jnp.cumsum(lens) - lens
+    meta = jnp.concatenate([jnp.stack([s, comm.z, comm.x, comm.y, comm.c]), starts, lens]).astype(jnp.int32)
+
+    down_view = down_weight.reshape(depth, n_grp, n_seq, f, cols)
+    out_view = out_weight.reshape(depth, n_grp, n_seq, q, cols)
+
+    def prepare(l, small):
+        args = [
+            (up_weight, (1, width, f), lambda i, m: (l, 0, m[0])),
+            (down_view, (1, n_grp, 1, f, cols), lambda i, m: (l, 0, m[0], 0, 0)),
+            (in_weight, (1, width, 3 * cols), lambda i, m: (l, 0, 0)),
+            (out_view, (1, n_grp, 1, q, cols), lambda i, m: (l, 0, m[0], 0, 0)),
+        ]
+        scratch = [((cols, width), F32)]
+        rows = width
+        if small:
+            args += [in_bias, conv_weight, conv_bias, skip_bias, filt_out, up_bias, norm_gain, norm_bias, branch_bias]
+            scratch.append(((4, 2 * SLOT, cols), F32))
+            rows += SMALL
+        outs = [((rows, cols), BF), ((width, f), BF), ((n_grp * f, cols), BF)]
+        return run(lambda *r: prep_kernel(small, *r), outs, meta, args, scratch)
+
+    def by_permutes(unit):
+        slab = jnp.stack([unit] + [comm.turn(unit, "grp", n_grp, k) for k in range(1, nz)])
+        return [slab, comm.flip(slab, "grp", n_grp)]
+
+    first_units = prepare(0, True)
+    hat0, low_first, sums_first = run(
+        first_norm_kernel,
+        [((tok_rows, width), BF), ((tok_rows, width), BF), ((8, width), F32)], meta, [tokens, cotangent])
+    ready = list(first_units)
+    for l in range(1, depth):
+        ready += prepare(l, False)
+    chunks, slab = [], None
+    for unit in ready:
+        if slab is not None:
+            unit = after(unit, slab)
+        slab = jnp.stack([unit] + [comm.turn(unit, "grp", n_grp, k) for k in range(1, nz)])
+        chunks.append([slab, comm.flip(slab, "grp", n_grp)])
+    weights = [tuple(chunks[3 * l : 3 * l + 3]) for l in range(depth)]
+
+    lane_from = jnp.arange(n_grp * cols, dtype=jnp.int32)[:, None]
+    lane_wide = jnp.arange(3 * chans, dtype=jnp.int32)[None, :]
+    lane_chan = jnp.arange(chans, dtype=jnp.int32)[None, :]
+    e_wide = ((lane_from // cols == lane_wide // (3 * q)) & (lane_from % cols == lane_wide % (3 * q))).astype(BF)
+    e_all = jnp.stack([
+        ((lane_from // cols == lane_chan // q) & (lane_from % cols == b * q + lane_chan % q)) for b in range(4)
+    ]).astype(BF)
+    slab, other = weights[0][0]
+    small_block = ((nz, SMALL, cols), lambda i, m: (0, width // SMALL, 0))
+    tok_all, rows5, skip, fout, b_up = run(
+        unpack_kernel,
+        [((6 * depth, width), F32), ((depth, 5, 3 * chans), F32), ((depth, 1, chans), F32),
+         ((depth, hid, chans), F32), ((depth, 1, n_grp * f), F32)],
+        meta, [(slab,) + small_block, (other,) + small_block, e_wide, e_all], [((SMALL, width), BF)])
+    tok_all = tok_all.reshape(3, depth, 2, 1, width)
+    gains, shifts, b_branch = tok_all[0], tok_all[1], tok_all[2]
+
+    mixer = Mixer(lens, total, most)
+    long, short, short0 = mixer.long, mixer.short, mixer.short0
+    long_t, short_t, short0_t = long.T, short.T, short0.T
+    feats, tpos = positions(half)
+    channel = (
+        jnp.arange(n_grp, dtype=jnp.int32)[:, None] * cols + s * q + jnp.arange(q, dtype=jnp.int32)[None, :]
+    ).reshape(-1).astype(F32)
+    rate = jnp.abs(FAST + (SLOW - FAST) * channel / (width - 1))
+    decay = jnp.exp(-tpos[:, None] * rate[None, :])
+    seconds, second_pull = jax.vjp(
+        lambda *a: jax.vmap(lambda *b: second_layer(*b, feats))(*a), filt_in, filt_mid, filt_bias, sine_freq)
+
+    def gather_parts(v):
+        across = comm.turn(v, "seq", n_seq, 1)
+        return [v, across, comm.flip(v, "seq", n_seq), comm.flip(across, "seq", n_seq)]
+
+    def scatter_parts(send, keep):
+        got = comm.flip(send, "seq", n_seq)
+        other = 1 - comm.y
+        crossed = (pick(keep, other, 0) + pick(got, other, 0).astype(F32)).astype(BF)
+        own = ((1, tok_rows, width), lambda i, m: (m[3], 0, 0))
+        return (keep,) + own, (got,) + own, comm.turn(crossed, "seq", n_seq, 1)
+
+    parts_out = [((2, tok_rows, width), BF), ((2, tok_rows, width), F32)]
+    io_scratch = [((3 * chans, width), BF), ((chans, width), BF)]
+    mlp_scratch = [((width, n_grp * f), BF), ((n_grp * f, width), BF)]
+    state = tokens
+    saved = []
+    normed = hat0
+    for l in range(depth):
+        w_io, w_up, w_down = weights[l]
+        parts = gather_parts(normed)
+        if l == 0:
+            low_parts = gather_parts(low_first)
+            parts[0] = after(parts[0], *low_parts, chunks[1][0])
+        else:
+            parts[0] = after(parts[0], chunks[4][1], chunks[5][0])
+        every, chan, inner, mixed, send, keep = run(
+            lambda *r, n=len(w_io), raw=l == 0: mix_forth_kernel(count, n, raw, *r),
+            [((total, width), BF), ((total, 3 * chans), BF), ((total, chans), F32), ((total, chans), BF)] + parts_out,
+            meta,
+            parts + w_io + [long, long_t, short, short_t, short0, seconds[l], decay, fout[l], rows5[l], skip[l],
+                            gains[l, 0], shifts[l, 0]],
+            io_scratch,
+            flops=3 * 10**9,
+        )
+        got = scatter_parts(send, keep)
+        if l == 0:
+            state = after(state, chunks[1][1], chunks[2][0])
+        mid, normed2 = run(
+            add_norm_kernel, [((tok_rows, width), F32), ((tok_rows, width), BF)], meta,
+            [state, *got, b_branch[l, 0], gains[l, 1], shifts[l, 1]],
+        )
+        parts = gather_parts(normed2)
+        if l == 0:
+            parts[0] = after(parts[0], chunks[2][1], chunks[3][0])
+        every2, hidden, slope, send, keep = run(
+            lambda *r, n=len(w_up), m=len(w_down): mlp_forth_kernel(n, m, *r),
+            [((total, width), BF), ((total, n_grp * f), BF), ((total, n_grp * f), BF)] + parts_out,
+            meta, parts + w_up + w_down + [b_up[l]], mlp_scratch,
+            flops=4 * 10**9,
+        )
+        saved.append((state, every, chan, inner, mixed, mid, every2, hidden, slope))
+        got = scatter_parts(send, keep)
+        if l == 0:
+            mid = after(mid, chunks[3][1], chunks[4][0])
+        if l + 1 < depth:
+            state, normed = run(
+                add_norm_kernel, [((tok_rows, width), F32), ((tok_rows, width), BF)], meta,
+                [mid, *got, b_branch[l, 1], gains[l + 1, 0], shifts[l + 1, 0]],
+            )
+        else:
+            (state,) = run(add_kernel, [((tok_rows, width), F32)], meta, [mid, *got, b_branch[l, 1]])
+
+    grad = cotangent
+    toks = [None] * (2 * depth) + [sums_first]
+    g_fouts, g_seconds, smalls, up_biases = ([None] * depth for _ in range(4))
+
+    def owner_turn(mine, got):
+        rows = mine.shape[1:]
+        own, *sends = run(owner_sum_kernel, [(rows, F32)] + [(rows, BF)] * (nz - 1), meta, [mine, got])
+        return [own] + [comm.turn(send, "grp", n_grp, k) for k, send in enumerate(sends, 1)]
+
+    def owner_end(pieces):
+        return run(last_sum_kernel, [(pieces[0].shape, BF)], meta, pieces)[0]
+
+    norm_outs = [((tok_rows, width), F32), ((tok_rows, width), BF), ((8, width), F32)]
+    mlp_units, io_units, sent = [None] * depth, [None] * depth, []
+    for l in reversed(range(depth)):
+        w_io, w_up, w_down = weights[l]
+        first, every, chan, inner, mixed, mid, every2, hidden, slope = saved[l]
+        if l == 0:
+            low_parts[0] = after(low_parts[0], io_units[1][1])
+        low, g_pre, up_biases[l], send, keep = run(
+            lambda *r, n=len(w_up), m=len(w_down): mlp_back_kernel(n, m, *r),
+            [((total, width), BF), ((total, n_grp * f), BF), ((1, n_grp * f), F32)] + parts_out,
+            meta, low_parts + w_up + w_down + [slope], mlp_scratch,
+            flops=4 * 10**9,
+        )
+        sent.append(send)
+        (g_mlp,) = run(
+            mlp_grads_kernel, [((n_grp, 2 * width, cols), BF)], meta, [every2, g_pre, hidden, low], flops=4 * 10**9)
+        mlp_units[l] = lax.psum_scatter(g_mlp, "grp", scatter_dimension=0, tiled=False)
+        grad, low_own, toks[2 * l + 1] = run(
+            norm_back_kernel, norm_outs, meta, [grad, *scatter_parts(send, keep), mid, gains[l, 1]])
+        low_parts = gather_parts(low_own)
+        low, g_proj, g_fouts[l], g_seconds[l], smalls[l], send, keep = run(
+            lambda *r, n=len(w_io): mix_back_kernel(count, n, *r),
+            [((total, width), BF), ((total, 3 * chans), BF), ((hid, chans), F32), ((half, hid), F32),
+             ((8, 3 * chans), F32)] + parts_out,
+            meta,
+            low_parts + w_io + [long, long_t, short, short_t, short0, short0_t, seconds[l], decay, fout[l], rows5[l],
+                                skip[l], chan, inner],
+            io_scratch,
+            flops=5 * 10**9,
+        )
+        sent.append(send)
+        send_io, mine = run(
+            io_grads_kernel, [((nz, width, cols), BF)] * 2, meta, [g_proj, every, mixed, low],
+            [((3 * chans, width), BF), ((chans, width), BF)], flops=2 * 10**9)
+        io_units[l] = (mine, comm.flip(send_io, "grp", n_grp))
+        grad, low_own, toks[2 * l] = run(
+            norm_back_kernel, norm_outs, meta, [grad, *scatter_parts(send, keep), first, gains[l, 0]])
+        if l:
+            low_parts = gather_parts(low_own)
+
+    send, mine = run(
+        lambda *r: pack_kernel(depth, *r), [((nz, SMALL, cols), BF)] * 2, meta,
+        up_biases + smalls + g_fouts + toks + [e_wide, e_all],
+        [((5, 2 * SLOT, 3 * chans), F32), ((SMALL, width), F32)])
+    small = owner_end(owner_turn(mine, comm.flip(send, "grp", n_grp)))
+    norm_gain_grad, norm_bias_grad, branch_grad, in_bias_grad, taps_grad, tap_bias_grad, skip_grad, fout_grad, up_bias_grad = run(
+        lambda *r: finish_small_kernel(q, *r),
+        [(v.shape, F32) for v in (norm_gain, norm_bias, branch_bias, in_bias, conv_weight, conv_bias, skip_bias,
+                                  filt_out, up_bias)],
+        meta, gather_parts(small))
+
+    def finish(kernel, unit, shapes, old, scratch=()):
+        outs = []
+        for shape in shapes:
+            outs.append(((depth,) + shape, F32, (1,) + shape, lambda i, m, l=l, n=len(shape): (l,) + (0,) * n))
+        return run(
+            lambda *r, n=len(old): kernel(n, *r), outs, meta, gather_parts(unit) + [(v, None, None) for v in old],
+            scratch, alias={5: 0, 6: 1} if old else None)
+
+    mlp_shapes = [(width, ff_shard), (n_grp, n_seq, f, cols)]
+    io_shapes = [(width, 3 * cols), (n_grp, n_seq, q, cols)]
+    mlp_grads, io_grads = [], []
+    for l in reversed(range(depth)):
+        mine, got = io_units[l]
+        pieces = owner_turn(mine, after(got, sent[2]) if l else got)
+        if l:
+            pieces = [pieces[0]] + [after(v, sent[3]) for v in pieces[1:]]
+        io_unit = owner_end(pieces)
+        mlp_unit = after(mlp_units[l], sent[3] if l else io_unit, *([] if l else [small]))
+        mlp_grads = finish(finish_mlp_kernel, mlp_unit, mlp_shapes, mlp_grads)
+        io_grads = finish(finish_io_kernel, io_unit, io_shapes, io_grads, [((3 * cols, width), F32)])
+    up_grad, down_grad = mlp_grads
+    in_grad, out_grad = io_grads
+
+    net_grads = second_pull(jnp.stack(g_seconds))
+    flat = jnp.concatenate([v.reshape(-1) for v in net_grads])
+    flat = jnp.pad(flat, (0, -flat.shape[0] % 1024)).reshape(-1, 128)
+    flat = comm.sum_all(comm.sum_all(flat, "seq", n_seq), "grp", n_grp).reshape(-1)
+    shared, at = [], 0
+    for v in net_grads:
+        shared.append(flat[at : at + v.size].reshape(v.shape))
+        at += v.size
+    return (
+        state, grad, norm_gain_grad, norm_bias_grad, in_grad, in_bias_grad, taps_grad, tap_bias_grad,
+        skip_grad, fout_grad, out_grad.reshape(depth, width, cols), up_grad, up_bias_grad,
+        down_grad.reshape(depth, n_grp * ff_shard, cols), branch_grad, shared[0], shared[1], shared[2], shared[3],
+    )
+
+
 def solution(mesh):
     tok = P(("grp", "seq"), None)
     last3, last2 = P(None, None, "grp"), P(None, "grp")
@@ -467,4 +1276,5 @@
         tok, tok, last3, last3, last3, last2, last3, last2, last2, last3,
         last3, last3, last2, last3, last3, P(), P(), P(), P(),
     )
-    return jax.shard_map(body, mesh=mesh, in_specs=in_specs, out_specs=out_specs, check_vma=False)
+    small = mesh.shape["seq"] == 4
+    return jax.shard_map(body if small else body_any, mesh=mesh, in_specs=in_specs, out_specs=out_specs, check_vma=False)

time: 764 us -> 579 us (0.76)
  the two profiles are of different devices: /device:TPU:0 before, /device:TPU:9 now
where the time goes in v2:
time: 579 us; the launch traced here: 570 us
  Pallas kernels  177 us (31%)
  waiting for transfers between devices  175 us (30%)
  starting transfers between devices  123 us (21%)
  local copies, waits for them, and re-layouts  42.2 us (7%)
  other arithmetic  28.8 us (5%)
  between operations  15.3 us (3%)
  matrix products  7.78 us (1%)
    pallas_call x36, Pallas kernels, run(): pl.pallas_call(kernel, out_shape=shapes, grid_spec=pltpu.PrefetchScalarGr...  177 us
    ppermute x52, waiting for transfers between devices, turn(): return lax.ppermute(v, axis, perm)  134 us
    ppermute x45, starting transfers between devices, flip(): return lax.ppermute(v, axis, [(i, i ^ 1) for i in range(size)])  68 us
    ppermute x52, starting transfers between devices, turn(): return lax.ppermute(v, axis, perm)  55.3 us
    ppermute x45, waiting for transfers between devices, flip(): return lax.ppermute(v, axis, [(i, i ^ 1) for i in range(size)])  41.1 us
    unnamed x209, local copies, waits for them, and re-layouts  21.5 us
  transfers between devices with their start and end apart: 99, of which 34 were waited for; matrix products, arithmetic and copies ran while one was open for 10% of the time, Pallas kernels for 24%

profile of v2, /device:TPU:9, one launch (start us, length us, event | category | flops | bytes accessed | tf_op | source)
XLA Modules:
  0.0 569.6 jit_solution(13448241747163727390)
XLA Ops:
  11.4 3.2 shard_map.339
  19.3 2.8 shard_map.340
  29.6 3.9 subtract_select_fusion.2
  45.9 2.8 collective-permute-start.4
  52.2 14.0 %collective-permute-start.12 = (bf16[128,1024]{1,0:T(8,128)(2,1)}, bf16[128,1024]{1,0:T(8,128)(2,1)}, u32[]{:S(2)}, u32[]{:S(2)}) collective-permute-start(bf16[128,1024]{1,0:T(8,128)(2,1)} %collective-permute-done.10.r_2_), channel_id=1, source_target_pairs={{0,1},{1,0},{2,3},{3,2},{4,5},{5,4},{6,7},{7,6},{8,9},{9,8},{10,11... | collective-permute-start | bytes 786440 | tf_op jit(solution)/shard_map/ppermute | solution.py:42
  75.0 4.2 shard_map.341
  87.3 7.5 %shard_map.342 = (bf16[512,1024]{1,0:T(8,128)(2,1)}, bf16[512,768]{1,0:T(8,128)(2,1)}, f32[512,256]{1,0:T(8,128)}, bf16[512,256]{1,0:T(8,128)(2,1)}, bf16[2,128,...) custom-call(s32[11]{0:T(128)} %concatenate.30.r_0_.meta, bf16[128,1024]{1,0:T(8,128)(2,1)} %get-tuple-element.156.r_1_, ...), custom_call_target="tpu_custom_call" | custom-call | flops 3000000 | bytes 9265 | tf_op jit(solution)/shard_map/pallas_call | solution.py:491
  102.5 3.1 shard_map.344
  105.5 3.2 collective-permute-start.21
  110.1 3.1 shard_map.343
  113.6 2.9 collective-permute-start.20
  116.7 3.6 collective-permute-start.28
  122.2 5.6 collective-permute-done.20
  127.8 5.6 collective-permute-done.19
  138.8 8.8 %shard_map.345 = (bf16[512,1024]{1,0:T(8,128)(2,1)}, bf16[512,1024]{1,0:T(8,128)(2,1)}, bf16[512,1024]{1,0:T(8,128)(2,1)}, bf16[2,128,1024]{2,1,0:T(8,128)(2,1)}, f32[2,128,1024]{2,1,0:T(8,128)}) custom-call(s32[11]{0:T(128)} %concatenate.30.r_0_.meta, bf16[128,1024]{1,0:T(8,128)(2,1)} %get-tuple-element.170.r_1_, bf16[128,1024]{1,0:T(8,128)(2,1)} %copy-done.44, ...), custom_call_target="tpu_custom_call" | custom-call | flops 4000000 | bytes 9965 | tf_op jit(solution)/shard_map/pallas_call | solution.py:491
  149.1 4.2 collective-permute-done.24
  153.3 5.6 collective-permute-done.23
  161.9 5.5 collective-permute-done.31.crossed
  168.1 3.1 shard_map.346
  171.6 2.7 collective-permute-start.33
  174.3 2.7 collective-permute-start.37
  180.1 6.6 %collective-permute-done.33 = bf16[1024,128]{1,0:T(8,128)(2,1)S(1)} collective-permute-done((bf16[1024,128]{1,0:T(8,128)(2,1)S(1)}, bf16[1024,128]{1,0:T(8,128)(2,1)S(1)}, u32[]{:S(2)}, u32[]{:S(2)}) %collective-permute-start.33) | collective-permute-done | bytes 262176 | tf_op jit(solution)/shard_map/ppermute | solution.py:48
  187.8 7.5 %shard_map.347 = (bf16[512,1024]{1,0:T(8,128)(2,1)}, bf16[512,768]{1,0:T(8,128)(2,1)}, f32[512,256]{1,0:T(8,128)}, bf16[512,256]{1,0:T(8,128)(2,1)}, bf16[2,128,...) custom-call(s32[11]{0:T(128)} %concatenate.30.r_0_.meta, bf16[128,1024]{1,0:T(8,128)(2,1)} %get-tuple-element.178.r_1_, ...), custom_call_target="tpu_custom_call" | custom-call | flops 3000000 | bytes 9134 | tf_op jit(solution)/shard_map/pallas_call | solution.py:491
  202.1 6.4 %collective-permute-done.40.crossed = bf16[128,1024]{1,0:T(8,128)(2,1)S(1)} collective-permute-done((bf16[128,1024]{1,0:T(8,128)(2,1)S(1)}, bf16[128,1024]{1,0:T(8,128)(2,1)S(1)}, u32[]{:S(2)}, u32[]{:S(2)}) %collective-permute-start.40) | collective-permute-done | bytes 262176 | tf_op jit(solution)/shard_map/ppermute | solution.py:48
  209.3 3.1 shard_map.348
  214.9 4.2 collective-permute-done.41.r_2_
  223.8 8.9 %shard_map.349 = (bf16[512,1024]{1,0:T(8,128)(2,1)}, bf16[512,1024]{1,0:T(8,128)(2,1)}, bf16[512,1024]{1,0:T(8,128)(2,1)}, bf16[2,128,1024]{2,1,0:T(8,128)(2,1)}, f32[2,128,1024]{2,1,0:T(8,128)}) custom-call(s32[11]{0:T(128)} %concatenate.30.r_0_.meta, bf16[128,1024]{1,0:T(8,128)(2,1)} %get-tuple-element.182.r_1_, bf16[128,1024]{1,0:T(8,128)(2,1)} %copy-done.58, ...), custom_call_target="tpu_custom_call" | custom-call | flops 4000000 | bytes 9965 | tf_op jit(solution)/shard_map/pallas_call | solution.py:491
  232.7 8.6 %shard_map.351 = (bf16[512,1024]{1,0:T(8,128)(2,1)}, bf16[512,1024]{1,0:T(8,128)(2,1)}, f32[1,1024]{1,0:T(1,128)}, bf16[2,128,1024]{2,1,0:T(8,128)(2,1)}, f32[2,128,1024]{2,1,0:T(8,128)}) custom-call(s32[11]{0:T(128)} %concatenate.30.r_0_.meta, bf16[128,1024]{1,0:T(8,128)(2,1)} %get-tuple-element.155.r_1_, bf16[128,1024]{1,0:T(8,128)(2,1)} %collective-permute-done.10.r_2_, ...), custom_call_target="tpu_custom_call" | custom-call | flops 4000000 | bytes 9965 | tf_op jit(solution)/shard_map/pallas_call | solution.py:491
  241.3 7.5 %shard_map.372 = bf16[8,2048,128]{2,1,0:T(8,128)(2,1)} custom-call(s32[11]{0:T(128)} %concatenate.30.r_0_.meta, bf16[512,1024]{1,0:T(8,128)(2,1)} %get-tuple-element.264.every, bf16[512,1024]{1,0:T(8,128)(2,1)} %get-tuple-element.265.g_pre, bf16[512,1024]{1,0:T(8,128)(2,1)} %get-tuple-element.266.hidden, bf16[512,1024]{1,0:T(8,128)(2,1)} %get-tuple-element.267.low), custom_call_target="tpu_custom_call" | custom-call | flops 4000000 | bytes 8388 | tf_op jit(solution)/shard_map/pallas_call | solution.py:491
  253.5 6.5 %collective-permute-done.48.crossed = bf16[128,1024]{1,0:T(8,128)(2,1)S(1)} collective-permute-done((bf16[128,1024]{1,0:T(8,128)(2,1)S(1)}, bf16[128,1024]{1,0:T(8,128)(2,1)S(1)}, u32[]{:S(2)}, u32[]{:S(2)}) %collective-permute-start.48) | collective-permute-done | bytes 262176 | tf_op jit(solution)/shard_map/ppermute | solution.py:48
  260.8 3.6 shard_map.352
  266.9 4.6 collective-permute-done.49.r_2_
  275.2 10.3 %shard_map.353 = (bf16[512,1024]{1,0:T(8,128)(2,1)}, bf16[512,768]{1,0:T(8,128)(2,1)}, f32[64,256]{1,0:T(8,128)}, f32[256,64]{1,0:T(8,128)}, f32[8,768]{1,0:T(8,...) custom-call(s32[11]{0:T(128)} %concatenate.30.r_0_.meta, bf16[128,1024]{1,0:T(8,128)(2,1)} %get-tuple-element.189.r_1_, ...), custom_call_target="tpu_custom_call" | custom-call | flops 5000000 | bytes 9871 | tf_op jit(solution)/shard_map/pallas_call | solution.py:491
  285.9 5.4 shard_map.355
  292.8 6.4 %collective-permute-done.53.crossed = bf16[128,1024]{1,0:T(8,128)(2,1)S(1)} collective-permute-done((bf16[128,1024]{1,0:T(8,128)(2,1)S(1)}, bf16[128,1024]{1,0:T(8,128)(2,1)S(1)}, u32[]{:S(2)}, u32[]{:S(2)}) %collective-permute-start.53) | collective-permute-done | bytes 262176 | tf_op jit(solution)/shard_map/ppermute | solution.py:48
  299.9 3.6 shard_map.354
  306.1 4.3 collective-permute-done.55.r_2_
  312.5 13.6 %collective-permute-done.54.got = bf16[4,1024,128]{2,1,0:T(8,128)(2,1)S(1)} collective-permute-done((bf16[4,1024,128]{2,1,0:T(8,128)(2,1)}, bf16[4,1024,128]{2,1,0:T(8,128)(2,1)S(1)}, u32[]{:S(2)}, u32[]{:S(2)}) %collective-permute-start.54) | collective-permute-done | bytes 1048608 | tf_op jit(solution)/shard_map/ppermute | solution.py:42
  327.0 8.6 %shard_map.356 = (bf16[512,1024]{1,0:T(8,128)(2,1)}, bf16[512,1024]{1,0:T(8,128)(2,1)}, f32[1,1024]{1,0:T(1,128)}, bf16[2,128,1024]{2,1,0:T(8,128)(2,1)}, f32[2,128,1024]{2,1,0:T(8,128)}) custom-call(s32[11]{0:T(128)} %concatenate.30.r_0_.meta, bf16[128,1024]{1,0:T(8,128)(2,1)} %get-tuple-element.201.r_1_, bf16[128,1024]{1,0:T(8,128)(2,1)} %copy-done.53, ...), custom_call_target="tpu_custom_call" | custom-call | flops 4000000 | bytes 9965 | tf_op jit(solution)/shard_map/pallas_call | solution.py:491
  335.5 7.6 %shard_map.371 = bf16[8,2048,128]{2,1,0:T(8,128)(2,1)} custom-call(s32[11]{0:T(128)} %concatenate.30.r_0_.meta, bf16[512,1024]{1,0:T(8,128)(2,1)} %get-tuple-element.259.every, bf16[512,1024]{1,0:T(8,128)(2,1)} %get-tuple-element.260.g_pre, bf16[512,1024]{1,0:T(8,128)(2,1)} %get-tuple-element.261.hidden, bf16[512,1024]{1,0:T(8,128)(2,1)} %get-tuple-element.262.low), custom_call_target="tpu_custom_call" | custom-call | flops 4000000 | bytes 8388 | tf_op jit(solution)/shard_map/pallas_call | solution.py:491
  347.6 6.3 %collective-permute-done.59.crossed = bf16[128,1024]{1,0:T(8,128)(2,1)S(1)} collective-permute-done((bf16[128,1024]{1,0:T(8,128)(2,1)S(1)}, bf16[128,1024]{1,0:T(8,128)(2,1)S(1)}, u32[]{:S(2)}, u32[]{:S(2)}) %collective-permute-start.59) | collective-permute-done | bytes 262176 | tf_op jit(solution)/shard_map/ppermute | solution.py:48
  354.6 3.6 shard_map.357
  360.9 4.2 collective-permute-done.60.r_2_
  369.1 10.2 %shard_map.358 = (bf16[512,1024]{1,0:T(8,128)(2,1)}, bf16[512,768]{1,0:T(8,128)(2,1)}, f32[64,256]{1,0:T(8,128)}, f32[256,64]{1,0:T(8,128)}, f32[8,768]{1,0:T(8,...) custom-call(s32[11]{0:T(128)} %concatenate.30.r_0_.meta, bf16[128,1024]{1,0:T(8,128)(2,1)} %get-tuple-element.206.r_1_, ...), custom_call_target="tpu_custom_call" | custom-call | flops 5000000 | bytes 10002 | tf_op jit(solution)/shard_map/pallas_call | solution.py:491
  379.8 3.4 shard_map.367
  386.9 5.6 shard_map.364
  400.2 3.5 collective-permute-done.64.crossed
  404.4 3.5 shard_map.359
  407.9 4.8 shard_map.360
  414.1 15.2 %collective-permute-done.65.got = bf16[4,64,128]{2,1,0:T(8,128)(2,1)S(1)} collective-permute-done((bf16[4,64,128]{2,1,0:T(8,128)(2,1)}, bf16[4,64,128]{2,1,0:T(8,128)(2,1)S(1)}, u32[]{:S(2)}, u32[]{:S(2)}) %collective-permute-start.65) | collective-permute-done | bytes 65568 | tf_op jit(solution)/shard_map/ppermute | solution.py:42
  435.7 3.5 shard_map.365
  448.5 2.7 shard_map.368.r_1_
  451.3 32.6 %collective-permute-done.68.refs_2_ = bf16[64,128]{1,0:T(8,128)(2,1)S(1)} collective-permute-done((bf16[64,128]{1,0:T(8,128)(2,1)S(1)}, bf16[64,128]{1,0:T(8,128)(2,1)S(1)}, u32[]{:S(2)}, u32[]{:S(2)}) %collective-permute-start.68) | collective-permute-done | bytes 16416 | tf_op jit(solution)/shard_map/ppermute | solution.py:48
  488.5 2.8 shard_map.366.r_1_
  494.0 2.9 collective-permute-done.93
  499.2 3.4 collective-permute-done.96
  502.7 3.9 collective-permute-done.95
  511.2 3.0 collective-permute-start.77
  514.5 10.9 %collective-permute-done.69.r_2_ = bf16[64,128]{1,0:T(8,128)(2,1)S(1)} collective-permute-done((bf16[64,128]{1,0:T(8,128)(2,1)}, bf16[64,128]{1,0:T(8,128)(2,1)S(1)}, u32[]{:S(2)}, u32[]{:S(2)}) %collective-permute-start.69) | collective-permute-done | bytes 16416 | tf_op jit(solution)/shard_map/ppermute | solution.py:48
  530.1 2.9 shard_map.350
  538.9 3.7 shard_map.369
  547.0 3.7 shard_map.370
  552.4 4.6 shard_map.373
  558.0 4.6 shard_map.374
  (480 shorter events, 182.8 us)
Async XLA Ops:
  7.2 484.1 %reduce-scatter.5.cloned.1.call-start = ((), (), s32[]{:S(2)}) async-start(), calls=%async_computation.3 | async-start | bytes 4718592 | tf_op jit(solution)/shard_map/reduce_scatter | solution.py:1195
  14.6 25.5 %collective-permute-start.2 = (bf16[1088,128]{1,0:T(8,128)(2,1)}, bf16[1088,128]{1,0:T(8,128)(2,1)S(1)}, u32[]{:S(2)}, u32[]{:S(2)}) collective-permute-start(bf16[1088,128]{1,0:T(8,128)(2,1)} %get-tuple-element.149), channel_id=1, source_target_pairs={{0,24},{4,28},{8,0},{12,4},{16,8},{20,12},{24,16},{28,20},{1,25},{... | collective-permute-start | bytes 835592 | tf_op jit(solution)/shard_map/ppermute | solution.py:48
  14.6 25.5 %collective-permute-start.1 = (bf16[1088,128]{1,0:T(8,128)(2,1)}, bf16[1088,128]{1,0:T(8,128)(2,1)S(1)}, u32[]{:S(2)}, u32[]{:S(2)}) collective-permute-start(bf16[1088,128]{1,0:T(8,128)(2,1)} %get-tuple-element.149), channel_id=1, source_target_pairs={{0,16},{4,20},{8,24},{12,28},{16,0},{20,4},{24,8},{28,12},{1,17},{... | collective-permute-start | bytes 835592 | tf_op jit(solution)/shard_map/ppermute | solution.py:48
  17.1 23.9 %collective-permute-start = (bf16[1088,128]{1,0:T(8,128)(2,1)}, bf16[1088,128]{1,0:T(8,128)(2,1)S(1)}, u32[]{:S(2)}, u32[]{:S(2)}) collective-permute-start(bf16[1088,128]{1,0:T(8,128)(2,1)} %get-tuple-element.149), channel_id=1, source_target_pairs={{0,8},{4,12},{8,16},{12,20},{16,24},{20,28},{24,0},{28,4},{1,9},{5... | collective-permute-start | bytes 835592 | tf_op jit(solution)/shard_map/ppermute | solution.py:48
  22.1 26.6 %collective-permute-start.10 = (bf16[128,1024]{1,0:T(8,128)(2,1)}, bf16[128,1024]{1,0:T(8,128)(2,1)}, u32[]{:S(2)}, u32[]{:S(2)}) collective-permute-start(bf16[128,1024]{1,0:T(8,128)(2,1)} %get-tuple-element.155.r_1_), channel_id=1, source_target_pairs={{0,2},{1,3},{2,0},{3,1},{4,6},{5,7},{6,4},{7,5},{8,10},{9,11},{10,... | collective-permute-start | bytes 786440 | tf_op jit(solution)/shard_map/ppermute | solution.py:48
  23.3 26.7 %collective-permute-start.13 = (bf16[128,1024]{1,0:T(8,128)(2,1)}, bf16[128,1024]{1,0:T(8,128)(2,1)S(1)}, u32[]{:S(2)}, u32[]{:S(2)}) collective-permute-start(bf16[128,1024]{1,0:T(8,128)(2,1)} %get-tuple-element.156.r_1_), channel_id=1, source_target_pairs={{0,2},{1,3},{2,0},{3,1},{4,6},{5,7},{6,4},{7,5},{8,10},{9,11},{10,... | collective-permute-start | bytes 786440 | tf_op jit(solution)/shard_map/ppermute | solution.py:48
  41.1 32.9 %collective-permute-start.16 = (bf16[4,1088,128]{2,1,0:T(8,128)(2,1)S(1)}, bf16[4,1088,128]{2,1,0:T(8,128)(2,1)S(1)}, u32[]{:S(2)}, u32[]{:S(2)}) collective-permute-start(bf16[4,1088,128]{2,1,0:T(8,128)(2,1)S(1)} %pad_maximum_fusion.slab.r_5_), channel_id=1, source_target_pairs={{0,4},{4,0},{8,12},{12,8},{16,20},{20,16},{24,28},{28,24},{1,5},{5... | collective-permute-start | bytes 3342344 | tf_op jit(solution)/shard_map/ppermute | solution.py:42
  45.9 24.8 %collective-permute-start.4 = (bf16[1024,128]{1,0:T(8,128)(2,1)}, bf16[1024,128]{1,0:T(8,128)(2,1)}, u32[]{:S(2)}, u32[]{:S(2)}) collective-permute-start(bf16[1024,128]{1,0:T(8,128)(2,1)} %get-tuple-element.150), channel_id=1, source_target_pairs={{0,16},{4,20},{8,24},{12,28},{16,0},{20,4},{24,8},{28,12},{1,17},{... | collective-permute-start | bytes 786440 | tf_op jit(solution)/shard_map/ppermute | solution.py:48
  48.7 22.7 %collective-permute-start.3 = (bf16[1024,128]{1,0:T(8,128)(2,1)}, bf16[1024,128]{1,0:T(8,128)(2,1)}, u32[]{:S(2)}, u32[]{:S(2)}) collective-permute-start(bf16[1024,128]{1,0:T(8,128)(2,1)} %get-tuple-element.150), channel_id=1, source_target_pairs={{0,8},{4,12},{8,16},{12,20},{16,24},{20,28},{24,0},{28,4},{1,9},{5... | collective-permute-start | bytes 786440 | tf_op jit(solution)/shard_map/ppermute | solution.py:48
  50.0 23.7 %collective-permute-start.11 = (bf16[128,1024]{1,0:T(8,128)(2,1)S(1)}, bf16[128,1024]{1,0:T(8,128)(2,1)}, u32[]{:S(2)}, u32[]{:S(2)}) collective-permute-start(bf16[128,1024]{1,0:T(8,128)(2,1)S(1)} %copy-done.41), channel_id=1, source_target_pairs={{0,1},{1,0},{2,3},{3,2},{4,5},{5,4},{6,7},{7,6},{8,9},{9,8},{10,11... | collective-permute-start | bytes 786440 | tf_op jit(solution)/shard_map/ppermute | solution.py:42
  52.2 21.8 %collective-permute-start.12 = (bf16[128,1024]{1,0:T(8,128)(2,1)}, bf16[128,1024]{1,0:T(8,128)(2,1)}, u32[]{:S(2)}, u32[]{:S(2)}) collective-permute-start(bf16[128,1024]{1,0:T(8,128)(2,1)} %collective-permute-done.10.r_2_), channel_id=1, source_target_pairs={{0,1},{1,0},{2,3},{3,2},{4,5},{5,4},{6,7},{7,6},{8,9},{9,8},{10,11... | collective-permute-start | bytes 786440 | tf_op jit(solution)/shard_map/ppermute | solution.py:42
  70.7 13.6 %collective-permute-start.14 = (bf16[128,1024]{1,0:T(8,128)(2,1)}, bf16[128,1024]{1,0:T(8,128)(2,1)}, u32[]{:S(2)}, u32[]{:S(2)}) collective-permute-start(bf16[128,1024]{1,0:T(8,128)(2,1)} %get-tuple-element.156.r_1_), channel_id=1, source_target_pairs={{0,1},{1,0},{2,3},{3,2},{4,5},{5,4},{6,7},{7,6},{8,9},{9,8},{10,11... | collective-permute-start | bytes 786440 | tf_op jit(solution)/shard_map/ppermute | solution.py:42
  71.3 16.0 %collective-permute-start.15 = (bf16[128,1024]{1,0:T(8,128)(2,1)}, bf16[128,1024]{1,0:T(8,128)(2,1)}, u32[]{:S(2)}, u32[]{:S(2)}) collective-permute-start(bf16[128,1024]{1,0:T(8,128)(2,1)} %copy-done.42), channel_id=1, source_target_pairs={{0,1},{1,0},{2,3},{3,2},{4,5},{5,4},{6,7},{7,6},{8,9},{9,8},{10,11... | collective-permute-start | bytes 786440 | tf_op jit(solution)/shard_map/ppermute | solution.py:42
  73.8 35.6 %collective-permute-start.6 = (bf16[4,1024,128]{2,1,0:T(8,128)(2,1)}, bf16[4,1024,128]{2,1,0:T(8,128)(2,1)}, u32[]{:S(2)}, u32[]{:S(2)}) collective-permute-start(bf16[4,1024,128]{2,1,0:T(8,128)(2,1)} %pad_maximum_fusion.1.r_5_), channel_id=1, source_target_pairs={{0,4},{4,0},{8,12},{12,8},{16,20},{20,16},{24,28},{28,24},{1,5},{5... | collective-permute-start | bytes 3145736 | tf_op jit(solution)/shard_map/ppermute | solution.py:42
  74.0 22.1 %collective-permute-start.9 = (bf16[1024,128]{1,0:T(8,128)(2,1)}, bf16[1024,128]{1,0:T(8,128)(2,1)}, u32[]{:S(2)}, u32[]{:S(2)}) collective-permute-start(bf16[1024,128]{1,0:T(8,128)(2,1)} %get-tuple-element.152), channel_id=1, source_target_pairs={{0,24},{4,28},{8,0},{12,4},{16,8},{20,12},{24,16},{28,20},{1,25},{... | collective-permute-start | bytes 786440 | tf_op jit(solution)/shard_map/ppermute | solution.py:48
  74.1 22.1 %collective-permute-start.8 = (bf16[1024,128]{1,0:T(8,128)(2,1)}, bf16[1024,128]{1,0:T(8,128)(2,1)S(1)}, u32[]{:S(2)}, u32[]{:S(2)}) collective-permute-start(bf16[1024,128]{1,0:T(8,128)(2,1)} %get-tuple-element.152), channel_id=1, source_target_pairs={{0,16},{4,20},{8,24},{12,28},{16,0},{20,4},{24,8},{28,12},{1,17},{... | collective-permute-start | bytes 786440 | tf_op jit(solution)/shard_map/ppermute | solution.py:48
  84.3 12.7 %collective-permute-start.7 = (bf16[1024,128]{1,0:T(8,128)(2,1)}, bf16[1024,128]{1,0:T(8,128)(2,1)S(1)}, u32[]{:S(2)}, u32[]{:S(2)}) collective-permute-start(bf16[1024,128]{1,0:T(8,128)(2,1)} %get-tuple-element.152), channel_id=1, source_target_pairs={{0,8},{4,12},{8,16},{12,20},{16,24},{20,28},{24,0},{28,4},{1,9},{5... | collective-permute-start | bytes 786440 | tf_op jit(solution)/shard_map/ppermute | solution.py:48
  98.2 38.0 %collective-permute-start.26 = (bf16[4,1024,128]{2,1,0:T(8,128)(2,1)S(1)}, bf16[4,1024,128]{2,1,0:T(8,128)(2,1)S(1)}, u32[]{:S(2)}, u32[]{:S(2)}) collective-permute-start(bf16[4,1024,128]{2,1,0:T(8,128)(2,1)S(1)} %pad_maximum_fusion.2.r_7_), channel_id=1, source_target_pairs={{0,4},{4,0},{8,12},{12,8},{16,20},{20,16},{24,28},{28,24},{1,5},{5... | collective-permute-start | bytes 3145736 | tf_op jit(solution)/shard_map/ppermute | solution.py:42
  105.5 11.2 %collective-permute-start.21 = (bf16[1024,128]{1,0:T(8,128)(2,1)}, bf16[1024,128]{1,0:T(8,128)(2,1)S(1)}, u32[]{:S(2)}, u32[]{:S(2)}) collective-permute-start(bf16[1024,128]{1,0:T(8,128)(2,1)} %get-tuple-element.165), channel_id=1, source_target_pairs={{0,24},{4,28},{8,0},{12,4},{16,8},{20,12},{24,16},{28,20},{1,25},{... | collective-permute-start | bytes 786440 | tf_op jit(solution)/shard_map/ppermute | solution.py:48
  113.6 14.3 %collective-permute-start.20 = (bf16[1024,128]{1,0:T(8,128)(2,1)S(1)}, bf16[1024,128]{1,0:T(8,128)(2,1)S(1)}, u32[]{:S(2)}, u32[]{:S(2)}) collective-permute-start(bf16[1024,128]{1,0:T(8,128)(2,1)S(1)} %copy-done.79), channel_id=1, source_target_pairs={{0,16},{4,20},{8,24},{12,28},{16,0},{20,4},{24,8},{28,12},{1,17},{... | collective-permute-start | bytes 786440 | tf_op jit(solution)/shard_map/ppermute | solution.py:48
  116.5 16.9 %collective-permute-start.19 = (bf16[1024,128]{1,0:T(8,128)(2,1)S(1)}, bf16[1024,128]{1,0:T(8,128)(2,1)S(1)}, u32[]{:S(2)}, u32[]{:S(2)}) collective-permute-start(bf16[1024,128]{1,0:T(8,128)(2,1)S(1)} %copy-done.79), channel_id=1, source_target_pairs={{0,8},{4,12},{8,16},{12,20},{16,24},{20,28},{24,0},{28,4},{1,9},{5... | collective-permute-start | bytes 786440 | tf_op jit(solution)/shard_map/ppermute | solution.py:48
  116.7 20.6 %collective-permute-start.28 = (bf16[128,1024]{1,0:T(8,128)(2,1)}, bf16[128,1024]{1,0:T(8,128)(2,1)S(1)}, u32[]{:S(2)}, u32[]{:S(2)}) collective-permute-start(bf16[128,1024]{1,0:T(8,128)(2,1)} %get-tuple-element.170.r_1_), channel_id=1, source_target_pairs={{0,1},{1,0},{2,3},{3,2},{4,5},{5,4},{6,7},{7,6},{8,9},{9,8},{10,11... | collective-permute-start | bytes 786440 | tf_op jit(solution)/shard_map/ppermute | solution.py:42
  120.4 17.7 %collective-permute-start.29 = (bf16[128,1024]{1,0:T(8,128)(2,1)S(1)}, bf16[128,1024]{1,0:T(8,128)(2,1)S(1)}, u32[]{:S(2)}, u32[]{:S(2)}) collective-permute-start(bf16[128,1024]{1,0:T(8,128)(2,1)S(1)} %collective-permute-done.27.r_2_), channel_id=1, source_target_pairs={{0,1},{1,0},{2,3},{3,2},{4,5},{5,4},{6,7},{7,6},{8,9},{9,8},{10,11... | collective-permute-start | bytes 786440 | tf_op jit(solution)/shard_map/ppermute | solution.py:42
  133.6 28.3 %collective-permute-start.22 = (bf16[4,1024,128]{2,1,0:T(8,128)(2,1)S(1)}, bf16[4,1024,128]{2,1,0:T(8,128)(2,1)S(1)}, u32[]{:S(2)}, u32[]{:S(2)}) collective-permute-start(bf16[4,1024,128]{2,1,0:T(8,128)(2,1)S(1)} %pad_maximum_fusion.3.r_5_), channel_id=1, source_target_pairs={{0,4},{4,0},{8,12},{12,8},{16,20},{20,16},{24,28},{28,24},{1,5},{5... | collective-permute-start | bytes 3145736 | tf_op jit(solution)/shard_map/ppermute | solution.py:42
  134.0 15.1 %collective-permute-start.25 = (bf16[1024,128]{1,0:T(8,128)(2,1)S(1)}, bf16[1024,128]{1,0:T(8,128)(2,1)S(1)}, u32[]{:S(2)}, u32[]{:S(2)}) collective-permute-start(bf16[1024,128]{1,0:T(8,128)(2,1)S(1)} %copy-done.77), channel_id=1, source_target_pairs={{0,24},{4,28},{8,0},{12,4},{16,8},{20,12},{24,16},{28,20},{1,25},{... | collective-permute-start | bytes 786440 | tf_op jit(solution)/shard_map/ppermute | solution.py:48
  136.2 17.0 %collective-permute-start.24 = (bf16[1024,128]{1,0:T(8,128)(2,1)S(1)}, bf16[1024,128]{1,0:T(8,128)(2,1)S(1)}, u32[]{:S(2)}, u32[]{:S(2)}) collective-permute-start(bf16[1024,128]{1,0:T(8,128)(2,1)S(1)} %copy-done.77), channel_id=1, source_target_pairs={{0,16},{4,20},{8,24},{12,28},{16,0},{20,4},{24,8},{28,12},{1,17},{... | collective-permute-start | bytes 786440 | tf_op jit(solution)/shard_map/ppermute | solution.py:48
  137.4 21.5 %collective-permute-start.23 = (bf16[1024,128]{1,0:T(8,128)(2,1)S(1)}, bf16[1024,128]{1,0:T(8,128)(2,1)S(1)}, u32[]{:S(2)}, u32[]{:S(2)}) collective-permute-start(bf16[1024,128]{1,0:T(8,128)(2,1)S(1)} %copy-done.77), channel_id=1, source_target_pairs={{0,8},{4,12},{8,16},{12,20},{16,24},{20,28},{24,0},{28,4},{1,9},{5... | collective-permute-start | bytes 786440 | tf_op jit(solution)/shard_map/ppermute | solution.py:48
  147.7 12.6 %collective-permute-start.30 = (bf16[2,128,1024]{2,1,0:T(8,128)(2,1)}, bf16[2,128,1024]{2,1,0:T(8,128)(2,1)S(1)}, u32[]{:S(2)}, u32[]{:S(2)}) collective-permute-start(bf16[2,128,1024]{2,1,0:T(8,128)(2,1)} %get-tuple-element.173), channel_id=1, source_target_pairs={{0,1},{1,0},{2,3},{3,2},{4,5},{5,4},{6,7},{7,6},{8,9},{9,8},{10,11... | collective-permute-start | bytes 1572872 | tf_op jit(solution)/shard_map/ppermute | solution.py:42
  159.0 27.9 %collective-permute-start.32 = (bf16[4,1024,128]{2,1,0:T(8,128)(2,1)S(1)}, bf16[4,1024,128]{2,1,0:T(8,128)(2,1)S(1)}, u32[]{:S(2)}, u32[]{:S(2)}) collective-permute-start(bf16[4,1024,128]{2,1,0:T(8,128)(2,1)S(1)} %pad_maximum_fusion.4.r_5_), channel_id=1, source_target_pairs={{0,4},{4,0},{8,12},{12,8},{16,20},{20,16},{24,28},{28,24},{1,5},{5... | collective-permute-start | bytes 3145736 | tf_op jit(solution)/shard_map/ppermute | solution.py:42
  160.7 13.5 %collective-permute-start.35 = (bf16[1024,128]{1,0:T(8,128)(2,1)S(1)}, bf16[1024,128]{1,0:T(8,128)(2,1)S(1)}, u32[]{:S(2)}, u32[]{:S(2)}) collective-permute-start(bf16[1024,128]{1,0:T(8,128)(2,1)S(1)} %copy-done.76), channel_id=1, source_target_pairs={{0,24},{4,28},{8,0},{12,4},{16,8},{20,12},{24,16},{28,20},{1,25},{... | collective-permute-start | bytes 786440 | tf_op jit(solution)/shard_map/ppermute | solution.py:48
  171.6 15.2 %collective-permute-start.33 = (bf16[1024,128]{1,0:T(8,128)(2,1)S(1)}, bf16[1024,128]{1,0:T(8,128)(2,1)S(1)}, u32[]{:S(2)}, u32[]{:S(2)}) collective-permute-start(bf16[1024,128]{1,0:T(8,128)(2,1)S(1)} %copy-done.76), channel_id=1, source_target_pairs={{0,8},{4,12},{8,16},{12,20},{16,24},{20,28},{24,0},{28,4},{1,9},{5... | collective-permute-start | bytes 786440 | tf_op jit(solution)/shard_map/ppermute | solution.py:48
  174.3 12.7 %collective-permute-start.37 = (bf16[128,1024]{1,0:T(8,128)(2,1)}, bf16[128,1024]{1,0:T(8,128)(2,1)S(1)}, u32[]{:S(2)}, u32[]{:S(2)}) collective-permute-start(bf16[128,1024]{1,0:T(8,128)(2,1)} %get-tuple-element.178.r_1_), channel_id=1, source_target_pairs={{0,1},{1,0},{2,3},{3,2},{4,5},{5,4},{6,7},{7,6},{8,9},{9,8},{10,11... | collective-permute-start | bytes 786440 | tf_op jit(solution)/shard_map/ppermute | solution.py:42
  177.6 9.4 %collective-permute-start.38 = (bf16[128,1024]{1,0:T(8,128)(2,1)S(1)}, bf16[128,1024]{1,0:T(8,128)(2,1)S(1)}, u32[]{:S(2)}, u32[]{:S(2)}) collective-permute-start(bf16[128,1024]{1,0:T(8,128)(2,1)S(1)} %collective-permute-done.36.r_2_), channel_id=1, source_target_pairs={{0,1},{1,0},{2,3},{3,2},{4,5},{5,4},{6,7},{7,6},{8,9},{9,8},{10,11... | collective-permute-start | bytes 786440 | tf_op jit(solution)/shard_map/ppermute | solution.py:42
  197.9 24.7 %collective-permute-start.44 = (bf16[4,1024,128]{2,1,0:T(8,128)(2,1)S(1)}, bf16[4,1024,128]{2,1,0:T(8,128)(2,1)S(1)}, u32[]{:S(2)}, u32[]{:S(2)}) collective-permute-start(bf16[4,1024,128]{2,1,0:T(8,128)(2,1)S(1)} %pad_maximum_fusion.5.r_7_), channel_id=1, source_target_pairs={{0,4},{4,0},{8,12},{12,8},{16,20},{20,16},{24,28},{28,24},{1,5},{5... | collective-permute-start | bytes 3145736 | tf_op jit(solution)/shard_map/ppermute | solution.py:42
  248.9 243.3 %reduce-scatter.3.cloned.1.call-start = ((), (), s32[]{:S(2)}) async-start(), calls=%async_computation.2 | async-start | bytes 4718592 | tf_op jit(solution)/shard_map/reduce_scatter | solution.py:1195
  291.4 34.7 %collective-permute-start.54 = (bf16[4,1024,128]{2,1,0:T(8,128)(2,1)}, bf16[4,1024,128]{2,1,0:T(8,128)(2,1)S(1)}, u32[]{:S(2)}, u32[]{:S(2)}) collective-permute-start(bf16[4,1024,128]{2,1,0:T(8,128)(2,1)} %get-tuple-element.200), channel_id=1, source_target_pairs={{0,4},{4,0},{8,12},{12,8},{16,20},{20,16},{24,28},{28,24},{1,5},{5... | collective-permute-start | bytes 3145736 | tf_op jit(solution)/shard_map/ppermute | solution.py:42
  304.6 21.5 %collective-permute-start.56 = (bf16[128,1024]{1,0:T(8,128)(2,1)}, bf16[128,1024]{1,0:T(8,128)(2,1)S(1)}, u32[]{:S(2)}, u32[]{:S(2)}) collective-permute-start(bf16[128,1024]{1,0:T(8,128)(2,1)} %get-tuple-element.201.r_1_), channel_id=1, source_target_pairs={{0,1},{1,0},{2,3},{3,2},{4,5},{5,4},{6,7},{7,6},{8,9},{9,8},{10,11... | collective-permute-start | bytes 786440 | tf_op jit(solution)/shard_map/ppermute | solution.py:42
  310.5 15.7 %collective-permute-start.57 = (bf16[128,1024]{1,0:T(8,128)(2,1)S(1)}, bf16[128,1024]{1,0:T(8,128)(2,1)S(1)}, u32[]{:S(2)}, u32[]{:S(2)}) collective-permute-start(bf16[128,1024]{1,0:T(8,128)(2,1)S(1)} %collective-permute-done.55.r_2_), channel_id=1, source_target_pairs={{0,1},{1,0},{2,3},{3,2},{4,5},{5,4},{6,7},{7,6},{8,9},{9,8},{10,11... | collective-permute-start | bytes 786440 | tf_op jit(solution)/shard_map/ppermute | solution.py:42
  379.2 17.3 %collective-permute-start.63 = (bf16[2,128,1024]{2,1,0:T(8,128)(2,1)}, bf16[2,128,1024]{2,1,0:T(8,128)(2,1)S(1)}, u32[]{:S(2)}, u32[]{:S(2)}) collective-permute-start(bf16[2,128,1024]{2,1,0:T(8,128)(2,1)} %get-tuple-element.210), channel_id=1, source_target_pairs={{0,1},{1,0},{2,3},{3,2},{4,5},{5,4},{6,7},{7,6},{8,9},{9,8},{10,11... | collective-permute-start | bytes 1572872 | tf_op jit(solution)/shard_map/ppermute | solution.py:42
  379.6 59.7 %collective-permute-start.45 = (bf16[2,128,1024]{2,1,0:T(8,128)(2,1)}, bf16[2,128,1024]{2,1,0:T(8,128)(2,1)S(1)}, u32[]{:S(2)}, u32[]{:S(2)}) collective-permute-start(bf16[2,128,1024]{2,1,0:T(8,128)(2,1)} %get-tuple-element.184), channel_id=1, source_target_pairs={{0,1},{1,0},{2,3},{3,2},{4,5},{5,4},{6,7},{7,6},{8,9},{9,8},{10,11... | collective-permute-start | bytes 1572872 | tf_op jit(solution)/shard_map/ppermute | solution.py:42
  383.2 57.8 %collective-permute-start.79 = (bf16[1024,128]{1,0:T(8,128)(2,1)}, bf16[1024,128]{1,0:T(8,128)(2,1)S(1)}, u32[]{:S(2)}, u32[]{:S(2)}) collective-permute-start(bf16[1024,128]{1,0:T(8,128)(2,1)} %get-tuple-element.244), channel_id=1, source_target_pairs={{0,8},{4,12},{8,16},{12,20},{16,24},{20,28},{24,0},{28,4},{1,9},{5... | collective-permute-start | bytes 786440 | tf_op jit(solution)/shard_map/ppermute | solution.py:48
  384.6 58.4 %collective-permute-start.80 = (bf16[1024,128]{1,0:T(8,128)(2,1)}, bf16[1024,128]{1,0:T(8,128)(2,1)S(1)}, u32[]{:S(2)}, u32[]{:S(2)}) collective-permute-start(bf16[1024,128]{1,0:T(8,128)(2,1)} %get-tuple-element.246), channel_id=1, source_target_pairs={{0,16},{4,20},{8,24},{12,28},{16,0},{20,4},{24,8},{28,12},{1,17},{... | collective-permute-start | bytes 786440 | tf_op jit(solution)/shard_map/ppermute | solution.py:48
  392.5 39.3 %collective-permute-start.72 = (bf16[4,1024,128]{2,1,0:T(8,128)(2,1)}, bf16[4,1024,128]{2,1,0:T(8,128)(2,1)S(1)}, u32[]{:S(2)}, u32[]{:S(2)}) collective-permute-start(bf16[4,1024,128]{2,1,0:T(8,128)(2,1)} %get-tuple-element.236), channel_id=1, source_target_pairs={{0,4},{4,0},{8,12},{12,8},{16,20},{20,16},{24,28},{28,24},{1,5},{5... | collective-permute-start | bytes 3145736 | tf_op jit(solution)/shard_map/ppermute | solution.py:42
  412.7 16.6 %collective-permute-start.65 = (bf16[4,64,128]{2,1,0:T(8,128)(2,1)}, bf16[4,64,128]{2,1,0:T(8,128)(2,1)S(1)}, u32[]{:S(2)}, u32[]{:S(2)}) collective-permute-start(bf16[4,64,128]{2,1,0:T(8,128)(2,1)} %get-tuple-element.224), channel_id=1, source_target_pairs={{0,4},{4,0},{8,12},{12,8},{16,20},{20,16},{24,28},{28,24},{1,5},{5... | collective-permute-start | bytes 196616 | tf_op jit(solution)/shard_map/ppermute | solution.py:42
  429.9 13.0 %collective-permute-start.81 = (bf16[1024,128]{1,0:T(8,128)(2,1)}, bf16[1024,128]{1,0:T(8,128)(2,1)S(1)}, u32[]{:S(2)}, u32[]{:S(2)}) collective-permute-start(bf16[1024,128]{1,0:T(8,128)(2,1)} %get-tuple-element.248), channel_id=1, source_target_pairs={{0,24},{4,28},{8,0},{12,4},{16,8},{20,12},{24,16},{28,20},{1,25},{... | collective-permute-start | bytes 786440 | tf_op jit(solution)/shard_map/ppermute | solution.py:48
  431.8 12.6 %collective-permute-start.91 = (f32[104,128]{1,0:T(8,128)S(1)}, f32[104,128]{1,0:T(8,128)S(1)}, u32[]{:S(2)}, u32[]{:S(2)}) collective-permute-start(f32[104,128]{1,0:T(8,128)S(1)} %fusion.29), channel_id=1, source_target_pairs={{0,1},{1,0},{2,3},{3,2},{4,5},{5,4},{6,7},{7,6},{8,9},{9,8},{10,11... | collective-permute-start | bytes 159752 | tf_op jit(solution)/shard_map/ppermute | solution.py:42
  442.9 44.2 %collective-permute-start.73 = (bf16[1024,128]{1,0:T(8,128)(2,1)}, bf16[1024,128]{1,0:T(8,128)(2,1)S(1)}, u32[]{:S(2)}, u32[]{:S(2)}) collective-permute-start(bf16[1024,128]{1,0:T(8,128)(2,1)} %get-tuple-element.238), channel_id=1, source_target_pairs={{0,8},{4,12},{8,16},{12,20},{16,24},{20,28},{24,0},{28,4},{1,9},{5... | collective-permute-start | bytes 786440 | tf_op jit(solution)/shard_map/ppermute | solution.py:48
  443.0 44.8 %collective-permute-start.74 = (bf16[1024,128]{1,0:T(8,128)(2,1)}, bf16[1024,128]{1,0:T(8,128)(2,1)S(1)}, u32[]{:S(2)}, u32[]{:S(2)}) collective-permute-start(bf16[1024,128]{1,0:T(8,128)(2,1)} %get-tuple-element.239), channel_id=1, source_target_pairs={{0,16},{4,20},{8,24},{12,28},{16,0},{20,4},{24,8},{28,12},{1,17},{... | collective-permute-start | bytes 786440 | tf_op jit(solution)/shard_map/ppermute | solution.py:48
  444.5 43.3 %collective-permute-start.75 = (bf16[1024,128]{1,0:T(8,128)(2,1)}, bf16[1024,128]{1,0:T(8,128)(2,1)S(1)}, u32[]{:S(2)}, u32[]{:S(2)}) collective-permute-start(bf16[1024,128]{1,0:T(8,128)(2,1)} %get-tuple-element.240), channel_id=1, source_target_pairs={{0,24},{4,28},{8,0},{12,4},{16,8},{20,12},{24,16},{28,20},{1,25},{... | collective-permute-start | bytes 786440 | tf_op jit(solution)/shard_map/ppermute | solution.py:48
  445.6 47.1 %collective-permute-start.92 = (f32[104,128]{1,0:T(8,128)}, f32[104,128]{1,0:T(8,128)}, u32[]{:S(2)}, u32[]{:S(2)}) collective-permute-start(f32[104,128]{1,0:T(8,128)} %fusion.58), channel_id=1, source_target_pairs={{0,2},{1,3},{2,0},{3,1},{4,6},{5,7},{6,4},{7,5},{8,10},{9,11},{10,... | collective-permute-start | bytes 159752 | tf_op jit(solution)/shard_map/ppermute | solution.py:48
  446.8 37.1 %collective-permute-start.68 = (bf16[64,128]{1,0:T(8,128)(2,1)S(1)}, bf16[64,128]{1,0:T(8,128)(2,1)S(1)}, u32[]{:S(2)}, u32[]{:S(2)}) collective-permute-start(bf16[64,128]{1,0:T(8,128)(2,1)S(1)} %copy-done.100), channel_id=1, source_target_pairs={{0,24},{4,28},{8,0},{12,4},{16,8},{20,12},{24,16},{28,20},{1,25},{... | collective-permute-start | bytes 49160 | tf_op jit(solution)/shard_map/ppermute | solution.py:48
  483.9 15.3 %collective-permute-start.46 = (bf16[128,1024]{1,0:T(8,128)(2,1)S(1)}, bf16[128,1024]{1,0:T(8,128)(2,1)S(1)}, u32[]{:S(2)}, u32[]{:S(2)}) collective-permute-start(bf16[128,1024]{1,0:T(8,128)(2,1)S(1)} %fusion.3), channel_id=1, source_target_pairs={{0,2},{1,3},{2,0},{3,1},{4,6},{5,7},{6,4},{7,5},{8,10},{9,11},{10,... | collective-permute-start | bytes 786440 | tf_op jit(solution)/shard_map/ppermute | solution.py:48
  487.1 19.6 %collective-permute-start.82 = (bf16[1024,128]{1,0:T(8,128)(2,1)}, bf16[1024,128]{1,0:T(8,128)(2,1)S(1)}, u32[]{:S(2)}, u32[]{:S(2)}) collective-permute-start(bf16[1024,128]{1,0:T(8,128)(2,1)} %shard_map.368.r_1_), channel_id=1, source_target_pairs={{0,2},{1,3},{2,0},{3,1},{4,6},{5,7},{6,4},{7,5},{8,10},{9,11},{10,... | collective-permute-start | bytes 786440 | tf_op jit(solution)/shard_map/ppermute | solution.py:48
  491.3 38.1 %collective-permute-start.88 = (bf16[2048,128]{1,0:T(8,128)(2,1)}, bf16[2048,128]{1,0:T(8,128)(2,1)S(1)}, u32[]{:S(2)}, u32[]{:S(2)}) collective-permute-start(bf16[2048,128]{1,0:T(8,128)(2,1)} %bitcast.204), channel_id=1, source_target_pairs={{0,2},{1,3},{2,0},{3,1},{4,6},{5,7},{6,4},{7,5},{8,10},{9,11},{10,... | collective-permute-start | bytes 1572872 | tf_op jit(solution)/shard_map/ppermute | solution.py:48
  492.2 37.8 %collective-permute-start.85 = (bf16[2048,128]{1,0:T(8,128)(2,1)}, bf16[2048,128]{1,0:T(8,128)(2,1)S(1)}, u32[]{:S(2)}, u32[]{:S(2)}) collective-permute-start(bf16[2048,128]{1,0:T(8,128)(2,1)} %bitcast.209), channel_id=1, source_target_pairs={{0,2},{1,3},{2,0},{3,1},{4,6},{5,7},{6,4},{7,5},{8,10},{9,11},{10,... | collective-permute-start | bytes 1572872 | tf_op jit(solution)/shard_map/ppermute | solution.py:48
  497.0 14.2 %collective-permute-start.83 = (bf16[1024,128]{1,0:T(8,128)(2,1)}, bf16[1024,128]{1,0:T(8,128)(2,1)S(1)}, u32[]{:S(2)}, u32[]{:S(2)}) collective-permute-start(bf16[1024,128]{1,0:T(8,128)(2,1)} %shard_map.368.r_1_), channel_id=1, source_target_pairs={{0,1},{1,0},{2,3},{3,2},{4,5},{5,4},{6,7},{7,6},{8,9},{9,8},{10,11... | collective-permute-start | bytes 786440 | tf_op jit(solution)/shard_map/ppermute | solution.py:42
  510.0 19.5 %collective-permute-start.76 = (bf16[1024,128]{1,0:T(8,128)(2,1)}, bf16[1024,128]{1,0:T(8,128)(2,1)}, u32[]{:S(2)}, u32[]{:S(2)}) collective-permute-start(bf16[1024,128]{1,0:T(8,128)(2,1)} %shard_map.366.r_1_), channel_id=1, source_target_pairs={{0,2},{1,3},{2,0},{3,1},{4,6},{5,7},{6,4},{7,5},{8,10},{9,11},{10,... | collective-permute-start | bytes 786440 | tf_op jit(solution)/shard_map/ppermute | solution.py:48
  511.2 21.9 %collective-permute-start.77 = (bf16[1024,128]{1,0:T(8,128)(2,1)}, bf16[1024,128]{1,0:T(8,128)(2,1)}, u32[]{:S(2)}, u32[]{:S(2)}) collective-permute-start(bf16[1024,128]{1,0:T(8,128)(2,1)} %shard_map.366.r_1_), channel_id=1, source_target_pairs={{0,1},{1,0},{2,3},{3,2},{4,5},{5,4},{6,7},{7,6},{8,9},{9,8},{10,11... | collective-permute-start | bytes 786440 | tf_op jit(solution)/shard_map/ppermute | solution.py:42
  514.2 11.2 %collective-permute-start.69 = (bf16[64,128]{1,0:T(8,128)(2,1)}, bf16[64,128]{1,0:T(8,128)(2,1)S(1)}, u32[]{:S(2)}, u32[]{:S(2)}) collective-permute-start(bf16[64,128]{1,0:T(8,128)(2,1)} %shard_map.362.r_1_), channel_id=1, source_target_pairs={{0,2},{1,3},{2,0},{3,1},{4,6},{5,7},{6,4},{7,5},{8,10},{9,11},{10,... | collective-permute-start | bytes 49160 | tf_op jit(solution)/shard_map/ppermute | solution.py:48
  529.0 21.7 %collective-permute-start.89 = (bf16[2048,128]{1,0:T(8,128)(2,1)}, bf16[2048,128]{1,0:T(8,128)(2,1)S(1)}, u32[]{:S(2)}, u32[]{:S(2)}) collective-permute-start(bf16[2048,128]{1,0:T(8,128)(2,1)} %bitcast.205), channel_id=1, source_target_pairs={{0,1},{1,0},{2,3},{3,2},{4,5},{5,4},{6,7},{7,6},{8,9},{9,8},{10,11... | collective-permute-start | bytes 1572872 | tf_op jit(solution)/shard_map/ppermute | solution.py:42
  529.4 21.4 %collective-permute-start.90 = (bf16[2048,128]{1,0:T(8,128)(2,1)S(1)}, bf16[2048,128]{1,0:T(8,128)(2,1)S(1)}, u32[]{:S(2)}, u32[]{:S(2)}) collective-permute-start(bf16[2048,128]{1,0:T(8,128)(2,1)S(1)} %collective-permute-done.88.r_2_), channel_id=1, source_target_pairs={{0,1},{1,0},{2,3},{3,2},{4,5},{5,4},{6,7},{7,6},{8,9},{9,8},{10,11... | collective-permute-start | bytes 1572872 | tf_op jit(solution)/shard_map/ppermute | solution.py:42
  529.6 27.4 %collective-permute-start.86 = (bf16[2048,128]{1,0:T(8,128)(2,1)}, bf16[2048,128]{1,0:T(8,128)(2,1)S(1)}, u32[]{:S(2)}, u32[]{:S(2)}) collective-permute-start(bf16[2048,128]{1,0:T(8,128)(2,1)} %bitcast.210), channel_id=1, source_target_pairs={{0,1},{1,0},{2,3},{3,2},{4,5},{5,4},{6,7},{7,6},{8,9},{9,8},{10,11... | collective-permute-start | bytes 1572872 | tf_op jit(solution)/shard_map/ppermute | solution.py:42
  530.0 27.0 %collective-permute-start.87 = (bf16[2048,128]{1,0:T(8,128)(2,1)S(1)}, bf16[2048,128]{1,0:T(8,128)(2,1)S(1)}, u32[]{:S(2)}, u32[]{:S(2)}) collective-permute-start(bf16[2048,128]{1,0:T(8,128)(2,1)S(1)} %collective-permute-done.85.r_2_), channel_id=1, source_target_pairs={{0,1},{1,0},{2,3},{3,2},{4,5},{5,4},{6,7},{7,6},{8,9},{9,8},{10,11... | collective-permute-start | bytes 1572872 | tf_op jit(solution)/shard_map/ppermute | solution.py:42
  533.1 13.3 %collective-permute-start.78 = (bf16[1024,128]{1,0:T(8,128)(2,1)}, bf16[1024,128]{1,0:T(8,128)(2,1)S(1)}, u32[]{:S(2)}, u32[]{:S(2)}) collective-permute-start(bf16[1024,128]{1,0:T(8,128)(2,1)} %collective-permute-done.76.r_2_), channel_id=1, source_target_pairs={{0,1},{1,0},{2,3},{3,2},{4,5},{5,4},{6,7},{7,6},{8,9},{9,8},{10,11... | collective-permute-start | bytes 786440 | tf_op jit(solution)/shard_map/ppermute | solution.py:42
  (138 other events, 1140.8 us)
Sparse Core Ops, SparseCore 0:
  249.0 100.9 reduce-scatter.4
  354.7 124.5 reduce-scatter.2

commit v3 on v2

--- a/solution.py
+++ b/solution.py
@@ -465,6 +465,7 @@
 COST = 1000
 UP_AT = 48
 TOK = 52
+NET = 112
 
 
 def run(kernel, outs, meta, args, scratch=(), flops=0, alias=None):
@@ -771,19 +772,6 @@
     sums[2:3, :] = jnp.sum(rounded.astype(F32), axis=0, keepdims=True)
 
 
-def split_io_kernel(meta, g_in, g_out, send, mine):
-    n_grp = g_in.shape[1] // 128
-    part = g_in.shape[0] // n_grp
-    q = part // 3
-    for k in range(send.shape[0]):
-        for x, target in ((meta[2], mine), (1 - meta[2], send)):
-            g = 2 * k + x
-            for lb in range(n_grp):
-                at = lb * 4 * q
-                target[k, at : at + part, :] = g_in[span(g, part), lb * 128 : (lb + 1) * 128]
-                target[k, at + part : at + part + q, :] = g_out[lb * q : (lb + 1) * q, span(g, 128)]
-
-
 def mlp_grads_kernel(meta, every, g_pre, hidden, low, out):
     tile = 256
     rows = every.shape[1]
@@ -795,30 +783,68 @@
             out[2 * n + 1, at : at + rows, :] = value[:, 128:]
 
 
-def io_grads_kernel(meta, g_proj, every, mixed, low, send, mine, g_in, g_out):
+def mlp_split_kernel(meta, every, g_pre, hidden, low, send, mine):
+    tile = 256
+    rows = every.shape[1]
+    first = meta[2] == 0
+    for at, left, right in ((0, every, g_pre), (rows, hidden, low)):
+        for n in range(right.shape[1] // tile):
+            value = dot(left[...], right[:, n * tile : (n + 1) * tile], 0, 0).astype(BF)
+            one, two = value[:, :128], value[:, 128:]
+            mine[n, at : at + rows, :] = jnp.where(first, one, two)
+            send[n, at : at + rows, :] = jnp.where(first, two, one)
+
+
+def io_grads_kernel(split, meta, g_proj, every, mixed, low, *refs):
+    outs, (g_in, g_out) = refs[:-2], refs[-2:]
     wide = mixed.shape[1]
     for j in range(g_proj.shape[1] // wide):
         w = slice(j * wide, (j + 1) * wide)
         g_in[w, :] = dot(g_proj[:, w], every[...], 0, 0).astype(BF)
     g_out[...] = dot(mixed[...], low[...], 0, 0).astype(BF)
-    split_io_kernel(meta, g_in, g_out, send, mine)
-
-
-def owner_sum_kernel(meta, mine, got, own, *sends):
+    n_grp = g_in.shape[1] // 128
+    part = g_in.shape[0] // n_grp
+    q = part // 3
+    if split:
+        send, mine = outs
+        places = [(2 * k + x, t.at[k]) for k in range(n_grp // 2) for x, t in ((meta[2], mine), (1 - meta[2], send))]
+    else:
+        places = [(g, outs[0].at[g]) for g in range(n_grp)]
+    for g, target in places:
+        for lb in range(n_grp):
+            at = lb * 4 * q
+            target[at : at + part, :] = g_in[span(g, part), lb * 128 : (lb + 1) * 128]
+            target[at + part : at + part + q, :] = g_out[lb * q : (lb + 1) * q, span(g, 128)]
+
+
+def owner_sum_kernel(meta, mine, got, keep, send):
+    for k in range(2):
+        near = meta[1] ^ (2 * k)
+        far = near ^ 1
+        keep[k] = mine[near].astype(F32) + got[near].astype(F32)
+        send[k] = (mine[far].astype(F32) + got[far].astype(F32)).astype(BF)
+
+
+def last_sum_kernel(meta, keep, got, crossed, out):
+    out[...] = (keep[0] + got[0].astype(F32) + crossed[...].astype(F32)).astype(BF)
+
+
+def small_last_kernel(meta, *refs):
+    pieces, out, held = refs[:-2], refs[-2], refs[-1]
+    half = len(pieces)
+    for k, v in enumerate(pieces):
+        held[lax.rem(meta[1] - k + half, half)] = v[...].astype(F32)
+    total = held[0]
+    for k in range(1, half):
+        total = total + held[k]
+    out[...] = total.astype(BF)
+
+
+def small_turn_kernel(meta, mine, got, own, *sends):
     half = got.shape[0]
-    z = meta[1]
-    own[...] = mine[z].astype(F32) + got[z].astype(F32)
-    for k, send in enumerate(sends, 1):
-        to = lax.rem(z + k, half)
+    for k, send in enumerate((own,) + sends):
+        to = lax.rem(meta[1] + k, half)
         send[...] = (mine[to].astype(F32) + got[to].astype(F32)).astype(BF)
-
-
-def last_sum_kernel(meta, own, *refs):
-    got, out = refs[:-1], refs[-1]
-    total = own[...]
-    for v in got:
-        total = total + v[...].astype(F32)
-    out[...] = total.astype(BF)
 
 
 def prep_kernel(small, meta, up, down, w_in, w_out, *refs):
@@ -875,6 +901,8 @@
 def unpack_kernel(meta, slab, other, e_wide, e_all, tok, rows5, skip, fout, b_up, wide):
     place_wide(meta, (slab, other), wide)
     depth = fout.shape[0]
+    hid = fout.shape[1] // depth
+    fout[...] = jnp.zeros_like(fout)
     tok[...] = wide[TOK:SMALL, :].astype(F32)
     low = wide[: 2 * SLOT, :]
     five = dot(low, e_wide[...], 1, 0)
@@ -884,11 +912,37 @@
     for b in range(4):
         found = dot(low, e_all[b], 1, 0)
         for l in range(depth):
-            at = l * SLOT
-            fout[l, 15 * b : 15 * b + 15, :] = found[at + 5 : at + 20]
+            at, to = l * SLOT, l * hid
+            fout[l, to + 15 * b : to + 15 * b + 15, :] = found[at + 5 : at + 20]
             if b == 3:
-                fout[l, 60:64, :] = found[at : at + 4]
+                fout[l, to + 60 : to + 64, :] = found[at : at + 4]
                 skip[l] = found[at + 4 : at + 5]
+
+
+def net_grads(depth, seconds, net):
+    feats_t, one_t, pre0, cos0, freq0, pre1, cos1, freq1, mid = net
+    g = seconds[0][...]
+    for v in seconds[1:]:
+        g = g + v[...]
+    lanes = g.shape[1]
+    hid = lanes // depth
+    g = g * cos1[...]
+    g_freq1 = jnp.sum(g * pre1[...], axis=0, keepdims=True)
+    g = g * freq1[...]
+    g_bias1 = jnp.sum(g, axis=0, keepdims=True)
+    full = exact(one_t[...], g, 1, 0)
+    lane = lax.broadcasted_iota(jnp.int32, (hid, lanes), 1)
+    g_mid = full[:hid]
+    for l in range(1, depth):
+        g_mid = jnp.where(lane >= l * hid, full[l * hid : (l + 1) * hid], g_mid)
+    g = exact(g, mid[...], 1, 1) * cos0[...]
+    g_freq0 = jnp.sum(g * pre0[...], axis=0, keepdims=True)
+    g = g * freq0[...]
+    g_bias0 = jnp.sum(g, axis=0, keepdims=True)
+    g_in = exact(feats_t[...], g, 1, 0)
+    rows = [g_mid, g_in[:33], g_bias0, g_bias1, g_freq0, g_freq1]
+    rows.append(jnp.zeros((NET - hid - 37, lanes), F32))
+    return jnp.concatenate(rows)
 
 
 def pack_kernel(depth, meta, *refs):
@@ -896,15 +950,18 @@
     smalls, refs = refs[:depth], refs[depth:]
     fouts, refs = refs[:depth], refs[depth:]
     toks, refs = refs[: 2 * depth + 1], refs[2 * depth + 1 :]
+    seconds, refs = refs[:depth], refs[depth:]
+    net, refs = refs[:9], refs[9:]
     e_wide, e_all, send, mine, rows, wide = refs
     chans = fouts[0].shape[1]
+    hid = fouts[0].shape[0] // depth
     rows[...] = jnp.zeros_like(rows)
     for l in range(depth):
         at = l * SLOT
         rows[4, at : at + 5, :] = smalls[l][:5, :]
         for b in range(4):
-            rows[b, at + 5 : at + 20, :chans] = fouts[l][15 * b : 15 * b + 15, :]
-        rows[3, at : at + 4, :chans] = fouts[l][60:64, :]
+            rows[b, at + 5 : at + 20, :chans] = fouts[l][hid * l + 15 * b : hid * l + 15 * b + 15, :]
+        rows[3, at : at + 4, :chans] = fouts[l][hid * l + 60 : hid * l + 64, :]
         rows[3, at + 4 : at + 5, :chans] = smalls[l][5:6, :chans]
     packed = dot(rows[4].astype(BF), e_wide[...], 1, 1)
     for b in range(4):
@@ -919,21 +976,34 @@
             wide[at : at + 1, :] = v[0:1, :]
             wide[at + 2 * depth : at + 2 * depth + 1, :] = v[1:2, :]
             wide[at + 4 * depth : at + 4 * depth + 1, :] = toks[2 * l + i + 1][2:3, :]
+    grads = net_grads(depth, seconds, net).astype(BF)
     for k in range(send.shape[0]):
-        mine[k] = wide[:, span(2 * k + meta[2], 128)].astype(BF)
-        send[k] = wide[:, span(2 * k + 1 - meta[2], 128)].astype(BF)
+        mine[k, :SMALL] = wide[:, span(2 * k + meta[2], 128)].astype(BF)
+        send[k, :SMALL] = wide[:, span(2 * k + 1 - meta[2], 128)].astype(BF)
+        mine[k, SMALL:] = grads
+        send[k, SMALL:] = grads
 
 
 def finish_small_kernel(q, meta, *refs):
     parts, refs = refs[:4], refs[4:]
-    gain, shift, branch, in_bias, conv_weight, conv_bias, skip, fout, up_bias = refs
+    gain, shift, branch, in_bias, conv_weight, conv_bias, skip, fout, up_bias, g_in, g_mid, g_bias, g_freq, held = refs
     depth = fout.shape[0]
+    hid = fout.shape[1]
     lanes = parts[0].shape[1]
     lane = lax.broadcasted_iota(jnp.int32, (lanes, lanes), 0)
     to = lax.broadcasted_iota(jnp.int32, (lanes, lanes), 1)
-    tok = parts[0][...].astype(F32)
-    for part in parts[1:]:
-        tok = tok + part[...].astype(F32)
+    for k, part in enumerate(parts):
+        held[meta[0] ^ ORDER[k]] = part[...].astype(F32)
+    tok = held[0]
+    for k in range(1, 4):
+        tok = tok + held[k]
+    for l in range(depth):
+        w = slice(l * hid, (l + 1) * hid)
+        at = SMALL + hid
+        g_mid[l] = tok[SMALL:at, w]
+        g_in[l] = tok[at : at + 33, w]
+        g_bias[l] = tok[at + 33 : at + 35, w]
+        g_freq[l] = tok[at + 35 : at + 37, w]
     for l in range(depth):
         for t, v in enumerate((gain, shift, branch)):
             at = TOK + 2 * depth * t + 2 * l
@@ -985,11 +1055,6 @@
             g_out[0, lb, s] = part[at + 3 * q : at + 4 * q, :].astype(F32)
     for j in range(3):
         g_in[0, :, j * 4 * q : (j + 1) * 4 * q] = turned[j * 4 * q : (j + 1) * 4 * q, :].T
-
-
-def second_layer(fin, fmid, fbias, freq, feats):
-    inner = jnp.sin(freq[0] * (jnp.dot(feats, fin, precision=HIGH) + fbias[0]))
-    return jnp.sin(freq[1] * (jnp.dot(inner, fmid, precision=HIGH) + fbias[1]))
 
 
 def after(value, *others):
@@ -1085,7 +1150,7 @@
     tok_all, rows5, skip, fout, b_up = run(
         unpack_kernel,
         [((6 * depth, width), F32), ((depth, 5, 3 * chans), F32), ((depth, 1, chans), F32),
-         ((depth, hid, chans), F32), ((depth, 1, n_grp * f), F32)],
+         ((depth, depth * hid, chans), F32), ((depth, 1, n_grp * f), F32)],
         meta, [(slab,) + small_block, (other,) + small_block, e_wide, e_all], [((SMALL, width), BF)])
     tok_all = tok_all.reshape(3, depth, 2, 1, width)
     gains, shifts, b_branch = tok_all[0], tok_all[1], tok_all[2]
@@ -1099,18 +1164,31 @@
     ).reshape(-1).astype(F32)
     rate = jnp.abs(FAST + (SLOW - FAST) * channel / (width - 1))
     decay = jnp.exp(-tpos[:, None] * rate[None, :])
-    seconds, second_pull = jax.vjp(
-        lambda *a: jax.vmap(lambda *b: second_layer(*b, feats))(*a), filt_in, filt_mid, filt_bias, sine_freq)
+    lanes = depth * hid
+    bias0, bias1 = (filt_bias[:, i].reshape(1, lanes) for i in range(2))
+    freq0, freq1 = (sine_freq[:, i].reshape(1, lanes) for i in range(2))
+    mid_all = jnp.zeros((lanes, lanes), F32)
+    for l in range(depth):
+        mid_all = lax.dynamic_update_slice(mid_all, filt_mid[l], (l * hid, l * hid))
+    pre0 = jnp.dot(feats, jnp.transpose(filt_in, (1, 0, 2)).reshape(-1, lanes), precision=HIGH) + bias0
+    one, cos0 = jnp.sin(freq0 * pre0), jnp.cos(freq0 * pre0)
+    pre1 = jnp.dot(one, mid_all, precision=HIGH) + bias1
+    second, cos1 = jnp.sin(freq1 * pre1), jnp.cos(freq1 * pre1)
+    feats_t = jnp.pad(feats.T, ((0, -feats.shape[1] % 8), (0, 0)))
+    network = [feats_t, one.T, pre0, cos0, freq0, pre1, cos1, freq1, mid_all]
 
     def gather_parts(v):
         across = comm.turn(v, "seq", n_seq, 1)
         return [v, across, comm.flip(v, "seq", n_seq), comm.flip(across, "seq", n_seq)]
+
+    leaving = []
 
     def scatter_parts(send, keep):
         got = comm.flip(send, "seq", n_seq)
         other = 1 - comm.y
         crossed = (pick(keep, other, 0) + pick(got, other, 0).astype(F32)).astype(BF)
         own = ((1, tok_rows, width), lambda i, m: (m[3], 0, 0))
+        leaving.append(crossed)
         return (keep,) + own, (got,) + own, comm.turn(crossed, "seq", n_seq, 1)
 
     parts_out = [((2, tok_rows, width), BF), ((2, tok_rows, width), F32)]
@@ -1131,7 +1209,7 @@
             lambda *r, n=len(w_io), raw=l == 0: mix_forth_kernel(count, n, raw, *r),
             [((total, width), BF), ((total, 3 * chans), BF), ((total, chans), F32), ((total, chans), BF)] + parts_out,
             meta,
-            parts + w_io + [long, long_t, short, short_t, short0, seconds[l], decay, fout[l], rows5[l], skip[l],
+            parts + w_io + [long, long_t, short, short_t, short0, second, decay, fout[l], rows5[l], skip[l],
                             gains[l, 0], shifts[l, 0]],
             io_scratch,
             flops=3 * 10**9,
@@ -1168,96 +1246,116 @@
     toks = [None] * (2 * depth) + [sums_first]
     g_fouts, g_seconds, smalls, up_biases = ([None] * depth for _ in range(4))
 
-    def owner_turn(mine, got):
+    def hop(v, bit):
+        return lax.ppermute(v, "grp", [(i, i ^ bit) for i in range(n_grp)])
+
+    def owner_first(mine, got):
         rows = mine.shape[1:]
-        own, *sends = run(owner_sum_kernel, [(rows, F32)] + [(rows, BF)] * (nz - 1), meta, [mine, got])
-        return [own] + [comm.turn(send, "grp", n_grp, k) for k, send in enumerate(sends, 1)]
+        keep, send = run(owner_sum_kernel, [((2,) + rows, F32), ((2,) + rows, BF)], meta, [mine, got])
+        return keep, hop(send, 2)
+
+    def owner_second(keep, got):
+        return [keep, got, hop((keep[1] + got[1].astype(F32)).astype(BF), 4)]
 
     def owner_end(pieces):
-        return run(last_sum_kernel, [(pieces[0].shape, BF)], meta, pieces)[0]
+        keep, got, crossed = pieces
+        block = ((1,) + crossed.shape, lambda i, m: (0, 0, 0))
+        return run(last_sum_kernel, [(crossed.shape, BF)], meta, [(keep,) + block, (got,) + block, crossed])[0]
 
     norm_outs = [((tok_rows, width), F32), ((tok_rows, width), BF), ((8, width), F32)]
-    mlp_units, io_units, sent = [None] * depth, [None] * depth, []
     for l in reversed(range(depth)):
         w_io, w_up, w_down = weights[l]
         first, every, chan, inner, mixed, mid, every2, hidden, slope = saved[l]
-        if l == 0:
-            low_parts[0] = after(low_parts[0], io_units[1][1])
         low, g_pre, up_biases[l], send, keep = run(
             lambda *r, n=len(w_up), m=len(w_down): mlp_back_kernel(n, m, *r),
             [((total, width), BF), ((total, n_grp * f), BF), ((1, n_grp * f), F32)] + parts_out,
             meta, low_parts + w_up + w_down + [slope], mlp_scratch,
             flops=4 * 10**9,
         )
-        sent.append(send)
-        (g_mlp,) = run(
-            mlp_grads_kernel, [((n_grp, 2 * width, cols), BF)], meta, [every2, g_pre, hidden, low], flops=4 * 10**9)
-        mlp_units[l] = lax.psum_scatter(g_mlp, "grp", scatter_dimension=0, tiled=False)
-        grad, low_own, toks[2 * l + 1] = run(
-            norm_back_kernel, norm_outs, meta, [grad, *scatter_parts(send, keep), mid, gains[l, 1]])
+        got = scatter_parts(send, keep)
+        operands = [every2, g_pre, hidden, low]
+        if l:
+            (g_mlp,) = run(mlp_grads_kernel, [((n_grp, 2 * width, cols), BF)], meta, operands)
+            grad = after(grad, g_mlp)
+        else:
+            mlp_send, mlp_mine = run(
+                mlp_split_kernel, [((nz, 2 * width, cols), BF)] * 2, meta, operands)
+            mlp_got = comm.flip(mlp_send, "grp", n_grp)
+            grad = after(grad, mlp_send)
+        grad, low_own, toks[2 * l + 1] = run(norm_back_kernel, norm_outs, meta, [grad, *got, mid, gains[l, 1]])
         low_parts = gather_parts(low_own)
+        if l:
+            mlp_unit = lax.psum_scatter(after(g_mlp, low_own), "grp", scatter_dimension=0, tiled=False)
         low, g_proj, g_fouts[l], g_seconds[l], smalls[l], send, keep = run(
             lambda *r, n=len(w_io): mix_back_kernel(count, n, *r),
-            [((total, width), BF), ((total, 3 * chans), BF), ((hid, chans), F32), ((half, hid), F32),
+            [((total, width), BF), ((total, 3 * chans), BF), ((lanes, chans), F32), ((half, lanes), F32),
              ((8, 3 * chans), F32)] + parts_out,
             meta,
-            low_parts + w_io + [long, long_t, short, short_t, short0, short0_t, seconds[l], decay, fout[l], rows5[l],
+            low_parts + w_io + [long, long_t, short, short_t, short0, short0_t, second, decay, fout[l], rows5[l],
                                 skip[l], chan, inner],
             io_scratch,
             flops=5 * 10**9,
         )
-        sent.append(send)
-        send_io, mine = run(
-            io_grads_kernel, [((nz, width, cols), BF)] * 2, meta, [g_proj, every, mixed, low],
-            [((3 * chans, width), BF), ((chans, width), BF)], flops=2 * 10**9)
-        io_units[l] = (mine, comm.flip(send_io, "grp", n_grp))
-        grad, low_own, toks[2 * l] = run(
-            norm_back_kernel, norm_outs, meta, [grad, *scatter_parts(send, keep), first, gains[l, 0]])
+        got = scatter_parts(send, keep)
+        operands = [g_proj, every, mixed, low]
+        scratch = [((3 * chans, width), BF), ((chans, width), BF)]
+        if l:
+            (g_io,) = run(lambda *r: io_grads_kernel(False, *r), [((n_grp, width, cols), BF)], meta, operands, scratch)
+            grad = after(grad, g_io)
+        else:
+            io_send, io_mine = run(
+                lambda *r: io_grads_kernel(True, *r), [((nz, width, cols), BF)] * 2, meta, operands, scratch)
+            io_got = comm.flip(io_send, "grp", n_grp)
+        grad, low_own, toks[2 * l] = run(norm_back_kernel, norm_outs, meta, [grad, *got, first, gains[l, 0]])
         if l:
             low_parts = gather_parts(low_own)
-
-    send, mine = run(
-        lambda *r: pack_kernel(depth, *r), [((nz, SMALL, cols), BF)] * 2, meta,
-        up_biases + smalls + g_fouts + toks + [e_wide, e_all],
-        [((5, 2 * SLOT, 3 * chans), F32), ((SMALL, width), F32)])
-    small = owner_end(owner_turn(mine, comm.flip(send, "grp", n_grp)))
-    norm_gain_grad, norm_bias_grad, branch_grad, in_bias_grad, taps_grad, tap_bias_grad, skip_grad, fout_grad, up_bias_grad = run(
-        lambda *r: finish_small_kernel(q, *r),
-        [(v.shape, F32) for v in (norm_gain, norm_bias, branch_bias, in_bias, conv_weight, conv_bias, skip_bias,
-                                  filt_out, up_bias)],
-        meta, gather_parts(small))
-
-    def finish(kernel, unit, shapes, old, scratch=()):
+            io_one = lax.psum_scatter(after(g_io, low_own), "grp", scatter_dimension=0, tiled=False)
+
+    def finish(kernel, parts, shapes, old, scratch=()):
         outs = []
         for shape in shapes:
             outs.append(((depth,) + shape, F32, (1,) + shape, lambda i, m, l=l, n=len(shape): (l,) + (0,) * n))
         return run(
-            lambda *r, n=len(old): kernel(n, *r), outs, meta, gather_parts(unit) + [(v, None, None) for v in old],
+            lambda *r, n=len(old): kernel(n, *r), outs, meta, parts + [(v, None, None) for v in old],
             scratch, alias={5: 0, 6: 1} if old else None)
 
     mlp_shapes = [(width, ff_shard), (n_grp, n_seq, f, cols)]
     io_shapes = [(width, 3 * cols), (n_grp, n_seq, q, cols)]
-    mlp_grads, io_grads = [], []
-    for l in reversed(range(depth)):
-        mine, got = io_units[l]
-        pieces = owner_turn(mine, after(got, sent[2]) if l else got)
-        if l:
-            pieces = [pieces[0]] + [after(v, sent[3]) for v in pieces[1:]]
-        io_unit = owner_end(pieces)
-        mlp_unit = after(mlp_units[l], sent[3] if l else io_unit, *([] if l else [small]))
-        mlp_grads = finish(finish_mlp_kernel, mlp_unit, mlp_shapes, mlp_grads)
-        io_grads = finish(finish_io_kernel, io_unit, io_shapes, io_grads, [((3 * cols, width), F32)])
-    up_grad, down_grad = mlp_grads
-    in_grad, out_grad = io_grads
-
-    net_grads = second_pull(jnp.stack(g_seconds))
-    flat = jnp.concatenate([v.reshape(-1) for v in net_grads])
-    flat = jnp.pad(flat, (0, -flat.shape[0] % 1024)).reshape(-1, 128)
-    flat = comm.sum_all(comm.sum_all(flat, "seq", n_seq), "grp", n_grp).reshape(-1)
-    shared, at = [], 0
-    for v in net_grads:
-        shared.append(flat[at : at + v.size].reshape(v.shape))
-        at += v.size
+    turned = [((3 * cols, width), F32)]
+
+    send, mine = run(
+        lambda *r: pack_kernel(depth, *r), [((nz, SMALL + NET, cols), BF)] * 2, meta,
+        up_biases + smalls + g_fouts + toks + g_seconds + network + [e_wide, e_all],
+        [((5, 2 * SLOT, 3 * chans), F32), ((SMALL, width), F32)])
+    mlp_first = owner_first(mlp_mine, after(mlp_got, io_send, low_own))
+    io_first = owner_first(io_mine, after(io_got, mlp_first[0], send))
+    parts_one = gather_parts(after(mlp_unit, low_own))
+    small_got = after(comm.flip(send, "grp", n_grp), parts_one[1])
+    small_rows = (SMALL + NET, cols)
+    own, *sends = run(small_turn_kernel, [(small_rows, BF)] * nz, meta, [mine, small_got])
+    pieces = [own] + [comm.turn(v, "grp", n_grp, k) for k, v in enumerate(sends, 1)]
+    mlp_pieces = owner_second(after(mlp_first[0], *pieces[1:]), mlp_first[1])
+    io_turn = owner_second(*io_first)
+    (small,) = run(small_last_kernel, [(small_rows, BF)], meta, pieces, [((nz,) + small_rows, F32)])
+    small_parts = gather_parts(small)
+
+    l = 1
+    mlp_grads = finish(finish_mlp_kernel, parts_one, mlp_shapes, [])
+    mlp_pieces[0], state, *mlp_grads = lax.optimization_barrier(
+        (after(mlp_pieces[0], io_first[1], *small_parts), state, *mlp_grads))
+    io_grads = finish(finish_io_kernel, gather_parts(after(io_one, *small_parts)), io_shapes, [], turned)
+    io_turn[0], *io_grads = lax.optimization_barrier((io_turn[0], *io_grads))
+    l = 0
+    mlp_unit = owner_end(mlp_pieces)
+    up_grad, down_grad = finish(finish_mlp_kernel, gather_parts(mlp_unit), mlp_shapes, mlp_grads)
+    in_grad, out_grad = finish(finish_io_kernel, gather_parts(owner_end(io_turn)), io_shapes, io_grads, turned)
+    shared_shapes = [v.shape for v in (filt_in, filt_mid, filt_bias, sine_freq)]
+    (norm_gain_grad, norm_bias_grad, branch_grad, in_bias_grad, taps_grad, tap_bias_grad, skip_grad, fout_grad,
+     up_bias_grad, *shared) = run(
+        lambda *r: finish_small_kernel(q, *r),
+        [(v.shape, F32) for v in (norm_gain, norm_bias, branch_bias, in_bias, conv_weight, conv_bias, skip_bias,
+                                  filt_out, up_bias)] + [(shape, F32) for shape in shared_shapes],
+        meta, small_parts, [((n_seq,) + small_rows, F32)])
     return (
         state, grad, norm_gain_grad, norm_bias_grad, in_grad, in_bias_grad, taps_grad, tap_bias_grad,
         skip_grad, fout_grad, out_grad.reshape(depth, width, cols), up_grad, up_bias_grad,
@@ -1276,5 +1374,5 @@
         tok, tok, last3, last3, last3, last2, last3, last2, last2, last3,
         last3, last3, last2, last3, last3, P(), P(), P(), P(),
     )
-    small = mesh.shape["seq"] == 4
+    small = mesh.shape["seq"] == 4 and mesh.shape["grp"] == 8
     return jax.shard_map(body if small else body_any, mesh=mesh, in_specs=in_specs, out_specs=out_specs, check_vma=False)

time: 579 us -> 526 us (0.908)
  the two profiles are of different devices: /device:TPU:9 before, /device:TPU:0 now
where the time goes in v3:
time: 526 us; the launch traced here: 517 us
  Pallas kernels  180 us (34%)
  waiting for transfers between devices  149 us (28%)
  starting transfers between devices  93.7 us (18%)
  local copies, waits for them, and re-layouts  45.6 us (9%)
  other arithmetic  30.7 us (6%)
  between operations  15.7 us (3%)
    pallas_call x36, Pallas kernels, run(): pl.pallas_call(kernel, out_shape=shapes, grid_spec=pltpu.PrefetchScalarGr...  180 us
    ppermute x42, waiting for transfers between devices, turn(): return lax.ppermute(v, axis, perm)  95.9 us
    ppermute x42, starting transfers between devices, turn(): return lax.ppermute(v, axis, perm)  71.5 us
    ppermute x43, waiting for transfers between devices, flip(): return lax.ppermute(v, axis, [(i, i ^ 1) for i in range(size)])  39.3 us
    unnamed x215, local copies, waits for them, and re-layouts  27.5 us
    ppermute x4, waiting for transfers between devices, hop(): return lax.ppermute(v, 'grp', [(i, i ^ bit) for i in range(n_grp)])  13.7 us
    ppermute x43, starting transfers between devices, flip(): return lax.ppermute(v, axis, [(i, i ^ 1) for i in range(size)])  13.7 us
  transfers between devices with their start and end apart: 91, of which 34 were waited for; matrix products, arithmetic and copies ran while one was open for 10% of the time, Pallas kernels for 28%

profile of v3, /device:TPU:0, one launch (start us, length us, event | category | flops | bytes accessed | tf_op | source)
XLA Modules:
  0.0 516.8 jit_solution(8169821611498801964)
XLA Ops:
  11.3 3.2 shard_map.339
  14.5 3.0 collective-permute-start
  17.6 2.6 collective-permute-start.1
  21.5 2.8 shard_map.340
  28.8 3.9 subtract_select_fusion.2
  53.2 4.8 collective-permute-done.3
  61.3 5.4 %collective-permute-done.4 = bf16[1024,128]{1,0:T(8,128)(2,1)} collective-permute-done((bf16[1024,128]{1,0:T(8,128)(2,1)}, bf16[1024,128]{1,0:T(8,128)(2,1)}, u32[]{:S(2)}, u32[]{:S(2)}) %collective-permute-start.4) | collective-permute-done | bytes 262176 | tf_op jit(solution)/shard_map/ppermute | solution.py:48
  69.6 5.6 %collective-permute-start.7 = (bf16[1024,128]{1,0:T(8,128)(2,1)}, bf16[1024,128]{1,0:T(8,128)(2,1)}, u32[]{:S(2)}, u32[]{:S(2)}) collective-permute-start(bf16[1024,128]{1,0:T(8,128)(2,1)} %get-tuple-element.165), channel_id=1, source_target_pairs={{0,8},{4,12},{8,16},{12,20},{16,24},{20,28},{24,0},{28,4},{1,9},{5... | collective-permute-start | bytes 786440 | tf_op jit(solution)/shard_map/ppermute | solution.py:48
  78.3 4.3 shard_map.341
  90.9 7.5 %shard_map.342 = (bf16[512,1024]{1,0:T(8,128)(2,1)}, bf16[512,768]{1,0:T(8,128)(2,1)}, f32[512,256]{1,0:T(8,128)}, bf16[512,256]{1,0:T(8,128)(2,1)}, bf16[2,128,...) custom-call(s32[11]{0:T(128)} %concatenate.27.r_0_.meta, bf16[128,1024]{1,0:T(8,128)(2,1)} %get-tuple-element.169.r_1_, ...), custom_call_target="tpu_custom_call" | custom-call | flops 3000000 | bytes 9396 | tf_op jit(solution)/shard_map/pallas_call | solution.py:492
  104.8 3.1 shard_map.344
  109.9 4.9 collective-permute-done.6.r_6_
  115.5 3.1 shard_map.343
  120.9 2.8 collective-permute-start.22
  125.2 7.9 %collective-permute-done.21 = bf16[1024,128]{1,0:T(8,128)(2,1)S(1)} collective-permute-done((bf16[1024,128]{1,0:T(8,128)(2,1)S(1)}, bf16[1024,128]{1,0:T(8,128)(2,1)S(1)}, u32[]{:S(2)}, u32[]{:S(2)}) %collective-permute-start.21) | collective-permute-done | bytes 262176 | tf_op jit(solution)/shard_map/ppermute | solution.py:48
  133.3 4.7 collective-permute-start.27
  142.3 8.8 %shard_map.345 = (bf16[512,1024]{1,0:T(8,128)(2,1)}, bf16[512,1024]{1,0:T(8,128)(2,1)}, bf16[512,1024]{1,0:T(8,128)(2,1)}, bf16[2,128,1024]{2,1,0:T(8,128)(2,1)}, f32[2,128,1024]{2,1,0:T(8,128)}) custom-call(s32[11]{0:T(128)} %concatenate.27.r_0_.meta, bf16[128,1024]{1,0:T(8,128)(2,1)} %get-tuple-element.179.r_1_, bf16[128,1024]{1,0:T(8,128)(2,1)} %copy-done.43, ...), custom_call_target="tpu_custom_call" | custom-call | flops 4000000 | bytes 9965 | tf_op jit(solution)/shard_map/pallas_call | solution.py:492
  151.2 5.0 collective-permute-done.28
  157.6 6.1 %collective-permute-start.33 = (bf16[1024,128]{1,0:T(8,128)(2,1)S(1)}, bf16[1024,128]{1,0:T(8,128)(2,1)S(1)}, u32[]{:S(2)}, u32[]{:S(2)}) collective-permute-start(bf16[1024,128]{1,0:T(8,128)(2,1)S(1)} %copy-done.73), channel_id=1, source_target_pairs={{0,8},{4,12},{8,16},{12,20},{16,24},{20,28},{24,0},{28,4},{1,9},{5... | collective-permute-start | bytes 786440 | tf_op jit(solution)/shard_map/ppermute | solution.py:48
  163.6 2.9 collective-permute-done.26.r_6_
  167.3 3.0 shard_map.346
  170.8 3.5 collective-permute-start.34
  174.3 3.8 collective-permute-start.35
  178.6 8.5 %collective-permute-done.34 = bf16[1024,128]{1,0:T(8,128)(2,1)S(1)} collective-permute-done((bf16[1024,128]{1,0:T(8,128)(2,1)S(1)}, bf16[1024,128]{1,0:T(8,128)(2,1)S(1)}, u32[]{:S(2)}, u32[]{:S(2)}) %collective-permute-start.34) | collective-permute-done | bytes 262176 | tf_op jit(solution)/shard_map/ppermute | solution.py:48
  188.5 7.5 %shard_map.347 = (bf16[512,1024]{1,0:T(8,128)(2,1)}, bf16[512,768]{1,0:T(8,128)(2,1)}, f32[512,256]{1,0:T(8,128)}, bf16[512,256]{1,0:T(8,128)(2,1)}, bf16[2,128,...) custom-call(s32[11]{0:T(128)} %concatenate.27.r_0_.meta, bf16[128,1024]{1,0:T(8,128)(2,1)} %get-tuple-element.192.r_1_, ...), custom_call_target="tpu_custom_call" | custom-call | flops 3000000 | bytes 9265 | tf_op jit(solution)/shard_map/pallas_call | solution.py:492
  201.1 6.8 %collective-permute-done.40.crossed = bf16[128,1024]{1,0:T(8,128)(2,1)S(1)} collective-permute-done((bf16[128,1024]{1,0:T(8,128)(2,1)S(1)}, bf16[128,1024]{1,0:T(8,128)(2,1)S(1)}, u32[]{:S(2)}, u32[]{:S(2)}) %collective-permute-start.40) | collective-permute-done | bytes 262176 | tf_op jit(solution)/shard_map/ppermute | solution.py:48
  208.7 3.0 shard_map.348
  213.2 6.2 %collective-permute-done.41.r_2_ = bf16[128,1024]{1,0:T(8,128)(2,1)S(1)} collective-permute-done((bf16[128,1024]{1,0:T(8,128)(2,1)}, bf16[128,1024]{1,0:T(8,128)(2,1)S(1)}, u32[]{:S(2)}, u32[]{:S(2)}) %collective-permute-start.41) | collective-permute-done | bytes 262176 | tf_op jit(solution)/shard_map/ppermute | solution.py:48
  222.9 9.0 %shard_map.349 = (bf16[512,1024]{1,0:T(8,128)(2,1)}, bf16[512,1024]{1,0:T(8,128)(2,1)}, bf16[512,1024]{1,0:T(8,128)(2,1)}, bf16[2,128,1024]{2,1,0:T(8,128)(2,1)}, f32[2,128,1024]{2,1,0:T(8,128)}) custom-call(s32[11]{0:T(128)} %concatenate.27.r_0_.meta, bf16[128,1024]{1,0:T(8,128)(2,1)} %get-tuple-element.195.r_1_, bf16[128,1024]{1,0:T(8,128)(2,1)} %copy-done.56, ...), custom_call_target="tpu_custom_call" | custom-call | flops 4000000 | bytes 9965 | tf_op jit(solution)/shard_map/pallas_call | solution.py:492
  231.8 8.6 %shard_map.350 = (bf16[512,1024]{1,0:T(8,128)(2,1)}, bf16[512,1024]{1,0:T(8,128)(2,1)}, f32[1,1024]{1,0:T(1,128)}, bf16[2,128,1024]{2,1,0:T(8,128)(2,1)}, f32[2,128,1024]{2,1,0:T(8,128)}) custom-call(s32[11]{0:T(128)} %concatenate.27.r_0_.meta, bf16[128,1024]{1,0:T(8,128)(2,1)} %get-tuple-element.168.r_1_, bf16[128,1024]{1,0:T(8,128)(2,1)} %collective-permute-done.10.r_2_, ...), custom_call_target="tpu_custom_call" | custom-call | flops 4000000 | bytes 9965 | tf_op jit(solution)/shard_map/pallas_call | solution.py:492
  245.5 7.5 %shard_map.351 = bf16[8,2048,128]{2,1,0:T(8,128)(2,1)} custom-call(s32[11]{0:T(128)} %concatenate.27.r_0_.meta, bf16[512,1024]{1,0:T(8,128)(2,1)} %get-tuple-element.196.every, bf16[512,1024]{1,0:T(8,128)(2,1)} %get-tuple-element.198.g_pre, bf16[512,1024]{1,0:T(8,128)(2,1)} %get-tuple-element.199.hidden, bf16[512,1024]{1,0:T(8,128)(2,1)} %get-tuple-element.200.low), custom_call_target="tpu_custom_call" | custom-call | bytes 8388 | tf_op jit(solution)/shard_map/pallas_call | solution.py:492
  253.7 3.6 shard_map.352
  259.1 7.3 %collective-permute-done.47.r_2_ = bf16[128,1024]{1,0:T(8,128)(2,1)S(1)} collective-permute-done((bf16[128,1024]{1,0:T(8,128)(2,1)S(1)}, bf16[128,1024]{1,0:T(8,128)(2,1)S(1)}, u32[]{:S(2)}, u32[]{:S(2)}) %collective-permute-start.47) | collective-permute-done | bytes 262176 | tf_op jit(solution)/shard_map/ppermute | solution.py:48
  268.6 10.0 %shard_map.353 = (bf16[512,1024]{1,0:T(8,128)(2,1)}, bf16[512,768]{1,0:T(8,128)(2,1)}, f32[128,256]{1,0:T(8,128)}, f32[256,128]{1,0:T(8,128)}, f32[8,768]{1,0:T(...) custom-call(s32[11]{0:T(128)} %concatenate.27.r_0_.meta, bf16[128,1024]{1,0:T(8,128)(2,1)} %get-tuple-element.206.r_1_, ...), custom_call_target="tpu_custom_call" | custom-call | flops 5000000 | bytes 10133 | tf_op jit(solution)/shard_map/pallas_call | solution.py:492
  282.8 5.4 %shard_map.354 = bf16[8,1024,128]{2,1,0:T(8,128)(2,1)} custom-call(s32[11]{0:T(128)} %concatenate.27.r_0_.meta, bf16[512,768]{1,0:T(8,128)(2,1)} %get-tuple-element.209.r_1_, bf16[512,1024]{1,0:T(8,128)(2,1)} %get-tuple-element.210.r_2_, bf16[512,256]{1,0:T(8,128)(2,1)} %get-tuple-element.211.r_3_, bf16[512,1024]{1,0:T(8,128)(2,1)} %get-tuple-element.212.r_4_), custom_call_target="tpu_custom_call" | custom-call | bytes 5242 | tf_op jit(solution)/shard_map/pallas_call | solution.py:492
  291.2 3.6 shard_map.355
  295.5 7.2 %collective-permute-done.52.r_2_ = bf16[128,1024]{1,0:T(8,128)(2,1)S(1)} collective-permute-done((bf16[128,1024]{1,0:T(8,128)(2,1)}, bf16[128,1024]{1,0:T(8,128)(2,1)S(1)}, u32[]{:S(2)}, u32[]{:S(2)}) %collective-permute-start.52) | collective-permute-done | bytes 262176 | tf_op jit(solution)/shard_map/ppermute | solution.py:48
  304.9 8.5 %shard_map.356 = (bf16[512,1024]{1,0:T(8,128)(2,1)}, bf16[512,1024]{1,0:T(8,128)(2,1)}, f32[1,1024]{1,0:T(1,128)}, bf16[2,128,1024]{2,1,0:T(8,128)(2,1)}, f32[2,128,1024]{2,1,0:T(8,128)}) custom-call(s32[11]{0:T(128)} %concatenate.27.r_0_.meta, bf16[128,1024]{1,0:T(8,128)(2,1)} %get-tuple-element.216.r_1_, bf16[128,1024]{1,0:T(8,128)(2,1)} %copy-done.57, ...), custom_call_target="tpu_custom_call" | custom-call | flops 4000000 | bytes 9965 | tf_op jit(solution)/shard_map/pallas_call | solution.py:492
  313.6 7.7 %shard_map.357 = (bf16[4,2048,128]{2,1,0:T(8,128)(2,1)}, bf16[4,2048,128]{2,1,0:T(8,128)(2,1)}) custom-call(s32[11]{0:T(128)} %concatenate.27.r_0_.meta, bf16[512,1024]{1,0:T(8,128)(2,1)} %get-tuple-element.181.every, bf16[512,1024]{1,0:T(8,128)(2,1)} %get-tuple-element.218.g_pre, bf16[512,1024]{1,0:T(8,128)(2,1)} %get-tuple-element.219.hidden, ...), custom_call_target="tpu_custom_call" | custom-call | bytes 8388 | tf_op jit(solution)/shard_map/pallas_call | solution.py:492
  323.6 7.7 %collective-permute-done.57.crossed = bf16[128,1024]{1,0:T(8,128)(2,1)S(1)} collective-permute-done((bf16[128,1024]{1,0:T(8,128)(2,1)S(1)}, bf16[128,1024]{1,0:T(8,128)(2,1)S(1)}, u32[]{:S(2)}, u32[]{:S(2)}) %collective-permute-start.57) | collective-permute-done | bytes 262176 | tf_op jit(solution)/shard_map/ppermute | solution.py:48
  331.9 3.6 shard_map.358
  336.2 7.1 %collective-permute-done.58.r_2_ = bf16[128,1024]{1,0:T(8,128)(2,1)S(1)} collective-permute-done((bf16[128,1024]{1,0:T(8,128)(2,1)}, bf16[128,1024]{1,0:T(8,128)(2,1)S(1)}, u32[]{:S(2)}, u32[]{:S(2)}) %collective-permute-start.58) | collective-permute-done | bytes 262176 | tf_op jit(solution)/shard_map/ppermute | solution.py:48
  345.5 9.9 %shard_map.359 = (bf16[512,1024]{1,0:T(8,128)(2,1)}, bf16[512,768]{1,0:T(8,128)(2,1)}, f32[128,256]{1,0:T(8,128)}, f32[256,128]{1,0:T(8,128)}, f32[8,768]{1,0:T(...) custom-call(s32[11]{0:T(128)} %concatenate.27.r_0_.meta, bf16[128,1024]{1,0:T(8,128)(2,1)} %get-tuple-element.227.r_1_, ...), custom_call_target="tpu_custom_call" | custom-call | flops 5000000 | bytes 10264 | tf_op jit(solution)/shard_map/pallas_call | solution.py:492
  359.7 5.4 %shard_map.360 = (bf16[4,1024,128]{2,1,0:T(8,128)(2,1)}, bf16[4,1024,128]{2,1,0:T(8,128)(2,1)}) custom-call(s32[11]{0:T(128)} %concatenate.27.r_0_.meta, bf16[512,768]{1,0:T(8,128)(2,1)} %get-tuple-element.230.r_1_, bf16[512,1024]{1,0:T(8,128)(2,1)} %get-tuple-element.231.r_2_, bf16[512,256]{1,0:T(8,128)(2,1)} %get-tuple-element.232.r_3_, ...), custom_call_target="tpu_custom_call" | custom-call | bytes 5242 | tf_op jit(solution)/shard_map/pallas_call | solution.py:492
  368.1 3.5 shard_map.361
  371.6 6.7 %collective-permute-done.55.got = bf16[4,2048,128]{2,1,0:T(8,128)(2,1)S(1)} collective-permute-done((bf16[4,2048,128]{2,1,0:T(8,128)(2,1)}, bf16[4,2048,128]{2,1,0:T(8,128)(2,1)S(1)}, u32[]{:S(2)}, u32[]{:S(2)}) %collective-permute-start.55) | collective-permute-done | bytes 2097184 | tf_op jit(solution)/shard_map/ppermute | solution.py:42
  379.8 5.1 shard_map.362
  384.9 5.6 %collective-permute-start.84 = (bf16[2,2048,128]{2,1,0:T(8,128)(2,1)}, bf16[2,2048,128]{2,1,0:T(8,128)(2,1)S(1)}, u32[]{:S(2)}, u32[]{:S(2)}) collective-permute-start(bf16[2,2048,128]{2,1,0:T(8,128)(2,1)} %get-tuple-element.292), channel_id=1, source_target_pairs={{0,8},{4,12},{8,0},{12,4},{16,24},{20,28},{24,16},{28,20},{1,9},{5... | collective-permute-start | bytes 3145736 | tf_op jit(solution)/shard_map/ppermute | solution.py:1250
  394.2 6.1 %shard_map.363 = (bf16[4,176,128]{2,1,0:T(8,128)(2,1)}, bf16[4,176,128]{2,1,0:T(8,128)(2,1)}) custom-call(s32[11]{0:T(128)} %concatenate.27.r_0_.meta, f32[1,1024]{1,0:T(1,128)} %get-tuple-element.241.r_1_, f32[1,1024]{1,0:T(1,128)} %get-tuple-element.242.r_2_, f32[8,768]{1,0:T(8,128)} %get-tuple-element.243.r_3_, f32[8,768]{1,0:T(8,128)} %get-tuple-element.244.r_4_, ...), custom_call_target="tpu_custom_call" | custom-call | bytes 5538 | tf_op jit(solution)/shard_map/pallas_call | solution.py:492
  402.1 10.4 %collective-permute-done.63.got = bf16[4,176,128]{2,1,0:T(8,128)(2,1)S(1)} collective-permute-done((bf16[4,176,128]{2,1,0:T(8,128)(2,1)}, bf16[4,176,128]{2,1,0:T(8,128)(2,1)S(1)}, u32[]{:S(2)}, u32[]{:S(2)}) %collective-permute-start.63) | collective-permute-done | bytes 180256 | tf_op jit(solution)/shard_map/ppermute | solution.py:42
  415.6 3.9 collective-permute-start.65
  419.5 3.7 collective-permute-start.66
  424.1 3.6 shard_map.365
  440.4 7.7 %collective-permute-done.74.crossed = bf16[128,1024]{1,0:T(8,128)(2,1)S(1)} collective-permute-done((bf16[128,1024]{1,0:T(8,128)(2,1)}, bf16[128,1024]{1,0:T(8,128)(2,1)S(1)}, u32[]{:S(2)}, u32[]{:S(2)}) %collective-permute-start.74) | collective-permute-done | bytes 262176 | tf_op jit(solution)/shard_map/ppermute | solution.py:48
  449.0 2.9 shard_map.367
  452.8 4.6 shard_map.368
  457.4 5.6 %collective-permute-done.85.crossed = bf16[2048,128]{1,0:T(8,128)(2,1)} collective-permute-done((bf16[2048,128]{1,0:T(8,128)(2,1)}, bf16[2048,128]{1,0:T(8,128)(2,1)}, u32[]{:S(2)}, u32[]{:S(2)}) %collective-permute-start.85) | collective-permute-done | bytes 524320 | tf_op jit(solution)/shard_map/ppermute | solution.py:1250
  462.9 3.1 shard_map.373.r_1_
  469.3 3.7 shard_map.370
  473.1 8.2 %collective-permute-done.80.crossed = bf16[1024,128]{1,0:T(8,128)(2,1)S(1)} collective-permute-done((bf16[1024,128]{1,0:T(8,128)(2,1)S(1)}, bf16[1024,128]{1,0:T(8,128)(2,1)S(1)}, u32[]{:S(2)}, u32[]{:S(2)}) %collective-permute-start.80) | collective-permute-done | bytes 262176 | tf_op jit(solution)/shard_map/ppermute | solution.py:1250
  481.9 2.6 shard_map.371.r_1_
  486.8 6.2 %collective-permute-done.81.r_2_ = bf16[1024,128]{1,0:T(8,128)(2,1)S(1)} collective-permute-done((bf16[1024,128]{1,0:T(8,128)(2,1)}, bf16[1024,128]{1,0:T(8,128)(2,1)S(1)}, u32[]{:S(2)}, u32[]{:S(2)}) %collective-permute-start.81) | collective-permute-done | bytes 262176 | tf_op jit(solution)/shard_map/ppermute | solution.py:48
  499.6 3.7 shard_map.372
  505.0 4.6 shard_map.374
  (460 shorter events, 152.5 us)
Async XLA Ops:
  7.2 383.3 %reduce-scatter.3.cloned.1.call-start = ((), (), s32[]{:S(2)}) async-start(), calls=%async_computation.2 | async-start | bytes 4718592 | tf_op jit(solution)/shard_map/reduce_scatter | solution.py:1288
  14.5 29.2 %collective-permute-start = (bf16[1088,128]{1,0:T(8,128)(2,1)}, bf16[1088,128]{1,0:T(8,128)(2,1)S(1)}, u32[]{:S(2)}, u32[]{:S(2)}) collective-permute-start(bf16[1088,128]{1,0:T(8,128)(2,1)} %get-tuple-element.162), channel_id=1, source_target_pairs={{0,8},{4,12},{8,16},{12,20},{16,24},{20,28},{24,0},{28,4},{1,9},{5... | collective-permute-start | bytes 835592 | tf_op jit(solution)/shard_map/ppermute | solution.py:48
  17.6 26.1 %collective-permute-start.1 = (bf16[1088,128]{1,0:T(8,128)(2,1)}, bf16[1088,128]{1,0:T(8,128)(2,1)S(1)}, u32[]{:S(2)}, u32[]{:S(2)}) collective-permute-start(bf16[1088,128]{1,0:T(8,128)(2,1)} %get-tuple-element.162), channel_id=1, source_target_pairs={{0,16},{4,20},{8,24},{12,28},{16,0},{20,4},{24,8},{28,12},{1,17},{... | collective-permute-start | bytes 835592 | tf_op jit(solution)/shard_map/ppermute | solution.py:48
  20.2 23.6 %collective-permute-start.2 = (bf16[1088,128]{1,0:T(8,128)(2,1)}, bf16[1088,128]{1,0:T(8,128)(2,1)S(1)}, u32[]{:S(2)}, u32[]{:S(2)}) collective-permute-start(bf16[1088,128]{1,0:T(8,128)(2,1)} %get-tuple-element.162), channel_id=1, source_target_pairs={{0,24},{4,28},{8,0},{12,4},{16,8},{20,12},{24,16},{28,20},{1,25},{... | collective-permute-start | bytes 835592 | tf_op jit(solution)/shard_map/ppermute | solution.py:48
  24.3 27.2 %collective-permute-start.10 = (bf16[128,1024]{1,0:T(8,128)(2,1)}, bf16[128,1024]{1,0:T(8,128)(2,1)}, u32[]{:S(2)}, u32[]{:S(2)}) collective-permute-start(bf16[128,1024]{1,0:T(8,128)(2,1)} %get-tuple-element.168.r_1_), channel_id=1, source_target_pairs={{0,2},{1,3},{2,0},{3,1},{4,6},{5,7},{6,4},{7,5},{8,10},{9,11},{10,... | collective-permute-start | bytes 786440 | tf_op jit(solution)/shard_map/ppermute | solution.py:48
  25.8 27.3 %collective-permute-start.13 = (bf16[128,1024]{1,0:T(8,128)(2,1)}, bf16[128,1024]{1,0:T(8,128)(2,1)}, u32[]{:S(2)}, u32[]{:S(2)}) collective-permute-start(bf16[128,1024]{1,0:T(8,128)(2,1)} %get-tuple-element.169.r_1_), channel_id=1, source_target_pairs={{0,2},{1,3},{2,0},{3,1},{4,6},{5,7},{6,4},{7,5},{8,10},{9,11},{10,... | collective-permute-start | bytes 786440 | tf_op jit(solution)/shard_map/ppermute | solution.py:48
  43.9 33.4 %collective-permute-start.16 = (bf16[4,1088,128]{2,1,0:T(8,128)(2,1)S(1)}, bf16[4,1088,128]{2,1,0:T(8,128)(2,1)S(1)}, u32[]{:S(2)}, u32[]{:S(2)}) collective-permute-start(bf16[4,1088,128]{2,1,0:T(8,128)(2,1)S(1)} %pad_maximum_fusion.slab.r_5_), channel_id=1, source_target_pairs={{0,4},{4,0},{8,12},{12,8},{16,20},{20,16},{24,28},{28,24},{1,5},{5... | collective-permute-start | bytes 3342344 | tf_op jit(solution)/shard_map/ppermute | solution.py:42
  46.9 11.1 %collective-permute-start.3 = (bf16[1024,128]{1,0:T(8,128)(2,1)}, bf16[1024,128]{1,0:T(8,128)(2,1)S(1)}, u32[]{:S(2)}, u32[]{:S(2)}) collective-permute-start(bf16[1024,128]{1,0:T(8,128)(2,1)} %get-tuple-element.163), channel_id=1, source_target_pairs={{0,8},{4,12},{8,16},{12,20},{16,24},{20,28},{24,0},{28,4},{1,9},{5... | collective-permute-start | bytes 786440 | tf_op jit(solution)/shard_map/ppermute | solution.py:48
  49.9 16.9 %collective-permute-start.4 = (bf16[1024,128]{1,0:T(8,128)(2,1)}, bf16[1024,128]{1,0:T(8,128)(2,1)}, u32[]{:S(2)}, u32[]{:S(2)}) collective-permute-start(bf16[1024,128]{1,0:T(8,128)(2,1)} %get-tuple-element.163), channel_id=1, source_target_pairs={{0,16},{4,20},{8,24},{12,28},{16,0},{20,4},{24,8},{28,12},{1,17},{... | collective-permute-start | bytes 786440 | tf_op jit(solution)/shard_map/ppermute | solution.py:48
  51.5 15.3 %collective-permute-start.5 = (bf16[1024,128]{1,0:T(8,128)(2,1)}, bf16[1024,128]{1,0:T(8,128)(2,1)}, u32[]{:S(2)}, u32[]{:S(2)}) collective-permute-start(bf16[1024,128]{1,0:T(8,128)(2,1)} %get-tuple-element.163), channel_id=1, source_target_pairs={{0,24},{4,28},{8,0},{12,4},{16,8},{20,12},{24,16},{28,20},{1,25},{... | collective-permute-start | bytes 786440 | tf_op jit(solution)/shard_map/ppermute | solution.py:48
  53.1 16.5 %collective-permute-start.11 = (bf16[128,1024]{1,0:T(8,128)(2,1)}, bf16[128,1024]{1,0:T(8,128)(2,1)}, u32[]{:S(2)}, u32[]{:S(2)}) collective-permute-start(bf16[128,1024]{1,0:T(8,128)(2,1)} %get-tuple-element.168.r_1_), channel_id=1, source_target_pairs={{0,1},{1,0},{2,3},{3,2},{4,5},{5,4},{6,7},{7,6},{8,9},{9,8},{10,11... | collective-permute-start | bytes 786440 | tf_op jit(solution)/shard_map/ppermute | solution.py:42
  58.0 17.2 %collective-permute-start.12 = (bf16[128,1024]{1,0:T(8,128)(2,1)}, bf16[128,1024]{1,0:T(8,128)(2,1)}, u32[]{:S(2)}, u32[]{:S(2)}) collective-permute-start(bf16[128,1024]{1,0:T(8,128)(2,1)} %collective-permute-done.10.r_2_), channel_id=1, source_target_pairs={{0,1},{1,0},{2,3},{3,2},{4,5},{5,4},{6,7},{7,6},{8,9},{9,8},{10,11... | collective-permute-start | bytes 786440 | tf_op jit(solution)/shard_map/ppermute | solution.py:42
  66.8 21.6 %collective-permute-start.14 = (bf16[128,1024]{1,0:T(8,128)(2,1)}, bf16[128,1024]{1,0:T(8,128)(2,1)S(1)}, u32[]{:S(2)}, u32[]{:S(2)}) collective-permute-start(bf16[128,1024]{1,0:T(8,128)(2,1)} %get-tuple-element.169.r_1_), channel_id=1, source_target_pairs={{0,1},{1,0},{2,3},{3,2},{4,5},{5,4},{6,7},{7,6},{8,9},{9,8},{10,11... | collective-permute-start | bytes 786440 | tf_op jit(solution)/shard_map/ppermute | solution.py:42
  66.8 23.5 %collective-permute-start.15 = (bf16[128,1024]{1,0:T(8,128)(2,1)}, bf16[128,1024]{1,0:T(8,128)(2,1)S(1)}, u32[]{:S(2)}, u32[]{:S(2)}) collective-permute-start(bf16[128,1024]{1,0:T(8,128)(2,1)} %collective-permute-done.13.r_2_), channel_id=1, source_target_pairs={{0,1},{1,0},{2,3},{3,2},{4,5},{5,4},{6,7},{7,6},{8,9},{9,8},{10,11... | collective-permute-start | bytes 786440 | tf_op jit(solution)/shard_map/ppermute | solution.py:42
  69.6 29.0 %collective-permute-start.7 = (bf16[1024,128]{1,0:T(8,128)(2,1)}, bf16[1024,128]{1,0:T(8,128)(2,1)}, u32[]{:S(2)}, u32[]{:S(2)}) collective-permute-start(bf16[1024,128]{1,0:T(8,128)(2,1)} %get-tuple-element.165), channel_id=1, source_target_pairs={{0,8},{4,12},{8,16},{12,20},{16,24},{20,28},{24,0},{28,4},{1,9},{5... | collective-permute-start | bytes 786440 | tf_op jit(solution)/shard_map/ppermute | solution.py:48
  75.2 23.4 %collective-permute-start.8 = (bf16[1024,128]{1,0:T(8,128)(2,1)}, bf16[1024,128]{1,0:T(8,128)(2,1)}, u32[]{:S(2)}, u32[]{:S(2)}) collective-permute-start(bf16[1024,128]{1,0:T(8,128)(2,1)} %get-tuple-element.165), channel_id=1, source_target_pairs={{0,16},{4,20},{8,24},{12,28},{16,0},{20,4},{24,8},{28,12},{1,17},{... | collective-permute-start | bytes 786440 | tf_op jit(solution)/shard_map/ppermute | solution.py:48
  77.3 21.3 %collective-permute-start.9 = (bf16[1024,128]{1,0:T(8,128)(2,1)}, bf16[1024,128]{1,0:T(8,128)(2,1)S(1)}, u32[]{:S(2)}, u32[]{:S(2)}) collective-permute-start(bf16[1024,128]{1,0:T(8,128)(2,1)} %get-tuple-element.165), channel_id=1, source_target_pairs={{0,24},{4,28},{8,0},{12,4},{16,8},{20,12},{24,16},{28,20},{1,25},{... | collective-permute-start | bytes 786440 | tf_op jit(solution)/shard_map/ppermute | solution.py:48
  88.4 26.4 %collective-permute-start.6 = (bf16[4,1024,128]{2,1,0:T(8,128)(2,1)}, bf16[4,1024,128]{2,1,0:T(8,128)(2,1)S(1)}, u32[]{:S(2)}, u32[]{:S(2)}) collective-permute-start(bf16[4,1024,128]{2,1,0:T(8,128)(2,1)} %pad_maximum_fusion.1.r_5_), channel_id=1, source_target_pairs={{0,4},{4,0},{8,12},{12,8},{16,20},{20,16},{24,28},{28,24},{1,5},{5... | collective-permute-start | bytes 3145736 | tf_op jit(solution)/shard_map/ppermute | solution.py:42
  100.6 39.2 %collective-permute-start.19 = (bf16[4,1024,128]{2,1,0:T(8,128)(2,1)S(1)}, bf16[4,1024,128]{2,1,0:T(8,128)(2,1)}, u32[]{:S(2)}, u32[]{:S(2)}) collective-permute-start(bf16[4,1024,128]{2,1,0:T(8,128)(2,1)S(1)} %pad_maximum_fusion.2.r_7_), channel_id=1, source_target_pairs={{0,4},{4,0},{8,12},{12,8},{16,20},{20,16},{24,28},{28,24},{1,5},{5... | collective-permute-start | bytes 3145736 | tf_op jit(solution)/shard_map/ppermute | solution.py:42
  103.2 11.5 %collective-permute-start.18 = (bf16[128,1024]{1,0:T(8,128)(2,1)S(1)}, bf16[128,1024]{1,0:T(8,128)(2,1)S(1)}, u32[]{:S(2)}, u32[]{:S(2)}) collective-permute-start(bf16[128,1024]{1,0:T(8,128)(2,1)S(1)} %fusion.1), channel_id=1, source_target_pairs={{0,2},{1,3},{2,0},{3,1},{4,6},{5,7},{6,4},{7,5},{8,10},{9,11},{10,... | collective-permute-start | bytes 786440 | tf_op jit(solution)/shard_map/ppermute | solution.py:48
  107.9 15.8 %collective-permute-start.20 = (bf16[1024,128]{1,0:T(8,128)(2,1)}, bf16[1024,128]{1,0:T(8,128)(2,1)S(1)}, u32[]{:S(2)}, u32[]{:S(2)}) collective-permute-start(bf16[1024,128]{1,0:T(8,128)(2,1)} %get-tuple-element.178), channel_id=1, source_target_pairs={{0,8},{4,12},{8,16},{12,20},{16,24},{20,28},{24,0},{28,4},{1,9},{5... | collective-permute-start | bytes 786440 | tf_op jit(solution)/shard_map/ppermute | solution.py:48
  120.1 13.0 %collective-permute-start.21 = (bf16[1024,128]{1,0:T(8,128)(2,1)S(1)}, bf16[1024,128]{1,0:T(8,128)(2,1)S(1)}, u32[]{:S(2)}, u32[]{:S(2)}) collective-permute-start(bf16[1024,128]{1,0:T(8,128)(2,1)S(1)} %copy-done.76), channel_id=1, source_target_pairs={{0,16},{4,20},{8,24},{12,28},{16,0},{20,4},{24,8},{28,12},{1,17},{... | collective-permute-start | bytes 786440 | tf_op jit(solution)/shard_map/ppermute | solution.py:48
  120.9 12.3 %collective-permute-start.22 = (bf16[1024,128]{1,0:T(8,128)(2,1)S(1)}, bf16[1024,128]{1,0:T(8,128)(2,1)S(1)}, u32[]{:S(2)}, u32[]{:S(2)}) collective-permute-start(bf16[1024,128]{1,0:T(8,128)(2,1)S(1)} %copy-done.76), channel_id=1, source_target_pairs={{0,24},{4,28},{8,0},{12,4},{16,8},{20,12},{24,16},{28,20},{1,25},{... | collective-permute-start | bytes 786440 | tf_op jit(solution)/shard_map/ppermute | solution.py:48
  123.7 16.7 %collective-permute-start.24 = (bf16[128,1024]{1,0:T(8,128)(2,1)}, bf16[128,1024]{1,0:T(8,128)(2,1)S(1)}, u32[]{:S(2)}, u32[]{:S(2)}) collective-permute-start(bf16[128,1024]{1,0:T(8,128)(2,1)} %get-tuple-element.179.r_1_), channel_id=1, source_target_pairs={{0,1},{1,0},{2,3},{3,2},{4,5},{5,4},{6,7},{7,6},{8,9},{9,8},{10,11... | collective-permute-start | bytes 786440 | tf_op jit(solution)/shard_map/ppermute | solution.py:42
  125.2 16.4 %collective-permute-start.25 = (bf16[128,1024]{1,0:T(8,128)(2,1)S(1)}, bf16[128,1024]{1,0:T(8,128)(2,1)S(1)}, u32[]{:S(2)}, u32[]{:S(2)}) collective-permute-start(bf16[128,1024]{1,0:T(8,128)(2,1)S(1)} %collective-permute-done.23.r_2_), channel_id=1, source_target_pairs={{0,1},{1,0},{2,3},{3,2},{4,5},{5,4},{6,7},{7,6},{8,9},{9,8},{10,11... | collective-permute-start | bytes 786440 | tf_op jit(solution)/shard_map/ppermute | solution.py:42
  133.3 17.9 %collective-permute-start.27 = (bf16[1024,128]{1,0:T(8,128)(2,1)S(1)}, bf16[1024,128]{1,0:T(8,128)(2,1)S(1)}, u32[]{:S(2)}, u32[]{:S(2)}) collective-permute-start(bf16[1024,128]{1,0:T(8,128)(2,1)S(1)} %copy-done.74), channel_id=1, source_target_pairs={{0,8},{4,12},{8,16},{12,20},{16,24},{20,28},{24,0},{28,4},{1,9},{5... | collective-permute-start | bytes 786440 | tf_op jit(solution)/shard_map/ppermute | solution.py:48
  138.0 18.2 %collective-permute-start.28 = (bf16[1024,128]{1,0:T(8,128)(2,1)S(1)}, bf16[1024,128]{1,0:T(8,128)(2,1)S(1)}, u32[]{:S(2)}, u32[]{:S(2)}) collective-permute-start(bf16[1024,128]{1,0:T(8,128)(2,1)S(1)} %copy-done.74), channel_id=1, source_target_pairs={{0,16},{4,20},{8,24},{12,28},{16,0},{20,4},{24,8},{28,12},{1,17},{... | collective-permute-start | bytes 786440 | tf_op jit(solution)/shard_map/ppermute | solution.py:48
  139.8 16.4 %collective-permute-start.29 = (bf16[1024,128]{1,0:T(8,128)(2,1)S(1)}, bf16[1024,128]{1,0:T(8,128)(2,1)S(1)}, u32[]{:S(2)}, u32[]{:S(2)}) collective-permute-start(bf16[1024,128]{1,0:T(8,128)(2,1)S(1)} %copy-done.74), channel_id=1, source_target_pairs={{0,24},{4,28},{8,0},{12,4},{16,8},{20,12},{24,16},{28,20},{1,25},{... | collective-permute-start | bytes 786440 | tf_op jit(solution)/shard_map/ppermute | solution.py:48
  140.4 26.1 %collective-permute-start.26 = (bf16[4,1024,128]{2,1,0:T(8,128)(2,1)S(1)}, bf16[4,1024,128]{2,1,0:T(8,128)(2,1)S(1)}, u32[]{:S(2)}, u32[]{:S(2)}) collective-permute-start(bf16[4,1024,128]{2,1,0:T(8,128)(2,1)S(1)} %pad_maximum_fusion.3.r_5_), channel_id=1, source_target_pairs={{0,4},{4,0},{8,12},{12,8},{16,20},{20,16},{24,28},{28,24},{1,5},{5... | collective-permute-start | bytes 3145736 | tf_op jit(solution)/shard_map/ppermute | solution.py:42
  156.3 31.0 %collective-permute-start.32 = (bf16[4,1024,128]{2,1,0:T(8,128)(2,1)S(1)}, bf16[4,1024,128]{2,1,0:T(8,128)(2,1)S(1)}, u32[]{:S(2)}, u32[]{:S(2)}) collective-permute-start(bf16[4,1024,128]{2,1,0:T(8,128)(2,1)S(1)} %pad_maximum_fusion.4.r_5_), channel_id=1, source_target_pairs={{0,4},{4,0},{8,12},{12,8},{16,20},{20,16},{24,28},{28,24},{1,5},{5... | collective-permute-start | bytes 3145736 | tf_op jit(solution)/shard_map/ppermute | solution.py:42
  157.0 9.5 %collective-permute-start.31 = (bf16[128,1024]{1,0:T(8,128)(2,1)S(1)}, bf16[128,1024]{1,0:T(8,128)(2,1)S(1)}, u32[]{:S(2)}, u32[]{:S(2)}) collective-permute-start(bf16[128,1024]{1,0:T(8,128)(2,1)S(1)} %fusion.2), channel_id=1, source_target_pairs={{0,2},{1,3},{2,0},{3,1},{4,6},{5,7},{6,4},{7,5},{8,10},{9,11},{10,... | collective-permute-start | bytes 786440 | tf_op jit(solution)/shard_map/ppermute | solution.py:48
  157.6 20.6 %collective-permute-start.33 = (bf16[1024,128]{1,0:T(8,128)(2,1)S(1)}, bf16[1024,128]{1,0:T(8,128)(2,1)S(1)}, u32[]{:S(2)}, u32[]{:S(2)}) collective-permute-start(bf16[1024,128]{1,0:T(8,128)(2,1)S(1)} %copy-done.73), channel_id=1, source_target_pairs={{0,8},{4,12},{8,16},{12,20},{16,24},{20,28},{24,0},{28,4},{1,9},{5... | collective-permute-start | bytes 786440 | tf_op jit(solution)/shard_map/ppermute | solution.py:48
  170.8 16.3 %collective-permute-start.34 = (bf16[1024,128]{1,0:T(8,128)(2,1)S(1)}, bf16[1024,128]{1,0:T(8,128)(2,1)S(1)}, u32[]{:S(2)}, u32[]{:S(2)}) collective-permute-start(bf16[1024,128]{1,0:T(8,128)(2,1)S(1)} %copy-done.73), channel_id=1, source_target_pairs={{0,16},{4,20},{8,24},{12,28},{16,0},{20,4},{24,8},{28,12},{1,17},{... | collective-permute-start | bytes 786440 | tf_op jit(solution)/shard_map/ppermute | solution.py:48
  174.3 12.8 %collective-permute-start.35 = (bf16[1024,128]{1,0:T(8,128)(2,1)S(1)}, bf16[1024,128]{1,0:T(8,128)(2,1)S(1)}, u32[]{:S(2)}, u32[]{:S(2)}) collective-permute-start(bf16[1024,128]{1,0:T(8,128)(2,1)S(1)} %copy-done.73), channel_id=1, source_target_pairs={{0,24},{4,28},{8,0},{12,4},{16,8},{20,12},{24,16},{28,20},{1,25},{... | collective-permute-start | bytes 786440 | tf_op jit(solution)/shard_map/ppermute | solution.py:48
  178.1 9.2 %collective-permute-start.37 = (bf16[128,1024]{1,0:T(8,128)(2,1)}, bf16[128,1024]{1,0:T(8,128)(2,1)S(1)}, u32[]{:S(2)}, u32[]{:S(2)}) collective-permute-start(bf16[128,1024]{1,0:T(8,128)(2,1)} %get-tuple-element.192.r_1_), channel_id=1, source_target_pairs={{0,1},{1,0},{2,3},{3,2},{4,5},{5,4},{6,7},{7,6},{8,9},{9,8},{10,11... | collective-permute-start | bytes 786440 | tf_op jit(solution)/shard_map/ppermute | solution.py:42
  178.1 9.2 %collective-permute-start.38 = (bf16[128,1024]{1,0:T(8,128)(2,1)S(1)}, bf16[128,1024]{1,0:T(8,128)(2,1)S(1)}, u32[]{:S(2)}, u32[]{:S(2)}) collective-permute-start(bf16[128,1024]{1,0:T(8,128)(2,1)S(1)} %collective-permute-done.36.r_2_), channel_id=1, source_target_pairs={{0,1},{1,0},{2,3},{3,2},{4,5},{5,4},{6,7},{7,6},{8,9},{9,8},{10,11... | collective-permute-start | bytes 786440 | tf_op jit(solution)/shard_map/ppermute | solution.py:42
  196.1 25.6 %collective-permute-start.44 = (bf16[4,1024,128]{2,1,0:T(8,128)(2,1)S(1)}, bf16[4,1024,128]{2,1,0:T(8,128)(2,1)S(1)}, u32[]{:S(2)}, u32[]{:S(2)}) collective-permute-start(bf16[4,1024,128]{2,1,0:T(8,128)(2,1)S(1)} %pad_maximum_fusion.5.r_7_), channel_id=1, source_target_pairs={{0,4},{4,0},{8,12},{12,8},{16,20},{20,16},{24,28},{28,24},{1,5},{5... | collective-permute-start | bytes 3145736 | tf_op jit(solution)/shard_map/ppermute | solution.py:42
  213.2 8.5 %collective-permute-start.42 = (bf16[128,1024]{1,0:T(8,128)(2,1)}, bf16[128,1024]{1,0:T(8,128)(2,1)S(1)}, u32[]{:S(2)}, u32[]{:S(2)}) collective-permute-start(bf16[128,1024]{1,0:T(8,128)(2,1)} %get-tuple-element.195.r_1_), channel_id=1, source_target_pairs={{0,1},{1,0},{2,3},{3,2},{4,5},{5,4},{6,7},{7,6},{8,9},{9,8},{10,11... | collective-permute-start | bytes 786440 | tf_op jit(solution)/shard_map/ppermute | solution.py:42
  243.9 9.1 %collective-permute-start.46 = (bf16[128,1024]{1,0:T(8,128)(2,1)S(1)}, bf16[128,1024]{1,0:T(8,128)(2,1)S(1)}, u32[]{:S(2)}, u32[]{:S(2)}) collective-permute-start(bf16[128,1024]{1,0:T(8,128)(2,1)S(1)} %fusion.4), channel_id=1, source_target_pairs={{0,2},{1,3},{2,0},{3,1},{4,6},{5,7},{6,4},{7,5},{8,10},{9,11},{10,... | collective-permute-start | bytes 786440 | tf_op jit(solution)/shard_map/ppermute | solution.py:48
  257.4 183.0 %reduce-scatter.5.cloned.1.call-start = ((), (), s32[]{:S(2)}) async-start(), calls=%async_computation.3 | async-start | bytes 2359296 | tf_op jit(solution)/shard_map/reduce_scatter | solution.py:1312
  282.1 8.4 %collective-permute-start.51 = (bf16[128,1024]{1,0:T(8,128)(2,1)S(1)}, bf16[128,1024]{1,0:T(8,128)(2,1)S(1)}, u32[]{:S(2)}, u32[]{:S(2)}) collective-permute-start(bf16[128,1024]{1,0:T(8,128)(2,1)S(1)} %fusion.5), channel_id=1, source_target_pairs={{0,2},{1,3},{2,0},{3,1},{4,6},{5,7},{6,4},{7,5},{8,10},{9,11},{10,... | collective-permute-start | bytes 786440 | tf_op jit(solution)/shard_map/ppermute | solution.py:48
  313.4 9.3 %collective-permute-start.56 = (bf16[2,128,1024]{2,1,0:T(8,128)(2,1)}, bf16[2,128,1024]{2,1,0:T(8,128)(2,1)S(1)}, u32[]{:S(2)}, u32[]{:S(2)}) collective-permute-start(bf16[2,128,1024]{2,1,0:T(8,128)(2,1)} %get-tuple-element.226), channel_id=1, source_target_pairs={{0,1},{1,0},{2,3},{3,2},{4,5},{5,4},{6,7},{7,6},{8,9},{9,8},{10,11... | collective-permute-start | bytes 1572872 | tf_op jit(solution)/shard_map/ppermute | solution.py:42
  321.3 57.1 %collective-permute-start.55 = (bf16[4,2048,128]{2,1,0:T(8,128)(2,1)}, bf16[4,2048,128]{2,1,0:T(8,128)(2,1)S(1)}, u32[]{:S(2)}, u32[]{:S(2)}) collective-permute-start(bf16[4,2048,128]{2,1,0:T(8,128)(2,1)} %get-tuple-element.222), channel_id=1, source_target_pairs={{0,4},{4,0},{8,12},{12,8},{16,20},{20,16},{24,28},{28,24},{1,5},{5... | collective-permute-start | bytes 6291464 | tf_op jit(solution)/shard_map/ppermute | solution.py:42
  322.8 8.4 %collective-permute-start.57 = (bf16[128,1024]{1,0:T(8,128)(2,1)S(1)}, bf16[128,1024]{1,0:T(8,128)(2,1)S(1)}, u32[]{:S(2)}, u32[]{:S(2)}) collective-permute-start(bf16[128,1024]{1,0:T(8,128)(2,1)S(1)} %fusion.6), channel_id=1, source_target_pairs={{0,2},{1,3},{2,0},{3,1},{4,6},{5,7},{6,4},{7,5},{8,10},{9,11},{10,... | collective-permute-start | bytes 786440 | tf_op jit(solution)/shard_map/ppermute | solution.py:48
  359.0 8.5 %collective-permute-start.62 = (bf16[128,1024]{1,0:T(8,128)(2,1)S(1)}, bf16[128,1024]{1,0:T(8,128)(2,1)S(1)}, u32[]{:S(2)}, u32[]{:S(2)}) collective-permute-start(bf16[128,1024]{1,0:T(8,128)(2,1)S(1)} %fusion.7), channel_id=1, source_target_pairs={{0,2},{1,3},{2,0},{3,1},{4,6},{5,7},{6,4},{7,5},{8,10},{9,11},{10,... | collective-permute-start | bytes 786440 | tf_op jit(solution)/shard_map/ppermute | solution.py:48
  365.1 58.1 %collective-permute-start.68 = (bf16[4,1024,128]{2,1,0:T(8,128)(2,1)}, bf16[4,1024,128]{2,1,0:T(8,128)(2,1)S(1)}, u32[]{:S(2)}, u32[]{:S(2)}) collective-permute-start(bf16[4,1024,128]{2,1,0:T(8,128)(2,1)} %get-tuple-element.234), channel_id=1, source_target_pairs={{0,4},{4,0},{8,12},{12,8},{16,20},{20,16},{24,28},{28,24},{1,5},{5... | collective-permute-start | bytes 3145736 | tf_op jit(solution)/shard_map/ppermute | solution.py:42
  384.9 48.2 %collective-permute-start.84 = (bf16[2,2048,128]{2,1,0:T(8,128)(2,1)}, bf16[2,2048,128]{2,1,0:T(8,128)(2,1)S(1)}, u32[]{:S(2)}, u32[]{:S(2)}) collective-permute-start(bf16[2,2048,128]{2,1,0:T(8,128)(2,1)} %get-tuple-element.292), channel_id=1, source_target_pairs={{0,8},{4,12},{8,0},{12,4},{16,24},{20,28},{24,16},{28,20},{1,9},{5... | collective-permute-start | bytes 3145736 | tf_op jit(solution)/shard_map/ppermute | solution.py:1250
  390.5 22.0 %collective-permute-start.64 = (bf16[2048,128]{1,0:T(8,128)(2,1)}, bf16[2048,128]{1,0:T(8,128)(2,1)}, u32[]{:S(2)}, u32[]{:S(2)}) collective-permute-start(bf16[2048,128]{1,0:T(8,128)(2,1)} %bitcast.164), channel_id=1, source_target_pairs={{0,2},{1,3},{2,0},{3,1},{4,6},{5,7},{6,4},{7,5},{8,10},{9,11},{10,... | collective-permute-start | bytes 1572872 | tf_op jit(solution)/shard_map/ppermute | solution.py:48
  400.4 12.2 %collective-permute-start.63 = (bf16[4,176,128]{2,1,0:T(8,128)(2,1)}, bf16[4,176,128]{2,1,0:T(8,128)(2,1)S(1)}, u32[]{:S(2)}, u32[]{:S(2)}) collective-permute-start(bf16[4,176,128]{2,1,0:T(8,128)(2,1)} %get-tuple-element.255), channel_id=1, source_target_pairs={{0,4},{4,0},{8,12},{12,8},{16,20},{20,16},{24,28},{28,24},{1,5},{5... | collective-permute-start | bytes 540680 | tf_op jit(solution)/shard_map/ppermute | solution.py:42
  415.6 12.2 %collective-permute-start.65 = (bf16[176,128]{1,0:T(8,128)(2,1)}, bf16[176,128]{1,0:T(8,128)(2,1)S(1)}, u32[]{:S(2)}, u32[]{:S(2)}) collective-permute-start(bf16[176,128]{1,0:T(8,128)(2,1)} %get-tuple-element.259), channel_id=1, source_target_pairs={{0,8},{4,12},{8,16},{12,20},{16,24},{20,28},{24,0},{28,4},{1,9},{5... | collective-permute-start | bytes 135176 | tf_op jit(solution)/shard_map/ppermute | solution.py:48
  419.5 10.3 %collective-permute-start.66 = (bf16[176,128]{1,0:T(8,128)(2,1)}, bf16[176,128]{1,0:T(8,128)(2,1)S(1)}, u32[]{:S(2)}, u32[]{:S(2)}) collective-permute-start(bf16[176,128]{1,0:T(8,128)(2,1)} %get-tuple-element.260), channel_id=1, source_target_pairs={{0,16},{4,20},{8,24},{12,28},{16,0},{20,4},{24,8},{28,12},{1,17},{... | collective-permute-start | bytes 135176 | tf_op jit(solution)/shard_map/ppermute | solution.py:48
  423.2 11.1 %collective-permute-start.73 = (bf16[2,128,1024]{2,1,0:T(8,128)(2,1)S(1)}, bf16[2,128,1024]{2,1,0:T(8,128)(2,1)S(1)}, u32[]{:S(2)}, u32[]{:S(2)}) collective-permute-start(bf16[2,128,1024]{2,1,0:T(8,128)(2,1)S(1)} %copy-done.105), channel_id=1, source_target_pairs={{0,1},{1,0},{2,3},{3,2},{4,5},{5,4},{6,7},{7,6},{8,9},{9,8},{10,11... | collective-permute-start | bytes 1572872 | tf_op jit(solution)/shard_map/ppermute | solution.py:42
  427.8 24.1 %collective-permute-start.69 = (bf16[2,1024,128]{2,1,0:T(8,128)(2,1)}, bf16[2,1024,128]{2,1,0:T(8,128)(2,1)S(1)}, u32[]{:S(2)}, u32[]{:S(2)}) collective-permute-start(bf16[2,1024,128]{2,1,0:T(8,128)(2,1)} %get-tuple-element.265), channel_id=1, source_target_pairs={{0,8},{4,12},{8,0},{12,4},{16,24},{20,28},{24,16},{28,20},{1,9},{5... | collective-permute-start | bytes 1572872 | tf_op jit(solution)/shard_map/ppermute | solution.py:1250
  429.8 22.1 %collective-permute-start.75 = (bf16[2048,128]{1,0:T(8,128)(2,1)S(1)}, bf16[2048,128]{1,0:T(8,128)(2,1)S(1)}, u32[]{:S(2)}, u32[]{:S(2)}) collective-permute-start(bf16[2048,128]{1,0:T(8,128)(2,1)S(1)} %bitcast.166), channel_id=1, source_target_pairs={{0,1},{1,0},{2,3},{3,2},{4,5},{5,4},{6,7},{7,6},{8,9},{9,8},{10,11... | collective-permute-start | bytes 1572872 | tf_op jit(solution)/shard_map/ppermute | solution.py:42
  434.3 17.7 %collective-permute-start.76 = (bf16[2048,128]{1,0:T(8,128)(2,1)}, bf16[2048,128]{1,0:T(8,128)(2,1)}, u32[]{:S(2)}, u32[]{:S(2)}) collective-permute-start(bf16[2048,128]{1,0:T(8,128)(2,1)} %collective-permute-done.64.r_2_), channel_id=1, source_target_pairs={{0,1},{1,0},{2,3},{3,2},{4,5},{5,4},{6,7},{7,6},{8,9},{9,8},{10,11... | collective-permute-start | bytes 1572872 | tf_op jit(solution)/shard_map/ppermute | solution.py:42
  437.0 26.0 %collective-permute-start.85 = (bf16[2048,128]{1,0:T(8,128)(2,1)}, bf16[2048,128]{1,0:T(8,128)(2,1)}, u32[]{:S(2)}, u32[]{:S(2)}) collective-permute-start(bf16[2048,128]{1,0:T(8,128)(2,1)} %fusion), channel_id=1, source_target_pairs={{0,16},{4,20},{8,24},{12,28},{16,0},{20,4},{24,8},{28,12},{1,17},{... | collective-permute-start | bytes 1572872 | tf_op jit(solution)/shard_map/ppermute | solution.py:1250
  439.5 8.6 %collective-permute-start.74 = (bf16[128,1024]{1,0:T(8,128)(2,1)}, bf16[128,1024]{1,0:T(8,128)(2,1)S(1)}, u32[]{:S(2)}, u32[]{:S(2)}) collective-permute-start(bf16[128,1024]{1,0:T(8,128)(2,1)} %fusion.8), channel_id=1, source_target_pairs={{0,2},{1,3},{2,0},{3,1},{4,6},{5,7},{6,4},{7,5},{8,10},{9,11},{10,... | collective-permute-start | bytes 786440 | tf_op jit(solution)/shard_map/ppermute | solution.py:48
  448.1 18.3 %collective-permute-start.77 = (bf16[1024,128]{1,0:T(8,128)(2,1)}, bf16[1024,128]{1,0:T(8,128)(2,1)S(1)}, u32[]{:S(2)}, u32[]{:S(2)}) collective-permute-start(bf16[1024,128]{1,0:T(8,128)(2,1)} %bitcast.173), channel_id=1, source_target_pairs={{0,2},{1,3},{2,0},{3,1},{4,6},{5,7},{6,4},{7,5},{8,10},{9,11},{10,... | collective-permute-start | bytes 786440 | tf_op jit(solution)/shard_map/ppermute | solution.py:48
  466.1 20.2 %collective-permute-start.86 = (bf16[2048,128]{1,0:T(8,128)(2,1)}, bf16[2048,128]{1,0:T(8,128)(2,1)S(1)}, u32[]{:S(2)}, u32[]{:S(2)}) collective-permute-start(bf16[2048,128]{1,0:T(8,128)(2,1)} %shard_map.373.r_1_), channel_id=1, source_target_pairs={{0,2},{1,3},{2,0},{3,1},{4,6},{5,7},{6,4},{7,5},{8,10},{9,11},{10,... | collective-permute-start | bytes 1572872 | tf_op jit(solution)/shard_map/ppermute | solution.py:48
  467.0 14.2 %collective-permute-start.80 = (bf16[1024,128]{1,0:T(8,128)(2,1)S(1)}, bf16[1024,128]{1,0:T(8,128)(2,1)S(1)}, u32[]{:S(2)}, u32[]{:S(2)}) collective-permute-start(bf16[1024,128]{1,0:T(8,128)(2,1)S(1)} %fusion.9), channel_id=1, source_target_pairs={{0,16},{4,20},{8,24},{12,28},{16,0},{20,4},{24,8},{28,12},{1,17},{... | collective-permute-start | bytes 786440 | tf_op jit(solution)/shard_map/ppermute | solution.py:1250
  484.6 8.4 %collective-permute-start.81 = (bf16[1024,128]{1,0:T(8,128)(2,1)}, bf16[1024,128]{1,0:T(8,128)(2,1)S(1)}, u32[]{:S(2)}, u32[]{:S(2)}) collective-permute-start(bf16[1024,128]{1,0:T(8,128)(2,1)} %shard_map.371.r_1_), channel_id=1, source_target_pairs={{0,2},{1,3},{2,0},{3,1},{4,6},{5,7},{6,4},{7,5},{8,10},{9,11},{10,... | collective-permute-start | bytes 786440 | tf_op jit(solution)/shard_map/ppermute | solution.py:48
  486.2 17.1 %collective-permute-start.87 = (bf16[2048,128]{1,0:T(8,128)(2,1)S(1)}, bf16[2048,128]{1,0:T(8,128)(2,1)S(1)}, u32[]{:S(2)}, u32[]{:S(2)}) collective-permute-start(bf16[2048,128]{1,0:T(8,128)(2,1)S(1)} %copy-done.22), channel_id=1, source_target_pairs={{0,1},{1,0},{2,3},{3,2},{4,5},{5,4},{6,7},{7,6},{8,9},{9,8},{10,11... | collective-permute-start | bytes 1572872 | tf_op jit(solution)/shard_map/ppermute | solution.py:42
  486.2 17.1 %collective-permute-start.88 = (bf16[2048,128]{1,0:T(8,128)(2,1)S(1)}, bf16[2048,128]{1,0:T(8,128)(2,1)S(1)}, u32[]{:S(2)}, u32[]{:S(2)}) collective-permute-start(bf16[2048,128]{1,0:T(8,128)(2,1)S(1)} %collective-permute-done.86.r_2_), channel_id=1, source_target_pairs={{0,1},{1,0},{2,3},{3,2},{4,5},{5,4},{6,7},{7,6},{8,9},{9,8},{10,11... | collective-permute-start | bytes 1572872 | tf_op jit(solution)/shard_map/ppermute | solution.py:42
  486.7 11.4 %collective-permute-start.82 = (bf16[1024,128]{1,0:T(8,128)(2,1)}, bf16[1024,128]{1,0:T(8,128)(2,1)S(1)}, u32[]{:S(2)}, u32[]{:S(2)}) collective-permute-start(bf16[1024,128]{1,0:T(8,128)(2,1)} %shard_map.371.r_1_), channel_id=1, source_target_pairs={{0,1},{1,0},{2,3},{3,2},{4,5},{5,4},{6,7},{7,6},{8,9},{9,8},{10,11... | collective-permute-start | bytes 786440 | tf_op jit(solution)/shard_map/ppermute | solution.py:42
  (133 other events, 1335.2 us)
Sparse Core Ops, SparseCore 0:
  257.5 96.5 reduce-scatter.2
  358.6 75.9 reduce-scatter.4

commit v4 on v3

--- a/solution.py
+++ b/solution.py
@@ -1204,7 +1204,7 @@
             low_parts = gather_parts(low_first)
             parts[0] = after(parts[0], *low_parts, chunks[1][0])
         else:
-            parts[0] = after(parts[0], chunks[4][1], chunks[5][0])
+            parts[0] = after(parts[0], chunks[4][0])
         every, chan, inner, mixed, send, keep = run(
             lambda *r, n=len(w_io), raw=l == 0: mix_forth_kernel(count, n, raw, *r),
             [((total, width), BF), ((total, 3 * chans), BF), ((total, chans), F32), ((total, chans), BF)] + parts_out,
@@ -1214,6 +1214,8 @@
             io_scratch,
             flops=3 * 10**9,
         )
+        if l:
+            send = after(send, chunks[4][1], chunks[5][0])
         got = scatter_parts(send, keep)
         if l == 0:
             state = after(state, chunks[1][1], chunks[2][0])
@@ -1345,17 +1347,19 @@
         (after(mlp_pieces[0], io_first[1], *small_parts), state, *mlp_grads))
     io_grads = finish(finish_io_kernel, gather_parts(after(io_one, *small_parts)), io_shapes, [], turned)
     io_turn[0], *io_grads = lax.optimization_barrier((io_turn[0], *io_grads))
+    shared_shapes = [v.shape for v in (filt_in, filt_mid, filt_bias, sine_freq)]
+    small_grads = run(
+        lambda *r: finish_small_kernel(q, *r),
+        [(v.shape, F32) for v in (norm_gain, norm_bias, branch_bias, in_bias, conv_weight, conv_bias, skip_bias,
+                                  filt_out, up_bias)] + [(shape, F32) for shape in shared_shapes],
+        meta, small_parts, [((n_seq,) + small_rows, F32)])
+    io_turn[0], *small_grads = lax.optimization_barrier((io_turn[0], *small_grads))
+    (norm_gain_grad, norm_bias_grad, branch_grad, in_bias_grad, taps_grad, tap_bias_grad, skip_grad, fout_grad,
+     up_bias_grad, *shared) = small_grads
     l = 0
     mlp_unit = owner_end(mlp_pieces)
     up_grad, down_grad = finish(finish_mlp_kernel, gather_parts(mlp_unit), mlp_shapes, mlp_grads)
     in_grad, out_grad = finish(finish_io_kernel, gather_parts(owner_end(io_turn)), io_shapes, io_grads, turned)
-    shared_shapes = [v.shape for v in (filt_in, filt_mid, filt_bias, sine_freq)]
-    (norm_gain_grad, norm_bias_grad, branch_grad, in_bias_grad, taps_grad, tap_bias_grad, skip_grad, fout_grad,
-     up_bias_grad, *shared) = run(
-        lambda *r: finish_small_kernel(q, *r),
-        [(v.shape, F32) for v in (norm_gain, norm_bias, branch_bias, in_bias, conv_weight, conv_bias, skip_bias,
-                                  filt_out, up_bias)] + [(shape, F32) for shape in shared_shapes],
-        meta, small_parts, [((n_seq,) + small_rows, F32)])
     return (
         state, grad, norm_gain_grad, norm_bias_grad, in_grad, in_bias_grad, taps_grad, tap_bias_grad,
         skip_grad, fout_grad, out_grad.reshape(depth, width, cols), up_grad, up_bias_grad,

time: 526 us -> 522 us (level)
    unnamed x215 -> x219, local copies, waits for them, and re-layouts: 27.5 us -> 25.9 us
  transfers between devices with their start and end apart: 91 -> 91, of which waited for: 34 -> 33; matrix products, arithmetic and copies ran while one was open for 10% -> 9% of each run, Pallas kernels for 28% -> 29%
where the time goes in v4:
time: 522 us; the launch traced here: 513 us
  Pallas kernels  180 us (34%)
  waiting for transfers between devices  146 us (28%)
  starting transfers between devices  93.8 us (18%)
  local copies, waits for them, and re-layouts  44 us (8%)
  other arithmetic  30.7 us (6%)
  between operations  15.7 us (3%)
    pallas_call x36, Pallas kernels, run(): pl.pallas_call(kernel, out_shape=shapes, grid_spec=pltpu.PrefetchScalarGr...  180 us
    ppermute x42, waiting for transfers between devices, turn(): return lax.ppermute(v, axis, perm)  95.5 us
    ppermute x42, starting transfers between devices, turn(): return lax.ppermute(v, axis, perm)  71.7 us
    ppermute x43, waiting for transfers between devices, flip(): return lax.ppermute(v, axis, [(i, i ^ 1) for i in range(size)])  38.4 us
    unnamed x219, local copies, waits for them, and re-layouts  25.9 us
    ppermute x43, starting transfers between devices, flip(): return lax.ppermute(v, axis, [(i, i ^ 1) for i in range(size)])  13.5 us
    ppermute x4, waiting for transfers between devices, hop(): return lax.ppermute(v, 'grp', [(i, i ^ bit) for i in range(n_grp)])  12 us
  transfers between devices with their start and end apart: 91, of which 33 were waited for; matrix products, arithmetic and copies ran while one was open for 9% of the time, Pallas kernels for 29%

profile of v4, /device:TPU:0, one launch (start us, length us, event | category | flops | bytes accessed | tf_op | source)
XLA Modules:
  0.0 512.6 jit_solution(6101429348735913556)
XLA Ops:
  11.3 3.2 shard_map.339
  14.6 3.0 collective-permute-start
  17.6 2.6 collective-permute-start.1
  21.5 2.8 shard_map.340
  28.8 3.9 subtract_select_fusion.2
  53.3 4.8 collective-permute-done.3
  61.4 5.4 %collective-permute-done.4 = bf16[1024,128]{1,0:T(8,128)(2,1)} collective-permute-done((bf16[1024,128]{1,0:T(8,128)(2,1)}, bf16[1024,128]{1,0:T(8,128)(2,1)}, u32[]{:S(2)}, u32[]{:S(2)}) %collective-permute-start.4) | collective-permute-done | bytes 262176 | tf_op jit(solution)/shard_map/ppermute | solution.py:48
  69.6 5.6 %collective-permute-start.7 = (bf16[1024,128]{1,0:T(8,128)(2,1)}, bf16[1024,128]{1,0:T(8,128)(2,1)}, u32[]{:S(2)}, u32[]{:S(2)}) collective-permute-start(bf16[1024,128]{1,0:T(8,128)(2,1)} %get-tuple-element.180), channel_id=1, source_target_pairs={{0,8},{4,12},{8,16},{12,20},{16,24},{20,28},{24,0},{28,4},{1,9},{5... | collective-permute-start | bytes 786440 | tf_op jit(solution)/shard_map/ppermute | solution.py:48
  78.4 4.3 shard_map.341
  91.0 7.5 %shard_map.342 = (bf16[512,1024]{1,0:T(8,128)(2,1)}, bf16[512,768]{1,0:T(8,128)(2,1)}, f32[512,256]{1,0:T(8,128)}, bf16[512,256]{1,0:T(8,128)(2,1)}, bf16[2,128,...) custom-call(s32[11]{0:T(128)} %concatenate.27.r_0_.meta, bf16[128,1024]{1,0:T(8,128)(2,1)} %get-tuple-element.184.r_1_, ...), custom_call_target="tpu_custom_call" | custom-call | flops 3000000 | bytes 9396 | tf_op jit(solution)/shard_map/pallas_call | solution.py:492
  104.8 3.1 shard_map.344
  109.9 4.8 collective-permute-done.6.r_6_
  115.5 3.1 shard_map.343
  120.9 2.8 collective-permute-start.22
  125.2 7.9 %collective-permute-done.21 = bf16[1024,128]{1,0:T(8,128)(2,1)S(1)} collective-permute-done((bf16[1024,128]{1,0:T(8,128)(2,1)S(1)}, bf16[1024,128]{1,0:T(8,128)(2,1)S(1)}, u32[]{:S(2)}, u32[]{:S(2)}) %collective-permute-start.21) | collective-permute-done | bytes 262176 | tf_op jit(solution)/shard_map/ppermute | solution.py:48
  133.3 4.7 collective-permute-start.27
  142.3 8.8 %shard_map.345 = (bf16[512,1024]{1,0:T(8,128)(2,1)}, bf16[512,1024]{1,0:T(8,128)(2,1)}, bf16[512,1024]{1,0:T(8,128)(2,1)}, bf16[2,128,1024]{2,1,0:T(8,128)(2,1)}, f32[2,128,1024]{2,1,0:T(8,128)}) custom-call(s32[11]{0:T(128)} %concatenate.27.r_0_.meta, bf16[128,1024]{1,0:T(8,128)(2,1)} %get-tuple-element.194.r_1_, bf16[128,1024]{1,0:T(8,128)(2,1)} %copy-done.43, ...), custom_call_target="tpu_custom_call" | custom-call | flops 4000000 | bytes 9965 | tf_op jit(solution)/shard_map/pallas_call | solution.py:492
  151.2 4.9 collective-permute-done.28
  157.6 6.1 %collective-permute-start.36 = (bf16[1024,128]{1,0:T(8,128)(2,1)S(1)}, bf16[1024,128]{1,0:T(8,128)(2,1)S(1)}, u32[]{:S(2)}, u32[]{:S(2)}) collective-permute-start(bf16[1024,128]{1,0:T(8,128)(2,1)S(1)} %copy-done.73), channel_id=1, source_target_pairs={{0,8},{4,12},{8,16},{12,20},{16,24},{20,28},{24,0},{28,4},{1,9},{5... | collective-permute-start | bytes 786440 | tf_op jit(solution)/shard_map/ppermute | solution.py:48
  163.7 2.9 collective-permute-done.26.r_6_
  167.3 3.0 shard_map.346
  170.8 3.5 collective-permute-start.37
  174.3 3.8 collective-permute-start.38
  178.6 8.5 %collective-permute-done.37 = bf16[1024,128]{1,0:T(8,128)(2,1)S(1)} collective-permute-done((bf16[1024,128]{1,0:T(8,128)(2,1)S(1)}, bf16[1024,128]{1,0:T(8,128)(2,1)S(1)}, u32[]{:S(2)}, u32[]{:S(2)}) %collective-permute-start.37) | collective-permute-done | bytes 262176 | tf_op jit(solution)/shard_map/ppermute | solution.py:48
  188.2 7.5 %shard_map.347 = (bf16[512,1024]{1,0:T(8,128)(2,1)}, bf16[512,768]{1,0:T(8,128)(2,1)}, f32[512,256]{1,0:T(8,128)}, bf16[512,256]{1,0:T(8,128)(2,1)}, bf16[2,128,...) custom-call(s32[11]{0:T(128)} %concatenate.27.r_0_.meta, bf16[128,1024]{1,0:T(8,128)(2,1)} %get-tuple-element.205.r_1_, ...), custom_call_target="tpu_custom_call" | custom-call | flops 3000000 | bytes 9265 | tf_op jit(solution)/shard_map/pallas_call | solution.py:492
  200.8 6.8 %collective-permute-done.40.crossed = bf16[128,1024]{1,0:T(8,128)(2,1)S(1)} collective-permute-done((bf16[128,1024]{1,0:T(8,128)(2,1)S(1)}, bf16[128,1024]{1,0:T(8,128)(2,1)S(1)}, u32[]{:S(2)}, u32[]{:S(2)}) %collective-permute-start.40) | collective-permute-done | bytes 262176 | tf_op jit(solution)/shard_map/ppermute | solution.py:48
  208.3 3.1 shard_map.348
  212.9 6.2 %collective-permute-done.41.r_2_ = bf16[128,1024]{1,0:T(8,128)(2,1)S(1)} collective-permute-done((bf16[128,1024]{1,0:T(8,128)(2,1)}, bf16[128,1024]{1,0:T(8,128)(2,1)S(1)}, u32[]{:S(2)}, u32[]{:S(2)}) %collective-permute-start.41) | collective-permute-done | bytes 262176 | tf_op jit(solution)/shard_map/ppermute | solution.py:48
  222.5 9.0 %shard_map.349 = (bf16[512,1024]{1,0:T(8,128)(2,1)}, bf16[512,1024]{1,0:T(8,128)(2,1)}, bf16[512,1024]{1,0:T(8,128)(2,1)}, bf16[2,128,1024]{2,1,0:T(8,128)(2,1)}, f32[2,128,1024]{2,1,0:T(8,128)}) custom-call(s32[11]{0:T(128)} %concatenate.27.r_0_.meta, bf16[128,1024]{1,0:T(8,128)(2,1)} %get-tuple-element.211.r_1_, bf16[128,1024]{1,0:T(8,128)(2,1)} %copy-done.57, ...), custom_call_target="tpu_custom_call" | custom-call | flops 4000000 | bytes 9965 | tf_op jit(solution)/shard_map/pallas_call | solution.py:492
  231.5 8.6 %shard_map.350 = (bf16[512,1024]{1,0:T(8,128)(2,1)}, bf16[512,1024]{1,0:T(8,128)(2,1)}, f32[1,1024]{1,0:T(1,128)}, bf16[2,128,1024]{2,1,0:T(8,128)(2,1)}, f32[2,128,1024]{2,1,0:T(8,128)}) custom-call(s32[11]{0:T(128)} %concatenate.27.r_0_.meta, bf16[128,1024]{1,0:T(8,128)(2,1)} %get-tuple-element.183.r_1_, bf16[128,1024]{1,0:T(8,128)(2,1)} %collective-permute-done.10.r_2_, ...), custom_call_target="tpu_custom_call" | custom-call | flops 4000000 | bytes 9965 | tf_op jit(solution)/shard_map/pallas_call | solution.py:492
  245.1 7.5 %shard_map.351 = bf16[8,2048,128]{2,1,0:T(8,128)(2,1)} custom-call(s32[11]{0:T(128)} %concatenate.27.r_0_.meta, bf16[512,1024]{1,0:T(8,128)(2,1)} %get-tuple-element.212.every, bf16[512,1024]{1,0:T(8,128)(2,1)} %get-tuple-element.214.g_pre, bf16[512,1024]{1,0:T(8,128)(2,1)} %get-tuple-element.215.hidden, bf16[512,1024]{1,0:T(8,128)(2,1)} %get-tuple-element.216.low), custom_call_target="tpu_custom_call" | custom-call | bytes 8388 | tf_op jit(solution)/shard_map/pallas_call | solution.py:492
  253.4 3.6 shard_map.352
  258.8 7.3 %collective-permute-done.47.r_2_ = bf16[128,1024]{1,0:T(8,128)(2,1)S(1)} collective-permute-done((bf16[128,1024]{1,0:T(8,128)(2,1)S(1)}, bf16[128,1024]{1,0:T(8,128)(2,1)S(1)}, u32[]{:S(2)}, u32[]{:S(2)}) %collective-permute-start.47) | collective-permute-done | bytes 262176 | tf_op jit(solution)/shard_map/ppermute | solution.py:48
  268.3 10.0 %shard_map.353 = (bf16[512,1024]{1,0:T(8,128)(2,1)}, bf16[512,768]{1,0:T(8,128)(2,1)}, f32[128,256]{1,0:T(8,128)}, f32[256,128]{1,0:T(8,128)}, f32[8,768]{1,0:T(...) custom-call(s32[11]{0:T(128)} %concatenate.27.r_0_.meta, bf16[128,1024]{1,0:T(8,128)(2,1)} %get-tuple-element.222.r_1_, ...), custom_call_target="tpu_custom_call" | custom-call | flops 5000000 | bytes 10133 | tf_op jit(solution)/shard_map/pallas_call | solution.py:492
  282.4 5.4 %shard_map.354 = bf16[8,1024,128]{2,1,0:T(8,128)(2,1)} custom-call(s32[11]{0:T(128)} %concatenate.27.r_0_.meta, bf16[512,768]{1,0:T(8,128)(2,1)} %get-tuple-element.225.r_1_, bf16[512,1024]{1,0:T(8,128)(2,1)} %get-tuple-element.226.r_2_, bf16[512,256]{1,0:T(8,128)(2,1)} %get-tuple-element.227.r_3_, bf16[512,1024]{1,0:T(8,128)(2,1)} %get-tuple-element.228.r_4_), custom_call_target="tpu_custom_call" | custom-call | bytes 5242 | tf_op jit(solution)/shard_map/pallas_call | solution.py:492
  290.9 3.6 shard_map.355
  295.1 7.2 %collective-permute-done.52.r_2_ = bf16[128,1024]{1,0:T(8,128)(2,1)S(1)} collective-permute-done((bf16[128,1024]{1,0:T(8,128)(2,1)}, bf16[128,1024]{1,0:T(8,128)(2,1)S(1)}, u32[]{:S(2)}, u32[]{:S(2)}) %collective-permute-start.52) | collective-permute-done | bytes 262176 | tf_op jit(solution)/shard_map/ppermute | solution.py:48
  304.6 8.6 %shard_map.356 = (bf16[512,1024]{1,0:T(8,128)(2,1)}, bf16[512,1024]{1,0:T(8,128)(2,1)}, f32[1,1024]{1,0:T(1,128)}, bf16[2,128,1024]{2,1,0:T(8,128)(2,1)}, f32[2,128,1024]{2,1,0:T(8,128)}) custom-call(s32[11]{0:T(128)} %concatenate.27.r_0_.meta, bf16[128,1024]{1,0:T(8,128)(2,1)} %get-tuple-element.232.r_1_, bf16[128,1024]{1,0:T(8,128)(2,1)} %copy-done.58, ...), custom_call_target="tpu_custom_call" | custom-call | flops 4000000 | bytes 9965 | tf_op jit(solution)/shard_map/pallas_call | solution.py:492
  313.3 7.7 %shard_map.357 = (bf16[4,2048,128]{2,1,0:T(8,128)(2,1)}, bf16[4,2048,128]{2,1,0:T(8,128)(2,1)}) custom-call(s32[11]{0:T(128)} %concatenate.27.r_0_.meta, bf16[512,1024]{1,0:T(8,128)(2,1)} %get-tuple-element.196.every, bf16[512,1024]{1,0:T(8,128)(2,1)} %get-tuple-element.234.g_pre, bf16[512,1024]{1,0:T(8,128)(2,1)} %get-tuple-element.235.hidden, ...), custom_call_target="tpu_custom_call" | custom-call | bytes 8388 | tf_op jit(solution)/shard_map/pallas_call | solution.py:492
  323.2 7.6 %collective-permute-done.57.crossed = bf16[128,1024]{1,0:T(8,128)(2,1)S(1)} collective-permute-done((bf16[128,1024]{1,0:T(8,128)(2,1)S(1)}, bf16[128,1024]{1,0:T(8,128)(2,1)S(1)}, u32[]{:S(2)}, u32[]{:S(2)}) %collective-permute-start.57) | collective-permute-done | bytes 262176 | tf_op jit(solution)/shard_map/ppermute | solution.py:48
  331.5 3.6 shard_map.358
  335.9 6.9 %collective-permute-done.58.r_2_ = bf16[128,1024]{1,0:T(8,128)(2,1)S(1)} collective-permute-done((bf16[128,1024]{1,0:T(8,128)(2,1)}, bf16[128,1024]{1,0:T(8,128)(2,1)S(1)}, u32[]{:S(2)}, u32[]{:S(2)}) %collective-permute-start.58) | collective-permute-done | bytes 262176 | tf_op jit(solution)/shard_map/ppermute | solution.py:48
  345.0 9.9 %shard_map.359 = (bf16[512,1024]{1,0:T(8,128)(2,1)}, bf16[512,768]{1,0:T(8,128)(2,1)}, f32[128,256]{1,0:T(8,128)}, f32[256,128]{1,0:T(8,128)}, f32[8,768]{1,0:T(...) custom-call(s32[11]{0:T(128)} %concatenate.27.r_0_.meta, bf16[128,1024]{1,0:T(8,128)(2,1)} %get-tuple-element.243.r_1_, ...), custom_call_target="tpu_custom_call" | custom-call | flops 5000000 | bytes 10264 | tf_op jit(solution)/shard_map/pallas_call | solution.py:492
  359.4 5.4 %shard_map.360 = (bf16[4,1024,128]{2,1,0:T(8,128)(2,1)}, bf16[4,1024,128]{2,1,0:T(8,128)(2,1)}) custom-call(s32[11]{0:T(128)} %concatenate.27.r_0_.meta, bf16[512,768]{1,0:T(8,128)(2,1)} %get-tuple-element.246.r_1_, bf16[512,1024]{1,0:T(8,128)(2,1)} %get-tuple-element.247.r_2_, bf16[512,256]{1,0:T(8,128)(2,1)} %get-tuple-element.248.r_3_, ...), custom_call_target="tpu_custom_call" | custom-call | bytes 5242 | tf_op jit(solution)/shard_map/pallas_call | solution.py:492
  367.6 3.5 shard_map.361
  371.1 6.9 %collective-permute-done.55.got = bf16[4,2048,128]{2,1,0:T(8,128)(2,1)S(1)} collective-permute-done((bf16[4,2048,128]{2,1,0:T(8,128)(2,1)}, bf16[4,2048,128]{2,1,0:T(8,128)(2,1)S(1)}, u32[]{:S(2)}, u32[]{:S(2)}) %collective-permute-start.55) | collective-permute-done | bytes 2097184 | tf_op jit(solution)/shard_map/ppermute | solution.py:42
  379.4 5.1 shard_map.362
  384.5 5.8 %collective-permute-start.84 = (bf16[2,2048,128]{2,1,0:T(8,128)(2,1)}, bf16[2,2048,128]{2,1,0:T(8,128)(2,1)S(1)}, u32[]{:S(2)}, u32[]{:S(2)}) collective-permute-start(bf16[2,2048,128]{2,1,0:T(8,128)(2,1)} %get-tuple-element.322), channel_id=1, source_target_pairs={{0,8},{4,12},{8,0},{12,4},{16,24},{20,28},{24,16},{28,20},{1,9},{5... | collective-permute-start | bytes 3145736 | tf_op jit(solution)/shard_map/ppermute | solution.py:1252
  394.0 6.1 %shard_map.363 = (bf16[4,176,128]{2,1,0:T(8,128)(2,1)}, bf16[4,176,128]{2,1,0:T(8,128)(2,1)}) custom-call(s32[11]{0:T(128)} %concatenate.27.r_0_.meta, f32[1,1024]{1,0:T(1,128)} %get-tuple-element.257.r_1_, f32[1,1024]{1,0:T(1,128)} %get-tuple-element.258.r_2_, f32[8,768]{1,0:T(8,128)} %get-tuple-element.259.r_3_, f32[8,768]{1,0:T(8,128)} %get-tuple-element.260.r_4_, ...), custom_call_target="tpu_custom_call" | custom-call | bytes 5538 | tf_op jit(solution)/shard_map/pallas_call | solution.py:492
  401.8 10.4 %collective-permute-done.63.got = bf16[4,176,128]{2,1,0:T(8,128)(2,1)S(1)} collective-permute-done((bf16[4,176,128]{2,1,0:T(8,128)(2,1)}, bf16[4,176,128]{2,1,0:T(8,128)(2,1)S(1)}, u32[]{:S(2)}, u32[]{:S(2)}) %collective-permute-start.63) | collective-permute-done | bytes 180256 | tf_op jit(solution)/shard_map/ppermute | solution.py:42
  415.2 3.9 collective-permute-start.65
  419.2 3.7 collective-permute-start.66
  423.8 3.6 shard_map.365
  440.0 7.7 %collective-permute-done.74.crossed = bf16[128,1024]{1,0:T(8,128)(2,1)S(1)} collective-permute-done((bf16[128,1024]{1,0:T(8,128)(2,1)}, bf16[128,1024]{1,0:T(8,128)(2,1)S(1)}, u32[]{:S(2)}, u32[]{:S(2)}) %collective-permute-start.74) | collective-permute-done | bytes 262176 | tf_op jit(solution)/shard_map/ppermute | solution.py:48
  448.6 2.9 shard_map.367
  452.4 4.6 shard_map.368
  457.0 5.6 %collective-permute-done.85.crossed = bf16[2048,128]{1,0:T(8,128)(2,1)} collective-permute-done((bf16[2048,128]{1,0:T(8,128)(2,1)}, bf16[2048,128]{1,0:T(8,128)(2,1)}, u32[]{:S(2)}, u32[]{:S(2)}) %collective-permute-start.85) | collective-permute-done | bytes 524320 | tf_op jit(solution)/shard_map/ppermute | solution.py:1252
  462.6 3.1 shard_map.373.r_1_
  470.7 3.7 shard_map.369
  474.5 6.4 %collective-permute-done.80.crossed = bf16[1024,128]{1,0:T(8,128)(2,1)S(1)} collective-permute-done((bf16[1024,128]{1,0:T(8,128)(2,1)S(1)}, bf16[1024,128]{1,0:T(8,128)(2,1)S(1)}, u32[]{:S(2)}, u32[]{:S(2)}) %collective-permute-start.80) | collective-permute-done | bytes 262176 | tf_op jit(solution)/shard_map/ppermute | solution.py:1252
  481.6 2.6 shard_map.371.r_1_
  486.5 6.2 %collective-permute-done.81.r_2_ = bf16[1024,128]{1,0:T(8,128)(2,1)S(1)} collective-permute-done((bf16[1024,128]{1,0:T(8,128)(2,1)}, bf16[1024,128]{1,0:T(8,128)(2,1)S(1)}, u32[]{:S(2)}, u32[]{:S(2)}) %collective-permute-start.81) | collective-permute-done | bytes 262176 | tf_op jit(solution)/shard_map/ppermute | solution.py:48
  495.4 3.7 shard_map.372
  500.8 4.6 shard_map.374
  (464 shorter events, 150.0 us)
Async XLA Ops:
  7.2 383.1 %reduce-scatter.3.cloned.1.call-start = ((), (), s32[]{:S(2)}) async-start(), calls=%async_computation.2 | async-start | bytes 4718592 | tf_op jit(solution)/shard_map/reduce_scatter | solution.py:1290
  14.6 29.2 %collective-permute-start = (bf16[1088,128]{1,0:T(8,128)(2,1)}, bf16[1088,128]{1,0:T(8,128)(2,1)S(1)}, u32[]{:S(2)}, u32[]{:S(2)}) collective-permute-start(bf16[1088,128]{1,0:T(8,128)(2,1)} %get-tuple-element.177), channel_id=1, source_target_pairs={{0,8},{4,12},{8,16},{12,20},{16,24},{20,28},{24,0},{28,4},{1,9},{5... | collective-permute-start | bytes 835592 | tf_op jit(solution)/shard_map/ppermute | solution.py:48
  17.6 26.2 %collective-permute-start.1 = (bf16[1088,128]{1,0:T(8,128)(2,1)}, bf16[1088,128]{1,0:T(8,128)(2,1)S(1)}, u32[]{:S(2)}, u32[]{:S(2)}) collective-permute-start(bf16[1088,128]{1,0:T(8,128)(2,1)} %get-tuple-element.177), channel_id=1, source_target_pairs={{0,16},{4,20},{8,24},{12,28},{16,0},{20,4},{24,8},{28,12},{1,17},{... | collective-permute-start | bytes 835592 | tf_op jit(solution)/shard_map/ppermute | solution.py:48
  20.2 23.6 %collective-permute-start.2 = (bf16[1088,128]{1,0:T(8,128)(2,1)}, bf16[1088,128]{1,0:T(8,128)(2,1)S(1)}, u32[]{:S(2)}, u32[]{:S(2)}) collective-permute-start(bf16[1088,128]{1,0:T(8,128)(2,1)} %get-tuple-element.177), channel_id=1, source_target_pairs={{0,24},{4,28},{8,0},{12,4},{16,8},{20,12},{24,16},{28,20},{1,25},{... | collective-permute-start | bytes 835592 | tf_op jit(solution)/shard_map/ppermute | solution.py:48
  24.3 27.2 %collective-permute-start.10 = (bf16[128,1024]{1,0:T(8,128)(2,1)}, bf16[128,1024]{1,0:T(8,128)(2,1)}, u32[]{:S(2)}, u32[]{:S(2)}) collective-permute-start(bf16[128,1024]{1,0:T(8,128)(2,1)} %get-tuple-element.183.r_1_), channel_id=1, source_target_pairs={{0,2},{1,3},{2,0},{3,1},{4,6},{5,7},{6,4},{7,5},{8,10},{9,11},{10,... | collective-permute-start | bytes 786440 | tf_op jit(solution)/shard_map/ppermute | solution.py:48
  25.9 27.3 %collective-permute-start.13 = (bf16[128,1024]{1,0:T(8,128)(2,1)}, bf16[128,1024]{1,0:T(8,128)(2,1)}, u32[]{:S(2)}, u32[]{:S(2)}) collective-permute-start(bf16[128,1024]{1,0:T(8,128)(2,1)} %get-tuple-element.184.r_1_), channel_id=1, source_target_pairs={{0,2},{1,3},{2,0},{3,1},{4,6},{5,7},{6,4},{7,5},{8,10},{9,11},{10,... | collective-permute-start | bytes 786440 | tf_op jit(solution)/shard_map/ppermute | solution.py:48
  44.0 33.4 %collective-permute-start.16 = (bf16[4,1088,128]{2,1,0:T(8,128)(2,1)S(1)}, bf16[4,1088,128]{2,1,0:T(8,128)(2,1)S(1)}, u32[]{:S(2)}, u32[]{:S(2)}) collective-permute-start(bf16[4,1088,128]{2,1,0:T(8,128)(2,1)S(1)} %pad_maximum_fusion.slab.r_5_), channel_id=1, source_target_pairs={{0,4},{4,0},{8,12},{12,8},{16,20},{20,16},{24,28},{28,24},{1,5},{5... | collective-permute-start | bytes 3342344 | tf_op jit(solution)/shard_map/ppermute | solution.py:42
  46.9 11.1 %collective-permute-start.3 = (bf16[1024,128]{1,0:T(8,128)(2,1)}, bf16[1024,128]{1,0:T(8,128)(2,1)S(1)}, u32[]{:S(2)}, u32[]{:S(2)}) collective-permute-start(bf16[1024,128]{1,0:T(8,128)(2,1)} %get-tuple-element.178), channel_id=1, source_target_pairs={{0,8},{4,12},{8,16},{12,20},{16,24},{20,28},{24,0},{28,4},{1,9},{5... | collective-permute-start | bytes 786440 | tf_op jit(solution)/shard_map/ppermute | solution.py:48
  49.9 16.9 %collective-permute-start.4 = (bf16[1024,128]{1,0:T(8,128)(2,1)}, bf16[1024,128]{1,0:T(8,128)(2,1)}, u32[]{:S(2)}, u32[]{:S(2)}) collective-permute-start(bf16[1024,128]{1,0:T(8,128)(2,1)} %get-tuple-element.178), channel_id=1, source_target_pairs={{0,16},{4,20},{8,24},{12,28},{16,0},{20,4},{24,8},{28,12},{1,17},{... | collective-permute-start | bytes 786440 | tf_op jit(solution)/shard_map/ppermute | solution.py:48
  51.5 15.3 %collective-permute-start.5 = (bf16[1024,128]{1,0:T(8,128)(2,1)}, bf16[1024,128]{1,0:T(8,128)(2,1)}, u32[]{:S(2)}, u32[]{:S(2)}) collective-permute-start(bf16[1024,128]{1,0:T(8,128)(2,1)} %get-tuple-element.178), channel_id=1, source_target_pairs={{0,24},{4,28},{8,0},{12,4},{16,8},{20,12},{24,16},{28,20},{1,25},{... | collective-permute-start | bytes 786440 | tf_op jit(solution)/shard_map/ppermute | solution.py:48
  53.2 16.4 %collective-permute-start.11 = (bf16[128,1024]{1,0:T(8,128)(2,1)}, bf16[128,1024]{1,0:T(8,128)(2,1)}, u32[]{:S(2)}, u32[]{:S(2)}) collective-permute-start(bf16[128,1024]{1,0:T(8,128)(2,1)} %get-tuple-element.183.r_1_), channel_id=1, source_target_pairs={{0,1},{1,0},{2,3},{3,2},{4,5},{5,4},{6,7},{7,6},{8,9},{9,8},{10,11... | collective-permute-start | bytes 786440 | tf_op jit(solution)/shard_map/ppermute | solution.py:42
  58.0 17.2 %collective-permute-start.12 = (bf16[128,1024]{1,0:T(8,128)(2,1)}, bf16[128,1024]{1,0:T(8,128)(2,1)}, u32[]{:S(2)}, u32[]{:S(2)}) collective-permute-start(bf16[128,1024]{1,0:T(8,128)(2,1)} %collective-permute-done.10.r_2_), channel_id=1, source_target_pairs={{0,1},{1,0},{2,3},{3,2},{4,5},{5,4},{6,7},{7,6},{8,9},{9,8},{10,11... | collective-permute-start | bytes 786440 | tf_op jit(solution)/shard_map/ppermute | solution.py:42
  66.8 21.6 %collective-permute-start.14 = (bf16[128,1024]{1,0:T(8,128)(2,1)}, bf16[128,1024]{1,0:T(8,128)(2,1)S(1)}, u32[]{:S(2)}, u32[]{:S(2)}) collective-permute-start(bf16[128,1024]{1,0:T(8,128)(2,1)} %get-tuple-element.184.r_1_), channel_id=1, source_target_pairs={{0,1},{1,0},{2,3},{3,2},{4,5},{5,4},{6,7},{7,6},{8,9},{9,8},{10,11... | collective-permute-start | bytes 786440 | tf_op jit(solution)/shard_map/ppermute | solution.py:42
  66.8 23.4 %collective-permute-start.15 = (bf16[128,1024]{1,0:T(8,128)(2,1)}, bf16[128,1024]{1,0:T(8,128)(2,1)S(1)}, u32[]{:S(2)}, u32[]{:S(2)}) collective-permute-start(bf16[128,1024]{1,0:T(8,128)(2,1)} %collective-permute-done.13.r_2_), channel_id=1, source_target_pairs={{0,1},{1,0},{2,3},{3,2},{4,5},{5,4},{6,7},{7,6},{8,9},{9,8},{10,11... | collective-permute-start | bytes 786440 | tf_op jit(solution)/shard_map/ppermute | solution.py:42
  69.6 29.0 %collective-permute-start.7 = (bf16[1024,128]{1,0:T(8,128)(2,1)}, bf16[1024,128]{1,0:T(8,128)(2,1)}, u32[]{:S(2)}, u32[]{:S(2)}) collective-permute-start(bf16[1024,128]{1,0:T(8,128)(2,1)} %get-tuple-element.180), channel_id=1, source_target_pairs={{0,8},{4,12},{8,16},{12,20},{16,24},{20,28},{24,0},{28,4},{1,9},{5... | collective-permute-start | bytes 786440 | tf_op jit(solution)/shard_map/ppermute | solution.py:48
  75.2 23.4 %collective-permute-start.8 = (bf16[1024,128]{1,0:T(8,128)(2,1)}, bf16[1024,128]{1,0:T(8,128)(2,1)}, u32[]{:S(2)}, u32[]{:S(2)}) collective-permute-start(bf16[1024,128]{1,0:T(8,128)(2,1)} %get-tuple-element.180), channel_id=1, source_target_pairs={{0,16},{4,20},{8,24},{12,28},{16,0},{20,4},{24,8},{28,12},{1,17},{... | collective-permute-start | bytes 786440 | tf_op jit(solution)/shard_map/ppermute | solution.py:48
  77.3 21.3 %collective-permute-start.9 = (bf16[1024,128]{1,0:T(8,128)(2,1)}, bf16[1024,128]{1,0:T(8,128)(2,1)S(1)}, u32[]{:S(2)}, u32[]{:S(2)}) collective-permute-start(bf16[1024,128]{1,0:T(8,128)(2,1)} %get-tuple-element.180), channel_id=1, source_target_pairs={{0,24},{4,28},{8,0},{12,4},{16,8},{20,12},{24,16},{28,20},{1,25},{... | collective-permute-start | bytes 786440 | tf_op jit(solution)/shard_map/ppermute | solution.py:48
  88.4 26.4 %collective-permute-start.6 = (bf16[4,1024,128]{2,1,0:T(8,128)(2,1)}, bf16[4,1024,128]{2,1,0:T(8,128)(2,1)S(1)}, u32[]{:S(2)}, u32[]{:S(2)}) collective-permute-start(bf16[4,1024,128]{2,1,0:T(8,128)(2,1)} %pad_maximum_fusion.1.r_5_), channel_id=1, source_target_pairs={{0,4},{4,0},{8,12},{12,8},{16,20},{20,16},{24,28},{28,24},{1,5},{5... | collective-permute-start | bytes 3145736 | tf_op jit(solution)/shard_map/ppermute | solution.py:42
  100.6 39.2 %collective-permute-start.19 = (bf16[4,1024,128]{2,1,0:T(8,128)(2,1)S(1)}, bf16[4,1024,128]{2,1,0:T(8,128)(2,1)}, u32[]{:S(2)}, u32[]{:S(2)}) collective-permute-start(bf16[4,1024,128]{2,1,0:T(8,128)(2,1)S(1)} %pad_maximum_fusion.2.r_7_), channel_id=1, source_target_pairs={{0,4},{4,0},{8,12},{12,8},{16,20},{20,16},{24,28},{28,24},{1,5},{5... | collective-permute-start | bytes 3145736 | tf_op jit(solution)/shard_map/ppermute | solution.py:42
  103.2 11.5 %collective-permute-start.18 = (bf16[128,1024]{1,0:T(8,128)(2,1)S(1)}, bf16[128,1024]{1,0:T(8,128)(2,1)S(1)}, u32[]{:S(2)}, u32[]{:S(2)}) collective-permute-start(bf16[128,1024]{1,0:T(8,128)(2,1)S(1)} %fusion.1), channel_id=1, source_target_pairs={{0,2},{1,3},{2,0},{3,1},{4,6},{5,7},{6,4},{7,5},{8,10},{9,11},{10,... | collective-permute-start | bytes 786440 | tf_op jit(solution)/shard_map/ppermute | solution.py:48
  107.9 15.8 %collective-permute-start.20 = (bf16[1024,128]{1,0:T(8,128)(2,1)}, bf16[1024,128]{1,0:T(8,128)(2,1)S(1)}, u32[]{:S(2)}, u32[]{:S(2)}) collective-permute-start(bf16[1024,128]{1,0:T(8,128)(2,1)} %get-tuple-element.193), channel_id=1, source_target_pairs={{0,8},{4,12},{8,16},{12,20},{16,24},{20,28},{24,0},{28,4},{1,9},{5... | collective-permute-start | bytes 786440 | tf_op jit(solution)/shard_map/ppermute | solution.py:48
  120.1 13.0 %collective-permute-start.21 = (bf16[1024,128]{1,0:T(8,128)(2,1)S(1)}, bf16[1024,128]{1,0:T(8,128)(2,1)S(1)}, u32[]{:S(2)}, u32[]{:S(2)}) collective-permute-start(bf16[1024,128]{1,0:T(8,128)(2,1)S(1)} %copy-done.76), channel_id=1, source_target_pairs={{0,16},{4,20},{8,24},{12,28},{16,0},{20,4},{24,8},{28,12},{1,17},{... | collective-permute-start | bytes 786440 | tf_op jit(solution)/shard_map/ppermute | solution.py:48
  120.9 12.3 %collective-permute-start.22 = (bf16[1024,128]{1,0:T(8,128)(2,1)S(1)}, bf16[1024,128]{1,0:T(8,128)(2,1)S(1)}, u32[]{:S(2)}, u32[]{:S(2)}) collective-permute-start(bf16[1024,128]{1,0:T(8,128)(2,1)S(1)} %copy-done.76), channel_id=1, source_target_pairs={{0,24},{4,28},{8,0},{12,4},{16,8},{20,12},{24,16},{28,20},{1,25},{... | collective-permute-start | bytes 786440 | tf_op jit(solution)/shard_map/ppermute | solution.py:48
  123.7 16.8 %collective-permute-start.24 = (bf16[128,1024]{1,0:T(8,128)(2,1)}, bf16[128,1024]{1,0:T(8,128)(2,1)S(1)}, u32[]{:S(2)}, u32[]{:S(2)}) collective-permute-start(bf16[128,1024]{1,0:T(8,128)(2,1)} %get-tuple-element.194.r_1_), channel_id=1, source_target_pairs={{0,1},{1,0},{2,3},{3,2},{4,5},{5,4},{6,7},{7,6},{8,9},{9,8},{10,11... | collective-permute-start | bytes 786440 | tf_op jit(solution)/shard_map/ppermute | solution.py:42
  125.2 16.4 %collective-permute-start.25 = (bf16[128,1024]{1,0:T(8,128)(2,1)S(1)}, bf16[128,1024]{1,0:T(8,128)(2,1)S(1)}, u32[]{:S(2)}, u32[]{:S(2)}) collective-permute-start(bf16[128,1024]{1,0:T(8,128)(2,1)S(1)} %collective-permute-done.23.r_2_), channel_id=1, source_target_pairs={{0,1},{1,0},{2,3},{3,2},{4,5},{5,4},{6,7},{7,6},{8,9},{9,8},{10,11... | collective-permute-start | bytes 786440 | tf_op jit(solution)/shard_map/ppermute | solution.py:42
  133.3 17.9 %collective-permute-start.27 = (bf16[1024,128]{1,0:T(8,128)(2,1)S(1)}, bf16[1024,128]{1,0:T(8,128)(2,1)S(1)}, u32[]{:S(2)}, u32[]{:S(2)}) collective-permute-start(bf16[1024,128]{1,0:T(8,128)(2,1)S(1)} %copy-done.74), channel_id=1, source_target_pairs={{0,8},{4,12},{8,16},{12,20},{16,24},{20,28},{24,0},{28,4},{1,9},{5... | collective-permute-start | bytes 786440 | tf_op jit(solution)/shard_map/ppermute | solution.py:48
  138.0 18.2 %collective-permute-start.28 = (bf16[1024,128]{1,0:T(8,128)(2,1)S(1)}, bf16[1024,128]{1,0:T(8,128)(2,1)S(1)}, u32[]{:S(2)}, u32[]{:S(2)}) collective-permute-start(bf16[1024,128]{1,0:T(8,128)(2,1)S(1)} %copy-done.74), channel_id=1, source_target_pairs={{0,16},{4,20},{8,24},{12,28},{16,0},{20,4},{24,8},{28,12},{1,17},{... | collective-permute-start | bytes 786440 | tf_op jit(solution)/shard_map/ppermute | solution.py:48
  139.8 16.4 %collective-permute-start.29 = (bf16[1024,128]{1,0:T(8,128)(2,1)S(1)}, bf16[1024,128]{1,0:T(8,128)(2,1)S(1)}, u32[]{:S(2)}, u32[]{:S(2)}) collective-permute-start(bf16[1024,128]{1,0:T(8,128)(2,1)S(1)} %copy-done.74), channel_id=1, source_target_pairs={{0,24},{4,28},{8,0},{12,4},{16,8},{20,12},{24,16},{28,20},{1,25},{... | collective-permute-start | bytes 786440 | tf_op jit(solution)/shard_map/ppermute | solution.py:48
  140.5 26.1 %collective-permute-start.26 = (bf16[4,1024,128]{2,1,0:T(8,128)(2,1)S(1)}, bf16[4,1024,128]{2,1,0:T(8,128)(2,1)S(1)}, u32[]{:S(2)}, u32[]{:S(2)}) collective-permute-start(bf16[4,1024,128]{2,1,0:T(8,128)(2,1)S(1)} %pad_maximum_fusion.3.r_5_), channel_id=1, source_target_pairs={{0,4},{4,0},{8,12},{12,8},{16,20},{20,16},{24,28},{28,24},{1,5},{5... | collective-permute-start | bytes 3145736 | tf_op jit(solution)/shard_map/ppermute | solution.py:42
  156.3 39.4 %collective-permute-start.35 = (bf16[4,1024,128]{2,1,0:T(8,128)(2,1)S(1)}, bf16[4,1024,128]{2,1,0:T(8,128)(2,1)S(1)}, u32[]{:S(2)}, u32[]{:S(2)}) collective-permute-start(bf16[4,1024,128]{2,1,0:T(8,128)(2,1)S(1)} %pad_maximum_fusion.4.r_5_), channel_id=1, source_target_pairs={{0,4},{4,0},{8,12},{12,8},{16,20},{20,16},{24,28},{28,24},{1,5},{5... | collective-permute-start | bytes 3145736 | tf_op jit(solution)/shard_map/ppermute | solution.py:42
  157.0 9.6 %collective-permute-start.31 = (bf16[128,1024]{1,0:T(8,128)(2,1)S(1)}, bf16[128,1024]{1,0:T(8,128)(2,1)S(1)}, u32[]{:S(2)}, u32[]{:S(2)}) collective-permute-start(bf16[128,1024]{1,0:T(8,128)(2,1)S(1)} %fusion.2), channel_id=1, source_target_pairs={{0,2},{1,3},{2,0},{3,1},{4,6},{5,7},{6,4},{7,5},{8,10},{9,11},{10,... | collective-permute-start | bytes 786440 | tf_op jit(solution)/shard_map/ppermute | solution.py:48
  157.6 20.6 %collective-permute-start.36 = (bf16[1024,128]{1,0:T(8,128)(2,1)S(1)}, bf16[1024,128]{1,0:T(8,128)(2,1)S(1)}, u32[]{:S(2)}, u32[]{:S(2)}) collective-permute-start(bf16[1024,128]{1,0:T(8,128)(2,1)S(1)} %copy-done.73), channel_id=1, source_target_pairs={{0,8},{4,12},{8,16},{12,20},{16,24},{20,28},{24,0},{28,4},{1,9},{5... | collective-permute-start | bytes 786440 | tf_op jit(solution)/shard_map/ppermute | solution.py:48
  170.8 16.3 %collective-permute-start.37 = (bf16[1024,128]{1,0:T(8,128)(2,1)S(1)}, bf16[1024,128]{1,0:T(8,128)(2,1)S(1)}, u32[]{:S(2)}, u32[]{:S(2)}) collective-permute-start(bf16[1024,128]{1,0:T(8,128)(2,1)S(1)} %copy-done.73), channel_id=1, source_target_pairs={{0,16},{4,20},{8,24},{12,28},{16,0},{20,4},{24,8},{28,12},{1,17},{... | collective-permute-start | bytes 786440 | tf_op jit(solution)/shard_map/ppermute | solution.py:48
  174.3 12.8 %collective-permute-start.38 = (bf16[1024,128]{1,0:T(8,128)(2,1)S(1)}, bf16[1024,128]{1,0:T(8,128)(2,1)S(1)}, u32[]{:S(2)}, u32[]{:S(2)}) collective-permute-start(bf16[1024,128]{1,0:T(8,128)(2,1)S(1)} %copy-done.73), channel_id=1, source_target_pairs={{0,24},{4,28},{8,0},{12,4},{16,8},{20,12},{24,16},{28,20},{1,25},{... | collective-permute-start | bytes 786440 | tf_op jit(solution)/shard_map/ppermute | solution.py:48
  178.1 9.2 %collective-permute-start.33 = (bf16[128,1024]{1,0:T(8,128)(2,1)}, bf16[128,1024]{1,0:T(8,128)(2,1)S(1)}, u32[]{:S(2)}, u32[]{:S(2)}) collective-permute-start(bf16[128,1024]{1,0:T(8,128)(2,1)} %get-tuple-element.205.r_1_), channel_id=1, source_target_pairs={{0,1},{1,0},{2,3},{3,2},{4,5},{5,4},{6,7},{7,6},{8,9},{9,8},{10,11... | collective-permute-start | bytes 786440 | tf_op jit(solution)/shard_map/ppermute | solution.py:42
  178.1 9.2 %collective-permute-start.34 = (bf16[128,1024]{1,0:T(8,128)(2,1)S(1)}, bf16[128,1024]{1,0:T(8,128)(2,1)S(1)}, u32[]{:S(2)}, u32[]{:S(2)}) collective-permute-start(bf16[128,1024]{1,0:T(8,128)(2,1)S(1)} %collective-permute-done.32.r_2_), channel_id=1, source_target_pairs={{0,1},{1,0},{2,3},{3,2},{4,5},{5,4},{6,7},{7,6},{8,9},{9,8},{10,11... | collective-permute-start | bytes 786440 | tf_op jit(solution)/shard_map/ppermute | solution.py:42
  195.8 25.6 %collective-permute-start.44 = (bf16[4,1024,128]{2,1,0:T(8,128)(2,1)S(1)}, bf16[4,1024,128]{2,1,0:T(8,128)(2,1)S(1)}, u32[]{:S(2)}, u32[]{:S(2)}) collective-permute-start(bf16[4,1024,128]{2,1,0:T(8,128)(2,1)S(1)} %pad_maximum_fusion.5.r_7_), channel_id=1, source_target_pairs={{0,4},{4,0},{8,12},{12,8},{16,20},{20,16},{24,28},{28,24},{1,5},{5... | collective-permute-start | bytes 3145736 | tf_op jit(solution)/shard_map/ppermute | solution.py:42
  199.2 8.4 %collective-permute-start.40 = (bf16[128,1024]{1,0:T(8,128)(2,1)S(1)}, bf16[128,1024]{1,0:T(8,128)(2,1)S(1)}, u32[]{:S(2)}, u32[]{:S(2)}) collective-permute-start(bf16[128,1024]{1,0:T(8,128)(2,1)S(1)} %fusion.3), channel_id=1, source_target_pairs={{0,2},{1,3},{2,0},{3,1},{4,6},{5,7},{6,4},{7,5},{8,10},{9,11},{10,... | collective-permute-start | bytes 786440 | tf_op jit(solution)/shard_map/ppermute | solution.py:48
  212.9 8.5 %collective-permute-start.42 = (bf16[128,1024]{1,0:T(8,128)(2,1)}, bf16[128,1024]{1,0:T(8,128)(2,1)S(1)}, u32[]{:S(2)}, u32[]{:S(2)}) collective-permute-start(bf16[128,1024]{1,0:T(8,128)(2,1)} %get-tuple-element.211.r_1_), channel_id=1, source_target_pairs={{0,1},{1,0},{2,3},{3,2},{4,5},{5,4},{6,7},{7,6},{8,9},{9,8},{10,11... | collective-permute-start | bytes 786440 | tf_op jit(solution)/shard_map/ppermute | solution.py:42
  243.5 9.1 %collective-permute-start.46 = (bf16[128,1024]{1,0:T(8,128)(2,1)S(1)}, bf16[128,1024]{1,0:T(8,128)(2,1)S(1)}, u32[]{:S(2)}, u32[]{:S(2)}) collective-permute-start(bf16[128,1024]{1,0:T(8,128)(2,1)S(1)} %fusion.4), channel_id=1, source_target_pairs={{0,2},{1,3},{2,0},{3,1},{4,6},{5,7},{6,4},{7,5},{8,10},{9,11},{10,... | collective-permute-start | bytes 786440 | tf_op jit(solution)/shard_map/ppermute | solution.py:48
  257.1 183.0 %reduce-scatter.5.cloned.1.call-start = ((), (), s32[]{:S(2)}) async-start(), calls=%async_computation.3 | async-start | bytes 2359296 | tf_op jit(solution)/shard_map/reduce_scatter | solution.py:1314
  281.7 8.4 %collective-permute-start.51 = (bf16[128,1024]{1,0:T(8,128)(2,1)S(1)}, bf16[128,1024]{1,0:T(8,128)(2,1)S(1)}, u32[]{:S(2)}, u32[]{:S(2)}) collective-permute-start(bf16[128,1024]{1,0:T(8,128)(2,1)S(1)} %fusion.5), channel_id=1, source_target_pairs={{0,2},{1,3},{2,0},{3,1},{4,6},{5,7},{6,4},{7,5},{8,10},{9,11},{10,... | collective-permute-start | bytes 786440 | tf_op jit(solution)/shard_map/ppermute | solution.py:48
  313.1 9.3 %collective-permute-start.56 = (bf16[2,128,1024]{2,1,0:T(8,128)(2,1)}, bf16[2,128,1024]{2,1,0:T(8,128)(2,1)S(1)}, u32[]{:S(2)}, u32[]{:S(2)}) collective-permute-start(bf16[2,128,1024]{2,1,0:T(8,128)(2,1)} %get-tuple-element.242), channel_id=1, source_target_pairs={{0,1},{1,0},{2,3},{3,2},{4,5},{5,4},{6,7},{7,6},{8,9},{9,8},{10,11... | collective-permute-start | bytes 1572872 | tf_op jit(solution)/shard_map/ppermute | solution.py:42
  320.9 57.1 %collective-permute-start.55 = (bf16[4,2048,128]{2,1,0:T(8,128)(2,1)}, bf16[4,2048,128]{2,1,0:T(8,128)(2,1)S(1)}, u32[]{:S(2)}, u32[]{:S(2)}) collective-permute-start(bf16[4,2048,128]{2,1,0:T(8,128)(2,1)} %get-tuple-element.238), channel_id=1, source_target_pairs={{0,4},{4,0},{8,12},{12,8},{16,20},{20,16},{24,28},{28,24},{1,5},{5... | collective-permute-start | bytes 6291464 | tf_op jit(solution)/shard_map/ppermute | solution.py:42
  322.5 8.4 %collective-permute-start.57 = (bf16[128,1024]{1,0:T(8,128)(2,1)S(1)}, bf16[128,1024]{1,0:T(8,128)(2,1)S(1)}, u32[]{:S(2)}, u32[]{:S(2)}) collective-permute-start(bf16[128,1024]{1,0:T(8,128)(2,1)S(1)} %fusion.6), channel_id=1, source_target_pairs={{0,2},{1,3},{2,0},{3,1},{4,6},{5,7},{6,4},{7,5},{8,10},{9,11},{10,... | collective-permute-start | bytes 786440 | tf_op jit(solution)/shard_map/ppermute | solution.py:48
  358.5 8.5 %collective-permute-start.62 = (bf16[128,1024]{1,0:T(8,128)(2,1)S(1)}, bf16[128,1024]{1,0:T(8,128)(2,1)S(1)}, u32[]{:S(2)}, u32[]{:S(2)}) collective-permute-start(bf16[128,1024]{1,0:T(8,128)(2,1)S(1)} %fusion.7), channel_id=1, source_target_pairs={{0,2},{1,3},{2,0},{3,1},{4,6},{5,7},{6,4},{7,5},{8,10},{9,11},{10,... | collective-permute-start | bytes 786440 | tf_op jit(solution)/shard_map/ppermute | solution.py:48
  364.8 58.1 %collective-permute-start.68 = (bf16[4,1024,128]{2,1,0:T(8,128)(2,1)}, bf16[4,1024,128]{2,1,0:T(8,128)(2,1)S(1)}, u32[]{:S(2)}, u32[]{:S(2)}) collective-permute-start(bf16[4,1024,128]{2,1,0:T(8,128)(2,1)} %get-tuple-element.250), channel_id=1, source_target_pairs={{0,4},{4,0},{8,12},{12,8},{16,20},{20,16},{24,28},{28,24},{1,5},{5... | collective-permute-start | bytes 3145736 | tf_op jit(solution)/shard_map/ppermute | solution.py:42
  384.5 48.2 %collective-permute-start.84 = (bf16[2,2048,128]{2,1,0:T(8,128)(2,1)}, bf16[2,2048,128]{2,1,0:T(8,128)(2,1)S(1)}, u32[]{:S(2)}, u32[]{:S(2)}) collective-permute-start(bf16[2,2048,128]{2,1,0:T(8,128)(2,1)} %get-tuple-element.322), channel_id=1, source_target_pairs={{0,8},{4,12},{8,0},{12,4},{16,24},{20,28},{24,16},{28,20},{1,9},{5... | collective-permute-start | bytes 3145736 | tf_op jit(solution)/shard_map/ppermute | solution.py:1252
  390.3 21.9 %collective-permute-start.64 = (bf16[2048,128]{1,0:T(8,128)(2,1)}, bf16[2048,128]{1,0:T(8,128)(2,1)}, u32[]{:S(2)}, u32[]{:S(2)}) collective-permute-start(bf16[2048,128]{1,0:T(8,128)(2,1)} %bitcast.164), channel_id=1, source_target_pairs={{0,2},{1,3},{2,0},{3,1},{4,6},{5,7},{6,4},{7,5},{8,10},{9,11},{10,... | collective-permute-start | bytes 1572872 | tf_op jit(solution)/shard_map/ppermute | solution.py:48
  400.2 12.0 %collective-permute-start.63 = (bf16[4,176,128]{2,1,0:T(8,128)(2,1)}, bf16[4,176,128]{2,1,0:T(8,128)(2,1)S(1)}, u32[]{:S(2)}, u32[]{:S(2)}) collective-permute-start(bf16[4,176,128]{2,1,0:T(8,128)(2,1)} %get-tuple-element.271), channel_id=1, source_target_pairs={{0,4},{4,0},{8,12},{12,8},{16,20},{20,16},{24,28},{28,24},{1,5},{5... | collective-permute-start | bytes 540680 | tf_op jit(solution)/shard_map/ppermute | solution.py:42
  415.2 12.2 %collective-permute-start.65 = (bf16[176,128]{1,0:T(8,128)(2,1)}, bf16[176,128]{1,0:T(8,128)(2,1)S(1)}, u32[]{:S(2)}, u32[]{:S(2)}) collective-permute-start(bf16[176,128]{1,0:T(8,128)(2,1)} %get-tuple-element.275), channel_id=1, source_target_pairs={{0,8},{4,12},{8,16},{12,20},{16,24},{20,28},{24,0},{28,4},{1,9},{5... | collective-permute-start | bytes 135176 | tf_op jit(solution)/shard_map/ppermute | solution.py:48
  419.2 10.3 %collective-permute-start.66 = (bf16[176,128]{1,0:T(8,128)(2,1)}, bf16[176,128]{1,0:T(8,128)(2,1)S(1)}, u32[]{:S(2)}, u32[]{:S(2)}) collective-permute-start(bf16[176,128]{1,0:T(8,128)(2,1)} %get-tuple-element.276), channel_id=1, source_target_pairs={{0,16},{4,20},{8,24},{12,28},{16,0},{20,4},{24,8},{28,12},{1,17},{... | collective-permute-start | bytes 135176 | tf_op jit(solution)/shard_map/ppermute | solution.py:48
  422.9 11.1 %collective-permute-start.73 = (bf16[2,128,1024]{2,1,0:T(8,128)(2,1)S(1)}, bf16[2,128,1024]{2,1,0:T(8,128)(2,1)S(1)}, u32[]{:S(2)}, u32[]{:S(2)}) collective-permute-start(bf16[2,128,1024]{2,1,0:T(8,128)(2,1)S(1)} %copy-done.107), channel_id=1, source_target_pairs={{0,1},{1,0},{2,3},{3,2},{4,5},{5,4},{6,7},{7,6},{8,9},{9,8},{10,11... | collective-permute-start | bytes 1572872 | tf_op jit(solution)/shard_map/ppermute | solution.py:42
  427.5 24.1 %collective-permute-start.69 = (bf16[2,1024,128]{2,1,0:T(8,128)(2,1)}, bf16[2,1024,128]{2,1,0:T(8,128)(2,1)S(1)}, u32[]{:S(2)}, u32[]{:S(2)}) collective-permute-start(bf16[2,1024,128]{2,1,0:T(8,128)(2,1)} %get-tuple-element.281), channel_id=1, source_target_pairs={{0,8},{4,12},{8,0},{12,4},{16,24},{20,28},{24,16},{28,20},{1,9},{5... | collective-permute-start | bytes 1572872 | tf_op jit(solution)/shard_map/ppermute | solution.py:1252
  429.5 22.0 %collective-permute-start.75 = (bf16[2048,128]{1,0:T(8,128)(2,1)S(1)}, bf16[2048,128]{1,0:T(8,128)(2,1)S(1)}, u32[]{:S(2)}, u32[]{:S(2)}) collective-permute-start(bf16[2048,128]{1,0:T(8,128)(2,1)S(1)} %bitcast.166), channel_id=1, source_target_pairs={{0,1},{1,0},{2,3},{3,2},{4,5},{5,4},{6,7},{7,6},{8,9},{9,8},{10,11... | collective-permute-start | bytes 1572872 | tf_op jit(solution)/shard_map/ppermute | solution.py:42
  434.0 17.6 %collective-permute-start.76 = (bf16[2048,128]{1,0:T(8,128)(2,1)}, bf16[2048,128]{1,0:T(8,128)(2,1)}, u32[]{:S(2)}, u32[]{:S(2)}) collective-permute-start(bf16[2048,128]{1,0:T(8,128)(2,1)} %collective-permute-done.64.r_2_), channel_id=1, source_target_pairs={{0,1},{1,0},{2,3},{3,2},{4,5},{5,4},{6,7},{7,6},{8,9},{9,8},{10,11... | collective-permute-start | bytes 1572872 | tf_op jit(solution)/shard_map/ppermute | solution.py:42
  436.7 26.0 %collective-permute-start.85 = (bf16[2048,128]{1,0:T(8,128)(2,1)}, bf16[2048,128]{1,0:T(8,128)(2,1)}, u32[]{:S(2)}, u32[]{:S(2)}) collective-permute-start(bf16[2048,128]{1,0:T(8,128)(2,1)} %fusion), channel_id=1, source_target_pairs={{0,16},{4,20},{8,24},{12,28},{16,0},{20,4},{24,8},{28,12},{1,17},{... | collective-permute-start | bytes 1572872 | tf_op jit(solution)/shard_map/ppermute | solution.py:1252
  439.1 8.6 %collective-permute-start.74 = (bf16[128,1024]{1,0:T(8,128)(2,1)}, bf16[128,1024]{1,0:T(8,128)(2,1)S(1)}, u32[]{:S(2)}, u32[]{:S(2)}) collective-permute-start(bf16[128,1024]{1,0:T(8,128)(2,1)} %fusion.8), channel_id=1, source_target_pairs={{0,2},{1,3},{2,0},{3,1},{4,6},{5,7},{6,4},{7,5},{8,10},{9,11},{10,... | collective-permute-start | bytes 786440 | tf_op jit(solution)/shard_map/ppermute | solution.py:48
  447.7 18.3 %collective-permute-start.77 = (bf16[1024,128]{1,0:T(8,128)(2,1)}, bf16[1024,128]{1,0:T(8,128)(2,1)S(1)}, u32[]{:S(2)}, u32[]{:S(2)}) collective-permute-start(bf16[1024,128]{1,0:T(8,128)(2,1)} %bitcast.173), channel_id=1, source_target_pairs={{0,2},{1,3},{2,0},{3,1},{4,6},{5,7},{6,4},{7,5},{8,10},{9,11},{10,... | collective-permute-start | bytes 786440 | tf_op jit(solution)/shard_map/ppermute | solution.py:48
  465.8 20.1 %collective-permute-start.86 = (bf16[2048,128]{1,0:T(8,128)(2,1)}, bf16[2048,128]{1,0:T(8,128)(2,1)S(1)}, u32[]{:S(2)}, u32[]{:S(2)}) collective-permute-start(bf16[2048,128]{1,0:T(8,128)(2,1)} %shard_map.373.r_1_), channel_id=1, source_target_pairs={{0,2},{1,3},{2,0},{3,1},{4,6},{5,7},{6,4},{7,5},{8,10},{9,11},{10,... | collective-permute-start | bytes 1572872 | tf_op jit(solution)/shard_map/ppermute | solution.py:48
  466.7 14.2 %collective-permute-start.80 = (bf16[1024,128]{1,0:T(8,128)(2,1)S(1)}, bf16[1024,128]{1,0:T(8,128)(2,1)S(1)}, u32[]{:S(2)}, u32[]{:S(2)}) collective-permute-start(bf16[1024,128]{1,0:T(8,128)(2,1)S(1)} %fusion.9), channel_id=1, source_target_pairs={{0,16},{4,20},{8,24},{12,28},{16,0},{20,4},{24,8},{28,12},{1,17},{... | collective-permute-start | bytes 786440 | tf_op jit(solution)/shard_map/ppermute | solution.py:1252
  484.2 8.4 %collective-permute-start.81 = (bf16[1024,128]{1,0:T(8,128)(2,1)}, bf16[1024,128]{1,0:T(8,128)(2,1)S(1)}, u32[]{:S(2)}, u32[]{:S(2)}) collective-permute-start(bf16[1024,128]{1,0:T(8,128)(2,1)} %shard_map.371.r_1_), channel_id=1, source_target_pairs={{0,2},{1,3},{2,0},{3,1},{4,6},{5,7},{6,4},{7,5},{8,10},{9,11},{10,... | collective-permute-start | bytes 786440 | tf_op jit(solution)/shard_map/ppermute | solution.py:48
  485.9 13.2 %collective-permute-start.87 = (bf16[2048,128]{1,0:T(8,128)(2,1)S(1)}, bf16[2048,128]{1,0:T(8,128)(2,1)S(1)}, u32[]{:S(2)}, u32[]{:S(2)}) collective-permute-start(bf16[2048,128]{1,0:T(8,128)(2,1)S(1)} %copy-done.22), channel_id=1, source_target_pairs={{0,1},{1,0},{2,3},{3,2},{4,5},{5,4},{6,7},{7,6},{8,9},{9,8},{10,11... | collective-permute-start | bytes 1572872 | tf_op jit(solution)/shard_map/ppermute | solution.py:42
  485.9 13.2 %collective-permute-start.88 = (bf16[2048,128]{1,0:T(8,128)(2,1)S(1)}, bf16[2048,128]{1,0:T(8,128)(2,1)S(1)}, u32[]{:S(2)}, u32[]{:S(2)}) collective-permute-start(bf16[2048,128]{1,0:T(8,128)(2,1)S(1)} %collective-permute-done.86.r_2_), channel_id=1, source_target_pairs={{0,1},{1,0},{2,3},{3,2},{4,5},{5,4},{6,7},{7,6},{8,9},{9,8},{10,11... | collective-permute-start | bytes 1572872 | tf_op jit(solution)/shard_map/ppermute | solution.py:42
  (135 other events, 1390.9 us)
Sparse Core Ops, SparseCore 0:
  257.2 96.4 reduce-scatter.2
  358.2 76.0 reduce-scatter.4

commit v5 on v4

--- a/solution.py
+++ b/solution.py
@@ -783,16 +783,15 @@
             out[2 * n + 1, at : at + rows, :] = value[:, 128:]
 
 
-def mlp_split_kernel(meta, every, g_pre, hidden, low, send, mine):
+def mlp_split_kernel(meta, every, g_pre, hidden, low, down_send, down_mine, up_send, up_mine):
     tile = 256
-    rows = every.shape[1]
     first = meta[2] == 0
-    for at, left, right in ((0, every, g_pre), (rows, hidden, low)):
+    for left, right, send, mine in ((hidden, low, down_send, down_mine), (every, g_pre, up_send, up_mine)):
         for n in range(right.shape[1] // tile):
             value = dot(left[...], right[:, n * tile : (n + 1) * tile], 0, 0).astype(BF)
             one, two = value[:, :128], value[:, 128:]
-            mine[n, at : at + rows, :] = jnp.where(first, one, two)
-            send[n, at : at + rows, :] = jnp.where(first, two, one)
+            mine[n] = jnp.where(first, one, two)
+            send[n] = jnp.where(first, two, one)
 
 
 def io_grads_kernel(split, meta, g_proj, every, mixed, low, *refs):
@@ -825,8 +824,13 @@
         send[k] = (mine[far].astype(F32) + got[far].astype(F32)).astype(BF)
 
 
-def last_sum_kernel(meta, keep, got, crossed, out):
-    out[...] = (keep[0] + got[0].astype(F32) + crossed[...].astype(F32)).astype(BF)
+def last_sum_kernel(meta, *refs):
+    out = refs[-1]
+    rows = refs[2].shape[0]
+    for k in range(len(refs) // 3):
+        keep, got, crossed = refs[3 * k : 3 * k + 3]
+        total = keep[0] + got[0].astype(F32) + crossed[...].astype(F32)
+        out[k * rows : (k + 1) * rows, :] = total.astype(BF)
 
 
 def small_last_kernel(meta, *refs):
@@ -1259,10 +1263,13 @@
     def owner_second(keep, got):
         return [keep, got, hop((keep[1] + got[1].astype(F32)).astype(BF), 4)]
 
-    def owner_end(pieces):
-        keep, got, crossed = pieces
-        block = ((1,) + crossed.shape, lambda i, m: (0, 0, 0))
-        return run(last_sum_kernel, [(crossed.shape, BF)], meta, [(keep,) + block, (got,) + block, crossed])[0]
+    def owner_end(*chunks):
+        args = []
+        for keep, got, crossed in chunks:
+            block = ((1,) + crossed.shape, lambda i, m: (0, 0, 0))
+            args += [(keep,) + block, (got,) + block, crossed]
+        rows, lanes_of = crossed.shape
+        return run(last_sum_kernel, [((len(chunks) * rows, lanes_of), BF)], meta, args)[0]
 
     norm_outs = [((tok_rows, width), F32), ((tok_rows, width), BF), ((8, width), F32)]
     for l in reversed(range(depth)):
@@ -1280,14 +1287,18 @@
             (g_mlp,) = run(mlp_grads_kernel, [((n_grp, 2 * width, cols), BF)], meta, operands)
             grad = after(grad, g_mlp)
         else:
-            mlp_send, mlp_mine = run(
-                mlp_split_kernel, [((nz, 2 * width, cols), BF)] * 2, meta, operands)
-            mlp_got = comm.flip(mlp_send, "grp", n_grp)
-            grad = after(grad, mlp_send)
+            down_send, down_mine, up_send, up_mine = run(
+                mlp_split_kernel, [((nz, width, cols), BF)] * 4, meta, operands)
+            down_got = comm.flip(down_send, "grp", n_grp)
+            up_got = comm.flip(up_send, "grp", n_grp)
+            grad = after(grad, down_send)
         grad, low_own, toks[2 * l + 1] = run(norm_back_kernel, norm_outs, meta, [grad, *got, mid, gains[l, 1]])
         low_parts = gather_parts(low_own)
         if l:
             mlp_unit = lax.psum_scatter(after(g_mlp, low_own), "grp", scatter_dimension=0, tiled=False)
+        if l == 0:
+            down_first = owner_first(down_mine, down_got)
+            low_parts[0] = after(low_parts[0], down_first[0])
         low, g_proj, g_fouts[l], g_seconds[l], smalls[l], send, keep = run(
             lambda *r, n=len(w_io): mix_back_kernel(count, n, *r),
             [((total, width), BF), ((total, 3 * chans), BF), ((lanes, chans), F32), ((half, lanes), F32),
@@ -1329,22 +1340,23 @@
         lambda *r: pack_kernel(depth, *r), [((nz, SMALL + NET, cols), BF)] * 2, meta,
         up_biases + smalls + g_fouts + toks + g_seconds + network + [e_wide, e_all],
         [((5, 2 * SLOT, 3 * chans), F32), ((SMALL, width), F32)])
-    mlp_first = owner_first(mlp_mine, after(mlp_got, io_send, low_own))
-    io_first = owner_first(io_mine, after(io_got, mlp_first[0], send))
+    up_first = owner_first(up_mine, after(up_got, io_send, low_own, down_first[1]))
+    down_pieces = owner_second(*down_first)
+    io_first = owner_first(io_mine, after(io_got, up_first[0], send))
+    up_pieces = owner_second(*up_first)
     parts_one = gather_parts(after(mlp_unit, low_own))
-    small_got = after(comm.flip(send, "grp", n_grp), parts_one[1])
+    small_got = after(comm.flip(send, "grp", n_grp), parts_one[1], down_pieces[2], io_first[0])
     small_rows = (SMALL + NET, cols)
     own, *sends = run(small_turn_kernel, [(small_rows, BF)] * nz, meta, [mine, small_got])
     pieces = [own] + [comm.turn(v, "grp", n_grp, k) for k, v in enumerate(sends, 1)]
-    mlp_pieces = owner_second(after(mlp_first[0], *pieces[1:]), mlp_first[1])
     io_turn = owner_second(*io_first)
     (small,) = run(small_last_kernel, [(small_rows, BF)], meta, pieces, [((nz,) + small_rows, F32)])
     small_parts = gather_parts(small)
 
     l = 1
     mlp_grads = finish(finish_mlp_kernel, parts_one, mlp_shapes, [])
-    mlp_pieces[0], state, *mlp_grads = lax.optimization_barrier(
-        (after(mlp_pieces[0], io_first[1], *small_parts), state, *mlp_grads))
+    up_pieces[0], state, *mlp_grads = lax.optimization_barrier(
+        (after(up_pieces[0], io_first[1], *small_parts), state, *mlp_grads))
     io_grads = finish(finish_io_kernel, gather_parts(after(io_one, *small_parts)), io_shapes, [], turned)
     io_turn[0], *io_grads = lax.optimization_barrier((io_turn[0], *io_grads))
     shared_shapes = [v.shape for v in (filt_in, filt_mid, filt_bias, sine_freq)]
@@ -1357,7 +1369,7 @@
     (norm_gain_grad, norm_bias_grad, branch_grad, in_bias_grad, taps_grad, tap_bias_grad, skip_grad, fout_grad,
      up_bias_grad, *shared) = small_grads
     l = 0
-    mlp_unit = owner_end(mlp_pieces)
+    mlp_unit = owner_end(up_pieces, down_pieces)
     up_grad, down_grad = finish(finish_mlp_kernel, gather_parts(mlp_unit), mlp_shapes, mlp_grads)
     in_grad, out_grad = finish(finish_io_kernel, gather_parts(owner_end(io_turn)), io_shapes, io_grads, turned)
     return (

time: 522 us -> 522 us (level)
    ppermute x43 -> x44, waiting for transfers between devices: 38.4 us -> 27.4 us  [flip(): return lax.ppermute(v, axis, [(i, i ^ 1) for i in range(size)])]
    ppermute x4 -> x6, waiting for transfers between devices: 12 us -> 17.4 us  [hop(): return lax.ppermute(v, 'grp', [(i, i ^ bit) for i in range(n_grp)])]
    ppermute x4 -> x6, starting transfers between devices: 8.5 us -> 11.1 us  [hop(): return lax.ppermute(v, 'grp', [(i, i ^ bit) for i in range(n_grp)])]
    pallas_call x36 -> x37, Pallas kernels: 180 us -> 182 us  [run(): pl.pallas_call(kernel, out_shape=shapes, grid_spec=pltpu.PrefetchScalarGr...]
    unnamed x219 -> x227, local copies, waits for them, and re-layouts: 25.9 us -> 25.1 us
    ppermute x43 -> x44, starting transfers between devices: 13.5 us -> 13.9 us  [flip(): return lax.ppermute(v, axis, [(i, i ^ 1) for i in range(size)])]
  transfers between devices with their start and end apart: 91 -> 94, of which waited for: 33 -> 36; matrix products, arithmetic and copies ran while one was open for 9% -> 9% of each run, Pallas kernels for 29% -> 30%
where the time goes in v5:
time: 522 us; the launch traced here: 512 us
  Pallas kernels  182 us (35%)
  waiting for transfers between devices  141 us (27%)
  starting transfers between devices  98 us (19%)
  local copies, waits for them, and re-layouts  43.3 us (8%)
  other arithmetic  30.1 us (6%)
  between operations  15.7 us (3%)
    pallas_call x37, Pallas kernels, run(): pl.pallas_call(kernel, out_shape=shapes, grid_spec=pltpu.PrefetchScalarGr...  182 us
    ppermute x42, waiting for transfers between devices, turn(): return lax.ppermute(v, axis, perm)  96.4 us
    ppermute x42, starting transfers between devices, turn(): return lax.ppermute(v, axis, perm)  73 us
    ppermute x44, waiting for transfers between devices, flip(): return lax.ppermute(v, axis, [(i, i ^ 1) for i in range(size)])  27.4 us
    unnamed x227, local copies, waits for them, and re-layouts  25.1 us
    ppermute x6, waiting for transfers between devices, hop(): return lax.ppermute(v, 'grp', [(i, i ^ bit) for i in range(n_grp)])  17.4 us
    ppermute x44, starting transfers between devices, flip(): return lax.ppermute(v, axis, [(i, i ^ 1) for i in range(size)])  13.9 us
    ppermute x6, starting transfers between devices, hop(): return lax.ppermute(v, 'grp', [(i, i ^ bit) for i in range(n_grp)])  11.1 us
  transfers between devices with their start and end apart: 94, of which 36 were waited for; matrix products, arithmetic and copies ran while one was open for 9% of the time, Pallas kernels for 30%

profile of v5, /device:TPU:0, one launch (start us, length us, event | category | flops | bytes accessed | tf_op | source)
XLA Modules:
  0.0 512.1 jit_solution(13349159069262748128)
XLA Ops:
  11.4 3.2 shard_map.339
  14.6 3.0 collective-permute-start
  21.6 2.8 shard_map.340
  28.9 3.9 subtract_select_fusion.2
  53.3 4.8 collective-permute-done.3
  61.5 5.4 %collective-permute-done.4 = bf16[1024,128]{1,0:T(8,128)(2,1)} collective-permute-done((bf16[1024,128]{1,0:T(8,128)(2,1)}, bf16[1024,128]{1,0:T(8,128)(2,1)}, u32[]{:S(2)}, u32[]{:S(2)}) %collective-permute-start.4) | collective-permute-done | bytes 262176 | tf_op jit(solution)/shard_map/ppermute | solution.py:48
  69.8 5.6 %collective-permute-start.7 = (bf16[1024,128]{1,0:T(8,128)(2,1)}, bf16[1024,128]{1,0:T(8,128)(2,1)}, u32[]{:S(2)}, u32[]{:S(2)}) collective-permute-start(bf16[1024,128]{1,0:T(8,128)(2,1)} %get-tuple-element.184), channel_id=1, source_target_pairs={{0,8},{4,12},{8,16},{12,20},{16,24},{20,28},{24,0},{28,4},{1,9},{5... | collective-permute-start | bytes 786440 | tf_op jit(solution)/shard_map/ppermute | solution.py:48
  78.4 4.3 shard_map.341
  91.1 7.5 %shard_map.342 = (bf16[512,1024]{1,0:T(8,128)(2,1)}, bf16[512,768]{1,0:T(8,128)(2,1)}, f32[512,256]{1,0:T(8,128)}, bf16[512,256]{1,0:T(8,128)(2,1)}, bf16[2,128,...) custom-call(s32[11]{0:T(128)} %concatenate.27.r_0_.meta, bf16[128,1024]{1,0:T(8,128)(2,1)} %get-tuple-element.188.r_1_, ...), custom_call_target="tpu_custom_call" | custom-call | flops 3000000 | bytes 9396 | tf_op jit(solution)/shard_map/pallas_call | solution.py:492
  104.9 3.1 shard_map.344
  110.0 4.8 collective-permute-done.6.r_6_
  115.6 3.1 shard_map.343
  121.0 2.8 collective-permute-start.22
  125.3 7.9 %collective-permute-done.21 = bf16[1024,128]{1,0:T(8,128)(2,1)S(1)} collective-permute-done((bf16[1024,128]{1,0:T(8,128)(2,1)S(1)}, bf16[1024,128]{1,0:T(8,128)(2,1)S(1)}, u32[]{:S(2)}, u32[]{:S(2)}) %collective-permute-start.21) | collective-permute-done | bytes 262176 | tf_op jit(solution)/shard_map/ppermute | solution.py:48
  133.4 4.8 collective-permute-start.27
  142.5 8.8 %shard_map.345 = (bf16[512,1024]{1,0:T(8,128)(2,1)}, bf16[512,1024]{1,0:T(8,128)(2,1)}, bf16[512,1024]{1,0:T(8,128)(2,1)}, bf16[2,128,1024]{2,1,0:T(8,128)(2,1)}, f32[2,128,1024]{2,1,0:T(8,128)}) custom-call(s32[11]{0:T(128)} %concatenate.27.r_0_.meta, bf16[128,1024]{1,0:T(8,128)(2,1)} %get-tuple-element.198.r_1_, bf16[128,1024]{1,0:T(8,128)(2,1)} %copy-done.47, ...), custom_call_target="tpu_custom_call" | custom-call | flops 4000000 | bytes 9965 | tf_op jit(solution)/shard_map/pallas_call | solution.py:492
  151.4 4.9 collective-permute-done.28
  157.8 6.1 %collective-permute-start.36 = (bf16[1024,128]{1,0:T(8,128)(2,1)S(1)}, bf16[1024,128]{1,0:T(8,128)(2,1)S(1)}, u32[]{:S(2)}, u32[]{:S(2)}) collective-permute-start(bf16[1024,128]{1,0:T(8,128)(2,1)S(1)} %copy-done.77), channel_id=1, source_target_pairs={{0,8},{4,12},{8,16},{12,20},{16,24},{20,28},{24,0},{28,4},{1,9},{5... | collective-permute-start | bytes 786440 | tf_op jit(solution)/shard_map/ppermute | solution.py:48
  163.9 2.9 collective-permute-done.26.r_6_
  167.5 3.0 shard_map.346
  171.0 3.5 collective-permute-start.37
  174.5 3.8 collective-permute-start.38
  178.9 8.5 %collective-permute-done.37 = bf16[1024,128]{1,0:T(8,128)(2,1)S(1)} collective-permute-done((bf16[1024,128]{1,0:T(8,128)(2,1)S(1)}, bf16[1024,128]{1,0:T(8,128)(2,1)S(1)}, u32[]{:S(2)}, u32[]{:S(2)}) %collective-permute-start.37) | collective-permute-done | bytes 262176 | tf_op jit(solution)/shard_map/ppermute | solution.py:48
  188.4 7.5 %shard_map.347 = (bf16[512,1024]{1,0:T(8,128)(2,1)}, bf16[512,768]{1,0:T(8,128)(2,1)}, f32[512,256]{1,0:T(8,128)}, bf16[512,256]{1,0:T(8,128)(2,1)}, bf16[2,128,...) custom-call(s32[11]{0:T(128)} %concatenate.27.r_0_.meta, bf16[128,1024]{1,0:T(8,128)(2,1)} %get-tuple-element.209.r_1_, ...), custom_call_target="tpu_custom_call" | custom-call | flops 3000000 | bytes 9265 | tf_op jit(solution)/shard_map/pallas_call | solution.py:492
  201.0 6.8 %collective-permute-done.40.crossed = bf16[128,1024]{1,0:T(8,128)(2,1)S(1)} collective-permute-done((bf16[128,1024]{1,0:T(8,128)(2,1)S(1)}, bf16[128,1024]{1,0:T(8,128)(2,1)S(1)}, u32[]{:S(2)}, u32[]{:S(2)}) %collective-permute-start.40) | collective-permute-done | bytes 262176 | tf_op jit(solution)/shard_map/ppermute | solution.py:48
  208.5 3.1 shard_map.348
  213.1 6.2 %collective-permute-done.41.r_2_ = bf16[128,1024]{1,0:T(8,128)(2,1)S(1)} collective-permute-done((bf16[128,1024]{1,0:T(8,128)(2,1)}, bf16[128,1024]{1,0:T(8,128)(2,1)S(1)}, u32[]{:S(2)}, u32[]{:S(2)}) %collective-permute-start.41) | collective-permute-done | bytes 262176 | tf_op jit(solution)/shard_map/ppermute | solution.py:48
  222.7 9.0 %shard_map.349 = (bf16[512,1024]{1,0:T(8,128)(2,1)}, bf16[512,1024]{1,0:T(8,128)(2,1)}, bf16[512,1024]{1,0:T(8,128)(2,1)}, bf16[2,128,1024]{2,1,0:T(8,128)(2,1)}, f32[2,128,1024]{2,1,0:T(8,128)}) custom-call(s32[11]{0:T(128)} %concatenate.27.r_0_.meta, bf16[128,1024]{1,0:T(8,128)(2,1)} %get-tuple-element.215.r_1_, bf16[128,1024]{1,0:T(8,128)(2,1)} %copy-done.62, ...), custom_call_target="tpu_custom_call" | custom-call | flops 4000000 | bytes 9965 | tf_op jit(solution)/shard_map/pallas_call | solution.py:492
  231.7 8.6 %shard_map.350 = (bf16[512,1024]{1,0:T(8,128)(2,1)}, bf16[512,1024]{1,0:T(8,128)(2,1)}, f32[1,1024]{1,0:T(1,128)}, bf16[2,128,1024]{2,1,0:T(8,128)(2,1)}, f32[2,128,1024]{2,1,0:T(8,128)}) custom-call(s32[11]{0:T(128)} %concatenate.27.r_0_.meta, bf16[128,1024]{1,0:T(8,128)(2,1)} %get-tuple-element.187.r_1_, bf16[128,1024]{1,0:T(8,128)(2,1)} %collective-permute-done.10.r_2_, ...), custom_call_target="tpu_custom_call" | custom-call | flops 4000000 | bytes 9965 | tf_op jit(solution)/shard_map/pallas_call | solution.py:492
  245.3 7.5 %shard_map.351 = bf16[8,2048,128]{2,1,0:T(8,128)(2,1)} custom-call(s32[11]{0:T(128)} %concatenate.27.r_0_.meta, bf16[512,1024]{1,0:T(8,128)(2,1)} %get-tuple-element.216.every, bf16[512,1024]{1,0:T(8,128)(2,1)} %get-tuple-element.218.g_pre, bf16[512,1024]{1,0:T(8,128)(2,1)} %get-tuple-element.219.hidden, bf16[512,1024]{1,0:T(8,128)(2,1)} %get-tuple-element.220.low), custom_call_target="tpu_custom_call" | custom-call | bytes 8388 | tf_op jit(solution)/shard_map/pallas_call | solution.py:492
  253.6 3.7 shard_map.352
  259.0 7.3 %collective-permute-done.47.r_2_ = bf16[128,1024]{1,0:T(8,128)(2,1)S(1)} collective-permute-done((bf16[128,1024]{1,0:T(8,128)(2,1)S(1)}, bf16[128,1024]{1,0:T(8,128)(2,1)S(1)}, u32[]{:S(2)}, u32[]{:S(2)}) %collective-permute-start.47) | collective-permute-done | bytes 262176 | tf_op jit(solution)/shard_map/ppermute | solution.py:48
  268.5 9.9 %shard_map.353 = (bf16[512,1024]{1,0:T(8,128)(2,1)}, bf16[512,768]{1,0:T(8,128)(2,1)}, f32[128,256]{1,0:T(8,128)}, f32[256,128]{1,0:T(8,128)}, f32[8,768]{1,0:T(...) custom-call(s32[11]{0:T(128)} %concatenate.27.r_0_.meta, bf16[128,1024]{1,0:T(8,128)(2,1)} %get-tuple-element.226.r_1_, ...), custom_call_target="tpu_custom_call" | custom-call | flops 5000000 | bytes 10133 | tf_op jit(solution)/shard_map/pallas_call | solution.py:492
  282.6 5.4 %shard_map.354 = bf16[8,1024,128]{2,1,0:T(8,128)(2,1)} custom-call(s32[11]{0:T(128)} %concatenate.27.r_0_.meta, bf16[512,768]{1,0:T(8,128)(2,1)} %get-tuple-element.229.r_1_, bf16[512,1024]{1,0:T(8,128)(2,1)} %get-tuple-element.230.r_2_, bf16[512,256]{1,0:T(8,128)(2,1)} %get-tuple-element.231.r_3_, bf16[512,1024]{1,0:T(8,128)(2,1)} %get-tuple-element.232.r_4_), custom_call_target="tpu_custom_call" | custom-call | bytes 5242 | tf_op jit(solution)/shard_map/pallas_call | solution.py:492
  291.0 3.6 shard_map.355
  296.2 7.0 %collective-permute-done.52.r_2_ = bf16[128,1024]{1,0:T(8,128)(2,1)S(1)} collective-permute-done((bf16[128,1024]{1,0:T(8,128)(2,1)S(1)}, bf16[128,1024]{1,0:T(8,128)(2,1)S(1)}, u32[]{:S(2)}, u32[]{:S(2)}) %collective-permute-start.52) | collective-permute-done | bytes 262176 | tf_op jit(solution)/shard_map/ppermute | solution.py:48
  305.5 8.5 %shard_map.356 = (bf16[512,1024]{1,0:T(8,128)(2,1)}, bf16[512,1024]{1,0:T(8,128)(2,1)}, f32[1,1024]{1,0:T(1,128)}, bf16[2,128,1024]{2,1,0:T(8,128)(2,1)}, f32[2,128,1024]{2,1,0:T(8,128)}) custom-call(s32[11]{0:T(128)} %concatenate.27.r_0_.meta, bf16[128,1024]{1,0:T(8,128)(2,1)} %get-tuple-element.236.r_1_, bf16[128,1024]{1,0:T(8,128)(2,1)} %copy-done.63, ...), custom_call_target="tpu_custom_call" | custom-call | flops 4000000 | bytes 9965 | tf_op jit(solution)/shard_map/pallas_call | solution.py:492
  314.2 6.9 %shard_map.357 = (bf16[4,1024,128]{2,1,0:T(8,128)(2,1)}, bf16[4,1024,128]{2,1,0:T(8,128)(2,1)}, bf16[4,1024,128]{2,1,0:T(8,128)(2,1)}, bf16[4,1024,128]{2,1,0:T(8,128)(2,1)}) custom-call(s32[11]{0:T(128)} %concatenate.27.r_0_.meta, bf16[512,1024]{1,0:T(8,128)(2,1)} %get-tuple-element.200.every, bf16[512,1024]{1,0:T(8,128)(2,1)} %get-tuple-element.238.g_pre, ...), custom_call_target="tpu_custom_call" | custom-call | bytes 8388 | tf_op jit(solution)/shard_map/pallas_call | solution.py:492
  323.4 7.6 %collective-permute-done.57.crossed = bf16[128,1024]{1,0:T(8,128)(2,1)S(1)} collective-permute-done((bf16[128,1024]{1,0:T(8,128)(2,1)S(1)}, bf16[128,1024]{1,0:T(8,128)(2,1)S(1)}, u32[]{:S(2)}, u32[]{:S(2)}) %collective-permute-start.57) | collective-permute-done | bytes 262176 | tf_op jit(solution)/shard_map/ppermute | solution.py:48
  331.7 3.6 shard_map.358
  336.0 7.0 %collective-permute-done.59.r_2_ = bf16[128,1024]{1,0:T(8,128)(2,1)S(1)} collective-permute-done((bf16[128,1024]{1,0:T(8,128)(2,1)}, bf16[128,1024]{1,0:T(8,128)(2,1)S(1)}, u32[]{:S(2)}, u32[]{:S(2)}) %collective-permute-start.59) | collective-permute-done | bytes 262176 | tf_op jit(solution)/shard_map/ppermute | solution.py:48
  343.5 9.4 %collective-permute-done.58.got = bf16[4,1024,128]{2,1,0:T(8,128)(2,1)S(1)} collective-permute-done((bf16[4,1024,128]{2,1,0:T(8,128)(2,1)}, bf16[4,1024,128]{2,1,0:T(8,128)(2,1)S(1)}, u32[]{:S(2)}, u32[]{:S(2)}) %collective-permute-start.58) | collective-permute-done | bytes 1048608 | tf_op jit(solution)/shard_map/ppermute | solution.py:42
  353.9 3.7 shard_map.359
  358.4 10.0 %shard_map.360 = (bf16[512,1024]{1,0:T(8,128)(2,1)}, bf16[512,768]{1,0:T(8,128)(2,1)}, f32[128,256]{1,0:T(8,128)}, f32[256,128]{1,0:T(8,128)}, f32[8,768]{1,0:T(...) custom-call(s32[11]{0:T(128)} %concatenate.27.r_0_.meta, bf16[128,1024]{1,0:T(8,128)(2,1)} %get-tuple-element.251.r_1_, ...), custom_call_target="tpu_custom_call" | custom-call | flops 5000000 | bytes 10264 | tf_op jit(solution)/shard_map/pallas_call | solution.py:492
  368.4 5.5 %shard_map.361 = (bf16[4,1024,128]{2,1,0:T(8,128)(2,1)}, bf16[4,1024,128]{2,1,0:T(8,128)(2,1)}) custom-call(s32[11]{0:T(128)} %concatenate.27.r_0_.meta, bf16[512,768]{1,0:T(8,128)(2,1)} %get-tuple-element.254.r_1_, bf16[512,1024]{1,0:T(8,128)(2,1)} %get-tuple-element.255.r_2_, bf16[512,256]{1,0:T(8,128)(2,1)} %get-tuple-element.256.r_3_, ...), custom_call_target="tpu_custom_call" | custom-call | bytes 5242 | tf_op jit(solution)/shard_map/pallas_call | solution.py:492
  375.4 4.1 collective-permute-start.64
  382.0 5.8 %collective-permute-done.63.crossed = bf16[128,1024]{1,0:T(8,128)(2,1)S(1)} collective-permute-done((bf16[128,1024]{1,0:T(8,128)(2,1)S(1)}, bf16[128,1024]{1,0:T(8,128)(2,1)S(1)}, u32[]{:S(2)}, u32[]{:S(2)}) %collective-permute-start.63) | collective-permute-done | bytes 262176 | tf_op jit(solution)/shard_map/ppermute | solution.py:48
  388.5 3.7 shard_map.362
  392.2 7.6 %collective-permute-done.64.refs_4_ = bf16[2,1024,128]{2,1,0:T(8,128)(2,1)S(1)} collective-permute-done((bf16[2,1024,128]{2,1,0:T(8,128)(2,1)S(1)}, bf16[2,1024,128]{2,1,0:T(8,128)(2,1)S(1)}, u32[]{:S(2)}, u32[]{:S(2)}) %collective-permute-start.64) | collective-permute-done | bytes 524320 | tf_op jit(solution)/shard_map/ppermute | solution.py:1256
  399.8 3.5 shard_map.363
  409.9 6.2 %shard_map.364 = (bf16[4,176,128]{2,1,0:T(8,128)(2,1)}, bf16[4,176,128]{2,1,0:T(8,128)(2,1)}) custom-call(s32[11]{0:T(128)} %concatenate.27.r_0_.meta, f32[1,1024]{1,0:T(1,128)} %get-tuple-element.267.r_1_, f32[1,1024]{1,0:T(1,128)} %get-tuple-element.268.r_2_, f32[8,768]{1,0:T(8,128)} %get-tuple-element.269.r_3_, f32[8,768]{1,0:T(8,128)} %get-tuple-element.270.r_4_, ...), custom_call_target="tpu_custom_call" | custom-call | bytes 5538 | tf_op jit(solution)/shard_map/pallas_call | solution.py:492
  416.7 3.5 shard_map.365
  420.3 3.6 collective-permute-done.69.refs_5_
  427.2 2.8 collective-permute-start.70
  430.2 2.9 collective-permute-start.72
  447.9 3.3 collective-permute-done.77.crossed
  452.4 2.9 shard_map.368
  456.2 4.6 shard_map.369
  461.5 3.1 shard_map.374.r_1_
  471.5 3.7 shard_map.370
  475.2 5.6 %collective-permute-done.83.refs_2_ = bf16[1024,128]{1,0:T(8,128)(2,1)S(1)} collective-permute-done((bf16[1024,128]{1,0:T(8,128)(2,1)S(1)}, bf16[1024,128]{1,0:T(8,128)(2,1)S(1)}, u32[]{:S(2)}, u32[]{:S(2)}) %collective-permute-start.83) | collective-permute-done | bytes 262176 | tf_op jit(solution)/shard_map/ppermute | solution.py:1256
  486.0 6.2 %collective-permute-done.84.r_2_ = bf16[1024,128]{1,0:T(8,128)(2,1)S(1)} collective-permute-done((bf16[1024,128]{1,0:T(8,128)(2,1)}, bf16[1024,128]{1,0:T(8,128)(2,1)S(1)}, u32[]{:S(2)}, u32[]{:S(2)}) %collective-permute-start.84) | collective-permute-done | bytes 262176 | tf_op jit(solution)/shard_map/ppermute | solution.py:48
  495.0 3.7 shard_map.373
  500.3 4.6 shard_map.375
  (480 shorter events, 158.6 us)
Async XLA Ops:
  7.2 396.5 %reduce-scatter.3.cloned.1.call-start = ((), (), s32[]{:S(2)}) async-start(), calls=%async_computation.2 | async-start | bytes 4718592 | tf_op jit(solution)/shard_map/reduce_scatter | solution.py:1298
  14.6 29.2 %collective-permute-start = (bf16[1088,128]{1,0:T(8,128)(2,1)}, bf16[1088,128]{1,0:T(8,128)(2,1)S(1)}, u32[]{:S(2)}, u32[]{:S(2)}) collective-permute-start(bf16[1088,128]{1,0:T(8,128)(2,1)} %get-tuple-element.181), channel_id=1, source_target_pairs={{0,8},{4,12},{8,16},{12,20},{16,24},{20,28},{24,0},{28,4},{1,9},{5... | collective-permute-start | bytes 835592 | tf_op jit(solution)/shard_map/ppermute | solution.py:48
  17.7 26.2 %collective-permute-start.1 = (bf16[1088,128]{1,0:T(8,128)(2,1)}, bf16[1088,128]{1,0:T(8,128)(2,1)S(1)}, u32[]{:S(2)}, u32[]{:S(2)}) collective-permute-start(bf16[1088,128]{1,0:T(8,128)(2,1)} %get-tuple-element.181), channel_id=1, source_target_pairs={{0,16},{4,20},{8,24},{12,28},{16,0},{20,4},{24,8},{28,12},{1,17},{... | collective-permute-start | bytes 835592 | tf_op jit(solution)/shard_map/ppermute | solution.py:48
  20.2 23.6 %collective-permute-start.2 = (bf16[1088,128]{1,0:T(8,128)(2,1)}, bf16[1088,128]{1,0:T(8,128)(2,1)S(1)}, u32[]{:S(2)}, u32[]{:S(2)}) collective-permute-start(bf16[1088,128]{1,0:T(8,128)(2,1)} %get-tuple-element.181), channel_id=1, source_target_pairs={{0,24},{4,28},{8,0},{12,4},{16,8},{20,12},{24,16},{28,20},{1,25},{... | collective-permute-start | bytes 835592 | tf_op jit(solution)/shard_map/ppermute | solution.py:48
  24.4 27.2 %collective-permute-start.10 = (bf16[128,1024]{1,0:T(8,128)(2,1)}, bf16[128,1024]{1,0:T(8,128)(2,1)}, u32[]{:S(2)}, u32[]{:S(2)}) collective-permute-start(bf16[128,1024]{1,0:T(8,128)(2,1)} %get-tuple-element.187.r_1_), channel_id=1, source_target_pairs={{0,2},{1,3},{2,0},{3,1},{4,6},{5,7},{6,4},{7,5},{8,10},{9,11},{10,... | collective-permute-start | bytes 786440 | tf_op jit(solution)/shard_map/ppermute | solution.py:48
  25.9 27.3 %collective-permute-start.13 = (bf16[128,1024]{1,0:T(8,128)(2,1)}, bf16[128,1024]{1,0:T(8,128)(2,1)}, u32[]{:S(2)}, u32[]{:S(2)}) collective-permute-start(bf16[128,1024]{1,0:T(8,128)(2,1)} %get-tuple-element.188.r_1_), channel_id=1, source_target_pairs={{0,2},{1,3},{2,0},{3,1},{4,6},{5,7},{6,4},{7,5},{8,10},{9,11},{10,... | collective-permute-start | bytes 786440 | tf_op jit(solution)/shard_map/ppermute | solution.py:48
  44.0 33.4 %collective-permute-start.16 = (bf16[4,1088,128]{2,1,0:T(8,128)(2,1)S(1)}, bf16[4,1088,128]{2,1,0:T(8,128)(2,1)S(1)}, u32[]{:S(2)}, u32[]{:S(2)}) collective-permute-start(bf16[4,1088,128]{2,1,0:T(8,128)(2,1)S(1)} %pad_maximum_fusion.slab.r_5_), channel_id=1, source_target_pairs={{0,4},{4,0},{8,12},{12,8},{16,20},{20,16},{24,28},{28,24},{1,5},{5... | collective-permute-start | bytes 3342344 | tf_op jit(solution)/shard_map/ppermute | solution.py:42
  47.0 11.1 %collective-permute-start.3 = (bf16[1024,128]{1,0:T(8,128)(2,1)}, bf16[1024,128]{1,0:T(8,128)(2,1)S(1)}, u32[]{:S(2)}, u32[]{:S(2)}) collective-permute-start(bf16[1024,128]{1,0:T(8,128)(2,1)} %get-tuple-element.182), channel_id=1, source_target_pairs={{0,8},{4,12},{8,16},{12,20},{16,24},{20,28},{24,0},{28,4},{1,9},{5... | collective-permute-start | bytes 786440 | tf_op jit(solution)/shard_map/ppermute | solution.py:48
  50.0 16.9 %collective-permute-start.4 = (bf16[1024,128]{1,0:T(8,128)(2,1)}, bf16[1024,128]{1,0:T(8,128)(2,1)}, u32[]{:S(2)}, u32[]{:S(2)}) collective-permute-start(bf16[1024,128]{1,0:T(8,128)(2,1)} %get-tuple-element.182), channel_id=1, source_target_pairs={{0,16},{4,20},{8,24},{12,28},{16,0},{20,4},{24,8},{28,12},{1,17},{... | collective-permute-start | bytes 786440 | tf_op jit(solution)/shard_map/ppermute | solution.py:48
  51.6 15.3 %collective-permute-start.5 = (bf16[1024,128]{1,0:T(8,128)(2,1)}, bf16[1024,128]{1,0:T(8,128)(2,1)}, u32[]{:S(2)}, u32[]{:S(2)}) collective-permute-start(bf16[1024,128]{1,0:T(8,128)(2,1)} %get-tuple-element.182), channel_id=1, source_target_pairs={{0,24},{4,28},{8,0},{12,4},{16,8},{20,12},{24,16},{28,20},{1,25},{... | collective-permute-start | bytes 786440 | tf_op jit(solution)/shard_map/ppermute | solution.py:48
  53.2 16.5 %collective-permute-start.11 = (bf16[128,1024]{1,0:T(8,128)(2,1)}, bf16[128,1024]{1,0:T(8,128)(2,1)}, u32[]{:S(2)}, u32[]{:S(2)}) collective-permute-start(bf16[128,1024]{1,0:T(8,128)(2,1)} %get-tuple-element.187.r_1_), channel_id=1, source_target_pairs={{0,1},{1,0},{2,3},{3,2},{4,5},{5,4},{6,7},{7,6},{8,9},{9,8},{10,11... | collective-permute-start | bytes 786440 | tf_op jit(solution)/shard_map/ppermute | solution.py:42
  58.1 17.3 %collective-permute-start.12 = (bf16[128,1024]{1,0:T(8,128)(2,1)}, bf16[128,1024]{1,0:T(8,128)(2,1)}, u32[]{:S(2)}, u32[]{:S(2)}) collective-permute-start(bf16[128,1024]{1,0:T(8,128)(2,1)} %collective-permute-done.10.r_2_), channel_id=1, source_target_pairs={{0,1},{1,0},{2,3},{3,2},{4,5},{5,4},{6,7},{7,6},{8,9},{9,8},{10,11... | collective-permute-start | bytes 786440 | tf_op jit(solution)/shard_map/ppermute | solution.py:42
  66.9 21.6 %collective-permute-start.14 = (bf16[128,1024]{1,0:T(8,128)(2,1)}, bf16[128,1024]{1,0:T(8,128)(2,1)S(1)}, u32[]{:S(2)}, u32[]{:S(2)}) collective-permute-start(bf16[128,1024]{1,0:T(8,128)(2,1)} %get-tuple-element.188.r_1_), channel_id=1, source_target_pairs={{0,1},{1,0},{2,3},{3,2},{4,5},{5,4},{6,7},{7,6},{8,9},{9,8},{10,11... | collective-permute-start | bytes 786440 | tf_op jit(solution)/shard_map/ppermute | solution.py:42
  66.9 23.5 %collective-permute-start.15 = (bf16[128,1024]{1,0:T(8,128)(2,1)}, bf16[128,1024]{1,0:T(8,128)(2,1)S(1)}, u32[]{:S(2)}, u32[]{:S(2)}) collective-permute-start(bf16[128,1024]{1,0:T(8,128)(2,1)} %collective-permute-done.13.r_2_), channel_id=1, source_target_pairs={{0,1},{1,0},{2,3},{3,2},{4,5},{5,4},{6,7},{7,6},{8,9},{9,8},{10,11... | collective-permute-start | bytes 786440 | tf_op jit(solution)/shard_map/ppermute | solution.py:42
  69.8 28.9 %collective-permute-start.7 = (bf16[1024,128]{1,0:T(8,128)(2,1)}, bf16[1024,128]{1,0:T(8,128)(2,1)}, u32[]{:S(2)}, u32[]{:S(2)}) collective-permute-start(bf16[1024,128]{1,0:T(8,128)(2,1)} %get-tuple-element.184), channel_id=1, source_target_pairs={{0,8},{4,12},{8,16},{12,20},{16,24},{20,28},{24,0},{28,4},{1,9},{5... | collective-permute-start | bytes 786440 | tf_op jit(solution)/shard_map/ppermute | solution.py:48
  75.4 23.3 %collective-permute-start.8 = (bf16[1024,128]{1,0:T(8,128)(2,1)}, bf16[1024,128]{1,0:T(8,128)(2,1)}, u32[]{:S(2)}, u32[]{:S(2)}) collective-permute-start(bf16[1024,128]{1,0:T(8,128)(2,1)} %get-tuple-element.184), channel_id=1, source_target_pairs={{0,16},{4,20},{8,24},{12,28},{16,0},{20,4},{24,8},{28,12},{1,17},{... | collective-permute-start | bytes 786440 | tf_op jit(solution)/shard_map/ppermute | solution.py:48
  77.5 21.2 %collective-permute-start.9 = (bf16[1024,128]{1,0:T(8,128)(2,1)}, bf16[1024,128]{1,0:T(8,128)(2,1)S(1)}, u32[]{:S(2)}, u32[]{:S(2)}) collective-permute-start(bf16[1024,128]{1,0:T(8,128)(2,1)} %get-tuple-element.184), channel_id=1, source_target_pairs={{0,24},{4,28},{8,0},{12,4},{16,8},{20,12},{24,16},{28,20},{1,25},{... | collective-permute-start | bytes 786440 | tf_op jit(solution)/shard_map/ppermute | solution.py:48
  88.5 26.4 %collective-permute-start.6 = (bf16[4,1024,128]{2,1,0:T(8,128)(2,1)}, bf16[4,1024,128]{2,1,0:T(8,128)(2,1)S(1)}, u32[]{:S(2)}, u32[]{:S(2)}) collective-permute-start(bf16[4,1024,128]{2,1,0:T(8,128)(2,1)} %pad_maximum_fusion.1.r_5_), channel_id=1, source_target_pairs={{0,4},{4,0},{8,12},{12,8},{16,20},{20,16},{24,28},{28,24},{1,5},{5... | collective-permute-start | bytes 3145736 | tf_op jit(solution)/shard_map/ppermute | solution.py:42
  100.8 39.2 %collective-permute-start.19 = (bf16[4,1024,128]{2,1,0:T(8,128)(2,1)S(1)}, bf16[4,1024,128]{2,1,0:T(8,128)(2,1)}, u32[]{:S(2)}, u32[]{:S(2)}) collective-permute-start(bf16[4,1024,128]{2,1,0:T(8,128)(2,1)S(1)} %pad_maximum_fusion.2.r_7_), channel_id=1, source_target_pairs={{0,4},{4,0},{8,12},{12,8},{16,20},{20,16},{24,28},{28,24},{1,5},{5... | collective-permute-start | bytes 3145736 | tf_op jit(solution)/shard_map/ppermute | solution.py:42
  103.3 11.5 %collective-permute-start.18 = (bf16[128,1024]{1,0:T(8,128)(2,1)S(1)}, bf16[128,1024]{1,0:T(8,128)(2,1)S(1)}, u32[]{:S(2)}, u32[]{:S(2)}) collective-permute-start(bf16[128,1024]{1,0:T(8,128)(2,1)S(1)} %fusion), channel_id=1, source_target_pairs={{0,2},{1,3},{2,0},{3,1},{4,6},{5,7},{6,4},{7,5},{8,10},{9,11},{10,... | collective-permute-start | bytes 786440 | tf_op jit(solution)/shard_map/ppermute | solution.py:48
  108.0 15.9 %collective-permute-start.20 = (bf16[1024,128]{1,0:T(8,128)(2,1)}, bf16[1024,128]{1,0:T(8,128)(2,1)S(1)}, u32[]{:S(2)}, u32[]{:S(2)}) collective-permute-start(bf16[1024,128]{1,0:T(8,128)(2,1)} %get-tuple-element.197), channel_id=1, source_target_pairs={{0,8},{4,12},{8,16},{12,20},{16,24},{20,28},{24,0},{28,4},{1,9},{5... | collective-permute-start | bytes 786440 | tf_op jit(solution)/shard_map/ppermute | solution.py:48
  120.2 13.0 %collective-permute-start.21 = (bf16[1024,128]{1,0:T(8,128)(2,1)S(1)}, bf16[1024,128]{1,0:T(8,128)(2,1)S(1)}, u32[]{:S(2)}, u32[]{:S(2)}) collective-permute-start(bf16[1024,128]{1,0:T(8,128)(2,1)S(1)} %copy-done.80), channel_id=1, source_target_pairs={{0,16},{4,20},{8,24},{12,28},{16,0},{20,4},{24,8},{28,12},{1,17},{... | collective-permute-start | bytes 786440 | tf_op jit(solution)/shard_map/ppermute | solution.py:48
  121.0 12.2 %collective-permute-start.22 = (bf16[1024,128]{1,0:T(8,128)(2,1)S(1)}, bf16[1024,128]{1,0:T(8,128)(2,1)S(1)}, u32[]{:S(2)}, u32[]{:S(2)}) collective-permute-start(bf16[1024,128]{1,0:T(8,128)(2,1)S(1)} %copy-done.80), channel_id=1, source_target_pairs={{0,24},{4,28},{8,0},{12,4},{16,8},{20,12},{24,16},{28,20},{1,25},{... | collective-permute-start | bytes 786440 | tf_op jit(solution)/shard_map/ppermute | solution.py:48
  123.8 16.8 %collective-permute-start.24 = (bf16[128,1024]{1,0:T(8,128)(2,1)}, bf16[128,1024]{1,0:T(8,128)(2,1)S(1)}, u32[]{:S(2)}, u32[]{:S(2)}) collective-permute-start(bf16[128,1024]{1,0:T(8,128)(2,1)} %get-tuple-element.198.r_1_), channel_id=1, source_target_pairs={{0,1},{1,0},{2,3},{3,2},{4,5},{5,4},{6,7},{7,6},{8,9},{9,8},{10,11... | collective-permute-start | bytes 786440 | tf_op jit(solution)/shard_map/ppermute | solution.py:42
  125.3 16.5 %collective-permute-start.25 = (bf16[128,1024]{1,0:T(8,128)(2,1)S(1)}, bf16[128,1024]{1,0:T(8,128)(2,1)S(1)}, u32[]{:S(2)}, u32[]{:S(2)}) collective-permute-start(bf16[128,1024]{1,0:T(8,128)(2,1)S(1)} %collective-permute-done.23.r_2_), channel_id=1, source_target_pairs={{0,1},{1,0},{2,3},{3,2},{4,5},{5,4},{6,7},{7,6},{8,9},{9,8},{10,11... | collective-permute-start | bytes 786440 | tf_op jit(solution)/shard_map/ppermute | solution.py:42
  133.4 18.0 %collective-permute-start.27 = (bf16[1024,128]{1,0:T(8,128)(2,1)S(1)}, bf16[1024,128]{1,0:T(8,128)(2,1)S(1)}, u32[]{:S(2)}, u32[]{:S(2)}) collective-permute-start(bf16[1024,128]{1,0:T(8,128)(2,1)S(1)} %copy-done.78), channel_id=1, source_target_pairs={{0,8},{4,12},{8,16},{12,20},{16,24},{20,28},{24,0},{28,4},{1,9},{5... | collective-permute-start | bytes 786440 | tf_op jit(solution)/shard_map/ppermute | solution.py:48
  138.2 18.2 %collective-permute-start.28 = (bf16[1024,128]{1,0:T(8,128)(2,1)S(1)}, bf16[1024,128]{1,0:T(8,128)(2,1)S(1)}, u32[]{:S(2)}, u32[]{:S(2)}) collective-permute-start(bf16[1024,128]{1,0:T(8,128)(2,1)S(1)} %copy-done.78), channel_id=1, source_target_pairs={{0,16},{4,20},{8,24},{12,28},{16,0},{20,4},{24,8},{28,12},{1,17},{... | collective-permute-start | bytes 786440 | tf_op jit(solution)/shard_map/ppermute | solution.py:48
  140.0 16.4 %collective-permute-start.29 = (bf16[1024,128]{1,0:T(8,128)(2,1)S(1)}, bf16[1024,128]{1,0:T(8,128)(2,1)S(1)}, u32[]{:S(2)}, u32[]{:S(2)}) collective-permute-start(bf16[1024,128]{1,0:T(8,128)(2,1)S(1)} %copy-done.78), channel_id=1, source_target_pairs={{0,24},{4,28},{8,0},{12,4},{16,8},{20,12},{24,16},{28,20},{1,25},{... | collective-permute-start | bytes 786440 | tf_op jit(solution)/shard_map/ppermute | solution.py:48
  140.7 26.1 %collective-permute-start.26 = (bf16[4,1024,128]{2,1,0:T(8,128)(2,1)S(1)}, bf16[4,1024,128]{2,1,0:T(8,128)(2,1)S(1)}, u32[]{:S(2)}, u32[]{:S(2)}) collective-permute-start(bf16[4,1024,128]{2,1,0:T(8,128)(2,1)S(1)} %pad_maximum_fusion.3.r_5_), channel_id=1, source_target_pairs={{0,4},{4,0},{8,12},{12,8},{16,20},{20,16},{24,28},{28,24},{1,5},{5... | collective-permute-start | bytes 3145736 | tf_op jit(solution)/shard_map/ppermute | solution.py:42
  156.5 39.4 %collective-permute-start.35 = (bf16[4,1024,128]{2,1,0:T(8,128)(2,1)S(1)}, bf16[4,1024,128]{2,1,0:T(8,128)(2,1)S(1)}, u32[]{:S(2)}, u32[]{:S(2)}) collective-permute-start(bf16[4,1024,128]{2,1,0:T(8,128)(2,1)S(1)} %pad_maximum_fusion.4.r_5_), channel_id=1, source_target_pairs={{0,4},{4,0},{8,12},{12,8},{16,20},{20,16},{24,28},{28,24},{1,5},{5... | collective-permute-start | bytes 3145736 | tf_op jit(solution)/shard_map/ppermute | solution.py:42
  157.2 9.6 %collective-permute-start.31 = (bf16[128,1024]{1,0:T(8,128)(2,1)S(1)}, bf16[128,1024]{1,0:T(8,128)(2,1)S(1)}, u32[]{:S(2)}, u32[]{:S(2)}) collective-permute-start(bf16[128,1024]{1,0:T(8,128)(2,1)S(1)} %fusion.1), channel_id=1, source_target_pairs={{0,2},{1,3},{2,0},{3,1},{4,6},{5,7},{6,4},{7,5},{8,10},{9,11},{10,... | collective-permute-start | bytes 786440 | tf_op jit(solution)/shard_map/ppermute | solution.py:48
  157.8 20.6 %collective-permute-start.36 = (bf16[1024,128]{1,0:T(8,128)(2,1)S(1)}, bf16[1024,128]{1,0:T(8,128)(2,1)S(1)}, u32[]{:S(2)}, u32[]{:S(2)}) collective-permute-start(bf16[1024,128]{1,0:T(8,128)(2,1)S(1)} %copy-done.77), channel_id=1, source_target_pairs={{0,8},{4,12},{8,16},{12,20},{16,24},{20,28},{24,0},{28,4},{1,9},{5... | collective-permute-start | bytes 786440 | tf_op jit(solution)/shard_map/ppermute | solution.py:48
  171.0 16.3 %collective-permute-start.37 = (bf16[1024,128]{1,0:T(8,128)(2,1)S(1)}, bf16[1024,128]{1,0:T(8,128)(2,1)S(1)}, u32[]{:S(2)}, u32[]{:S(2)}) collective-permute-start(bf16[1024,128]{1,0:T(8,128)(2,1)S(1)} %copy-done.77), channel_id=1, source_target_pairs={{0,16},{4,20},{8,24},{12,28},{16,0},{20,4},{24,8},{28,12},{1,17},{... | collective-permute-start | bytes 786440 | tf_op jit(solution)/shard_map/ppermute | solution.py:48
  174.5 12.8 %collective-permute-start.38 = (bf16[1024,128]{1,0:T(8,128)(2,1)S(1)}, bf16[1024,128]{1,0:T(8,128)(2,1)S(1)}, u32[]{:S(2)}, u32[]{:S(2)}) collective-permute-start(bf16[1024,128]{1,0:T(8,128)(2,1)S(1)} %copy-done.77), channel_id=1, source_target_pairs={{0,24},{4,28},{8,0},{12,4},{16,8},{20,12},{24,16},{28,20},{1,25},{... | collective-permute-start | bytes 786440 | tf_op jit(solution)/shard_map/ppermute | solution.py:48
  178.4 9.2 %collective-permute-start.33 = (bf16[128,1024]{1,0:T(8,128)(2,1)}, bf16[128,1024]{1,0:T(8,128)(2,1)S(1)}, u32[]{:S(2)}, u32[]{:S(2)}) collective-permute-start(bf16[128,1024]{1,0:T(8,128)(2,1)} %get-tuple-element.209.r_1_), channel_id=1, source_target_pairs={{0,1},{1,0},{2,3},{3,2},{4,5},{5,4},{6,7},{7,6},{8,9},{9,8},{10,11... | collective-permute-start | bytes 786440 | tf_op jit(solution)/shard_map/ppermute | solution.py:42
  178.4 9.2 %collective-permute-start.34 = (bf16[128,1024]{1,0:T(8,128)(2,1)S(1)}, bf16[128,1024]{1,0:T(8,128)(2,1)S(1)}, u32[]{:S(2)}, u32[]{:S(2)}) collective-permute-start(bf16[128,1024]{1,0:T(8,128)(2,1)S(1)} %collective-permute-done.32.r_2_), channel_id=1, source_target_pairs={{0,1},{1,0},{2,3},{3,2},{4,5},{5,4},{6,7},{7,6},{8,9},{9,8},{10,11... | collective-permute-start | bytes 786440 | tf_op jit(solution)/shard_map/ppermute | solution.py:42
  196.0 25.6 %collective-permute-start.44 = (bf16[4,1024,128]{2,1,0:T(8,128)(2,1)S(1)}, bf16[4,1024,128]{2,1,0:T(8,128)(2,1)S(1)}, u32[]{:S(2)}, u32[]{:S(2)}) collective-permute-start(bf16[4,1024,128]{2,1,0:T(8,128)(2,1)S(1)} %pad_maximum_fusion.5.r_7_), channel_id=1, source_target_pairs={{0,4},{4,0},{8,12},{12,8},{16,20},{20,16},{24,28},{28,24},{1,5},{5... | collective-permute-start | bytes 3145736 | tf_op jit(solution)/shard_map/ppermute | solution.py:42
  199.4 8.4 %collective-permute-start.40 = (bf16[128,1024]{1,0:T(8,128)(2,1)S(1)}, bf16[128,1024]{1,0:T(8,128)(2,1)S(1)}, u32[]{:S(2)}, u32[]{:S(2)}) collective-permute-start(bf16[128,1024]{1,0:T(8,128)(2,1)S(1)} %fusion.2), channel_id=1, source_target_pairs={{0,2},{1,3},{2,0},{3,1},{4,6},{5,7},{6,4},{7,5},{8,10},{9,11},{10,... | collective-permute-start | bytes 786440 | tf_op jit(solution)/shard_map/ppermute | solution.py:48
  213.1 8.5 %collective-permute-start.42 = (bf16[128,1024]{1,0:T(8,128)(2,1)}, bf16[128,1024]{1,0:T(8,128)(2,1)S(1)}, u32[]{:S(2)}, u32[]{:S(2)}) collective-permute-start(bf16[128,1024]{1,0:T(8,128)(2,1)} %get-tuple-element.215.r_1_), channel_id=1, source_target_pairs={{0,1},{1,0},{2,3},{3,2},{4,5},{5,4},{6,7},{7,6},{8,9},{9,8},{10,11... | collective-permute-start | bytes 786440 | tf_op jit(solution)/shard_map/ppermute | solution.py:42
  243.7 9.1 %collective-permute-start.46 = (bf16[128,1024]{1,0:T(8,128)(2,1)S(1)}, bf16[128,1024]{1,0:T(8,128)(2,1)S(1)}, u32[]{:S(2)}, u32[]{:S(2)}) collective-permute-start(bf16[128,1024]{1,0:T(8,128)(2,1)S(1)} %fusion.3), channel_id=1, source_target_pairs={{0,2},{1,3},{2,0},{3,1},{4,6},{5,7},{6,4},{7,5},{8,10},{9,11},{10,... | collective-permute-start | bytes 786440 | tf_op jit(solution)/shard_map/ppermute | solution.py:48
  257.2 190.6 %reduce-scatter.5.cloned.1.call-start = ((), (), s32[]{:S(2)}) async-start(), calls=%async_computation.3 | async-start | bytes 2359296 | tf_op jit(solution)/shard_map/reduce_scatter | solution.py:1325
  281.9 8.4 %collective-permute-start.51 = (bf16[128,1024]{1,0:T(8,128)(2,1)S(1)}, bf16[128,1024]{1,0:T(8,128)(2,1)S(1)}, u32[]{:S(2)}, u32[]{:S(2)}) collective-permute-start(bf16[128,1024]{1,0:T(8,128)(2,1)S(1)} %fusion.4), channel_id=1, source_target_pairs={{0,2},{1,3},{2,0},{3,1},{4,6},{5,7},{6,4},{7,5},{8,10},{9,11},{10,... | collective-permute-start | bytes 786440 | tf_op jit(solution)/shard_map/ppermute | solution.py:48
  314.0 8.5 %collective-permute-start.56 = (bf16[2,128,1024]{2,1,0:T(8,128)(2,1)}, bf16[2,128,1024]{2,1,0:T(8,128)(2,1)S(1)}, u32[]{:S(2)}, u32[]{:S(2)}) collective-permute-start(bf16[2,128,1024]{2,1,0:T(8,128)(2,1)} %get-tuple-element.247), channel_id=1, source_target_pairs={{0,1},{1,0},{2,3},{3,2},{4,5},{5,4},{6,7},{7,6},{8,9},{9,8},{10,11... | collective-permute-start | bytes 1572872 | tf_op jit(solution)/shard_map/ppermute | solution.py:42
  321.1 31.8 %collective-permute-start.58 = (bf16[4,1024,128]{2,1,0:T(8,128)(2,1)}, bf16[4,1024,128]{2,1,0:T(8,128)(2,1)S(1)}, u32[]{:S(2)}, u32[]{:S(2)}) collective-permute-start(bf16[4,1024,128]{2,1,0:T(8,128)(2,1)} %get-tuple-element.244), channel_id=1, source_target_pairs={{0,4},{4,0},{8,12},{12,8},{16,20},{20,16},{24,28},{28,24},{1,5},{5... | collective-permute-start | bytes 3145736 | tf_op jit(solution)/shard_map/ppermute | solution.py:42
  322.6 8.3 %collective-permute-start.57 = (bf16[128,1024]{1,0:T(8,128)(2,1)S(1)}, bf16[128,1024]{1,0:T(8,128)(2,1)S(1)}, u32[]{:S(2)}, u32[]{:S(2)}) collective-permute-start(bf16[128,1024]{1,0:T(8,128)(2,1)S(1)} %fusion.5), channel_id=1, source_target_pairs={{0,2},{1,3},{2,0},{3,1},{4,6},{5,7},{6,4},{7,5},{8,10},{9,11},{10,... | collective-permute-start | bytes 786440 | tf_op jit(solution)/shard_map/ppermute | solution.py:48
  336.0 21.6 %collective-permute-start.60 = (bf16[128,1024]{1,0:T(8,128)(2,1)}, bf16[128,1024]{1,0:T(8,128)(2,1)S(1)}, u32[]{:S(2)}, u32[]{:S(2)}) collective-permute-start(bf16[128,1024]{1,0:T(8,128)(2,1)} %get-tuple-element.251.r_1_), channel_id=1, source_target_pairs={{0,1},{1,0},{2,3},{3,2},{4,5},{5,4},{6,7},{7,6},{8,9},{9,8},{10,11... | collective-permute-start | bytes 786440 | tf_op jit(solution)/shard_map/ppermute | solution.py:42
  343.0 14.6 %collective-permute-start.61 = (bf16[128,1024]{1,0:T(8,128)(2,1)S(1)}, bf16[128,1024]{1,0:T(8,128)(2,1)S(1)}, u32[]{:S(2)}, u32[]{:S(2)}) collective-permute-start(bf16[128,1024]{1,0:T(8,128)(2,1)S(1)} %collective-permute-done.59.r_2_), channel_id=1, source_target_pairs={{0,1},{1,0},{2,3},{3,2},{4,5},{5,4},{6,7},{7,6},{8,9},{9,8},{10,11... | collective-permute-start | bytes 786440 | tf_op jit(solution)/shard_map/ppermute | solution.py:42
  343.0 49.2 %collective-permute-start.55 = (bf16[4,1024,128]{2,1,0:T(8,128)(2,1)}, bf16[4,1024,128]{2,1,0:T(8,128)(2,1)}, u32[]{:S(2)}, u32[]{:S(2)}) collective-permute-start(bf16[4,1024,128]{2,1,0:T(8,128)(2,1)} %get-tuple-element.242), channel_id=1, source_target_pairs={{0,4},{4,0},{8,12},{12,8},{16,20},{20,16},{24,28},{28,24},{1,5},{5... | collective-permute-start | bytes 3145736 | tf_op jit(solution)/shard_map/ppermute | solution.py:42
  368.3 11.2 %collective-permute-start.62 = (bf16[2,128,1024]{2,1,0:T(8,128)(2,1)}, bf16[2,128,1024]{2,1,0:T(8,128)(2,1)S(1)}, u32[]{:S(2)}, u32[]{:S(2)}) collective-permute-start(bf16[2,128,1024]{2,1,0:T(8,128)(2,1)} %get-tuple-element.261), channel_id=1, source_target_pairs={{0,1},{1,0},{2,3},{3,2},{4,5},{5,4},{6,7},{7,6},{8,9},{9,8},{10,11... | collective-permute-start | bytes 1572872 | tf_op jit(solution)/shard_map/ppermute | solution.py:42
  374.0 42.1 %collective-permute-start.65 = (bf16[4,1024,128]{2,1,0:T(8,128)(2,1)}, bf16[4,1024,128]{2,1,0:T(8,128)(2,1)}, u32[]{:S(2)}, u32[]{:S(2)}) collective-permute-start(bf16[4,1024,128]{2,1,0:T(8,128)(2,1)} %get-tuple-element.258), channel_id=1, source_target_pairs={{0,4},{4,0},{8,12},{12,8},{16,20},{20,16},{24,28},{28,24},{1,5},{5... | collective-permute-start | bytes 3145736 | tf_op jit(solution)/shard_map/ppermute | solution.py:42
  375.4 24.4 %collective-permute-start.64 = (bf16[2,1024,128]{2,1,0:T(8,128)(2,1)S(1)}, bf16[2,1024,128]{2,1,0:T(8,128)(2,1)S(1)}, u32[]{:S(2)}, u32[]{:S(2)}) collective-permute-start(bf16[2,1024,128]{2,1,0:T(8,128)(2,1)S(1)} %copy-done.111), channel_id=1, source_target_pairs={{0,8},{4,12},{8,0},{12,4},{16,24},{20,28},{24,16},{28,20},{1,9},{5... | collective-permute-start | bytes 1572872 | tf_op jit(solution)/shard_map/ppermute | solution.py:1256
  382.0 56.9 %collective-permute-start.76 = (bf16[2,128,1024]{2,1,0:T(8,128)(2,1)}, bf16[2,128,1024]{2,1,0:T(8,128)(2,1)S(1)}, u32[]{:S(2)}, u32[]{:S(2)}) collective-permute-start(bf16[2,128,1024]{2,1,0:T(8,128)(2,1)} %get-tuple-element.294), channel_id=1, source_target_pairs={{0,1},{1,0},{2,3},{3,2},{4,5},{5,4},{6,7},{7,6},{8,9},{9,8},{10,11... | collective-permute-start | bytes 1572872 | tf_op jit(solution)/shard_map/ppermute | solution.py:42
  403.3 36.8 %collective-permute-start.87 = (bf16[2,1024,128]{2,1,0:T(8,128)(2,1)}, bf16[2,1024,128]{2,1,0:T(8,128)(2,1)S(1)}, u32[]{:S(2)}, u32[]{:S(2)}) collective-permute-start(bf16[2,1024,128]{2,1,0:T(8,128)(2,1)} %get-tuple-element.330), channel_id=1, source_target_pairs={{0,8},{4,12},{8,0},{12,4},{16,24},{20,28},{24,16},{28,20},{1,9},{5... | collective-permute-start | bytes 1572872 | tf_op jit(solution)/shard_map/ppermute | solution.py:1256
  403.7 20.5 %collective-permute-start.68 = (bf16[2048,128]{1,0:T(8,128)(2,1)}, bf16[2048,128]{1,0:T(8,128)(2,1)S(1)}, u32[]{:S(2)}, u32[]{:S(2)}) collective-permute-start(bf16[2048,128]{1,0:T(8,128)(2,1)} %bitcast.166), channel_id=1, source_target_pairs={{0,2},{1,3},{2,0},{3,1},{4,6},{5,7},{6,4},{7,5},{8,10},{9,11},{10,... | collective-permute-start | bytes 1572872 | tf_op jit(solution)/shard_map/ppermute | solution.py:48
  406.1 17.8 %collective-permute-start.69 = (bf16[1024,128]{1,0:T(8,128)(2,1)}, bf16[1024,128]{1,0:T(8,128)(2,1)S(1)}, u32[]{:S(2)}, u32[]{:S(2)}) collective-permute-start(bf16[1024,128]{1,0:T(8,128)(2,1)} %fusion.7), channel_id=1, source_target_pairs={{0,16},{4,20},{8,24},{12,28},{16,0},{20,4},{24,8},{28,12},{1,17},{... | collective-permute-start | bytes 786440 | tf_op jit(solution)/shard_map/ppermute | solution.py:1256
  434.4 21.0 %collective-permute-start.66 = (bf16[2,1024,128]{2,1,0:T(8,128)(2,1)}, bf16[2,1024,128]{2,1,0:T(8,128)(2,1)S(1)}, u32[]{:S(2)}, u32[]{:S(2)}) collective-permute-start(bf16[2,1024,128]{2,1,0:T(8,128)(2,1)} %get-tuple-element.282), channel_id=1, source_target_pairs={{0,8},{4,12},{8,0},{12,4},{16,24},{20,28},{24,16},{28,20},{1,9},{5... | collective-permute-start | bytes 1572872 | tf_op jit(solution)/shard_map/ppermute | solution.py:1256
  435.9 19.4 %collective-permute-start.78 = (bf16[2048,128]{1,0:T(8,128)(2,1)S(1)}, bf16[2048,128]{1,0:T(8,128)(2,1)S(1)}, u32[]{:S(2)}, u32[]{:S(2)}) collective-permute-start(bf16[2048,128]{1,0:T(8,128)(2,1)S(1)} %bitcast.168), channel_id=1, source_target_pairs={{0,1},{1,0},{2,3},{3,2},{4,5},{5,4},{6,7},{7,6},{8,9},{9,8},{10,11... | collective-permute-start | bytes 1572872 | tf_op jit(solution)/shard_map/ppermute | solution.py:42
  436.1 19.3 %collective-permute-start.79 = (bf16[2048,128]{1,0:T(8,128)(2,1)S(1)}, bf16[2048,128]{1,0:T(8,128)(2,1)}, u32[]{:S(2)}, u32[]{:S(2)}) collective-permute-start(bf16[2048,128]{1,0:T(8,128)(2,1)S(1)} %collective-permute-done.68.r_2_), channel_id=1, source_target_pairs={{0,1},{1,0},{2,3},{3,2},{4,5},{5,4},{6,7},{7,6},{8,9},{9,8},{10,11... | collective-permute-start | bytes 1572872 | tf_op jit(solution)/shard_map/ppermute | solution.py:42
  446.3 15.2 %collective-permute-start.88 = (bf16[1024,128]{1,0:T(8,128)(2,1)}, bf16[1024,128]{1,0:T(8,128)(2,1)}, u32[]{:S(2)}, u32[]{:S(2)}) collective-permute-start(bf16[1024,128]{1,0:T(8,128)(2,1)} %fusion.10), channel_id=1, source_target_pairs={{0,16},{4,20},{8,24},{12,28},{16,0},{20,4},{24,8},{28,12},{1,17},{... | collective-permute-start | bytes 786440 | tf_op jit(solution)/shard_map/ppermute | solution.py:1256
  451.2 14.1 %collective-permute-start.80 = (bf16[1024,128]{1,0:T(8,128)(2,1)}, bf16[1024,128]{1,0:T(8,128)(2,1)S(1)}, u32[]{:S(2)}, u32[]{:S(2)}) collective-permute-start(bf16[1024,128]{1,0:T(8,128)(2,1)} %bitcast.175), channel_id=1, source_target_pairs={{0,2},{1,3},{2,0},{3,1},{4,6},{5,7},{6,4},{7,5},{8,10},{9,11},{10,... | collective-permute-start | bytes 786440 | tf_op jit(solution)/shard_map/ppermute | solution.py:48
  464.6 20.8 %collective-permute-start.89 = (bf16[2048,128]{1,0:T(8,128)(2,1)}, bf16[2048,128]{1,0:T(8,128)(2,1)S(1)}, u32[]{:S(2)}, u32[]{:S(2)}) collective-permute-start(bf16[2048,128]{1,0:T(8,128)(2,1)} %shard_map.374.r_1_), channel_id=1, source_target_pairs={{0,2},{1,3},{2,0},{3,1},{4,6},{5,7},{6,4},{7,5},{8,10},{9,11},{10,... | collective-permute-start | bytes 1572872 | tf_op jit(solution)/shard_map/ppermute | solution.py:48
  465.9 14.9 %collective-permute-start.83 = (bf16[1024,128]{1,0:T(8,128)(2,1)S(1)}, bf16[1024,128]{1,0:T(8,128)(2,1)S(1)}, u32[]{:S(2)}, u32[]{:S(2)}) collective-permute-start(bf16[1024,128]{1,0:T(8,128)(2,1)S(1)} %fusion.9), channel_id=1, source_target_pairs={{0,16},{4,20},{8,24},{12,28},{16,0},{20,4},{24,8},{28,12},{1,17},{... | collective-permute-start | bytes 786440 | tf_op jit(solution)/shard_map/ppermute | solution.py:1256
  485.4 13.3 %collective-permute-start.90 = (bf16[2048,128]{1,0:T(8,128)(2,1)S(1)}, bf16[2048,128]{1,0:T(8,128)(2,1)S(1)}, u32[]{:S(2)}, u32[]{:S(2)}) collective-permute-start(bf16[2048,128]{1,0:T(8,128)(2,1)S(1)} %copy-done.22), channel_id=1, source_target_pairs={{0,1},{1,0},{2,3},{3,2},{4,5},{5,4},{6,7},{7,6},{8,9},{9,8},{10,11... | collective-permute-start | bytes 1572872 | tf_op jit(solution)/shard_map/ppermute | solution.py:42
  485.4 13.3 %collective-permute-start.91 = (bf16[2048,128]{1,0:T(8,128)(2,1)S(1)}, bf16[2048,128]{1,0:T(8,128)(2,1)S(1)}, u32[]{:S(2)}, u32[]{:S(2)}) collective-permute-start(bf16[2048,128]{1,0:T(8,128)(2,1)S(1)} %collective-permute-done.89.r_2_), channel_id=1, source_target_pairs={{0,1},{1,0},{2,3},{3,2},{4,5},{5,4},{6,7},{7,6},{8,9},{9,8},{10,11... | collective-permute-start | bytes 1572872 | tf_op jit(solution)/shard_map/ppermute | solution.py:42
  (142 other events, 1500.2 us)
Sparse Core Ops, SparseCore 0:
  257.4 96.6 reduce-scatter.2
  358.5 77.7 reduce-scatter.4
